TPU v7x, 32 devices: a whole 2x2x4 slice. The times are simulated.
32 devices in a mesh: section: 8 (over z, core), dp: 4 (over y, x).
Axes of the slice: x: 2, y: 2, z: 4, core: 2. Of those that a mesh axis runs over, the one named last changes fastest.
Arguments:
- section_inputs: bfloat16 [8, 512, 4096], P('section', 'dp'), may hold values from -6 to 6
- norm_gain: bfloat16 [8, 4096], P('section'), may hold values from 0.5 to 1.5
- down_proj: bfloat16 [8, 4096, 256], P('section', 'dp'), may hold values from -0.09375 to 0.09375
- up_proj: bfloat16 [8, 256, 4096], P('section', None, 'dp'), may hold values from -0.1875 to 0.1875
- readout_matrix: bfloat16 [4096, 128], P('dp'), may hold values from -0.09375 to 0.09375
- ground_truth_series: float32 [512, 128], P('dp'), may hold values from -6 to 6
- valid_len: int32 [32], P('dp'), may hold values from 1 to 16
Outputs:
- input_grads: bfloat16 [8, 512, 4096], P('section', 'dp')
- down_grads: bfloat16 [8, 4096, 256], P('section', 'dp')
- up_grads: bfloat16 [8, 256, 4096], P('section', None, 'dp')
All inputs are finite; a program needn't handle non-finite values.
Results may differ from a plain program's by a relative error of at most 0.035.
Values may be sent and summed in bfloat16 or wider, within the bound.
No kernel may reach another device: no remote copies, remote signals or barrier semaphores. Data moves between devices by JAX's collectives and lax.ppermute only.
A program may use at most 64 MiB of HBM per device.

v0:
```python
import jax
import jax.numpy as jnp
from jax import lax
from jax.sharding import PartitionSpec as P

EPSILON = 1e-05


def from_behind(block, axis, distance):
    devices = range(lax.axis_size(axis))
    route = [(i - distance, i) for i in devices if i - distance in devices]
    return lax.ppermute(block, axis, route)


def normalize(inputs, gain_row):
    values = inputs.astype(jnp.float32)
    inverse = lax.rsqrt(jnp.mean(values * values, axis=-1, keepdims=True) + EPSILON)
    unit = values * inverse
    normed = (unit * gain_row.astype(jnp.float32)).astype(jnp.bfloat16)
    return (inverse, unit, normed)


def multiply_trailing_factor(left, right):
    return lax.dot_general(
        left, right, (((1,), (1,)), ((), ())), preferred_element_type=jnp.float32
    )


def contract_rows(left, right):
    return lax.dot_general(
        left, right, (((0,), (0,)), ((), ())), preferred_element_type=jnp.float32
    )


def block_backward(inverse, unit, latent, gain_row, down_full, up_full, arriving_gradient):
    sigmoid = jax.nn.sigmoid(latent)
    hidden_grad = multiply_trailing_factor(arriving_gradient, up_full)
    latent_grad = (hidden_grad * sigmoid * (1.0 + latent * (1.0 - sigmoid))).astype(jnp.bfloat16)
    scaled = multiply_trailing_factor(latent_grad, down_full) * gain_row.astype(jnp.float32)
    inputs_grad = arriving_gradient.astype(jnp.float32) + inverse * (
        scaled - unit * jnp.mean(scaled * unit, axis=-1, keepdims=True)
    )
    return (inputs_grad.astype(jnp.bfloat16), latent_grad)


def per_device(
    section_inputs, norm_gain, down_proj, up_proj, readout_matrix, ground_truth_series, valid_len
):
    down_full, up_full, entire_readout_matrix = (
        lax.all_gather(down_proj[0], "dp", axis=0, tiled=True),
        lax.all_gather(up_proj[0], "dp", axis=1, tiled=True),
        lax.all_gather(readout_matrix, "dp", axis=0, tiled=True),
    )
    inputs = section_inputs[0]
    gain_row = norm_gain[0]
    microbatch_count = valid_len.shape[0]
    token_count = inputs.shape[0]
    row_count = token_count // microbatch_count
    width = inputs.shape[1]
    latent_width = down_full.shape[1]
    inverse, unit, normed = normalize(inputs, gain_row)
    latent = jnp.dot(normed, down_full, preferred_element_type=jnp.float32)
    activated = jax.nn.silu(latent).astype(jnp.bfloat16)
    section_index = lax.axis_index("section")
    section_last = lax.axis_size("section") - 1
    observed_entry_indicator = (
        (jnp.arange(row_count)[None, :] < valid_len[:, None])
        .astype(jnp.float32)
        .reshape(token_count)
    )

    def loss_grad(unused):
        adapter_output = (
            inputs.astype(jnp.float32)
            + jnp.dot(activated, up_full, preferred_element_type=jnp.float32)
        ).astype(jnp.bfloat16)
        estimated_horizon = jnp.dot(
            adapter_output, entire_readout_matrix, preferred_element_type=jnp.float32
        )
        prediction_discrepancy = (
            observed_entry_indicator[:, None] * (estimated_horizon - ground_truth_series)
        ).astype(jnp.bfloat16)
        return multiply_trailing_factor(prediction_discrepancy, entire_readout_matrix).astype(
            jnp.bfloat16
        )

    def no_loss(unused):
        return jnp.zeros((token_count, width), jnp.bfloat16)

    top_grads = lax.cond(section_index == section_last, loss_grad, no_loss, 0).reshape(
        microbatch_count, row_count, width
    )
    inverse_micro = inverse.reshape(microbatch_count, row_count, 1)
    unit_micro = unit.reshape(microbatch_count, row_count, width)
    latent_micro = latent.reshape(microbatch_count, row_count, latent_width)

    def tick(tick_num, carry):
        outgoing, grads_in, latent_grads, cotangents = carry
        received = from_behind(outgoing, "section", -1)
        micro_num = tick_num - (section_last - section_index)
        is_valid = (micro_num >= 0) & (micro_num < microbatch_count)
        picked = jnp.clip(micro_num, 0, microbatch_count - 1)

        def process(state):
            arrived, grads_prev, latent_prev, cotangent_prev = state
            top_piece = lax.dynamic_index_in_dim(top_grads, picked, 0, keepdims=False)
            arriving_gradient = jnp.where(section_index == section_last, top_piece, arrived)
            inputs_grad, latent_grad = block_backward(
                lax.dynamic_index_in_dim(inverse_micro, picked, 0, keepdims=False),
                lax.dynamic_index_in_dim(unit_micro, picked, 0, keepdims=False),
                lax.dynamic_index_in_dim(latent_micro, picked, 0, keepdims=False),
                gain_row,
                down_full,
                up_full,
                arriving_gradient,
            )
            grads_next = lax.dynamic_update_index_in_dim(grads_prev, inputs_grad, picked, 0)
            latent_next = lax.dynamic_update_index_in_dim(latent_prev, latent_grad, picked, 0)
            cotangent_next = lax.dynamic_update_index_in_dim(
                cotangent_prev, arriving_gradient, picked, 0
            )
            return (inputs_grad, grads_next, latent_next, cotangent_next)

        def skipped(state):
            return state

        return lax.cond(is_valid, process, skipped, (received, grads_in, latent_grads, cotangents))

    initial = (
        jnp.zeros((row_count, width), jnp.bfloat16),
        jnp.zeros((microbatch_count, row_count, width), jnp.bfloat16),
        jnp.zeros((microbatch_count, row_count, latent_width), jnp.bfloat16),
        jnp.zeros((microbatch_count, row_count, width), jnp.bfloat16),
    )
    tick_total = lax.axis_size("section") + microbatch_count - 1
    final_state = lax.fori_loop(0, tick_total, tick, initial)
    grads_in = final_state[1].reshape(1, token_count, width)
    latent_grads = final_state[2].reshape(token_count, latent_width)
    cotangents = final_state[3].reshape(token_count, width)
    activated_all, latent_all = (
        lax.all_gather(activated, "dp", axis=0, tiled=True),
        lax.all_gather(latent_grads, "dp", axis=0, tiled=True),
    )
    normed_cols, cotangent_cols = (
        lax.all_to_all(normed, "dp", split_axis=1, concat_axis=0, tiled=True),
        lax.all_to_all(cotangents, "dp", split_axis=1, concat_axis=0, tiled=True),
    )
    down_sum = contract_rows(normed_cols, latent_all)
    up_sum = contract_rows(activated_all, cotangent_cols)
    down_grads = down_sum.astype(jnp.bfloat16)[None]
    up_grads = up_sum.astype(jnp.bfloat16)[None]
    return (grads_in, down_grads, up_grads)


def solution(mesh):
    placed = (
        P("section", "dp", None),
        P("section", None),
        P("section", "dp", None),
        P("section", None, "dp"),
        P("dp", None),
        P("dp", None),
        P("dp"),
    )
    return jax.shard_map(
        per_device,
        mesh=mesh,
        in_specs=placed,
        out_specs=(P("section", "dp", None), P("section", "dp", None), P("section", None, "dp")),
        check_vma=False,
    )
```

profile of v0, /device:TPU:0, one launch (start us, length us, event | category | flops | bytes accessed | tf_op | source)
XLA Modules:
  0.0 333.2 jit_solution(3427100317179303807)
XLA Ops:
  12.8 5.2 %all-to-all-start = ((bf16[128,4,1024]{0,2,1:T(8,128)(2,1)}), bf16[128,4,1024]{0,2,1:T(8,128)(2,1)}, u32[]{:S(2)}, u32[]{:S(2)}) async-start(bf16[128,4,1024]{0,2,1:T(8,128)(2,1)} %multiply_convert_fusion), calls=%async_computation | async-start | bytes 2097152 | tf_op jit(solution)/shard_map/all_to_all | solution.py:145
  20.1 37.4 %all-gather.8.cloned.1.call-done = bf16[1,4096,256]{2,1,0:T(8,128)(2,1)} async-done(((bf16[1,1024,256]{2,1,0:T(8,128)(2,1)}), bf16[1,4096,256]{2,1,0:T(8,128)(2,1)}) %all-gather.8.cloned.1.call-update) | async-done | bytes 2097168 | tf_op jit(solution)/shard_map/all_gather | solution.py:50
  57.4 2.8 multiply_convert_fusion.1
  60.2 25.7 %all-gather.6.cloned.1.call-done = bf16[4096,128]{1,0:T(8,128)(2,1)} async-done(((bf16[1024,128]{1,0:T(8,128)(2,1)}), bf16[4096,128]{1,0:T(8,128)(2,1)}) %all-gather.6.cloned.1.call-update) | async-done | bytes 1048592 | tf_op jit(solution)/shard_map/all_gather | solution.py:52
  85.9 37.2 %all-gather.10.cloned.1.call-done = bf16[1,256,4096]{2,1,0:T(8,128)(2,1)} async-done(((bf16[1,256,1024]{2,1,0:T(8,128)(2,1)}), bf16[1,256,4096]{2,1,0:T(8,128)(2,1)}) %all-gather.10.cloned.1.call-update) | async-done | bytes 2097168 | tf_op jit(solution)/shard_map/all_gather | solution.py:51
  125.5 168.2 %while.20 = (s32[]{:T(128)}, bf16[16,4096]{1,0:T(8,128)(2,1)S(1)}, bf16[8,16,4096]{2,1,0:T(8,128)(2,1)}, bf16[8,16,256]{2,1,0:T(8,128)(2,1)S(1)}, bf16[8,16,4096...) while((s32[]{:T(128)}, bf16[16,4096]{1,0:T(8,128)(2,1)S(1)}, ...), condition=%wide.region_7.8_spmd, body=%wide.region_3.7_spmd.sunk | while | flops 67805192 | bytes 15549357 | solution.py:136
  126.9 1.9 collective-permute-done
  130.1 4.3 %collective-permute-done = bf16[16,4096]{1,0:T(8,128)(2,1)S(1)} collective-permute-done((bf16[16,4096]{1,0:T(8,128)(2,1)S(1)}, bf16[16,4096]{1,0:T(8,128)(2,1)S(1)}, u32[]{:S(2)}, u32[]{:S(2)}) %collective-permute-start) | collective-permute-done | bytes 131104 | tf_op jit(solution)/shard_map/while/body/eval_jaxpr/ppermute | solution.py:12
  135.8 5.0 %collective-permute-done = bf16[16,4096]{1,0:T(8,128)(2,1)S(1)} collective-permute-done((bf16[16,4096]{1,0:T(8,128)(2,1)S(1)}, bf16[16,4096]{1,0:T(8,128)(2,1)S(1)}, u32[]{:S(2)}, u32[]{:S(2)}) %collective-permute-start) | collective-permute-done | bytes 131104 | tf_op jit(solution)/shard_map/while/body/eval_jaxpr/ppermute | solution.py:12
  142.1 5.0 %collective-permute-done = bf16[16,4096]{1,0:T(8,128)(2,1)S(1)} collective-permute-done((bf16[16,4096]{1,0:T(8,128)(2,1)S(1)}, bf16[16,4096]{1,0:T(8,128)(2,1)S(1)}, u32[]{:S(2)}, u32[]{:S(2)}) %collective-permute-start) | collective-permute-done | bytes 131104 | tf_op jit(solution)/shard_map/while/body/eval_jaxpr/ppermute | solution.py:12
  148.5 5.0 %collective-permute-done = bf16[16,4096]{1,0:T(8,128)(2,1)S(1)} collective-permute-done((bf16[16,4096]{1,0:T(8,128)(2,1)S(1)}, bf16[16,4096]{1,0:T(8,128)(2,1)S(1)}, u32[]{:S(2)}, u32[]{:S(2)}) %collective-permute-start) | collective-permute-done | bytes 131104 | tf_op jit(solution)/shard_map/while/body/eval_jaxpr/ppermute | solution.py:12
  154.8 5.0 %collective-permute-done = bf16[16,4096]{1,0:T(8,128)(2,1)S(1)} collective-permute-done((bf16[16,4096]{1,0:T(8,128)(2,1)S(1)}, bf16[16,4096]{1,0:T(8,128)(2,1)S(1)}, u32[]{:S(2)}, u32[]{:S(2)}) %collective-permute-start) | collective-permute-done | bytes 131104 | tf_op jit(solution)/shard_map/while/body/eval_jaxpr/ppermute | solution.py:12
  161.1 5.0 %collective-permute-done = bf16[16,4096]{1,0:T(8,128)(2,1)S(1)} collective-permute-done((bf16[16,4096]{1,0:T(8,128)(2,1)S(1)}, bf16[16,4096]{1,0:T(8,128)(2,1)S(1)}, u32[]{:S(2)}, u32[]{:S(2)}) %collective-permute-start) | collective-permute-done | bytes 131104 | tf_op jit(solution)/shard_map/while/body/eval_jaxpr/ppermute | solution.py:12
  167.4 34.3 %collective-permute-done = bf16[16,4096]{1,0:T(8,128)(2,1)S(1)} collective-permute-done((bf16[16,4096]{1,0:T(8,128)(2,1)S(1)}, bf16[16,4096]{1,0:T(8,128)(2,1)S(1)}, u32[]{:S(2)}, u32[]{:S(2)}) %collective-permute-start) | collective-permute-done | bytes 131104 | tf_op jit(solution)/shard_map/while/body/eval_jaxpr/ppermute | solution.py:12
  201.7 6.0 %conditional.4 = ((bf16[16,4096]{1,0:T(8,128)(2,1)S(1)}, bf16[8,16,4096]{2,1,0:T(8,128)(2,1)}, bf16[8,16,256]{2,1,0:T(8,128)(2,1)S(1)}, bf16[8,16,4096]{2,1,0:T(8,128)(2,1)S(1)})) conditional(s32[]{:T(128)} %convert_element_type.143, (bf16[16,4096]{1,0:T(8,128)(2,1)S(1)}, bf16[8,16,4096]{2,1,0:T(8,128)(2,1)}, bf16[8,16,256]{2,1,0:T(8,128)(2,1)S(1)}, ...), branch_computations={%region_4.4_spmd, %region_5.6_spmd} | conditional | flops 67805184 | bytes 14762554 | solution.py:127
  209.0 5.0 %collective-permute-done = bf16[16,4096]{1,0:T(8,128)(2,1)S(1)} collective-permute-done((bf16[16,4096]{1,0:T(8,128)(2,1)S(1)}, bf16[16,4096]{1,0:T(8,128)(2,1)S(1)}, u32[]{:S(2)}, u32[]{:S(2)}) %collective-permute-start) | collective-permute-done | bytes 131104 | tf_op jit(solution)/shard_map/while/body/eval_jaxpr/ppermute | solution.py:12
  214.0 6.0 %conditional.4 = ((bf16[16,4096]{1,0:T(8,128)(2,1)S(1)}, bf16[8,16,4096]{2,1,0:T(8,128)(2,1)}, bf16[8,16,256]{2,1,0:T(8,128)(2,1)S(1)}, bf16[8,16,4096]{2,1,0:T(8,128)(2,1)S(1)})) conditional(s32[]{:T(128)} %convert_element_type.143, (bf16[16,4096]{1,0:T(8,128)(2,1)S(1)}, bf16[8,16,4096]{2,1,0:T(8,128)(2,1)}, bf16[8,16,256]{2,1,0:T(8,128)(2,1)S(1)}, ...), branch_computations={%region_4.4_spmd, %region_5.6_spmd} | conditional | flops 67805184 | bytes 14762554 | solution.py:127
  221.3 5.0 %collective-permute-done = bf16[16,4096]{1,0:T(8,128)(2,1)S(1)} collective-permute-done((bf16[16,4096]{1,0:T(8,128)(2,1)S(1)}, bf16[16,4096]{1,0:T(8,128)(2,1)S(1)}, u32[]{:S(2)}, u32[]{:S(2)}) %collective-permute-start) | collective-permute-done | bytes 131104 | tf_op jit(solution)/shard_map/while/body/eval_jaxpr/ppermute | solution.py:12
  226.3 6.0 %conditional.4 = ((bf16[16,4096]{1,0:T(8,128)(2,1)S(1)}, bf16[8,16,4096]{2,1,0:T(8,128)(2,1)}, bf16[8,16,256]{2,1,0:T(8,128)(2,1)S(1)}, bf16[8,16,4096]{2,1,0:T(8,128)(2,1)S(1)})) conditional(s32[]{:T(128)} %convert_element_type.143, (bf16[16,4096]{1,0:T(8,128)(2,1)S(1)}, bf16[8,16,4096]{2,1,0:T(8,128)(2,1)}, bf16[8,16,256]{2,1,0:T(8,128)(2,1)S(1)}, ...), branch_computations={%region_4.4_spmd, %region_5.6_spmd} | conditional | flops 67805184 | bytes 14762554 | solution.py:127
  233.6 5.0 %collective-permute-done = bf16[16,4096]{1,0:T(8,128)(2,1)S(1)} collective-permute-done((bf16[16,4096]{1,0:T(8,128)(2,1)S(1)}, bf16[16,4096]{1,0:T(8,128)(2,1)S(1)}, u32[]{:S(2)}, u32[]{:S(2)}) %collective-permute-start) | collective-permute-done | bytes 131104 | tf_op jit(solution)/shard_map/while/body/eval_jaxpr/ppermute | solution.py:12
  238.6 6.0 %conditional.4 = ((bf16[16,4096]{1,0:T(8,128)(2,1)S(1)}, bf16[8,16,4096]{2,1,0:T(8,128)(2,1)}, bf16[8,16,256]{2,1,0:T(8,128)(2,1)S(1)}, bf16[8,16,4096]{2,1,0:T(8,128)(2,1)S(1)})) conditional(s32[]{:T(128)} %convert_element_type.143, (bf16[16,4096]{1,0:T(8,128)(2,1)S(1)}, bf16[8,16,4096]{2,1,0:T(8,128)(2,1)}, bf16[8,16,256]{2,1,0:T(8,128)(2,1)S(1)}, ...), branch_computations={%region_4.4_spmd, %region_5.6_spmd} | conditional | flops 67805184 | bytes 14762554 | solution.py:127
  245.9 5.0 %collective-permute-done = bf16[16,4096]{1,0:T(8,128)(2,1)S(1)} collective-permute-done((bf16[16,4096]{1,0:T(8,128)(2,1)S(1)}, bf16[16,4096]{1,0:T(8,128)(2,1)S(1)}, u32[]{:S(2)}, u32[]{:S(2)}) %collective-permute-start) | collective-permute-done | bytes 131104 | tf_op jit(solution)/shard_map/while/body/eval_jaxpr/ppermute | solution.py:12
  250.8 6.0 %conditional.4 = ((bf16[16,4096]{1,0:T(8,128)(2,1)S(1)}, bf16[8,16,4096]{2,1,0:T(8,128)(2,1)}, bf16[8,16,256]{2,1,0:T(8,128)(2,1)S(1)}, bf16[8,16,4096]{2,1,0:T(8,128)(2,1)S(1)})) conditional(s32[]{:T(128)} %convert_element_type.143, (bf16[16,4096]{1,0:T(8,128)(2,1)S(1)}, bf16[8,16,4096]{2,1,0:T(8,128)(2,1)}, bf16[8,16,256]{2,1,0:T(8,128)(2,1)S(1)}, ...), branch_computations={%region_4.4_spmd, %region_5.6_spmd} | conditional | flops 67805184 | bytes 14762554 | solution.py:127
  258.2 5.0 %collective-permute-done = bf16[16,4096]{1,0:T(8,128)(2,1)S(1)} collective-permute-done((bf16[16,4096]{1,0:T(8,128)(2,1)S(1)}, bf16[16,4096]{1,0:T(8,128)(2,1)S(1)}, u32[]{:S(2)}, u32[]{:S(2)}) %collective-permute-start) | collective-permute-done | bytes 131104 | tf_op jit(solution)/shard_map/while/body/eval_jaxpr/ppermute | solution.py:12
  263.1 6.0 %conditional.4 = ((bf16[16,4096]{1,0:T(8,128)(2,1)S(1)}, bf16[8,16,4096]{2,1,0:T(8,128)(2,1)}, bf16[8,16,256]{2,1,0:T(8,128)(2,1)S(1)}, bf16[8,16,4096]{2,1,0:T(8,128)(2,1)S(1)})) conditional(s32[]{:T(128)} %convert_element_type.143, (bf16[16,4096]{1,0:T(8,128)(2,1)S(1)}, bf16[8,16,4096]{2,1,0:T(8,128)(2,1)}, bf16[8,16,256]{2,1,0:T(8,128)(2,1)S(1)}, ...), branch_computations={%region_4.4_spmd, %region_5.6_spmd} | conditional | flops 67805184 | bytes 14762554 | solution.py:127
  270.5 5.0 %collective-permute-done = bf16[16,4096]{1,0:T(8,128)(2,1)S(1)} collective-permute-done((bf16[16,4096]{1,0:T(8,128)(2,1)S(1)}, bf16[16,4096]{1,0:T(8,128)(2,1)S(1)}, u32[]{:S(2)}, u32[]{:S(2)}) %collective-permute-start) | collective-permute-done | bytes 131104 | tf_op jit(solution)/shard_map/while/body/eval_jaxpr/ppermute | solution.py:12
  275.4 6.0 %conditional.4 = ((bf16[16,4096]{1,0:T(8,128)(2,1)S(1)}, bf16[8,16,4096]{2,1,0:T(8,128)(2,1)}, bf16[8,16,256]{2,1,0:T(8,128)(2,1)S(1)}, bf16[8,16,4096]{2,1,0:T(8,128)(2,1)S(1)})) conditional(s32[]{:T(128)} %convert_element_type.143, (bf16[16,4096]{1,0:T(8,128)(2,1)S(1)}, bf16[8,16,4096]{2,1,0:T(8,128)(2,1)}, bf16[8,16,256]{2,1,0:T(8,128)(2,1)S(1)}, ...), branch_computations={%region_4.4_spmd, %region_5.6_spmd} | conditional | flops 67805184 | bytes 14762554 | solution.py:127
  282.8 5.0 %collective-permute-done = bf16[16,4096]{1,0:T(8,128)(2,1)S(1)} collective-permute-done((bf16[16,4096]{1,0:T(8,128)(2,1)S(1)}, bf16[16,4096]{1,0:T(8,128)(2,1)S(1)}, u32[]{:S(2)}, u32[]{:S(2)}) %collective-permute-start) | collective-permute-done | bytes 131104 | tf_op jit(solution)/shard_map/while/body/eval_jaxpr/ppermute | solution.py:12
  287.7 6.0 %conditional.4 = ((bf16[16,4096]{1,0:T(8,128)(2,1)S(1)}, bf16[8,16,4096]{2,1,0:T(8,128)(2,1)}, bf16[8,16,256]{2,1,0:T(8,128)(2,1)S(1)}, bf16[8,16,4096]{2,1,0:T(8,128)(2,1)S(1)})) conditional(s32[]{:T(128)} %convert_element_type.143, (bf16[16,4096]{1,0:T(8,128)(2,1)S(1)}, bf16[8,16,4096]{2,1,0:T(8,128)(2,1)}, bf16[8,16,256]{2,1,0:T(8,128)(2,1)S(1)}, ...), branch_computations={%region_4.4_spmd, %region_5.6_spmd} | conditional | flops 67805184 | bytes 14762554 | solution.py:127
  295.9 3.5 %all-to-all-start.1 = ((bf16[128,4,1024]{2,0,1:T(8,128)(2,1)}), bf16[128,4,1024]{2,0,1:T(8,128)(2,1)S(1)}, u32[]{:S(2)}, u32[]{:S(2)}) async-start(bf16[128,4,1024]{2,0,1:T(8,128)(2,1)} %copy.25), calls=%async_computation.1 | async-start | bytes 2097152 | tf_op jit(solution)/shard_map/all_to_all | solution.py:146
  300.9 15.2 %all_gather.19 = bf16[512,256]{1,0:T(8,128)(2,1)S(1)} all-gather(bf16[128,256]{1,0:T(8,128)(2,1)S(1)} %get-tuple-element.506), channel_id=1, replica_groups=mesh['section'=8,'dp'=4] {'dp'}, dimensions={0}, use_global_device_ids=true | all-gather | bytes 327680 | tf_op jit(solution)/shard_map/all_gather | solution.py:141
  316.1 8.0 %all_gather.18 = bf16[512,256]{1,0:T(8,128)(2,1)S(1)} all-gather(bf16[128,256]{1,0:T(8,128)(2,1)S(1)} %bitcast.94), channel_id=1, replica_groups=mesh['section'=8,'dp'=4] {'dp'}, dimensions={0}, use_global_device_ids=true | all-gather | bytes 327680 | tf_op jit(solution)/shard_map/all_gather | solution.py:142
  (152 shorter events, 83.3 us)
Async XLA Ops:
  7.2 50.3 %all-gather.8.cloned.1.call-start = ((), (), s32[]{:S(2)}) async-start(), calls=%async_computation.3 | async-start | bytes 2621440 | tf_op jit(solution)/shard_map/all_gather | solution.py:50
  7.9 3.0 copy-start.6
  7.9 3.1 copy-start.2
  7.9 78.0 %all-gather.6.cloned.1.call-start = ((), (), s32[]{:S(2)}) async-start(), calls=%async_computation.2 | async-start | bytes 1310720 | tf_op jit(solution)/shard_map/all_gather | solution.py:52
  8.7 114.5 %all-gather.10.cloned.1.call-start = ((), (), s32[]{:S(2)}) async-start(), calls=%async_computation.4 | async-start | bytes 2621440 | tf_op jit(solution)/shard_map/all_gather | solution.py:51
  12.8 283.1 %all-to-all-start = ((bf16[128,4,1024]{0,2,1:T(8,128)(2,1)}), bf16[128,4,1024]{0,2,1:T(8,128)(2,1)}, u32[]{:S(2)}, u32[]{:S(2)}) async-start(bf16[128,4,1024]{0,2,1:T(8,128)(2,1)} %multiply_convert_fusion), calls=%async_computation | async-start | bytes 2097152 | tf_op jit(solution)/shard_map/all_to_all | solution.py:145
  57.4 65.7 %copy-start.5 = (f32[128,128]{1,0:T(8,128)S(1)}, f32[128,128]{1,0:T(8,128)}, u32[]{:S(2)}) copy-start(f32[128,128]{1,0:T(8,128)} %param.18) | copy-start | bytes 196612
  123.3 2.3 copy-start
  125.5 3.2 collective-permute-start
  128.8 5.7 %collective-permute-start = (bf16[16,4096]{1,0:T(8,128)(2,1)S(1)}, bf16[16,4096]{1,0:T(8,128)(2,1)S(1)}, u32[]{:S(2)}, u32[]{:S(2)}) collective-permute-start(bf16[16,4096]{1,0:T(8,128)(2,1)S(1)} %get-tuple-element.627), channel_id=1, source_target_pairs={{4,0},{8,4},{12,8},{16,12},{20,16},{24,20},{28,24},{5,1},{9,5},{13... | collective-permute-start | bytes 393224 | tf_op jit(solution)/shard_map/while/body/eval_jaxpr/ppermute | solution.py:12
  134.5 6.3 %collective-permute-start = (bf16[16,4096]{1,0:T(8,128)(2,1)S(1)}, bf16[16,4096]{1,0:T(8,128)(2,1)S(1)}, u32[]{:S(2)}, u32[]{:S(2)}) collective-permute-start(bf16[16,4096]{1,0:T(8,128)(2,1)S(1)} %get-tuple-element.627), channel_id=1, source_target_pairs={{4,0},{8,4},{12,8},{16,12},{20,16},{24,20},{28,24},{5,1},{9,5},{13... | collective-permute-start | bytes 393224 | tf_op jit(solution)/shard_map/while/body/eval_jaxpr/ppermute | solution.py:12
  140.8 6.3 %collective-permute-start = (bf16[16,4096]{1,0:T(8,128)(2,1)S(1)}, bf16[16,4096]{1,0:T(8,128)(2,1)S(1)}, u32[]{:S(2)}, u32[]{:S(2)}) collective-permute-start(bf16[16,4096]{1,0:T(8,128)(2,1)S(1)} %get-tuple-element.627), channel_id=1, source_target_pairs={{4,0},{8,4},{12,8},{16,12},{20,16},{24,20},{28,24},{5,1},{9,5},{13... | collective-permute-start | bytes 393224 | tf_op jit(solution)/shard_map/while/body/eval_jaxpr/ppermute | solution.py:12
  147.1 6.3 %collective-permute-start = (bf16[16,4096]{1,0:T(8,128)(2,1)S(1)}, bf16[16,4096]{1,0:T(8,128)(2,1)S(1)}, u32[]{:S(2)}, u32[]{:S(2)}) collective-permute-start(bf16[16,4096]{1,0:T(8,128)(2,1)S(1)} %get-tuple-element.627), channel_id=1, source_target_pairs={{4,0},{8,4},{12,8},{16,12},{20,16},{24,20},{28,24},{5,1},{9,5},{13... | collective-permute-start | bytes 393224 | tf_op jit(solution)/shard_map/while/body/eval_jaxpr/ppermute | solution.py:12
  153.5 6.3 %collective-permute-start = (bf16[16,4096]{1,0:T(8,128)(2,1)S(1)}, bf16[16,4096]{1,0:T(8,128)(2,1)S(1)}, u32[]{:S(2)}, u32[]{:S(2)}) collective-permute-start(bf16[16,4096]{1,0:T(8,128)(2,1)S(1)} %get-tuple-element.627), channel_id=1, source_target_pairs={{4,0},{8,4},{12,8},{16,12},{20,16},{24,20},{28,24},{5,1},{9,5},{13... | collective-permute-start | bytes 393224 | tf_op jit(solution)/shard_map/while/body/eval_jaxpr/ppermute | solution.py:12
  159.8 6.3 %collective-permute-start = (bf16[16,4096]{1,0:T(8,128)(2,1)S(1)}, bf16[16,4096]{1,0:T(8,128)(2,1)S(1)}, u32[]{:S(2)}, u32[]{:S(2)}) collective-permute-start(bf16[16,4096]{1,0:T(8,128)(2,1)S(1)} %get-tuple-element.627), channel_id=1, source_target_pairs={{4,0},{8,4},{12,8},{16,12},{20,16},{24,20},{28,24},{5,1},{9,5},{13... | collective-permute-start | bytes 393224 | tf_op jit(solution)/shard_map/while/body/eval_jaxpr/ppermute | solution.py:12
  166.1 35.6 %collective-permute-start = (bf16[16,4096]{1,0:T(8,128)(2,1)S(1)}, bf16[16,4096]{1,0:T(8,128)(2,1)S(1)}, u32[]{:S(2)}, u32[]{:S(2)}) collective-permute-start(bf16[16,4096]{1,0:T(8,128)(2,1)S(1)} %get-tuple-element.627), channel_id=1, source_target_pairs={{4,0},{8,4},{12,8},{16,12},{20,16},{24,20},{28,24},{5,1},{9,5},{13... | collective-permute-start | bytes 393224 | tf_op jit(solution)/shard_map/while/body/eval_jaxpr/ppermute | solution.py:12
  201.7 2.5 copy-start.1
  207.7 6.3 %collective-permute-start = (bf16[16,4096]{1,0:T(8,128)(2,1)S(1)}, bf16[16,4096]{1,0:T(8,128)(2,1)S(1)}, u32[]{:S(2)}, u32[]{:S(2)}) collective-permute-start(bf16[16,4096]{1,0:T(8,128)(2,1)S(1)} %get-tuple-element.627), channel_id=1, source_target_pairs={{4,0},{8,4},{12,8},{16,12},{20,16},{24,20},{28,24},{5,1},{9,5},{13... | collective-permute-start | bytes 393224 | tf_op jit(solution)/shard_map/while/body/eval_jaxpr/ppermute | solution.py:12
  214.0 2.5 copy-start.1
  220.0 6.3 %collective-permute-start = (bf16[16,4096]{1,0:T(8,128)(2,1)S(1)}, bf16[16,4096]{1,0:T(8,128)(2,1)S(1)}, u32[]{:S(2)}, u32[]{:S(2)}) collective-permute-start(bf16[16,4096]{1,0:T(8,128)(2,1)S(1)} %get-tuple-element.627), channel_id=1, source_target_pairs={{4,0},{8,4},{12,8},{16,12},{20,16},{24,20},{28,24},{5,1},{9,5},{13... | collective-permute-start | bytes 393224 | tf_op jit(solution)/shard_map/while/body/eval_jaxpr/ppermute | solution.py:12
  226.3 2.5 copy-start.1
  232.3 6.3 %collective-permute-start = (bf16[16,4096]{1,0:T(8,128)(2,1)S(1)}, bf16[16,4096]{1,0:T(8,128)(2,1)S(1)}, u32[]{:S(2)}, u32[]{:S(2)}) collective-permute-start(bf16[16,4096]{1,0:T(8,128)(2,1)S(1)} %get-tuple-element.627), channel_id=1, source_target_pairs={{4,0},{8,4},{12,8},{16,12},{20,16},{24,20},{28,24},{5,1},{9,5},{13... | collective-permute-start | bytes 393224 | tf_op jit(solution)/shard_map/while/body/eval_jaxpr/ppermute | solution.py:12
  238.6 2.5 copy-start.1
  244.6 6.3 %collective-permute-start = (bf16[16,4096]{1,0:T(8,128)(2,1)S(1)}, bf16[16,4096]{1,0:T(8,128)(2,1)S(1)}, u32[]{:S(2)}, u32[]{:S(2)}) collective-permute-start(bf16[16,4096]{1,0:T(8,128)(2,1)S(1)} %get-tuple-element.627), channel_id=1, source_target_pairs={{4,0},{8,4},{12,8},{16,12},{20,16},{24,20},{28,24},{5,1},{9,5},{13... | collective-permute-start | bytes 393224 | tf_op jit(solution)/shard_map/while/body/eval_jaxpr/ppermute | solution.py:12
  250.8 2.5 copy-start.1
  256.9 6.3 %collective-permute-start = (bf16[16,4096]{1,0:T(8,128)(2,1)S(1)}, bf16[16,4096]{1,0:T(8,128)(2,1)S(1)}, u32[]{:S(2)}, u32[]{:S(2)}) collective-permute-start(bf16[16,4096]{1,0:T(8,128)(2,1)S(1)} %get-tuple-element.627), channel_id=1, source_target_pairs={{4,0},{8,4},{12,8},{16,12},{20,16},{24,20},{28,24},{5,1},{9,5},{13... | collective-permute-start | bytes 393224 | tf_op jit(solution)/shard_map/while/body/eval_jaxpr/ppermute | solution.py:12
  263.1 2.5 copy-start.1
  269.2 6.3 %collective-permute-start = (bf16[16,4096]{1,0:T(8,128)(2,1)S(1)}, bf16[16,4096]{1,0:T(8,128)(2,1)S(1)}, u32[]{:S(2)}, u32[]{:S(2)}) collective-permute-start(bf16[16,4096]{1,0:T(8,128)(2,1)S(1)} %get-tuple-element.627), channel_id=1, source_target_pairs={{4,0},{8,4},{12,8},{16,12},{20,16},{24,20},{28,24},{5,1},{9,5},{13... | collective-permute-start | bytes 393224 | tf_op jit(solution)/shard_map/while/body/eval_jaxpr/ppermute | solution.py:12
  275.4 2.5 copy-start.1
  281.4 6.3 %collective-permute-start = (bf16[16,4096]{1,0:T(8,128)(2,1)S(1)}, bf16[16,4096]{1,0:T(8,128)(2,1)S(1)}, u32[]{:S(2)}, u32[]{:S(2)}) collective-permute-start(bf16[16,4096]{1,0:T(8,128)(2,1)S(1)} %get-tuple-element.627), channel_id=1, source_target_pairs={{4,0},{8,4},{12,8},{16,12},{20,16},{24,20},{28,24},{5,1},{9,5},{13... | collective-permute-start | bytes 393224 | tf_op jit(solution)/shard_map/while/body/eval_jaxpr/ppermute | solution.py:12
  287.7 2.5 copy-start.1
  295.9 29.6 %all-to-all-start.1 = ((bf16[128,4,1024]{2,0,1:T(8,128)(2,1)}), bf16[128,4,1024]{2,0,1:T(8,128)(2,1)S(1)}, u32[]{:S(2)}, u32[]{:S(2)}) async-start(bf16[128,4,1024]{2,0,1:T(8,128)(2,1)} %copy.25), calls=%async_computation.1 | async-start | bytes 2097152 | tf_op jit(solution)/shard_map/all_to_all | solution.py:146
  (2 other events, 2.6 us)
Sparse Core Ops, SparseCore 0:
  9.8 47.5 all-gather.7
  59.3 26.6 all-gather.5
  87.8 35.2 all-gather.9
where the time goes:
time: 335 us; the launch traced here: 333 us
  waiting for transfers between devices  203 us (61%)
  matrix products  30.1 us (9%)
  starting transfers between devices  28.2 us (8%)
  other arithmetic  26.4 us (8%)
  blocking collectives  23.3 us (7%)
  between operations  13.9 us (4%)
  local copies, waits for them, and re-layouts  7.84 us (2%)
    ppermute x15, waiting for transfers between devices, from_behind(): return lax.ppermute(block, axis, route)  100 us
    all_gather x1, waiting for transfers between devices, per_device(): lax.all_gather(down_proj[0], 'dp', axis=0, tiled=True)  37.4 us
    all_gather x1, waiting for transfers between devices, per_device(): lax.all_gather(up_proj[0], 'dp', axis=1, tiled=True)  37.2 us
    all_gather x1, waiting for transfers between devices, per_device(): lax.all_gather(readout_matrix, 'dp', axis=0, tiled=True)  25.7 us
    dot_general x16, matrix products, multiply_trailing_factor(): lax.dot_general(left, right, (((1,), (1,)), ((), ())), preferred_element_...  24.8 us
    ppermute x15, starting transfers between devices, from_behind(): return lax.ppermute(block, axis, route)  19.4 us
    all_gather x1, blocking collectives, per_device(): lax.all_gather(activated, 'dp', axis=0, tiled=True)  15.2 us
    dynamic_update_slice x8, other arithmetic, process(): lax.dynamic_update_index_in_dim(grads_prev, inputs_grad, picked, 0)  13.8 us
  transfers between devices with their start and end apart: 20, of which 18 were waited for; matrix products, arithmetic and copies ran while one was open for 18% of the time, Pallas kernels for 0%

commit v1 on v0

v1 whole, which is shorter than its diff:
```python
import functools

import jax
import jax.numpy as jnp
from jax import lax
from jax.experimental import pallas as pl
from jax.experimental.pallas import tpu as pltpu
from jax.sharding import PartitionSpec as P

EPSILON = 1e-05
CHUNKS = 2
ANY = pl.BlockSpec(memory_space=pl.ANY)
VMEM = pl.BlockSpec(memory_space=pltpu.VMEM)
SMEM = pl.BlockSpec(memory_space=pltpu.SMEM)
PARAMS = pltpu.CompilerParams(vmem_limit_bytes=40 * 1024 * 1024)


def dot_nn(left, right):
    return lax.dot_general(
        left, right, (((1,), (0,)), ((), ())), preferred_element_type=jnp.float32
    )


def dot_nt(left, right):
    return lax.dot_general(
        left, right, (((1,), (1,)), ((), ())), preferred_element_type=jnp.float32
    )


def dot_tn(left, right):
    return lax.dot_general(
        left, right, (((0,), (0,)), ((), ())), preferred_element_type=jnp.float32
    )


def silu_slope(latent):
    sigmoid = jax.nn.sigmoid(latent)
    return sigmoid * (1.0 + latent * (1.0 - sigmoid))


def move(block, pairs):
    return lax.ppermute(block, ("section", "dp"), pairs)


def peers(sections, size, k):
    return [(s * size + i, s * size + (i ^ k)) for s in sections for i in range(size)]


def gather_pieces(block, sections, size):
    rows = block.shape[0]
    if size == 4:
        half = rows // 2
        from_x = move(block, peers(sections, size, 1))
        from_y = move(block, peers(sections, size, 2))
        low = move(from_y[:half], peers(sections, size, 1))
        high = move(from_x[half:], peers(sections, size, 2))
        return [[(0, rows, from_x)], [(0, rows, from_y)], [(0, half, low), (half, half, high)]]
    return [[(0, rows, move(block, peers(sections, size, k)))] for k in range(1, size)]


def flatten(pieces):
    return [part[2] for piece in pieces for part in piece]


def shapes_of(pieces):
    return [[(row, count) for row, count, _ in piece] for piece in pieces]


def copies(refs, layout, held, sems, base):
    out, at = [], 0
    for slot, parts in enumerate(layout, 1):
        group = []
        for row, count in parts:
            group.append(
                pltpu.make_async_copy(
                    refs[at], held.at[slot, pl.ds(row, count)], sems.at[base + at]
                )
            )
            at += 1
        out.append(group)
    return out


def start_all(groups):
    for group in groups:
        for copy in group:
            copy.start()


def wait_all(group):
    for copy in group:
        copy.wait()


def columns(flag, k, width):
    return pl.ds(pl.multiple_of((flag ^ k) * width, width), width)


def latent_of(normed_ref, held, dp_index, size, wait):
    total = None
    for k in range(size):
        wait(k)
        part = dot_nn(normed_ref[:, columns(dp_index, k, held.shape[1])], held[k])
        total = part if total is None else total + part
    return total


def latent_kernel(size, layout, want, *refs):
    flags, normed, own = refs[:3]
    count = sum(len(parts) for parts in layout)
    pieces = refs[3 : 3 + count]
    latent, held, sems = refs[3 + count :]

    @pl.when(flags[1] == want)
    def _():
        mine = pltpu.make_async_copy(own, held.at[0], sems.at[0])
        mine.start()
        groups = [[mine]] + copies(pieces, layout, held, sems, 1)
        start_all(groups[1:])
        latent[...] = latent_of(normed, held, flags[0], size, lambda k: wait_all(groups[k]))


def top_kernel(size, layout, head_layout, *refs):
    flags, x, normed, gain, inverse, truth, mask, own, own_head = refs[:9]
    count = sum(len(parts) for parts in layout)
    head_count = sum(len(parts) for parts in head_layout)
    pieces = refs[9 : 9 + count]
    head_pieces = refs[9 + count : 9 + count + head_count]
    latent_out, latent_grad_out, arriving_out, grads_out, held, head, sems = refs[
        9 + count + head_count :
    ]
    dp_index = flags[0]
    is_top = flags[2] == 1
    width = held.shape[1]

    @pl.when(flags[1] == 1)
    def _():
        mine = pltpu.make_async_copy(own, held.at[0], sems.at[0])
        mine.start()
        groups = [[mine]] + copies(pieces, layout, held, sems, 1)
        start_all(groups[1:])
        latent_out[...] = latent_of(normed, held, dp_index, size, lambda k: wait_all(groups[k]))

    @pl.when(is_top)
    def _():
        mine = pltpu.make_async_copy(own_head, head.at[0], sems.at[1 + count])
        mine.start()
        groups = [[mine]] + copies(head_pieces, head_layout, head, sems, 2 + count)
        start_all(groups[1:])
        latent = latent_out[...]
        activated = jax.nn.silu(latent).astype(jnp.bfloat16)
        estimate = None
        product = None
        for k in range(size):
            wait_all(groups[k])
            part = dot_nn(x[:, columns(dp_index, k, width)], head[k, :width])
            extra = head[k, width:].astype(jnp.float32)
            estimate = part if estimate is None else estimate + part
            product = extra if product is None else product + extra
        product = product.astype(jnp.bfloat16)
        estimate = estimate + dot_nn(activated, product)
        error = (mask[:, :1] * (estimate - truth[...])).astype(jnp.bfloat16)
        hidden_grad = dot_nt(error, product)
        latent_grad = (hidden_grad * silu_slope(latent)).astype(jnp.bfloat16)
        latent_grad_out[...] = latent_grad
        scale = inverse[:, :1]
        mean = jnp.sum(latent_grad.astype(jnp.float32) * latent, axis=-1, keepdims=True) / (
            width * size
        )
        slope = scale * scale * mean
        for k in range(size):
            at = columns(dp_index, k, width)
            arriving = dot_nt(error, head[k, :width]).astype(jnp.bfloat16)
            arriving_out[:, at] = arriving
            scaled = dot_nt(latent_grad, held[k]) * gain[:, at].astype(jnp.float32)
            grads = (
                arriving.astype(jnp.float32)
                + scale * scaled
                - x[:, at].astype(jnp.float32) * slope
            )
            grads_out[:, at] = grads.astype(jnp.bfloat16)


def tick_kernel(size, down_layout, even_layout, up_layout, *refs):
    flags, received, gain, x_all, inverse_all, latent_odd, latent_even, down_own, up_own = refs[:9]
    at = 9
    groups_of_refs = []
    for layout in (down_layout, even_layout, up_layout):
        count = sum(len(parts) for parts in layout)
        groups_of_refs.append(refs[at : at + count])
        at += count
    odd_refs, even_refs, up_refs = groups_of_refs
    at += 3
    send, latent_grads, arrivals, grads = refs[at : at + 4]
    down, up, arriving, x, inverse, latent, latent_grad, result, sems, up_sems, io_sems = refs[
        at + 4 :
    ]
    dp_index, odd, active, row = flags[0], flags[1], flags[3], flags[4]
    rows = arriving.shape[0]
    width = down.shape[1]
    row = pl.multiple_of(row, rows)

    @pl.when(active == 1)
    def _():
        fetch = pltpu.make_async_copy(received, arriving, io_sems.at[0])
        fetch.start()
        up_mine = pltpu.make_async_copy(up_own, up.at[0], up_sems.at[0])
        up_mine.start()
        up_groups = [[up_mine]] + copies(up_refs, up_layout, up, up_sems, 1)
        start_all(up_groups[1:])
        fetch_inverse = pltpu.make_async_copy(
            inverse_all.at[pl.ds(row, rows)], inverse, io_sems.at[1]
        )
        fetch_inverse.start()
        latent_from_odd = pltpu.make_async_copy(
            latent_odd.at[pl.ds(row, rows)], latent, io_sems.at[2]
        )
        latent_from_even = pltpu.make_async_copy(
            latent_even.at[pl.ds(row, rows)], latent, io_sems.at[2]
        )
        mine = pltpu.make_async_copy(down_own, down.at[0], sems.at[0])
        mine.start()
        odd_groups = [[mine]] + copies(odd_refs, down_layout, down, sems, 1)
        even_groups = [[mine]] + copies(even_refs, even_layout, down, sems, 1)

        @pl.when(odd == 1)
        def _():
            latent_from_odd.start()
            start_all(odd_groups[1:])

        @pl.when(odd == 0)
        def _():
            latent_from_even.start()
            start_all(even_groups[1:])

        fetch_x = pltpu.make_async_copy(x_all.at[pl.ds(row, rows)], x, io_sems.at[3])
        fetch_x.start()
        fetch.wait()
        keep = pltpu.make_async_copy(arriving, arrivals.at[pl.ds(row, rows)], io_sems.at[0])
        keep.start()
        hidden_grad = None
        for k in range(size):
            wait_all(up_groups[k])
            part = dot_nt(arriving[:, columns(dp_index, k, width)], up[k])
            hidden_grad = part if hidden_grad is None else hidden_grad + part
        fetch_inverse.wait()
        latent_from_odd.wait()
        lat = latent[...]
        lat_grad = (hidden_grad * silu_slope(lat)).astype(jnp.bfloat16)
        latent_grad[...] = lat_grad
        keep_grad = pltpu.make_async_copy(
            latent_grad, latent_grads.at[pl.ds(row, rows)], io_sems.at[4]
        )
        keep_grad.start()
        scale = inverse[:, :1]
        mean = jnp.sum(lat_grad.astype(jnp.float32) * lat, axis=-1, keepdims=True) / (width * size)
        slope = scale * scale * mean
        fetch_x.wait()
        for k in range(size):
            wait_all(odd_groups[k])
            at_k = columns(dp_index, k, width)
            scaled = dot_nt(lat_grad, down[k]) * gain[:, at_k].astype(jnp.float32)
            value = (
                arriving[:, at_k].astype(jnp.float32)
                + scale * scaled
                - x[:, at_k].astype(jnp.float32) * slope
            )
            result[:, at_k] = value.astype(jnp.bfloat16)
        put = pltpu.make_async_copy(result, send, io_sems.at[5])
        put.start()
        keep_result = pltpu.make_async_copy(result, grads.at[pl.ds(row, rows)], io_sems.at[6])
        keep_result.start()
        keep.wait()
        keep_grad.wait()
        put.wait()
        keep_result.wait()


def per_device(
    section_inputs, norm_gain, down_proj, up_proj, readout_matrix, ground_truth_series, valid_len
):
    size = lax.axis_size("dp")
    sections = lax.axis_size("section")
    top = sections - 1
    dp_index = lax.axis_index("dp")
    section = lax.axis_index("section")
    odds = [s for s in range(sections) if s % 2 == 1]
    evens = [s for s in range(sections) if s % 2 == 0]

    x = section_inputs[0]
    down_own, up_own = down_proj[0], up_proj[0]
    tokens, width = x.shape
    shard, latent_width = down_own.shape
    horizon = readout_matrix.shape[1]
    rows = tokens // CHUNKS

    values = x.astype(jnp.float32)
    inverse = lax.rsqrt(jnp.mean(values * values, axis=-1, keepdims=True) + EPSILON)
    normed = (values * inverse * norm_gain.astype(jnp.float32)).astype(jnp.bfloat16)
    inverse = jnp.broadcast_to(inverse, (tokens, 128))
    per_micro = tokens // valid_len.shape[0]
    mask = (
        (jnp.arange(per_micro)[None, :] < valid_len[:, None]).astype(jnp.float32).reshape(tokens, 1)
    )
    mask = jnp.broadcast_to(mask, (tokens, 128))

    head_own = jnp.concatenate(
        [readout_matrix, dot_nn(up_own, readout_matrix).astype(jnp.bfloat16)], axis=0
    )
    odd_pieces = gather_pieces(down_own, odds, size)
    head_pieces = gather_pieces(head_own, [top], size)
    up_pieces = gather_pieces(up_own, [s for s in range(sections) if s != top], size)
    even_pieces = gather_pieces(down_own, evens, size)

    odd = (section % 2).astype(jnp.int32)
    is_top = (section == top).astype(jnp.int32)
    zero = jnp.int32(0)

    def flags_at(active, row):
        return jnp.stack([dp_index.astype(jnp.int32), odd, is_top, active, row])

    still = flags_at(zero, zero)
    f32, bf16 = jnp.float32, jnp.bfloat16
    odd_refs, head_refs = flatten(odd_pieces), flatten(head_pieces)
    latent_odd, latent_grads, arrivals, grads = pl.pallas_call(
        functools.partial(top_kernel, size, shapes_of(odd_pieces), shapes_of(head_pieces)),
        out_shape=(
            jax.ShapeDtypeStruct((tokens, latent_width), f32),
            jax.ShapeDtypeStruct((tokens, latent_width), bf16),
            jax.ShapeDtypeStruct((tokens, width), bf16),
            jax.ShapeDtypeStruct((tokens, width), bf16),
        ),
        in_specs=[SMEM] + [VMEM] * 6 + [ANY] * (2 + len(odd_refs) + len(head_refs)),
        out_specs=(VMEM,) * 4,
        scratch_shapes=[
            pltpu.VMEM((size, shard, latent_width), bf16),
            pltpu.VMEM((size, shard + latent_width, horizon), bf16),
            pltpu.SemaphoreType.DMA((2 + len(odd_refs) + len(head_refs),)),
        ],
        compiler_params=PARAMS,
    )(
        still, x, normed, norm_gain, inverse, ground_truth_series, mask, down_own, head_own,
        *odd_refs, *head_refs,
    )

    even_refs = flatten(even_pieces)
    latent_even = pl.pallas_call(
        functools.partial(latent_kernel, size, shapes_of(even_pieces), 0),
        out_shape=jax.ShapeDtypeStruct((tokens, latent_width), f32),
        in_specs=[SMEM, VMEM] + [ANY] * (1 + len(even_refs)),
        out_specs=VMEM,
        scratch_shapes=[
            pltpu.VMEM((size, shard, latent_width), bf16),
            pltpu.SemaphoreType.DMA((1 + len(even_refs),)),
        ],
        compiler_params=PARAMS,
    )(still, normed, down_own, *even_refs)

    up_refs = flatten(up_pieces)
    fixed = 9 + len(odd_refs) + len(even_refs) + len(up_refs)
    tick = pl.pallas_call(
        functools.partial(
            tick_kernel, size, shapes_of(odd_pieces), shapes_of(even_pieces), shapes_of(up_pieces)
        ),
        out_shape=(
            jax.ShapeDtypeStruct((rows, width), bf16),
            jax.ShapeDtypeStruct((tokens, latent_width), bf16),
            jax.ShapeDtypeStruct((tokens, width), bf16),
            jax.ShapeDtypeStruct((tokens, width), bf16),
        ),
        in_specs=[SMEM, ANY, VMEM] + [ANY] * (fixed - 3 + 3),
        out_specs=(ANY,) * 4,
        input_output_aliases={fixed: 1, fixed + 1: 2, fixed + 2: 3},
        scratch_shapes=[
            pltpu.VMEM((size, shard, latent_width), bf16),
            pltpu.VMEM((size, latent_width, shard), bf16),
            pltpu.VMEM((rows, width), bf16),
            pltpu.VMEM((rows, width), bf16),
            pltpu.VMEM((rows, 128), f32),
            pltpu.VMEM((rows, latent_width), f32),
            pltpu.VMEM((rows, latent_width), bf16),
            pltpu.VMEM((rows, width), bf16),
            pltpu.SemaphoreType.DMA((1 + len(odd_refs),)),
            pltpu.SemaphoreType.DMA((1 + len(up_refs),)),
            pltpu.SemaphoreType.DMA((7,)),
        ],
        compiler_params=PARAMS,
    )

    def hop(block, senders):
        return move(
            block, [(s * size + i, (s - 1) * size + i) for s in senders for i in range(size)]
        )

    first = [hop(grads[c * rows : (c + 1) * rows], [top]) for c in range(CHUNKS)]
    send = None
    for step in range(1, top + CHUNKS):
        piece = step - (top - section)
        active = ((piece >= 0) & (piece < CHUNKS) & (section < top)).astype(jnp.int32)
        row = jnp.clip(piece, 0, CHUNKS - 1).astype(jnp.int32) * rows
        if send is None:
            received = first[0]
        else:
            senders = [
                s
                for s in range(1, top)
                if 0 <= step - 1 - (top - s) < CHUNKS
            ]
            received = hop(send, senders)
            if step - 1 < CHUNKS:
                received = jnp.where(section == top - 1, first[step - 1], received)
        send, latent_grads, arrivals, grads = tick(
            flags_at(active, row), received, norm_gain, x, inverse, latent_odd, latent_even,
            down_own, up_own, *odd_refs, *even_refs, *up_refs, latent_grads, arrivals, grads,
        )

    def exchange(block):
        out = [lax.dynamic_slice_in_dim(block, dp_index * shard, shard, 1)]
        for k in range(1, size):
            part = lax.dynamic_slice_in_dim(block, (dp_index ^ k) * shard, shard, 1)
            out.append(move(part, peers(range(sections), size, k)))
        return jnp.concatenate(out, axis=0)

    def spread(block):
        return jnp.concatenate(
            [block]
            + [move(block, peers(range(sections), size, k)) for k in range(1, size)],
            axis=0,
        )

    latent = jnp.where(odd == 1, latent_odd, latent_even)
    activated = jax.nn.silu(latent).astype(bf16)
    normed_columns = exchange(normed)
    activated_all = spread(activated)
    arriving_columns = exchange(arrivals)
    latent_grads_all = spread(latent_grads)
    down_grads = dot_tn(normed_columns, latent_grads_all).astype(bf16)
    up_grads = dot_tn(activated_all, arriving_columns).astype(bf16)
    return (grads[None], down_grads[None], up_grads[None])


def solution(mesh):
    placed = (
        P("section", "dp", None),
        P("section", None),
        P("section", "dp", None),
        P("section", None, "dp"),
        P("dp", None),
        P("dp", None),
        P("dp"),
    )
    return jax.shard_map(
        per_device,
        mesh=mesh,
        in_specs=placed,
        out_specs=(P("section", "dp", None), P("section", "dp", None), P("section", None, "dp")),
        check_vma=False,
    )
```

time: 335 us -> 259 us (0.77)
  waiting for transfers between devices: 203 us -> 77.3 us
  local copies, waits for them, and re-layouts: 7.84 us -> 89.6 us
  starting transfers between devices: 28.2 us -> 58.2 us
  matrix products: 30.1 us -> 5.05 us
  blocking collectives: 23.3 us -> 0 us
  other arithmetic: 26.4 us -> 4.03 us
  Pallas kernels: 0 us -> 20.1 us
  between operations: 13.9 us -> 1.45 us
    all_gather x3 -> x0, waiting for transfers between devices: 100 us -> none  [the longest x1 37.4 us: per_device(): lax.all_gather(down_proj[0], 'dp', axis=0, tiled=True)]
    unnamed x12 -> x214, local copies, waits for them, and re-layouts: 1.06 us -> 72.5 us
    ppermute x15 -> x37, starting transfers between devices: 19.4 us -> 58.2 us  [move(): return lax.ppermute(block, ('section', 'dp'), pairs)]
    dot_general x19 -> x3, matrix products: 30.1 us -> 5.05 us  [the longest x2 3.66 us: dot_tn(): lax.dot_general(left, right, (((0,), (0,)), ((), ())), preferred_element_...]
    all_gather x2 -> x0, blocking collectives: 23.3 us -> none  [the longest x1 15.2 us: per_device(): lax.all_gather(activated, 'dp', axis=0, tiled=True)]
    ppermute x15 -> x37, waiting for transfers between devices: 100 us -> 77.3 us  [move(): return lax.ppermute(block, ('section', 'dp'), pairs)]
    dynamic_update_slice x16 -> x0, other arithmetic: 22.5 us -> none  [the longest x8 13.8 us: process(): lax.dynamic_update_index_in_dim(grads_prev, inputs_grad, picked, 0)]
    pallas_call x0 -> x10, Pallas kernels: none -> 20.1 us  [the longest x8 16.3 us: per_device(): tick(flags_at(active, row), received, norm_gain, x, inverse, latent_odd,...]
  transfers between devices with their start and end apart: 20 -> 37, of which waited for: 18 -> 5; matrix products, arithmetic and copies ran while one was open for 18% -> 9% of each run, Pallas kernels for 0% -> 4%
where the time goes in v1:
time: 259 us; the launch traced here: 256 us
  local copies, waits for them, and re-layouts  89.6 us (35%)
  waiting for transfers between devices  77.3 us (30%)
  starting transfers between devices  58.2 us (22%)
  Pallas kernels  20.1 us (8%)
  matrix products  5.05 us (2%)
  other arithmetic  4.03 us (2%)
    ppermute x37, waiting for transfers between devices, move(): return lax.ppermute(block, ('section', 'dp'), pairs)  77.3 us
    unnamed x214, local copies, waits for them, and re-layouts  72.5 us
    ppermute x37, starting transfers between devices, move(): return lax.ppermute(block, ('section', 'dp'), pairs)  58.2 us
    pallas_call x8, Pallas kernels, per_device(): tick(flags_at(active, row), received, norm_gain, x, inverse, latent_odd,...  16.3 us
  transfers between devices with their start and end apart: 37, of which 5 were waited for; matrix products, arithmetic and copies ran while one was open for 9% of the time, Pallas kernels for 4%

profile of v1, /device:TPU:0, one launch (start us, length us, event | category | flops | bytes accessed | tf_op | source)
XLA Modules:
  0.0 255.7 jit_solution(13122268391980040189)
XLA Ops:
  6.0 4.9 %collective-permute-start.11 = (bf16[1024,256]{1,0:T(8,128)(2,1)}, bf16[1024,256]{1,0:T(8,128)(2,1)}, u32[]{:S(2)}, u32[]{:S(2)}) collective-permute-start(bf16[1024,256]{1,0:T(8,128)(2,1)} %bitcast.44), channel_id=1, source_target_pairs={{0,2},{1,3},{2,0},{3,1},{8,10},{9,11},{10,8},{11,9},{16,18},{17,19... | collective-permute-start | bytes 1572872 | tf_op jit(solution)/shard_map/ppermute | solution.py:42
  20.2 3.4 %collective-permute-start.10 = (bf16[1024,256]{1,0:T(8,128)(2,1)S(1)}, bf16[1024,256]{1,0:T(8,128)(2,1)S(1)}, u32[]{:S(2)}, u32[]{:S(2)}) collective-permute-start(bf16[1024,256]{1,0:T(8,128)(2,1)S(1)} %bitcast.45), channel_id=1, source_target_pairs={{0,1},{1,0},{2,3},{3,2},{8,9},{9,8},{10,11},{11,10},{16,17},{17,16... | collective-permute-start | bytes 1572872 | tf_op jit(solution)/shard_map/ppermute | solution.py:42
  23.6 2.4 collective-permute-start.15
  26.0 2.0 collective-permute-start.14
  36.6 1.6 shard_map.94
  38.2 2.3 fusion.37
  40.6 1.5 collective-permute-start.9
  42.0 1.7 slice.44
  43.7 3.9 %collective-permute-start.12 = (bf16[512,256]{1,0:T(8,128)(2,1)}, bf16[512,256]{1,0:T(8,128)(2,1)}, u32[]{:S(2)}, u32[]{:S(2)}) collective-permute-start(bf16[512,256]{1,0:T(8,128)(2,1)} %slice.44), channel_id=1, source_target_pairs={{0,1},{1,0},{2,3},{3,2},{8,9},{9,8},{10,11},{11,10},{16,17},{17,16... | collective-permute-start | bytes 786440 | tf_op jit(solution)/shard_map/ppermute | solution.py:42
  49.1 3.4 %collective-permute-start.13 = (bf16[512,256]{1,0:T(8,128)(2,1)}, bf16[512,256]{1,0:T(8,128)(2,1)}, u32[]{:S(2)}, u32[]{:S(2)}) collective-permute-start(bf16[512,256]{1,0:T(8,128)(2,1)} %slice.45), channel_id=1, source_target_pairs={{0,2},{1,3},{2,0},{3,1},{8,10},{9,11},{10,8},{11,9},{16,18},{17,19... | collective-permute-start | bytes 786440 | tf_op jit(solution)/shard_map/ppermute | solution.py:42
  54.1 2.4 collective-permute-start.16
  58.1 1.9 collective-permute-start.17
  60.7 1.6 collective-permute-start.8
  65.2 2.2 shard_map.95.refs_6_
  69.0 1.5 collective-permute-start.18
  90.2 1.5 collective-permute-start.20
  102.0 1.5 collective-permute-start.21
  113.7 1.5 collective-permute-start.22
  127.3 61.2 %collective-permute-done.23.refs_1_ = bf16[64,4096]{1,0:T(8,128)(2,1)} collective-permute-done((bf16[64,4096]{1,0:T(8,128)(2,1)}, bf16[64,4096]{1,0:T(8,128)(2,1)}, u32[]{:S(2)}, u32[]{:S(2)}) %collective-permute-start.23) | collective-permute-done | bytes 524320 | tf_op jit(solution)/shard_map/ppermute | solution.py:42
  196.9 6.0 %shard_map.102 = (bf16[64,4096]{1,0:T(8,128)(2,1)}, bf16[128,256]{1,0:T(8,128)(2,1)S(1)}, bf16[128,4096]{1,0:T(8,128)(2,1)S(1)}, bf16[128,4096]{1,0:T(8,128)(2,1)}) custom-call(s32[5]{0:T(128)S(1)} %copy-done.103, bf16[64,4096]{1,0:T(8,128)(2,1)} %collective-permute-done.23.refs_1_, ...), custom_call_target="tpu_custom_call", output_to_operand_aliasing={{1}: (21, {}), {2}: (22, {}), {3}: (23, {})} | custom-call | tf_op jit(solution)/shard_map/pallas_call | solution.py:412
  204.8 2.2 constant_dynamic-slice_fusion.7
  207.0 1.5 collective-permute-start.25
  208.5 1.5 collective-permute-start.26
  211.1 1.6 collective-permute-start.31
  222.0 6.0 %shard_map.103 = (bf16[64,4096]{1,0:T(8,128)(2,1)}, bf16[128,256]{1,0:T(8,128)(2,1)S(1)}, bf16[128,4096]{1,0:T(8,128)(2,1)S(1)}, bf16[128,4096]{1,0:T(8,128)(2,1)}) custom-call(s32[5]{0:T(128)S(1)} %copy-done.96, bf16[64,4096]{1,0:T(8,128)(2,1)} %collective-permute-done.24.refs_1_, ...), custom_call_target="tpu_custom_call", output_to_operand_aliasing={{1}: (21, {}), {2}: (22, {}), {3}: (23, {})} | custom-call | tf_op jit(solution)/shard_map/pallas_call | solution.py:412
  227.9 1.6 collective-permute-start.28
  230.2 1.5 collective-permute-start.35
  233.1 1.5 collective-permute-start.29
  235.2 12.6 %collective-permute-done.29 = bf16[128,256]{1,0:T(8,128)(2,1)S(1)} collective-permute-done((bf16[128,256]{1,0:T(8,128)(2,1)S(1)}, bf16[128,256]{1,0:T(8,128)(2,1)S(1)}, u32[]{:S(2)}, u32[]{:S(2)}) %collective-permute-start.29) | collective-permute-done | bytes 65568 | tf_op jit(solution)/shard_map/ppermute | solution.py:42
  247.8 1.5 collective-permute-start.32
  249.8 2.4 fusion.3
  252.2 2.3 collective-permute-done.33
  (301 shorter events, 110.0 us)
Async XLA Ops:
  0.6 16.4 %collective-permute-start.1 = (bf16[1024,256]{1,0:T(8,128)(2,1)}, bf16[1024,256]{1,0:T(8,128)(2,1)S(1)}, u32[]{:S(2)}, u32[]{:S(2)}) collective-permute-start(bf16[1024,256]{1,0:T(8,128)(2,1)} %bitcast.42), channel_id=1, source_target_pairs={{4,6},{5,7},{6,4},{7,5},{12,14},{13,15},{14,12},{15,13},{20,22},{2... | collective-permute-start | bytes 1572872 | tf_op jit(solution)/shard_map/ppermute | solution.py:42
  1.5 17.0 %collective-permute-start = (bf16[1024,256]{1,0:T(8,128)(2,1)}, bf16[1024,256]{1,0:T(8,128)(2,1)S(1)}, u32[]{:S(2)}, u32[]{:S(2)}) collective-permute-start(bf16[1024,256]{1,0:T(8,128)(2,1)} %bitcast.43), channel_id=1, source_target_pairs={{4,5},{5,4},{6,7},{7,6},{12,13},{13,12},{14,15},{15,14},{20,21},{2... | collective-permute-start | bytes 1572872 | tf_op jit(solution)/shard_map/ppermute | solution.py:42
  4.6 8.5 %collective-permute-start.5 = (bf16[1280,128]{1,0:T(8,128)(2,1)S(1)}, bf16[1280,128]{1,0:T(8,128)(2,1)S(1)}, u32[]{:S(2)}, u32[]{:S(2)}) collective-permute-start(bf16[1280,128]{1,0:T(8,128)(2,1)S(1)} %pad_maximum_fusion.refs_8_), channel_id=1, source_target_pairs={{28,30},{29,31},{30,28},{31,29}} | collective-permute-start | bytes 983048 | tf_op jit(solution)/shard_map/ppermute | solution.py:42
  5.3 9.8 %collective-permute-start.4 = (bf16[1280,128]{1,0:T(8,128)(2,1)S(1)}, bf16[1280,128]{1,0:T(8,128)(2,1)S(1)}, u32[]{:S(2)}, u32[]{:S(2)}) collective-permute-start(bf16[1280,128]{1,0:T(8,128)(2,1)S(1)} %pad_maximum_fusion.refs_8_), channel_id=1, source_target_pairs={{28,29},{29,28},{30,31},{31,30}} | collective-permute-start | bytes 983048 | tf_op jit(solution)/shard_map/ppermute | solution.py:42
  6.0 36.1 %collective-permute-start.11 = (bf16[1024,256]{1,0:T(8,128)(2,1)}, bf16[1024,256]{1,0:T(8,128)(2,1)}, u32[]{:S(2)}, u32[]{:S(2)}) collective-permute-start(bf16[1024,256]{1,0:T(8,128)(2,1)} %bitcast.44), channel_id=1, source_target_pairs={{0,2},{1,3},{2,0},{3,1},{8,10},{9,11},{10,8},{11,9},{16,18},{17,19... | collective-permute-start | bytes 1572872 | tf_op jit(solution)/shard_map/ppermute | solution.py:42
  13.7 6.4 %collective-permute-start.6 = (bf16[640,128]{1,0:T(8,128)(2,1)}, bf16[640,128]{1,0:T(8,128)(2,1)}, u32[]{:S(2)}, u32[]{:S(2)}) collective-permute-start(bf16[640,128]{1,0:T(8,128)(2,1)} %slice.42), channel_id=1, source_target_pairs={{28,29},{29,28},{30,31},{31,30}} | collective-permute-start | bytes 491528 | tf_op jit(solution)/shard_map/ppermute | solution.py:42
  15.8 7.8 %collective-permute-start.7 = (bf16[640,128]{1,0:T(8,128)(2,1)}, bf16[640,128]{1,0:T(8,128)(2,1)}, u32[]{:S(2)}, u32[]{:S(2)}) collective-permute-start(bf16[640,128]{1,0:T(8,128)(2,1)} %slice.43), channel_id=1, source_target_pairs={{28,30},{29,31},{30,28},{31,29}} | collective-permute-start | bytes 491528 | tf_op jit(solution)/shard_map/ppermute | solution.py:42
  17.8 8.2 %collective-permute-start.2 = (bf16[512,256]{1,0:T(8,128)(2,1)}, bf16[512,256]{1,0:T(8,128)(2,1)S(1)}, u32[]{:S(2)}, u32[]{:S(2)}) collective-permute-start(bf16[512,256]{1,0:T(8,128)(2,1)} %slice.40), channel_id=1, source_target_pairs={{4,5},{5,4},{6,7},{7,6},{12,13},{13,12},{14,15},{15,14},{20,21},{2... | collective-permute-start | bytes 786440 | tf_op jit(solution)/shard_map/ppermute | solution.py:42
  19.3 8.7 %collective-permute-start.3 = (bf16[512,256]{1,0:T(8,128)(2,1)}, bf16[512,256]{1,0:T(8,128)(2,1)S(1)}, u32[]{:S(2)}, u32[]{:S(2)}) collective-permute-start(bf16[512,256]{1,0:T(8,128)(2,1)} %slice.41), channel_id=1, source_target_pairs={{4,6},{5,7},{6,4},{7,5},{12,14},{13,15},{14,12},{15,13},{20,22},{2... | collective-permute-start | bytes 786440 | tf_op jit(solution)/shard_map/ppermute | solution.py:42
  20.2 27.4 %collective-permute-start.10 = (bf16[1024,256]{1,0:T(8,128)(2,1)S(1)}, bf16[1024,256]{1,0:T(8,128)(2,1)S(1)}, u32[]{:S(2)}, u32[]{:S(2)}) collective-permute-start(bf16[1024,256]{1,0:T(8,128)(2,1)S(1)} %bitcast.45), channel_id=1, source_target_pairs={{0,1},{1,0},{2,3},{3,2},{8,9},{9,8},{10,11},{11,10},{16,17},{17,16... | collective-permute-start | bytes 1572872 | tf_op jit(solution)/shard_map/ppermute | solution.py:42
  23.6 29.0 %collective-permute-start.15 = (bf16[256,1024]{1,0:T(8,128)(2,1)}, bf16[256,1024]{1,0:T(8,128)(2,1)S(1)}, u32[]{:S(2)}, u32[]{:S(2)}) collective-permute-start(bf16[256,1024]{1,0:T(8,128)(2,1)} %bitcast.20.refs_8_), channel_id=1, source_target_pairs={{0,2},{1,3},{2,0},{3,1},{4,6},{5,7},{6,4},{7,5},{8,10},{9,11},{10,... | collective-permute-start | bytes 1572872 | tf_op jit(solution)/shard_map/ppermute | solution.py:42
  26.0 30.5 %collective-permute-start.14 = (bf16[256,1024]{1,0:T(8,128)(2,1)}, bf16[256,1024]{1,0:T(8,128)(2,1)S(1)}, u32[]{:S(2)}, u32[]{:S(2)}) collective-permute-start(bf16[256,1024]{1,0:T(8,128)(2,1)} %bitcast.20.refs_8_), channel_id=1, source_target_pairs={{0,1},{1,0},{2,3},{3,2},{4,5},{5,4},{6,7},{7,6},{8,9},{9,8},{10,11... | collective-permute-start | bytes 1572872 | tf_op jit(solution)/shard_map/ppermute | solution.py:42
  40.6 27.0 %collective-permute-start.9 = (bf16[64,4096]{1,0:T(8,128)(2,1)}, bf16[64,4096]{1,0:T(8,128)(2,1)}, u32[]{:S(2)}, u32[]{:S(2)}) collective-permute-start(bf16[64,4096]{1,0:T(8,128)(2,1)} %get-tuple-element.81), channel_id=1, source_target_pairs={{28,24},{29,25},{30,26},{31,27}} | collective-permute-start | bytes 1572872 | tf_op jit(solution)/shard_map/ppermute | solution.py:42
  43.7 17.0 %collective-permute-start.12 = (bf16[512,256]{1,0:T(8,128)(2,1)}, bf16[512,256]{1,0:T(8,128)(2,1)}, u32[]{:S(2)}, u32[]{:S(2)}) collective-permute-start(bf16[512,256]{1,0:T(8,128)(2,1)} %slice.44), channel_id=1, source_target_pairs={{0,1},{1,0},{2,3},{3,2},{8,9},{9,8},{10,11},{11,10},{16,17},{17,16... | collective-permute-start | bytes 786440 | tf_op jit(solution)/shard_map/ppermute | solution.py:42
  49.1 13.2 %collective-permute-start.13 = (bf16[512,256]{1,0:T(8,128)(2,1)}, bf16[512,256]{1,0:T(8,128)(2,1)}, u32[]{:S(2)}, u32[]{:S(2)}) collective-permute-start(bf16[512,256]{1,0:T(8,128)(2,1)} %slice.45), channel_id=1, source_target_pairs={{0,2},{1,3},{2,0},{3,1},{8,10},{9,11},{10,8},{11,9},{16,18},{17,19... | collective-permute-start | bytes 786440 | tf_op jit(solution)/shard_map/ppermute | solution.py:42
  54.1 13.3 %collective-permute-start.16 = (bf16[128,1024]{1,0:T(8,128)(2,1)}, bf16[128,1024]{1,0:T(8,128)(2,1)}, u32[]{:S(2)}, u32[]{:S(2)}) collective-permute-start(bf16[128,1024]{1,0:T(8,128)(2,1)} %slice.46), channel_id=1, source_target_pairs={{0,1},{1,0},{2,3},{3,2},{4,5},{5,4},{6,7},{7,6},{8,9},{9,8},{10,11... | collective-permute-start | bytes 786440 | tf_op jit(solution)/shard_map/ppermute | solution.py:42
  58.1 9.5 %collective-permute-start.17 = (bf16[128,1024]{1,0:T(8,128)(2,1)}, bf16[128,1024]{1,0:T(8,128)(2,1)}, u32[]{:S(2)}, u32[]{:S(2)}) collective-permute-start(bf16[128,1024]{1,0:T(8,128)(2,1)} %slice.47), channel_id=1, source_target_pairs={{0,2},{1,3},{2,0},{3,1},{4,6},{5,7},{6,4},{7,5},{8,10},{9,11},{10,... | collective-permute-start | bytes 786440 | tf_op jit(solution)/shard_map/ppermute | solution.py:42
  60.7 10.4 %collective-permute-start.8 = (bf16[64,4096]{1,0:T(8,128)(2,1)}, bf16[64,4096]{1,0:T(8,128)(2,1)}, u32[]{:S(2)}, u32[]{:S(2)}) collective-permute-start(bf16[64,4096]{1,0:T(8,128)(2,1)} %get-tuple-element.82), channel_id=1, source_target_pairs={{28,24},{29,25},{30,26},{31,27}} | collective-permute-start | bytes 1572872 | tf_op jit(solution)/shard_map/ppermute | solution.py:42
  125.4 63.2 %collective-permute-start.23 = (bf16[64,4096]{1,0:T(8,128)(2,1)}, bf16[64,4096]{1,0:T(8,128)(2,1)}, u32[]{:S(2)}, u32[]{:S(2)}) collective-permute-start(bf16[64,4096]{1,0:T(8,128)(2,1)} %get-tuple-element.62), channel_id=1, source_target_pairs={{4,0},{5,1},{6,2},{7,3},{8,4},{9,5},{10,6},{11,7}} | collective-permute-start | bytes 1572872 | tf_op jit(solution)/shard_map/ppermute | solution.py:42
  203.5 10.2 %collective-permute-start.24 = (bf16[64,4096]{1,0:T(8,128)(2,1)}, bf16[64,4096]{1,0:T(8,128)(2,1)}, u32[]{:S(2)}, u32[]{:S(2)}) collective-permute-start(bf16[64,4096]{1,0:T(8,128)(2,1)} %get-tuple-element.66), channel_id=1, source_target_pairs={{4,0},{5,1},{6,2},{7,3}} | collective-permute-start | bytes 1572872 | tf_op jit(solution)/shard_map/ppermute | solution.py:42
  207.0 22.6 %collective-permute-start.25 = (bf16[128,1024]{1,0:T(8,128)(2,1)}, bf16[128,1024]{1,0:T(8,128)(2,1)}, u32[]{:S(2)}, u32[]{:S(2)}) collective-permute-start(bf16[128,1024]{1,0:T(8,128)(2,1)} %get-tuple-element.80), channel_id=1, source_target_pairs={{0,1},{1,0},{2,3},{3,2},{4,5},{5,4},{6,7},{7,6},{8,9},{9,8},{10,11... | collective-permute-start | bytes 786440 | tf_op jit(solution)/shard_map/ppermute | solution.py:42
  208.5 21.7 %collective-permute-start.26 = (bf16[128,1024]{1,0:T(8,128)(2,1)}, bf16[128,1024]{1,0:T(8,128)(2,1)}, u32[]{:S(2)}, u32[]{:S(2)}) collective-permute-start(bf16[128,1024]{1,0:T(8,128)(2,1)} %get-tuple-element.79), channel_id=1, source_target_pairs={{0,2},{1,3},{2,0},{3,1},{4,6},{5,7},{6,4},{7,5},{8,10},{9,11},{10,... | collective-permute-start | bytes 786440 | tf_op jit(solution)/shard_map/ppermute | solution.py:42
  210.0 21.7 %collective-permute-start.27 = (bf16[128,1024]{1,0:T(8,128)(2,1)}, bf16[128,1024]{1,0:T(8,128)(2,1)}, u32[]{:S(2)}, u32[]{:S(2)}) collective-permute-start(bf16[128,1024]{1,0:T(8,128)(2,1)} %get-tuple-element.78), channel_id=1, source_target_pairs={{0,3},{1,2},{2,1},{3,0},{4,7},{5,6},{6,5},{7,4},{8,11},{9,10},{10,... | collective-permute-start | bytes 786440 | tf_op jit(solution)/shard_map/ppermute | solution.py:42
  211.1 22.0 %collective-permute-start.31 = (bf16[128,256]{1,0:T(8,128)(2,1)S(1)}, bf16[128,256]{1,0:T(8,128)(2,1)S(1)}, u32[]{:S(2)}, u32[]{:S(2)}) collective-permute-start(bf16[128,256]{1,0:T(8,128)(2,1)S(1)} %multiply_convert_fusion), channel_id=1, source_target_pairs={{0,1},{1,0},{2,3},{3,2},{4,5},{5,4},{6,7},{7,6},{8,9},{9,8},{10,11... | collective-permute-start | bytes 196616 | tf_op jit(solution)/shard_map/ppermute | solution.py:42
  227.9 6.8 %collective-permute-start.28 = (bf16[128,256]{1,0:T(8,128)(2,1)S(1)}, bf16[128,256]{1,0:T(8,128)(2,1)S(1)}, u32[]{:S(2)}, u32[]{:S(2)}) collective-permute-start(bf16[128,256]{1,0:T(8,128)(2,1)S(1)} %get-tuple-element.71), channel_id=1, source_target_pairs={{0,1},{1,0},{2,3},{3,2},{4,5},{5,4},{6,7},{7,6},{8,9},{9,8},{10,11... | collective-permute-start | bytes 196616 | tf_op jit(solution)/shard_map/ppermute | solution.py:42
  229.6 24.9 %collective-permute-start.34 = (bf16[128,1024]{1,0:T(8,128)(2,1)S(1)}, bf16[128,1024]{1,0:T(8,128)(2,1)S(1)}, u32[]{:S(2)}, u32[]{:S(2)}) collective-permute-start(bf16[128,1024]{1,0:T(8,128)(2,1)S(1)} %get-tuple-element.76), channel_id=1, source_target_pairs={{0,1},{1,0},{2,3},{3,2},{4,5},{5,4},{6,7},{7,6},{8,9},{9,8},{10,11... | collective-permute-start | bytes 786440 | tf_op jit(solution)/shard_map/ppermute | solution.py:42
  230.2 24.3 %collective-permute-start.35 = (bf16[128,1024]{1,0:T(8,128)(2,1)S(1)}, bf16[128,1024]{1,0:T(8,128)(2,1)S(1)}, u32[]{:S(2)}, u32[]{:S(2)}) collective-permute-start(bf16[128,1024]{1,0:T(8,128)(2,1)S(1)} %get-tuple-element.75), channel_id=1, source_target_pairs={{0,2},{1,3},{2,0},{3,1},{4,6},{5,7},{6,4},{7,5},{8,10},{9,11},{10,... | collective-permute-start | bytes 786440 | tf_op jit(solution)/shard_map/ppermute | solution.py:42
  231.7 22.7 %collective-permute-start.36 = (bf16[128,1024]{1,0:T(8,128)(2,1)S(1)}, bf16[128,1024]{1,0:T(8,128)(2,1)S(1)}, u32[]{:S(2)}, u32[]{:S(2)}) collective-permute-start(bf16[128,1024]{1,0:T(8,128)(2,1)S(1)} %get-tuple-element.74), channel_id=1, source_target_pairs={{0,3},{1,2},{2,1},{3,0},{4,7},{5,6},{6,5},{7,4},{8,11},{9,10},{10,... | collective-permute-start | bytes 786440 | tf_op jit(solution)/shard_map/ppermute | solution.py:42
  233.1 14.6 %collective-permute-start.29 = (bf16[128,256]{1,0:T(8,128)(2,1)S(1)}, bf16[128,256]{1,0:T(8,128)(2,1)S(1)}, u32[]{:S(2)}, u32[]{:S(2)}) collective-permute-start(bf16[128,256]{1,0:T(8,128)(2,1)S(1)} %get-tuple-element.71), channel_id=1, source_target_pairs={{0,2},{1,3},{2,0},{3,1},{4,6},{5,7},{6,4},{7,5},{8,10},{9,11},{10,... | collective-permute-start | bytes 196616 | tf_op jit(solution)/shard_map/ppermute | solution.py:42
  234.7 14.6 %collective-permute-start.30 = (bf16[128,256]{1,0:T(8,128)(2,1)S(1)}, bf16[128,256]{1,0:T(8,128)(2,1)S(1)}, u32[]{:S(2)}, u32[]{:S(2)}) collective-permute-start(bf16[128,256]{1,0:T(8,128)(2,1)S(1)} %get-tuple-element.71), channel_id=1, source_target_pairs={{0,3},{1,2},{2,1},{3,0},{4,7},{5,6},{6,5},{7,4},{8,11},{9,10},{10,... | collective-permute-start | bytes 196616 | tf_op jit(solution)/shard_map/ppermute | solution.py:42
  247.8 4.4 %collective-permute-start.32 = (bf16[128,256]{1,0:T(8,128)(2,1)S(1)}, bf16[128,256]{1,0:T(8,128)(2,1)S(1)}, u32[]{:S(2)}, u32[]{:S(2)}) collective-permute-start(bf16[128,256]{1,0:T(8,128)(2,1)S(1)} %multiply_convert_fusion), channel_id=1, source_target_pairs={{0,2},{1,3},{2,0},{3,1},{4,6},{5,7},{6,4},{7,5},{8,10},{9,11},{10,... | collective-permute-start | bytes 196616 | tf_op jit(solution)/shard_map/ppermute | solution.py:42
  249.3 5.2 %collective-permute-start.33 = (bf16[128,256]{1,0:T(8,128)(2,1)S(1)}, bf16[128,256]{1,0:T(8,128)(2,1)S(1)}, u32[]{:S(2)}, u32[]{:S(2)}) collective-permute-start(bf16[128,256]{1,0:T(8,128)(2,1)S(1)} %multiply_convert_fusion), channel_id=1, source_target_pairs={{0,3},{1,2},{2,1},{3,0},{4,7},{5,6},{6,5},{7,4},{8,11},{9,10},{10,... | collective-permute-start | bytes 196616 | tf_op jit(solution)/shard_map/ppermute | solution.py:42
  (112 other events, 241.7 us)

commit v2 on v0

v2 whole, which is shorter than its diff:
```python
import functools

import jax
import jax.numpy as jnp
from jax import lax
from jax.experimental import pallas as pl
from jax.experimental.pallas import tpu as pltpu
from jax.sharding import PartitionSpec as P

EPSILON = 1e-05
CHUNKS = 2
ANY = pl.BlockSpec(memory_space=pl.ANY)
VMEM = pl.BlockSpec(memory_space=pltpu.VMEM)
SMEM = pl.BlockSpec(memory_space=pltpu.SMEM)
PARAMS = pltpu.CompilerParams(vmem_limit_bytes=20 * 1024 * 1024)


def dot_nn(left, right):
    return lax.dot_general(
        left, right, (((1,), (0,)), ((), ())), preferred_element_type=jnp.float32
    )


def dot_nt(left, right):
    return lax.dot_general(
        left, right, (((1,), (1,)), ((), ())), preferred_element_type=jnp.float32
    )


def dot_tn(left, right):
    return lax.dot_general(
        left, right, (((0,), (0,)), ((), ())), preferred_element_type=jnp.float32
    )


def silu_slope(latent):
    sigmoid = jax.nn.sigmoid(latent)
    return sigmoid * (1.0 + latent * (1.0 - sigmoid))


def move(block, pairs):
    return lax.ppermute(block, ("section", "dp"), pairs)


def peers(sections, size, k):
    return [(s * size + i, s * size + (i ^ k)) for s in sections for i in range(size)]


def gather_pieces(block, sections, size, relay):
    rows = block.shape[0]
    if relay and size == 4:
        half = rows // 2
        from_x = move(block, peers(sections, size, 1))
        from_y = move(block, peers(sections, size, 2))
        low = move(from_y[:half], peers(sections, size, 1))
        high = move(from_x[half:], peers(sections, size, 2))
        return [[(0, rows, from_x)], [(0, rows, from_y)], [(0, half, low), (half, half, high)]]
    return [[(0, rows, move(block, peers(sections, size, k)))] for k in range(1, size)]


def flatten(pieces):
    return [part[2] for piece in pieces for part in piece]


def shapes_of(pieces):
    return [[(row, count) for row, count, _ in piece] for piece in pieces]


def pin(block):
    return pltpu.with_memory_space_constraint(block, pltpu.VMEM)


def columns(dp_index, k, width):
    return pl.ds(pl.multiple_of((dp_index ^ k) * width, width), width)


def top_kernel(size, layout, head_layout, *refs):
    flags, x, normed, gain, inverse, truth, mask = refs[:7]
    count = 1 + sum(len(parts) for parts in layout)
    head_count = 1 + sum(len(parts) for parts in head_layout)
    pieces = refs[7 : 7 + count]
    head_pieces = refs[7 + count : 7 + count + head_count]
    latent_out, latent_grad_out, arriving_out, grads_out, held, head, sems = refs[
        7 + count + head_count :
    ]
    dp_index = flags[0]
    width = held.shape[1]

    @pl.when(flags[2] == 1)
    def _():
        groups, at = [], 0
        for refs_of, layout_of, place in ((pieces, layout, held), (head_pieces, head_layout, head)):
            rows = place.shape[1]
            ref_at = 0
            for slot, parts in enumerate([[(0, rows)]] + layout_of):
                group = []
                for row, part_rows in parts:
                    copy = pltpu.make_async_copy(
                        refs_of[ref_at], place.at[slot, pl.ds(row, part_rows)], sems.at[at]
                    )
                    copy.start()
                    group.append(copy)
                    ref_at += 1
                    at += 1
                groups.append(group)
        latent = None
        for k in range(size):
            for copy in groups[k]:
                copy.wait()
            part = dot_nn(normed[:, columns(dp_index, k, width)], held[k])
            latent = part if latent is None else latent + part
        latent_out[...] = latent
        activated = jax.nn.silu(latent).astype(jnp.bfloat16)
        estimate = None
        product = None
        for k in range(size):
            for copy in groups[size + k]:
                copy.wait()
            part = dot_nn(x[:, columns(dp_index, k, width)], head[k, :width])
            extra = head[k, width:].astype(jnp.float32)
            estimate = part if estimate is None else estimate + part
            product = extra if product is None else product + extra
        product = product.astype(jnp.bfloat16)
        estimate = estimate + dot_nn(activated, product)
        error = (mask[:, :1] * (estimate - truth[...])).astype(jnp.bfloat16)
        hidden_grad = dot_nt(error, product)
        latent_grad = (hidden_grad * silu_slope(latent)).astype(jnp.bfloat16)
        latent_grad_out[...] = latent_grad
        scale = inverse[:, :1]
        mean = jnp.sum(latent_grad.astype(jnp.float32) * latent, axis=-1, keepdims=True) / (
            width * size
        )
        slope = scale * scale * mean
        for k in range(size):
            at_k = columns(dp_index, k, width)
            arriving = dot_nt(error, head[k, :width]).astype(jnp.bfloat16)
            arriving_out[:, at_k] = arriving
            scaled = dot_nt(latent_grad, held[k]) * gain[:, at_k].astype(jnp.float32)
            grads = (
                arriving.astype(jnp.float32)
                + scale * scaled
                - x[:, at_k].astype(jnp.float32) * slope
            )
            grads_out[:, at_k] = grads.astype(jnp.bfloat16)


def assemble_kernel(size, down_layout, up_layout, *refs):
    flags, normed, latent_in = refs[:3]
    down_count = 1 + sum(len(parts) for parts in down_layout)
    up_count = 1 + sum(len(parts) for parts in up_layout)
    down_refs = refs[3 : 3 + down_count]
    up_refs = refs[3 + down_count : 3 + down_count + up_count]
    latent, down, up, sems = refs[3 + down_count + up_count :]
    dp_index = flags[0]
    width = down.shape[0] // size
    latent_rows = up.shape[0] // size

    @pl.when(flags[2] == 0)
    def _():
        at = 0
        groups = []
        for refs_of, layout_of, place, rows in (
            (down_refs, down_layout, down, width),
            (up_refs, up_layout, up, latent_rows),
        ):
            ref_at = 0
            for slot, parts in enumerate([[(0, rows)]] + layout_of):
                group = []
                for row, part_rows in parts:
                    start = pl.multiple_of((dp_index ^ slot) * rows + row, 128)
                    copy = pltpu.make_async_copy(
                        refs_of[ref_at], place.at[pl.ds(start, part_rows)], sems.at[at]
                    )
                    copy.start()
                    group.append(copy)
                    ref_at += 1
                    at += 1
                groups.append(group)
        total = None
        for k in range(size):
            for copy in groups[k]:
                copy.wait()
            at_k = columns(dp_index, k, width)
            part = dot_nn(normed[:, at_k], down[at_k, :])
            total = part if total is None else total + part
        latent[...] = total
        for k in range(size):
            for copy in groups[size + k]:
                copy.wait()


def tick_kernel(step, size, sections, *refs):
    flags, received, gain, inverse = refs[:4]
    send, latent, down, up, x, latent_grads, arrivals, grads = refs[11:]
    rows, width = received.shape
    shard = width // size
    top = sections - 1
    section = flags[1]
    piece = step - (top - section)

    if step < CHUNKS:

        @pl.when(section == top)
        def _():
            send[...] = grads[step * rows : (step + 1) * rows]

    @pl.when((section < top) & (piece >= 0) & (piece < CHUNKS))
    def _():
        at_rows = pl.ds(pl.multiple_of(piece * rows, rows), rows)
        hidden_grad = None
        for k in range(size):
            at_k = slice(k * shard, (k + 1) * shard)
            part = dot_nt(received[:, at_k], up[k * up.shape[0] // size : (k + 1) * up.shape[0] // size])
            hidden_grad = part if hidden_grad is None else hidden_grad + part
        lat = latent[at_rows]
        latent_grad = (hidden_grad * silu_slope(lat)).astype(jnp.bfloat16)
        latent_grads[at_rows] = latent_grad
        scale = inverse[at_rows][:, :1]
        mean = jnp.sum(latent_grad.astype(jnp.float32) * lat, axis=-1, keepdims=True) / width
        slope = scale * scale * mean
        for k in range(size):
            at_k = slice(k * shard, (k + 1) * shard)
            arriving = received[:, at_k]
            arrivals[at_rows, at_k] = arriving
            scaled = dot_nt(latent_grad, down[at_k]) * gain[:, at_k].astype(jnp.float32)
            value = (
                arriving.astype(jnp.float32)
                + scale * scaled
                - x[at_rows, at_k].astype(jnp.float32) * slope
            ).astype(jnp.bfloat16)
            send[:, at_k] = value
            grads[at_rows, at_k] = value


def per_device(
    section_inputs, norm_gain, down_proj, up_proj, readout_matrix, ground_truth_series, valid_len
):
    size = lax.axis_size("dp")
    sections = lax.axis_size("section")
    top = sections - 1
    dp_index = lax.axis_index("dp")
    section = lax.axis_index("section")
    f32, bf16 = jnp.float32, jnp.bfloat16

    x = section_inputs[0]
    down_own, up_own = down_proj[0], up_proj[0]
    tokens, width = x.shape
    shard, latent_width = down_own.shape
    horizon = readout_matrix.shape[1]
    rows = tokens // CHUNKS

    down_top = gather_pieces(down_own, [top], size, False)
    head_own = jnp.concatenate(
        [readout_matrix, dot_nn(up_own, readout_matrix).astype(bf16)], axis=0
    )
    head_pieces = gather_pieces(head_own, [top], size, False)

    values = x.astype(f32)
    inverse = lax.rsqrt(jnp.mean(values * values, axis=-1, keepdims=True) + EPSILON)
    normed = (values * inverse * norm_gain.astype(f32)).astype(bf16)
    inverse = jnp.broadcast_to(inverse, (tokens, 128))
    per_micro = tokens // valid_len.shape[0]
    mask = (
        (jnp.arange(per_micro)[None, :] < valid_len[:, None]).astype(f32).reshape(tokens, 1)
    )
    mask = jnp.broadcast_to(mask, (tokens, 128))

    rest = list(range(top))
    up_rest, down_rest, _ = lax.optimization_barrier((up_own, down_own, down_top[0][0][2]))
    up_pieces = gather_pieces(up_rest, rest, size, True)
    down_pieces = gather_pieces(down_rest, rest, size, True)

    flags = jnp.stack(
        [dp_index.astype(jnp.int32), section.astype(jnp.int32), (section == top).astype(jnp.int32)]
    )

    down_refs = [down_own] + flatten(down_top)
    head_refs = [head_own] + flatten(head_pieces)
    latent, latent_grads, arrivals, grads = pl.pallas_call(
        functools.partial(top_kernel, size, shapes_of(down_top), shapes_of(head_pieces)),
        out_shape=(
            pltpu.VMEM((tokens, latent_width), f32),
            pltpu.VMEM((tokens, latent_width), bf16),
            pltpu.VMEM((tokens, width), bf16),
            pltpu.VMEM((tokens, width), bf16),
        ),
        in_specs=[SMEM] + [VMEM] * 6 + [ANY] * (len(down_refs) + len(head_refs)),
        out_specs=(VMEM,) * 4,
        scratch_shapes=[
            pltpu.VMEM((size, shard, latent_width), bf16),
            pltpu.VMEM((size, shard + latent_width, horizon), bf16),
            pltpu.SemaphoreType.DMA((len(down_refs) + len(head_refs),)),
        ],
        compiler_params=PARAMS,
    )(flags, x, normed, norm_gain, inverse, ground_truth_series, mask, *down_refs, *head_refs)

    def hop(block, senders):
        return move(
            block, [(s * size + i, (s - 1) * size + i) for s in senders for i in range(size)]
        )

    received = hop(grads[:rows], [top])

    down_refs = [down_own] + flatten(down_pieces)
    up_refs = [up_own] + flatten(up_pieces)
    latent, down, up = pl.pallas_call(
        functools.partial(assemble_kernel, size, shapes_of(down_pieces), shapes_of(up_pieces)),
        out_shape=(
            pltpu.VMEM((tokens, latent_width), f32),
            pltpu.VMEM((width, latent_width), bf16),
            pltpu.VMEM((size * latent_width, shard), bf16),
        ),
        in_specs=[SMEM, VMEM, VMEM] + [ANY] * (len(down_refs) + len(up_refs)),
        out_specs=(VMEM,) * 3,
        input_output_aliases={2: 0},
        scratch_shapes=[pltpu.SemaphoreType.DMA((len(down_refs) + len(up_refs),))],
        compiler_params=PARAMS,
    )(flags, normed, pin(latent), *down_refs, *up_refs)

    state = (latent, down, up, x, latent_grads, arrivals, grads)

    def tick(step, received, state):
        out = pl.pallas_call(
            functools.partial(tick_kernel, step, size, sections),
            out_shape=(jax.ShapeDtypeStruct((rows, width), bf16),)
            + tuple(pltpu.VMEM(part.shape, part.dtype) for part in state),
            in_specs=[SMEM, VMEM, VMEM, VMEM] + [VMEM] * len(state),
            out_specs=(VMEM,) * (1 + len(state)),
            input_output_aliases={4 + i: 1 + i for i in range(len(state))},
            compiler_params=PARAMS,
        )(flags, received, norm_gain, inverse, *[pin(part) for part in state])
        return out[0], tuple(out[1:])

    def exchange(block):
        out = [lax.dynamic_slice_in_dim(block, dp_index * shard, shard, 1)]
        for k in range(1, size):
            part = lax.dynamic_slice_in_dim(block, (dp_index ^ k) * shard, shard, 1)
            out.append(move(part, peers(range(sections), size, k)))
        return out

    def spread(block):
        return jnp.concatenate(
            [block]
            + [move(block, peers(range(sections), size, k)) for k in range(1, size)],
            axis=0,
        )

    exchanged = []
    for step in range(1, top + CHUNKS):
        if step >= top:
            piece = step - top
            block = state[5][piece * rows : (piece + 1) * rows]
            exchanged.append(exchange(jnp.where(section == 0, received, block)))
        send, state = tick(step, received, state)
        senders = [s for s in range(1, sections) if 0 <= step - (top - s) < CHUNKS]
        if senders:
            received = hop(send, senders)
    latent, _, _, _, latent_grads, arrivals, grads = state

    activated = jax.nn.silu(latent).astype(bf16)
    normed_columns = jnp.concatenate(exchange(normed), axis=0)
    activated_all = spread(activated)
    arriving_columns = jnp.concatenate(
        [exchanged[piece][k] for k in range(size) for piece in range(CHUNKS)], axis=0
    )
    latent_grads_all = spread(latent_grads)
    down_grads = dot_tn(normed_columns, latent_grads_all).astype(bf16)
    up_grads = dot_tn(activated_all, arriving_columns).astype(bf16)
    return (grads[None], down_grads[None], up_grads[None])


def solution(mesh):
    placed = (
        P("section", "dp", None),
        P("section", None),
        P("section", "dp", None),
        P("section", None, "dp"),
        P("dp", None),
        P("dp", None),
        P("dp"),
    )
    return jax.shard_map(
        per_device,
        mesh=mesh,
        in_specs=placed,
        out_specs=(P("section", "dp", None), P("section", "dp", None), P("section", None, "dp")),
        check_vma=False,
    )
```

time: 335 us -> 179 us (0.53)
  waiting for transfers between devices: 203 us -> 73.7 us
  matrix products: 30.1 us -> 3.87 us
  starting transfers between devices: 28.2 us -> 53.8 us
  blocking collectives: 23.3 us -> 0 us
  other arithmetic: 26.4 us -> 4.85 us
  local copies, waits for them, and re-layouts: 7.84 us -> 24.5 us
  Pallas kernels: 0 us -> 16 us
  between operations: 13.9 us -> 1.29 us
    all_gather x3 -> x0, waiting for transfers between devices: 100 us -> none  [the longest x1 37.4 us: per_device(): lax.all_gather(down_proj[0], 'dp', axis=0, tiled=True)]
    ppermute x15 -> x37, starting transfers between devices: 19.4 us -> 53.8 us  [move(): return lax.ppermute(block, ('section', 'dp'), pairs)]
    ppermute x15 -> x37, waiting for transfers between devices: 100 us -> 73.7 us  [move(): return lax.ppermute(block, ('section', 'dp'), pairs)]
    dot_general x19 -> x3, matrix products: 30.1 us -> 3.87 us  [the longest x2 2.55 us: dot_tn(): lax.dot_general(left, right, (((0,), (0,)), ((), ())), preferred_element_...]
    all_gather x2 -> x0, blocking collectives: 23.3 us -> none  [the longest x1 15.2 us: per_device(): lax.all_gather(activated, 'dp', axis=0, tiled=True)]
    dynamic_update_slice x16 -> x0, other arithmetic: 22.5 us -> none  [the longest x8 13.8 us: process(): lax.dynamic_update_index_in_dim(grads_prev, inputs_grad, picked, 0)]
    unnamed x12 -> x51, local copies, waits for them, and re-layouts: 1.06 us -> 17.8 us
    pallas_call x0 -> x10, Pallas kernels: none -> 16 us  [the longest x8 12.7 us: tick(): pl.pallas_call(functools.partial(tick_kernel, step, size, sections), out_...]
  transfers between devices with their start and end apart: 20 -> 37, of which waited for: 18 -> 9; matrix products, arithmetic and copies ran while one was open for 18% -> 7% of each run, Pallas kernels for 0% -> 4%
where the time goes in v2:
time: 179 us; the launch traced here: 178 us
  waiting for transfers between devices  73.7 us (41%)
  starting transfers between devices  53.8 us (30%)
  local copies, waits for them, and re-layouts  24.5 us (14%)
  Pallas kernels  16 us (9%)
  other arithmetic  4.85 us (3%)
  matrix products  3.87 us (2%)
    ppermute x37, waiting for transfers between devices, move(): return lax.ppermute(block, ('section', 'dp'), pairs)  73.7 us
    ppermute x37, starting transfers between devices, move(): return lax.ppermute(block, ('section', 'dp'), pairs)  53.8 us
    unnamed x51, local copies, waits for them, and re-layouts  17.8 us
    pallas_call x8, Pallas kernels, tick(): pl.pallas_call(functools.partial(tick_kernel, step, size, sections), out_...  12.7 us
  transfers between devices with their start and end apart: 37, of which 9 were waited for; matrix products, arithmetic and copies ran while one was open for 7% of the time, Pallas kernels for 4%

profile of v2, /device:TPU:0, one launch (start us, length us, event | category | flops | bytes accessed | tf_op | source)
XLA Modules:
  0.0 178.1 jit_solution(13856760005884003294)
XLA Ops:
  5.4 1.4 collective-permute-start.3
  6.8 1.4 collective-permute-start.4
  8.5 1.4 collective-permute-start.5
  11.2 4.8 %collective-permute-start.7 = (bf16[1024,256]{1,0:T(8,128)(2,1)}, bf16[1024,256]{1,0:T(8,128)(2,1)}, u32[]{:S(2)}, u32[]{:S(2)}) collective-permute-start(bf16[1024,256]{1,0:T(8,128)(2,1)} %bitcast.5.refs_7_.refs_3_), channel_id=1, source_target_pairs={{0,1},{1,0},{2,3},{3,2},{4,5},{5,4},{6,7},{7,6},{8,9},{9,8},{10,11... | collective-permute-start | bytes 1572872 | tf_op jit(solution)/shard_map/ppermute | solution.py:42
  16.1 3.4 %collective-permute-start.8 = (bf16[1024,256]{1,0:T(8,128)(2,1)}, bf16[1024,256]{1,0:T(8,128)(2,1)}, u32[]{:S(2)}, u32[]{:S(2)}) collective-permute-start(bf16[1024,256]{1,0:T(8,128)(2,1)} %bitcast.5.refs_7_.refs_3_), channel_id=1, source_target_pairs={{0,2},{1,3},{2,0},{3,1},{4,6},{5,7},{6,4},{7,5},{8,10},{9,11},{10,... | collective-permute-start | bytes 1572872 | tf_op jit(solution)/shard_map/ppermute | solution.py:42
  19.6 2.4 %collective-permute-start.11 = (bf16[256,1024]{1,0:T(8,128)(2,1)}, bf16[256,1024]{1,0:T(8,128)(2,1)}, u32[]{:S(2)}, u32[]{:S(2)}) collective-permute-start(bf16[256,1024]{1,0:T(8,128)(2,1)} %bitcast.6.refs_8_), channel_id=1, source_target_pairs={{0,1},{1,0},{2,3},{3,2},{4,5},{5,4},{6,7},{7,6},{8,9},{9,8},{10,11... | collective-permute-start | bytes 1572872 | tf_op jit(solution)/shard_map/ppermute | solution.py:42
  22.8 1.9 %collective-permute-start.12 = (bf16[256,1024]{1,0:T(8,128)(2,1)}, bf16[256,1024]{1,0:T(8,128)(2,1)}, u32[]{:S(2)}, u32[]{:S(2)}) collective-permute-start(bf16[256,1024]{1,0:T(8,128)(2,1)} %bitcast.6.refs_8_), channel_id=1, source_target_pairs={{0,2},{1,3},{2,0},{3,1},{4,6},{5,7},{6,4},{7,5},{8,10},{9,11},{10,... | collective-permute-start | bytes 1572872 | tf_op jit(solution)/shard_map/ppermute | solution.py:42
  34.1 3.5 %collective-permute-start.9 = (bf16[512,256]{1,0:T(8,128)(2,1)S(1)}, bf16[512,256]{1,0:T(8,128)(2,1)S(1)}, u32[]{:S(2)}, u32[]{:S(2)}) collective-permute-start(bf16[512,256]{1,0:T(8,128)(2,1)S(1)} %slice.28), channel_id=1, source_target_pairs={{0,1},{1,0},{2,3},{3,2},{4,5},{5,4},{6,7},{7,6},{8,9},{9,8},{10,11... | collective-permute-start | bytes 786440 | tf_op jit(solution)/shard_map/ppermute | solution.py:42
  38.7 3.4 %collective-permute-start.10 = (bf16[512,256]{1,0:T(8,128)(2,1)S(1)}, bf16[512,256]{1,0:T(8,128)(2,1)S(1)}, u32[]{:S(2)}, u32[]{:S(2)}) collective-permute-start(bf16[512,256]{1,0:T(8,128)(2,1)S(1)} %slice.29), channel_id=1, source_target_pairs={{0,2},{1,3},{2,0},{3,1},{4,6},{5,7},{6,4},{7,5},{8,10},{9,11},{10,... | collective-permute-start | bytes 786440 | tf_op jit(solution)/shard_map/ppermute | solution.py:42
  42.1 2.0 %collective-permute-done.12.refs_10_ = bf16[256,1024]{1,0:T(8,128)(2,1)} collective-permute-done((bf16[256,1024]{1,0:T(8,128)(2,1)}, bf16[256,1024]{1,0:T(8,128)(2,1)}, u32[]{:S(2)}, u32[]{:S(2)}) %collective-permute-start.12) | collective-permute-done | bytes 524320 | tf_op jit(solution)/shard_map/ppermute | solution.py:42
  45.1 2.2 %collective-permute-start.13 = (bf16[128,1024]{1,0:T(8,128)(2,1)S(1)}, bf16[128,1024]{1,0:T(8,128)(2,1)S(1)}, u32[]{:S(2)}, u32[]{:S(2)}) collective-permute-start(bf16[128,1024]{1,0:T(8,128)(2,1)S(1)} %slice.30), channel_id=1, source_target_pairs={{0,1},{1,0},{2,3},{3,2},{4,5},{5,4},{6,7},{7,6},{8,9},{9,8},{10,11... | collective-permute-start | bytes 786440 | tf_op jit(solution)/shard_map/ppermute | solution.py:42
  48.3 3.7 %collective-permute-start.14 = (bf16[128,1024]{1,0:T(8,128)(2,1)S(1)}, bf16[128,1024]{1,0:T(8,128)(2,1)S(1)}, u32[]{:S(2)}, u32[]{:S(2)}) collective-permute-start(bf16[128,1024]{1,0:T(8,128)(2,1)S(1)} %slice.31), channel_id=1, source_target_pairs={{0,2},{1,3},{2,0},{3,1},{4,6},{5,7},{6,4},{7,5},{8,10},{9,11},{10,... | collective-permute-start | bytes 786440 | tf_op jit(solution)/shard_map/ppermute | solution.py:42
  52.0 1.4 collective-permute-done.13.refs_11_
  53.3 3.2 %collective-permute-done.14.refs_12_ = bf16[128,1024]{1,0:T(8,128)(2,1)S(1)} collective-permute-done((bf16[128,1024]{1,0:T(8,128)(2,1)S(1)}, bf16[128,1024]{1,0:T(8,128)(2,1)S(1)}, u32[]{:S(2)}, u32[]{:S(2)}) %collective-permute-start.14) | collective-permute-done | bytes 262176 | tf_op jit(solution)/shard_map/ppermute | solution.py:42
  56.5 2.7 %shard_map.95 = (f32[128,256]{1,0:T(8,128)S(1)}, bf16[4096,256]{1,0:T(8,128)(2,1)S(1)}, bf16[1024,1024]{1,0:T(8,128)(2,1)S(1)}) custom-call(s32[3]{0:T(128)S(1)} %pad_add_fusion.refs_0_, bf16[128,4096]{1,0:T(8,128)(2,1)S(1)} %copy-done.9, f32[128,256]{1,0:T(8,128)S(1)} %get-tuple-element.72.refs_2_, ...), custom_call_target="tpu_custom_call", output_to_operand_aliasing={{0}: (2, {})} | custom-call | tf_op jit(solution)/shard_map/pallas_call | solution.py:306
  65.9 1.4 shard_map.101
  67.2 1.3 copy-done
  71.2 50.6 %collective-permute-done.20.refs_1_ = bf16[64,4096]{1,0:T(8,128)(2,1)} collective-permute-done((bf16[64,4096]{1,0:T(8,128)(2,1)}, bf16[64,4096]{1,0:T(8,128)(2,1)}, u32[]{:S(2)}, u32[]{:S(2)}) %collective-permute-start.20) | collective-permute-done | bytes 524320 | tf_op jit(solution)/shard_map/ppermute | solution.py:42
  121.8 1.9 %slice_select_fusion.1 = bf16[64,4096]{1,0:T(8,128)(2,1)} fusion(bf16[64,4096]{1,0:T(8,128)(2,1)} %collective-permute-done.20.refs_1_, bf16[128,4096]{1,0:T(8,128)(2,1)S(1)} %get-tuple-element.126.refs_9_, pred[]{:T(512)S(6)} %eq.8), kind=kLoop, calls=%fused_computation.18 | loop fusion | flops 262144 | bytes 1572865 | tf_op jit(solution)/shard_map/jit(_where)/select_n | solution.py:353
  123.7 1.6 copy-done.1
  125.3 1.6 copy-done.5
  126.9 4.2 %shard_map.102 = (bf16[64,4096]{1,0:T(8,128)(2,1)}, f32[128,256]{1,0:T(8,128)S(1)}, bf16[4096,256]{1,0:T(8,128)(2,1)S(1)}, bf16[1024,1024]{1,0:T(8,128)(2,1)S(1)...) custom-call(s32[3]{0:T(128)S(1)} %pad_add_fusion.refs_0_, ...), custom_call_target="tpu_custom_call", output_to_operand_aliasing={{1}: (4, {}), {2}: (5, {}), {3}: (6, {}), {4}: (7, {}), {5}... | custom-call | tf_op jit(solution)/shard_map/pallas_call | solution.py:323
  131.1 1.3 copy-done.2
  135.1 1.4 constant_dynamic-slice_fusion.9
  137.2 1.7 collective-permute-start.23
  144.1 4.3 %shard_map.103 = (bf16[64,4096]{1,0:T(8,128)(2,1)}, f32[128,256]{1,0:T(8,128)S(1)}, bf16[4096,256]{1,0:T(8,128)(2,1)S(1)}, bf16[1024,1024]{1,0:T(8,128)(2,1)S(1)...) custom-call(s32[3]{0:T(128)S(1)} %pad_add_fusion.refs_0_, ...), custom_call_target="tpu_custom_call", output_to_operand_aliasing={{1}: (4, {}), {2}: (5, {}), {3}: (6, {}), {4}: (7, {}), {5}... | custom-call | tf_op jit(solution)/shard_map/pallas_call | solution.py:323
  150.0 1.7 collective-permute-start.26
  153.1 2.2 %collective-permute-start.35 = (bf16[64,1024]{1,0:T(8,128)(2,1)S(1)}, bf16[64,1024]{1,0:T(8,128)(2,1)S(1)}, u32[]{:S(2)}, u32[]{:S(2)}) collective-permute-start(bf16[64,1024]{1,0:T(8,128)(2,1)S(1)} %get-tuple-element.147), channel_id=1, source_target_pairs={{0,3},{1,2},{2,1},{3,0},{4,7},{5,6},{6,5},{7,4},{8,11},{9,10},{10,... | collective-permute-start | bytes 393224 | tf_op jit(solution)/shard_map/ppermute | solution.py:42
  156.1 1.9 %collective-permute-start.29 = (bf16[128,256]{1,0:T(8,128)(2,1)S(1)}, bf16[128,256]{1,0:T(8,128)(2,1)S(1)}, u32[]{:S(2)}, u32[]{:S(2)}) collective-permute-start(bf16[128,256]{1,0:T(8,128)(2,1)S(1)} %multiply_convert_fusion), channel_id=1, source_target_pairs={{0,2},{1,3},{2,0},{3,1},{4,6},{5,7},{6,4},{7,5},{8,10},{9,11},{10,... | collective-permute-start | bytes 196616 | tf_op jit(solution)/shard_map/ppermute | solution.py:42
  160.1 4.1 %collective-permute-done.32 = bf16[64,1024]{1,0:T(8,128)(2,1)S(1)} collective-permute-done((bf16[64,1024]{1,0:T(8,128)(2,1)S(1)}, bf16[64,1024]{1,0:T(8,128)(2,1)S(1)}, u32[]{:S(2)}, u32[]{:S(2)}) %collective-permute-start.32) | collective-permute-done | bytes 131104 | tf_op jit(solution)/shard_map/ppermute | solution.py:42
  165.5 4.8 %collective-permute-done.34 = bf16[64,1024]{1,0:T(8,128)(2,1)S(1)} collective-permute-done((bf16[64,1024]{1,0:T(8,128)(2,1)S(1)}, bf16[64,1024]{1,0:T(8,128)(2,1)S(1)}, u32[]{:S(2)}, u32[]{:S(2)}) %collective-permute-start.34) | collective-permute-done | bytes 131104 | tf_op jit(solution)/shard_map/ppermute | solution.py:42
  170.4 6.4 %collective-permute-done.36 = bf16[64,1024]{1,0:T(8,128)(2,1)S(1)} collective-permute-done((bf16[64,1024]{1,0:T(8,128)(2,1)S(1)}, bf16[64,1024]{1,0:T(8,128)(2,1)S(1)}, u32[]{:S(2)}, u32[]{:S(2)}) %collective-permute-start.36) | collective-permute-done | bytes 131104 | tf_op jit(solution)/shard_map/ppermute | solution.py:42
  (128 shorter events, 45.5 us)
Async XLA Ops:
  1.9 6.6 %collective-permute-start = (bf16[1024,256]{1,0:T(8,128)(2,1)}, bf16[1024,256]{1,0:T(8,128)(2,1)S(1)}, u32[]{:S(2)}, u32[]{:S(2)}) collective-permute-start(bf16[1024,256]{1,0:T(8,128)(2,1)} %bitcast.5.refs_7_.refs_3_), channel_id=1, source_target_pairs={{28,29},{29,28},{30,31},{31,30}} | collective-permute-start | bytes 1572872 | tf_op jit(solution)/shard_map/ppermute | solution.py:42
  2.6 19.4 %collective-permute-start.1 = (bf16[1024,256]{1,0:T(8,128)(2,1)}, bf16[1024,256]{1,0:T(8,128)(2,1)S(1)}, u32[]{:S(2)}, u32[]{:S(2)}) collective-permute-start(bf16[1024,256]{1,0:T(8,128)(2,1)} %bitcast.5.refs_7_.refs_3_), channel_id=1, source_target_pairs={{28,30},{29,31},{30,28},{31,29}} | collective-permute-start | bytes 1572872 | tf_op jit(solution)/shard_map/ppermute | solution.py:42
  3.3 21.7 %collective-permute-start.2 = (bf16[1024,256]{1,0:T(8,128)(2,1)}, bf16[1024,256]{1,0:T(8,128)(2,1)S(1)}, u32[]{:S(2)}, u32[]{:S(2)}) collective-permute-start(bf16[1024,256]{1,0:T(8,128)(2,1)} %bitcast.5.refs_7_.refs_3_), channel_id=1, source_target_pairs={{28,31},{29,30},{30,29},{31,28}} | collective-permute-start | bytes 1572872 | tf_op jit(solution)/shard_map/ppermute | solution.py:42
  5.4 5.8 %collective-permute-start.3 = (bf16[1280,128]{1,0:T(8,128)(2,1)S(1)}, bf16[1280,128]{1,0:T(8,128)(2,1)}, u32[]{:S(2)}, u32[]{:S(2)}) collective-permute-start(bf16[1280,128]{1,0:T(8,128)(2,1)S(1)} %pad_maximum_fusion.refs_11_), channel_id=1, source_target_pairs={{28,29},{29,28},{30,31},{31,30}} | collective-permute-start | bytes 983048 | tf_op jit(solution)/shard_map/ppermute | solution.py:42
  6.8 9.3 %collective-permute-start.4 = (bf16[1280,128]{1,0:T(8,128)(2,1)S(1)}, bf16[1280,128]{1,0:T(8,128)(2,1)}, u32[]{:S(2)}, u32[]{:S(2)}) collective-permute-start(bf16[1280,128]{1,0:T(8,128)(2,1)S(1)} %pad_maximum_fusion.refs_11_), channel_id=1, source_target_pairs={{28,30},{29,31},{30,28},{31,29}} | collective-permute-start | bytes 983048 | tf_op jit(solution)/shard_map/ppermute | solution.py:42
  8.5 11.0 %collective-permute-start.5 = (bf16[1280,128]{1,0:T(8,128)(2,1)S(1)}, bf16[1280,128]{1,0:T(8,128)(2,1)}, u32[]{:S(2)}, u32[]{:S(2)}) collective-permute-start(bf16[1280,128]{1,0:T(8,128)(2,1)S(1)} %pad_maximum_fusion.refs_11_), channel_id=1, source_target_pairs={{28,31},{29,30},{30,29},{31,28}} | collective-permute-start | bytes 983048 | tf_op jit(solution)/shard_map/ppermute | solution.py:42
  11.2 26.4 %collective-permute-start.7 = (bf16[1024,256]{1,0:T(8,128)(2,1)}, bf16[1024,256]{1,0:T(8,128)(2,1)}, u32[]{:S(2)}, u32[]{:S(2)}) collective-permute-start(bf16[1024,256]{1,0:T(8,128)(2,1)} %bitcast.5.refs_7_.refs_3_), channel_id=1, source_target_pairs={{0,1},{1,0},{2,3},{3,2},{4,5},{5,4},{6,7},{7,6},{8,9},{9,8},{10,11... | collective-permute-start | bytes 1572872 | tf_op jit(solution)/shard_map/ppermute | solution.py:42
  16.1 17.1 %collective-permute-start.8 = (bf16[1024,256]{1,0:T(8,128)(2,1)}, bf16[1024,256]{1,0:T(8,128)(2,1)}, u32[]{:S(2)}, u32[]{:S(2)}) collective-permute-start(bf16[1024,256]{1,0:T(8,128)(2,1)} %bitcast.5.refs_7_.refs_3_), channel_id=1, source_target_pairs={{0,2},{1,3},{2,0},{3,1},{4,6},{5,7},{6,4},{7,5},{8,10},{9,11},{10,... | collective-permute-start | bytes 1572872 | tf_op jit(solution)/shard_map/ppermute | solution.py:42
  19.6 27.7 %collective-permute-start.11 = (bf16[256,1024]{1,0:T(8,128)(2,1)}, bf16[256,1024]{1,0:T(8,128)(2,1)}, u32[]{:S(2)}, u32[]{:S(2)}) collective-permute-start(bf16[256,1024]{1,0:T(8,128)(2,1)} %bitcast.6.refs_8_), channel_id=1, source_target_pairs={{0,1},{1,0},{2,3},{3,2},{4,5},{5,4},{6,7},{7,6},{8,9},{9,8},{10,11... | collective-permute-start | bytes 1572872 | tf_op jit(solution)/shard_map/ppermute | solution.py:42
  22.8 21.3 %collective-permute-start.12 = (bf16[256,1024]{1,0:T(8,128)(2,1)}, bf16[256,1024]{1,0:T(8,128)(2,1)}, u32[]{:S(2)}, u32[]{:S(2)}) collective-permute-start(bf16[256,1024]{1,0:T(8,128)(2,1)} %bitcast.6.refs_8_), channel_id=1, source_target_pairs={{0,2},{1,3},{2,0},{3,1},{4,6},{5,7},{6,4},{7,5},{8,10},{9,11},{10,... | collective-permute-start | bytes 1572872 | tf_op jit(solution)/shard_map/ppermute | solution.py:42
  32.0 27.3 %collective-permute-start.6 = (bf16[64,4096]{1,0:T(8,128)(2,1)S(1)}, bf16[64,4096]{1,0:T(8,128)(2,1)S(1)}, u32[]{:S(2)}, u32[]{:S(2)}) collective-permute-start(bf16[64,4096]{1,0:T(8,128)(2,1)S(1)} %slice.21), channel_id=1, source_target_pairs={{28,24},{29,25},{30,26},{31,27}} | collective-permute-start | bytes 1572872 | tf_op jit(solution)/shard_map/ppermute | solution.py:42
  34.1 17.8 %collective-permute-start.9 = (bf16[512,256]{1,0:T(8,128)(2,1)S(1)}, bf16[512,256]{1,0:T(8,128)(2,1)S(1)}, u32[]{:S(2)}, u32[]{:S(2)}) collective-permute-start(bf16[512,256]{1,0:T(8,128)(2,1)S(1)} %slice.28), channel_id=1, source_target_pairs={{0,1},{1,0},{2,3},{3,2},{4,5},{5,4},{6,7},{7,6},{8,9},{9,8},{10,11... | collective-permute-start | bytes 786440 | tf_op jit(solution)/shard_map/ppermute | solution.py:42
  38.7 13.3 %collective-permute-start.10 = (bf16[512,256]{1,0:T(8,128)(2,1)S(1)}, bf16[512,256]{1,0:T(8,128)(2,1)S(1)}, u32[]{:S(2)}, u32[]{:S(2)}) collective-permute-start(bf16[512,256]{1,0:T(8,128)(2,1)S(1)} %slice.29), channel_id=1, source_target_pairs={{0,2},{1,3},{2,0},{3,1},{4,6},{5,7},{6,4},{7,5},{8,10},{9,11},{10,... | collective-permute-start | bytes 786440 | tf_op jit(solution)/shard_map/ppermute | solution.py:42
  45.1 8.3 %collective-permute-start.13 = (bf16[128,1024]{1,0:T(8,128)(2,1)S(1)}, bf16[128,1024]{1,0:T(8,128)(2,1)S(1)}, u32[]{:S(2)}, u32[]{:S(2)}) collective-permute-start(bf16[128,1024]{1,0:T(8,128)(2,1)S(1)} %slice.30), channel_id=1, source_target_pairs={{0,1},{1,0},{2,3},{3,2},{4,5},{5,4},{6,7},{7,6},{8,9},{9,8},{10,11... | collective-permute-start | bytes 786440 | tf_op jit(solution)/shard_map/ppermute | solution.py:42
  48.3 8.3 %collective-permute-start.14 = (bf16[128,1024]{1,0:T(8,128)(2,1)S(1)}, bf16[128,1024]{1,0:T(8,128)(2,1)S(1)}, u32[]{:S(2)}, u32[]{:S(2)}) collective-permute-start(bf16[128,1024]{1,0:T(8,128)(2,1)S(1)} %slice.31), channel_id=1, source_target_pairs={{0,2},{1,3},{2,0},{3,1},{4,6},{5,7},{6,4},{7,5},{8,10},{9,11},{10,... | collective-permute-start | bytes 786440 | tf_op jit(solution)/shard_map/ppermute | solution.py:42
  69.9 51.9 %collective-permute-start.20 = (bf16[64,4096]{1,0:T(8,128)(2,1)}, bf16[64,4096]{1,0:T(8,128)(2,1)}, u32[]{:S(2)}, u32[]{:S(2)}) collective-permute-start(bf16[64,4096]{1,0:T(8,128)(2,1)} %get-tuple-element.120), channel_id=1, source_target_pairs={{4,0},{5,1},{6,2},{7,3},{8,4},{9,5},{10,6},{11,7}} | collective-permute-start | bytes 1572872 | tf_op jit(solution)/shard_map/ppermute | solution.py:42
  133.8 9.1 %collective-permute-start.21 = (bf16[64,4096]{1,0:T(8,128)(2,1)}, bf16[64,4096]{1,0:T(8,128)(2,1)}, u32[]{:S(2)}, u32[]{:S(2)}) collective-permute-start(bf16[64,4096]{1,0:T(8,128)(2,1)} %get-tuple-element.128), channel_id=1, source_target_pairs={{4,0},{5,1},{6,2},{7,3}} | collective-permute-start | bytes 1572872 | tf_op jit(solution)/shard_map/ppermute | solution.py:42
  136.6 13.4 %collective-permute-start.24 = (bf16[128,1024]{1,0:T(8,128)(2,1)S(1)}, bf16[128,1024]{1,0:T(8,128)(2,1)S(1)}, u32[]{:S(2)}, u32[]{:S(2)}) collective-permute-start(bf16[128,1024]{1,0:T(8,128)(2,1)S(1)} %get-tuple-element.140), channel_id=1, source_target_pairs={{0,3},{1,2},{2,1},{3,0},{4,7},{5,6},{6,5},{7,4},{8,11},{9,10},{10,... | collective-permute-start | bytes 786440 | tf_op jit(solution)/shard_map/ppermute | solution.py:42
  137.2 15.8 %collective-permute-start.23 = (bf16[128,1024]{1,0:T(8,128)(2,1)S(1)}, bf16[128,1024]{1,0:T(8,128)(2,1)S(1)}, u32[]{:S(2)}, u32[]{:S(2)}) collective-permute-start(bf16[128,1024]{1,0:T(8,128)(2,1)S(1)} %get-tuple-element.141), channel_id=1, source_target_pairs={{0,2},{1,3},{2,0},{3,1},{4,6},{5,7},{6,4},{7,5},{8,10},{9,11},{10,... | collective-permute-start | bytes 786440 | tf_op jit(solution)/shard_map/ppermute | solution.py:42
  138.9 14.3 %collective-permute-start.22 = (bf16[128,1024]{1,0:T(8,128)(2,1)S(1)}, bf16[128,1024]{1,0:T(8,128)(2,1)S(1)}, u32[]{:S(2)}, u32[]{:S(2)}) collective-permute-start(bf16[128,1024]{1,0:T(8,128)(2,1)S(1)} %get-tuple-element.142), channel_id=1, source_target_pairs={{0,1},{1,0},{2,3},{3,2},{4,5},{5,4},{6,7},{7,6},{8,9},{9,8},{10,11... | collective-permute-start | bytes 786440 | tf_op jit(solution)/shard_map/ppermute | solution.py:42
  141.3 10.5 %collective-permute-start.31 = (bf16[64,1024]{1,0:T(8,128)(2,1)S(1)}, bf16[64,1024]{1,0:T(8,128)(2,1)S(1)}, u32[]{:S(2)}, u32[]{:S(2)}) collective-permute-start(bf16[64,1024]{1,0:T(8,128)(2,1)S(1)} %get-tuple-element.149), channel_id=1, source_target_pairs={{0,1},{1,0},{2,3},{3,2},{4,5},{5,4},{6,7},{7,6},{8,9},{9,8},{10,11... | collective-permute-start | bytes 393224 | tf_op jit(solution)/shard_map/ppermute | solution.py:42
  149.4 5.9 %collective-permute-start.27 = (bf16[128,256]{1,0:T(8,128)(2,1)S(1)}, bf16[128,256]{1,0:T(8,128)(2,1)S(1)}, u32[]{:S(2)}, u32[]{:S(2)}) collective-permute-start(bf16[128,256]{1,0:T(8,128)(2,1)S(1)} %get-tuple-element.137), channel_id=1, source_target_pairs={{0,3},{1,2},{2,1},{3,0},{4,7},{5,6},{6,5},{7,4},{8,11},{9,10},{10,... | collective-permute-start | bytes 196616 | tf_op jit(solution)/shard_map/ppermute | solution.py:42
  150.0 6.1 %collective-permute-start.26 = (bf16[128,256]{1,0:T(8,128)(2,1)S(1)}, bf16[128,256]{1,0:T(8,128)(2,1)S(1)}, u32[]{:S(2)}, u32[]{:S(2)}) collective-permute-start(bf16[128,256]{1,0:T(8,128)(2,1)S(1)} %get-tuple-element.137), channel_id=1, source_target_pairs={{0,2},{1,3},{2,0},{3,1},{4,6},{5,7},{6,4},{7,5},{8,10},{9,11},{10,... | collective-permute-start | bytes 196616 | tf_op jit(solution)/shard_map/ppermute | solution.py:42
  151.7 6.3 %collective-permute-start.25 = (bf16[128,256]{1,0:T(8,128)(2,1)S(1)}, bf16[128,256]{1,0:T(8,128)(2,1)S(1)}, u32[]{:S(2)}, u32[]{:S(2)}) collective-permute-start(bf16[128,256]{1,0:T(8,128)(2,1)S(1)} %get-tuple-element.137), channel_id=1, source_target_pairs={{0,1},{1,0},{2,3},{3,2},{4,5},{5,4},{6,7},{7,6},{8,9},{9,8},{10,11... | collective-permute-start | bytes 196616 | tf_op jit(solution)/shard_map/ppermute | solution.py:42
  153.0 11.5 %collective-permute-start.33 = (bf16[64,1024]{1,0:T(8,128)(2,1)S(1)}, bf16[64,1024]{1,0:T(8,128)(2,1)S(1)}, u32[]{:S(2)}, u32[]{:S(2)}) collective-permute-start(bf16[64,1024]{1,0:T(8,128)(2,1)S(1)} %get-tuple-element.148), channel_id=1, source_target_pairs={{0,2},{1,3},{2,0},{3,1},{4,6},{5,7},{6,4},{7,5},{8,10},{9,11},{10,... | collective-permute-start | bytes 393224 | tf_op jit(solution)/shard_map/ppermute | solution.py:42
  153.1 17.2 %collective-permute-start.35 = (bf16[64,1024]{1,0:T(8,128)(2,1)S(1)}, bf16[64,1024]{1,0:T(8,128)(2,1)S(1)}, u32[]{:S(2)}, u32[]{:S(2)}) collective-permute-start(bf16[64,1024]{1,0:T(8,128)(2,1)S(1)} %get-tuple-element.147), channel_id=1, source_target_pairs={{0,3},{1,2},{2,1},{3,0},{4,7},{5,6},{6,5},{7,4},{8,11},{9,10},{10,... | collective-permute-start | bytes 393224 | tf_op jit(solution)/shard_map/ppermute | solution.py:42
  155.3 21.5 %collective-permute-start.30 = (bf16[128,256]{1,0:T(8,128)(2,1)S(1)}, bf16[128,256]{1,0:T(8,128)(2,1)S(1)}, u32[]{:S(2)}, u32[]{:S(2)}) collective-permute-start(bf16[128,256]{1,0:T(8,128)(2,1)S(1)} %multiply_convert_fusion), channel_id=1, source_target_pairs={{0,3},{1,2},{2,1},{3,0},{4,7},{5,6},{6,5},{7,4},{8,11},{9,10},{10,... | collective-permute-start | bytes 196616 | tf_op jit(solution)/shard_map/ppermute | solution.py:42
  156.1 20.7 %collective-permute-start.29 = (bf16[128,256]{1,0:T(8,128)(2,1)S(1)}, bf16[128,256]{1,0:T(8,128)(2,1)S(1)}, u32[]{:S(2)}, u32[]{:S(2)}) collective-permute-start(bf16[128,256]{1,0:T(8,128)(2,1)S(1)} %multiply_convert_fusion), channel_id=1, source_target_pairs={{0,2},{1,3},{2,0},{3,1},{4,6},{5,7},{6,4},{7,5},{8,10},{9,11},{10,... | collective-permute-start | bytes 196616 | tf_op jit(solution)/shard_map/ppermute | solution.py:42
  158.0 6.1 %collective-permute-start.32 = (bf16[64,1024]{1,0:T(8,128)(2,1)S(1)}, bf16[64,1024]{1,0:T(8,128)(2,1)S(1)}, u32[]{:S(2)}, u32[]{:S(2)}) collective-permute-start(bf16[64,1024]{1,0:T(8,128)(2,1)S(1)} %get-tuple-element.145), channel_id=1, source_target_pairs={{0,1},{1,0},{2,3},{3,2},{4,5},{5,4},{6,7},{7,6},{8,9},{9,8},{10,11... | collective-permute-start | bytes 393224 | tf_op jit(solution)/shard_map/ppermute | solution.py:42
  164.1 6.2 %collective-permute-start.34 = (bf16[64,1024]{1,0:T(8,128)(2,1)S(1)}, bf16[64,1024]{1,0:T(8,128)(2,1)S(1)}, u32[]{:S(2)}, u32[]{:S(2)}) collective-permute-start(bf16[64,1024]{1,0:T(8,128)(2,1)S(1)} %get-tuple-element.144), channel_id=1, source_target_pairs={{0,2},{1,3},{2,0},{3,1},{4,6},{5,7},{6,4},{7,5},{8,10},{9,11},{10,... | collective-permute-start | bytes 393224 | tf_op jit(solution)/shard_map/ppermute | solution.py:42
  164.5 12.3 %collective-permute-start.28 = (bf16[128,256]{1,0:T(8,128)(2,1)S(1)}, bf16[128,256]{1,0:T(8,128)(2,1)S(1)}, u32[]{:S(2)}, u32[]{:S(2)}) collective-permute-start(bf16[128,256]{1,0:T(8,128)(2,1)S(1)} %multiply_convert_fusion), channel_id=1, source_target_pairs={{0,1},{1,0},{2,3},{3,2},{4,5},{5,4},{6,7},{7,6},{8,9},{9,8},{10,11... | collective-permute-start | bytes 196616 | tf_op jit(solution)/shard_map/ppermute | solution.py:42
  170.3 6.4 %collective-permute-start.36 = (bf16[64,1024]{1,0:T(8,128)(2,1)S(1)}, bf16[64,1024]{1,0:T(8,128)(2,1)S(1)}, u32[]{:S(2)}, u32[]{:S(2)}) collective-permute-start(bf16[64,1024]{1,0:T(8,128)(2,1)S(1)} %get-tuple-element.143), channel_id=1, source_target_pairs={{0,3},{1,2},{2,1},{3,0},{4,7},{5,6},{6,5},{7,4},{8,11},{9,10},{10,... | collective-permute-start | bytes 393224 | tf_op jit(solution)/shard_map/ppermute | solution.py:42
  (27 other events, 150.4 us)

commit v3 on v2

v3 whole, which is shorter than its diff:
```python
import functools

import jax
import jax.numpy as jnp
from jax import lax
from jax.experimental import pallas as pl
from jax.experimental.pallas import tpu as pltpu
from jax.sharding import PartitionSpec as P

EPSILON = 1e-05
CHUNKS = 2
VMEM = pl.BlockSpec(memory_space=pltpu.VMEM)
SMEM = pl.BlockSpec(memory_space=pltpu.SMEM)
PARAMS = pltpu.CompilerParams(vmem_limit_bytes=20 * 1024 * 1024)


def dot_nn(left, right):
    return lax.dot_general(
        left, right, (((1,), (0,)), ((), ())), preferred_element_type=jnp.float32
    )


def dot_nt(left, right):
    return lax.dot_general(
        left, right, (((1,), (1,)), ((), ())), preferred_element_type=jnp.float32
    )


def dot_tn(left, right):
    return lax.dot_general(
        left, right, (((0,), (0,)), ((), ())), preferred_element_type=jnp.float32
    )


def silu_slope(latent):
    sigmoid = jax.nn.sigmoid(latent)
    return sigmoid * (1.0 + latent * (1.0 - sigmoid))


def move(block, pairs):
    return lax.ppermute(block, ("section", "dp"), pairs)


def peers(sections, size, k):
    return [(s * size + i, s * size + (i ^ k)) for s in sections for i in range(size)]


def gather_pieces(block, sections, size, relay):
    rows = block.shape[0]
    if relay and size == 4:
        half = rows // 2
        from_x = move(block, peers(sections, size, 1))
        from_y = move(block, peers(sections, size, 2))
        low = move(from_y[:half], peers(sections, size, 1))
        high = move(from_x[half:], peers(sections, size, 2))
        return [[(0, rows, from_x)], [(0, rows, from_y)], [(0, half, low), (half, half, high)]]
    return [[(0, rows, move(block, peers(sections, size, k)))] for k in range(1, size)]


def flatten(pieces):
    return [part[2] for piece in pieces for part in piece]


def shapes_of(pieces):
    return [[(row, count) for row, count, _ in piece] for piece in pieces]


def pin(block):
    return pltpu.with_memory_space_constraint(block, pltpu.VMEM)


def held_like(block):
    return pltpu.VMEM(block.shape, block.dtype)


def columns(dp_index, k, width):
    return pl.ds(pl.multiple_of((dp_index ^ k) * width, width), width)


def by_slot(refs, layout):
    out, at = [], 0
    for parts in layout:
        out.append([(row, rows, refs[at + i]) for i, (row, rows) in enumerate(parts)])
        at += len(parts)
    return out


def shift(dp_index, k, width, row, rows):
    return pl.ds(pl.multiple_of((dp_index ^ k) * width + row, 128), rows)


def head_kernel(readout, up, out):
    shard = readout.shape[0]
    out[:shard] = readout[...]
    out[shard:] = dot_nn(up[...], readout[...]).astype(jnp.bfloat16)


def norm_kernel(x, gain, x_out, normed_out, inverse_out):
    values = x[...].astype(jnp.float32)
    inverse = lax.rsqrt(jnp.mean(values * values, axis=-1, keepdims=True) + EPSILON)
    x_out[...] = x[...]
    normed_out[...] = (values * inverse * gain[...].astype(jnp.float32)).astype(jnp.bfloat16)
    inverse_out[...] = jnp.broadcast_to(inverse, inverse_out.shape)


def top_kernel(size, layout, head_layout, *refs):
    flags, gain, truth, mask = refs[:4]
    count = sum(len(parts) for parts in layout)
    head_count = sum(len(parts) for parts in head_layout)
    pieces = by_slot(refs[7 : 7 + count], layout)
    head = by_slot(refs[7 + count : 7 + count + head_count], head_layout)
    x, normed, inverse, latent_out, latent_grad_out, arriving_out, grads_out = refs[
        7 + count + head_count : 14 + count + head_count
    ]
    sends = refs[14 + count + head_count :]
    dp_index = flags[0]
    width = x.shape[1] // size
    rows = sends[0].shape[0]

    @pl.when(flags[2] == 1)
    def _():
        latent = None
        for k in range(size):
            for row, count, ref in pieces[k]:
                part = dot_nn(normed[:, shift(dp_index, k, width, row, count)], ref[...])
                latent = part if latent is None else latent + part
        latent_out[...] = latent
        activated = jax.nn.silu(latent).astype(jnp.bfloat16)
        estimate = None
        product = None
        for k in range(size):
            ref = head[k][0][2]
            part = dot_nn(x[:, columns(dp_index, k, width)], ref[:width])
            extra = ref[width:].astype(jnp.float32)
            estimate = part if estimate is None else estimate + part
            product = extra if product is None else product + extra
        product = product.astype(jnp.bfloat16)
        estimate = estimate + dot_nn(activated, product)
        error = (mask[:, :1] * (estimate - truth[...])).astype(jnp.bfloat16)
        hidden_grad = dot_nt(error, product)
        latent_grad = (hidden_grad * silu_slope(latent)).astype(jnp.bfloat16)
        latent_grad_out[...] = latent_grad
        scale = inverse[:, :1]
        mean = jnp.sum(latent_grad.astype(jnp.float32) * latent, axis=-1, keepdims=True) / (
            width * size
        )
        slope = scale * scale * mean
        for k in range(size):
            for row, count, ref in pieces[k]:
                at_k = shift(dp_index, k, width, row, count)
                arriving = dot_nt(error, head[k][0][2][row : row + count]).astype(jnp.bfloat16)
                arriving_out[:, at_k] = arriving
                scaled = dot_nt(latent_grad, ref[...]) * gain[:, at_k].astype(jnp.float32)
                grads = (
                    arriving.astype(jnp.float32)
                    + scale * scaled
                    - x[:, at_k].astype(jnp.float32) * slope
                ).astype(jnp.bfloat16)
                grads_out[:, at_k] = grads
                for i, send in enumerate(sends):
                    send[:, at_k] = grads[i * rows : (i + 1) * rows]


def latent_kernel(size, layout, *refs):
    flags = refs[0]
    count = sum(len(parts) for parts in layout)
    normed, latent = refs[3 + count : 5 + count]
    down = by_slot(refs[5 + count :], layout)
    width = normed.shape[1] // size

    @pl.when(flags[2] == 0)
    def _():
        total = None
        for k in range(size):
            for row, rows, ref in down[k]:
                part = dot_nn(normed[:, shift(flags[0], k, width, row, rows)], ref[...])
                total = part if total is None else total + part
        latent[...] = total


def message_kernel(size, *refs):
    flags = refs[0]
    normed, latent = refs[3:5]
    messages = refs[5:]
    shard = normed.shape[1] // size
    activated = jax.nn.silu(latent[...]).astype(jnp.bfloat16)
    for k in range(size):
        messages[k][:, :shard] = normed[:, columns(flags[0], k, shard)]
        messages[k][:, shard:] = activated


def stage_kernel(stage, piece, size, down_layout, up_layout, *refs):
    flags, received = refs[:2]
    down_count = sum(len(parts) for parts in down_layout)
    held = 7 + down_count + sum(len(parts) for parts in up_layout)
    state = refs[2 + held : 2 + 2 * held]
    gain, inverse, latent, x, latent_grads, arrivals, grads = state[:7]
    down = by_slot(state[7 : 7 + down_count], down_layout)
    up = by_slot(state[7 + down_count :], up_layout)
    outs = refs[2 + 2 * held :]
    rows, width = received.shape
    shard = width // size
    at_rows = slice(piece * rows, (piece + 1) * rows)

    @pl.when(flags[1] == stage)
    def _():
        hidden_grad = None
        for k in range(size):
            block = received[:, columns(flags[0], k, shard)]
            parts = [dot_nt(block, ref[...]) for _, _, ref in up[k]]
            part = parts[0] if len(parts) == 1 else jnp.concatenate(parts, axis=1)
            hidden_grad = part if hidden_grad is None else hidden_grad + part
        lat = latent[at_rows]
        latent_grad = (hidden_grad * silu_slope(lat)).astype(jnp.bfloat16)
        latent_grads[at_rows] = latent_grad
        scale = inverse[at_rows][:, :1]
        mean = jnp.sum(latent_grad.astype(jnp.float32) * lat, axis=-1, keepdims=True) / width
        slope = scale * scale * mean
        for k in range(size):
            for row, count, ref in down[k]:
                at_k = shift(flags[0], k, shard, row, count)
                arriving = received[:, at_k]
                arrivals[at_rows, at_k] = arriving
                scaled = dot_nt(latent_grad, ref[...]) * gain[:, at_k].astype(jnp.float32)
                value = (
                    arriving.astype(jnp.float32)
                    + scale * scaled
                    - x[at_rows, at_k].astype(jnp.float32) * slope
                ).astype(jnp.bfloat16)
                grads[at_rows, at_k] = value
                if stage:
                    outs[0][:, at_k] = value

    if stage == 0:
        for k in range(size):
            outs[k][:, :shard] = arrivals[at_rows, columns(flags[0], k, shard)]
            outs[k][:, shard:] = latent_grads[at_rows]


def weight_kernel(size, *refs):
    early = refs[:size]
    late = refs[size : size + size * CHUNKS]
    down_grads, up_grads, left, right = refs[size + size * CHUNKS :]
    tokens = early[0].shape[0]
    rows = tokens // CHUNKS
    shard = down_grads.shape[0]
    for k in range(size):
        left[k * tokens : (k + 1) * tokens] = early[k][...]
        for i in range(CHUNKS):
            at = k * tokens + i * rows
            right[at : at + rows] = late[i * size + k][...]
    down_grads[...] = dot_tn(left[:, :shard], right[:, shard:]).astype(jnp.bfloat16)
    up_grads[...] = dot_tn(left[:, shard:], right[:, :shard]).astype(jnp.bfloat16)


def per_device(
    section_inputs, norm_gain, down_proj, up_proj, readout_matrix, ground_truth_series, valid_len
):
    size = lax.axis_size("dp")
    sections = lax.axis_size("section")
    top = sections - 1
    dp_index = lax.axis_index("dp")
    section = lax.axis_index("section")
    f32, bf16 = jnp.float32, jnp.bfloat16

    x = section_inputs[0]
    down_own, up_own = down_proj[0], up_proj[0]
    tokens, width = x.shape
    shard, latent_width = down_own.shape
    horizon = readout_matrix.shape[1]
    rows = tokens // CHUNKS

    flags = jnp.stack(
        [dp_index.astype(jnp.int32), section.astype(jnp.int32), (section == top).astype(jnp.int32)]
    )
    down_top = gather_pieces(down_own, [top], size, False)
    head_own = pl.pallas_call(
        head_kernel,
        out_shape=jax.ShapeDtypeStruct((shard + latent_width, horizon), bf16),
        in_specs=[VMEM] * 2,
        out_specs=VMEM,
        compiler_params=PARAMS,
    )(readout_matrix, up_own)
    head_pieces = gather_pieces(head_own, [top], size, False)

    x, normed, inverse = pl.pallas_call(
        norm_kernel,
        out_shape=(
            pltpu.VMEM((tokens, width), bf16),
            pltpu.VMEM((tokens, width), bf16),
            pltpu.VMEM((tokens, 128), f32),
        ),
        in_specs=[VMEM] * 2,
        out_specs=(VMEM,) * 3,
        compiler_params=PARAMS,
    )(x, norm_gain)
    per_micro = tokens // valid_len.shape[0]
    mask = (
        (jnp.arange(per_micro)[None, :] < valid_len[:, None]).astype(f32).reshape(tokens, 1)
    )
    mask = jnp.broadcast_to(mask, (tokens, 128))

    rest = list(range(top))
    token = move(
        down_top[0][0][2][:16, :128], [(top * size + i, (top - 1) * size + i) for i in range(size)]
    )
    up_rest, down_rest, _ = lax.optimization_barrier((up_own, down_own, token))
    up_pieces = gather_pieces(up_rest, rest, size, False)
    down_pieces = gather_pieces(down_rest, rest, size, False)

    down_refs = [pin(part) for part in [down_own] + flatten(down_top)]
    head_refs = [pin(part) for part in [head_own] + flatten(head_pieces)]
    down_layout = [[(0, shard)]] + shapes_of(down_top)
    head_layout = [[(0, shard + latent_width)]] + shapes_of(head_pieces)
    x, normed, inverse, latent, latent_grads, arrivals, grads, *sends = pl.pallas_call(
        functools.partial(top_kernel, size, down_layout, head_layout),
        out_shape=(
            held_like(x),
            held_like(normed),
            held_like(inverse),
            pltpu.VMEM((tokens, latent_width), f32),
            pltpu.VMEM((tokens, latent_width), bf16),
            pltpu.VMEM((tokens, width), bf16),
            pltpu.VMEM((tokens, width), bf16),
        )
        + (jax.ShapeDtypeStruct((rows, width), bf16),) * CHUNKS,
        in_specs=[SMEM] + [VMEM] * (6 + len(down_refs) + len(head_refs)),
        out_specs=(VMEM,) * (7 + CHUNKS),
        input_output_aliases={4: 0, 5: 1, 6: 2},
        compiler_params=PARAMS,
    )(
        flags, norm_gain, ground_truth_series, mask, pin(x), pin(normed), pin(inverse),
        *down_refs, *head_refs,
    )

    def hop(block, sender):
        return move(block, [(sender * size + i, (sender - 1) * size + i) for i in range(size)])

    received = [hop(send, top) for send in sends]

    down_refs = [down_own] + flatten(down_pieces)
    up_refs = [up_own] + flatten(up_pieces)
    down_layout = [[(0, shard)]] + shapes_of(down_pieces)
    up_layout = [[(0, latent_width)]] + shapes_of(up_pieces)
    normed, latent, *down_refs = pl.pallas_call(
        functools.partial(latent_kernel, size, down_layout),
        out_shape=tuple(held_like(part) for part in (normed, latent, *down_refs)),
        in_specs=[SMEM] + [VMEM] * (2 + len(down_refs)),
        out_specs=(VMEM,) * (2 + len(down_refs)),
        input_output_aliases={1 + i: i for i in range(2 + len(down_refs))},
        compiler_params=PARAMS,
    )(flags, pin(normed), pin(latent), *[pin(part) for part in down_refs])

    message = jax.ShapeDtypeStruct((tokens, shard + latent_width), bf16)
    late_message = jax.ShapeDtypeStruct((rows, shard + latent_width), bf16)
    state = (norm_gain, inverse, latent, x, latent_grads, arrivals, grads, *down_refs, *up_refs)

    def run_stage(stage, piece, received, state):
        outs = (late_message,) * size if stage == 0 else (jax.ShapeDtypeStruct((rows, width), bf16),)
        results = pl.pallas_call(
            functools.partial(stage_kernel, stage, piece, size, down_layout, up_layout),
            out_shape=tuple(held_like(part) for part in state) + outs,
            in_specs=[SMEM] + [VMEM] * (1 + len(state)),
            out_specs=(VMEM,) * (len(state) + len(outs)),
            input_output_aliases={2 + i: i for i in range(len(state))},
            compiler_params=PARAMS,
        )(flags, received, *[pin(part) for part in state])
        return tuple(results[: len(state)]), results[len(state) :]

    def send_messages(messages):
        return [messages[0]] + [
            move(messages[k], peers(range(sections), size, k)) for k in range(1, size)
        ]

    late = []
    for stage in range(top - 1, -1, -1):
        sent = []
        for piece in range(CHUNKS):
            state, outs = run_stage(stage, piece, received[piece], state)
            if stage:
                sent.append(hop(outs[0], stage))
            else:
                late += send_messages(outs)
        received = sent
        if stage == top - 1:
            _, latent, *messages = pl.pallas_call(
                functools.partial(message_kernel, size),
                out_shape=(held_like(normed), held_like(latent)) + (message,) * size,
                in_specs=[SMEM, VMEM, VMEM],
                out_specs=(VMEM,) * (2 + size),
                input_output_aliases={1: 0, 2: 1},
                compiler_params=PARAMS,
            )(flags, pin(normed), pin(state[2]))
            state = state[:2] + (latent,) + state[3:]
            early = send_messages(messages)

    down_grads, up_grads = pl.pallas_call(
        functools.partial(weight_kernel, size),
        out_shape=(
            jax.ShapeDtypeStruct((shard, latent_width), bf16),
            jax.ShapeDtypeStruct((latent_width, shard), bf16),
        ),
        in_specs=[VMEM] * (size * (1 + CHUNKS)),
        out_specs=(VMEM,) * 2,
        scratch_shapes=[pltpu.VMEM((size * tokens, shard + latent_width), bf16)] * 2,
        compiler_params=PARAMS,
    )(*early, *late)
    return (state[6][None], down_grads[None], up_grads[None])


def solution(mesh):
    placed = (
        P("section", "dp", None),
        P("section", None),
        P("section", "dp", None),
        P("section", None, "dp"),
        P("dp", None),
        P("dp", None),
        P("dp"),
    )
    return jax.shard_map(
        per_device,
        mesh=mesh,
        in_specs=placed,
        out_specs=(P("section", "dp", None), P("section", "dp", None), P("section", None, "dp")),
        check_vma=False,
    )
```

time: 179 us -> 147 us (0.82)
  local copies, waits for them, and re-layouts: 24.5 us -> 7.11 us
  starting transfers between devices: 53.8 us -> 48.5 us
  other arithmetic: 4.85 us -> 0.15 us
  matrix products: 3.87 us -> 0 us
  waiting for transfers between devices: 73.7 us -> 70.7 us
  Pallas kernels: 16 us -> 18.6 us
    unnamed x51 -> x28, local copies, waits for them, and re-layouts: 17.8 us -> 6.96 us
    ppermute x37 -> x35, starting transfers between devices: 53.8 us -> 48.5 us  [move(): return lax.ppermute(block, ('section', 'dp'), pairs)]
    slice x5 -> x0, local copies, waits for them, and re-layouts: 3.91 us -> none  [the longest x2 1.94 us: gather_pieces(): high = move(from_x[half:], peers(sections, size, 2))]
    dot_general x3 -> x0, matrix products: 3.87 us -> none  [the longest x2 2.55 us: dot_tn(): lax.dot_general(left, right, (((0,), (0,)), ((), ())), preferred_element_...]
    ppermute x37 -> x35, waiting for transfers between devices: 73.7 us -> 70.7 us  [move(): return lax.ppermute(block, ('section', 'dp'), pairs)]
    select_n x2 -> x0, other arithmetic: 3 us -> none  [per_device(): exchanged.append(exchange(jnp.where(section == 0, received, block)))]
    dynamic_slice x3 -> x0, local copies, waits for them, and re-layouts: 2.59 us -> none  [the longest x1 1.42 us: exchange(): out = [lax.dynamic_slice_in_dim(block, dp_index * shard, shard, 1)]]
    pallas_call x10 -> x20, Pallas kernels: 16 us -> 18.6 us  [the longest x14 13 us: run_stage(): pl.pallas_call(functools.partial(stage_kernel, stage, piece, size, down_l...]
  transfers between devices with their start and end apart: 37 -> 35, of which waited for: 9 -> 10; matrix products, arithmetic and copies ran while one was open for 7% -> 1% of each run, Pallas kernels for 4% -> 12%
where the time goes in v3:
time: 147 us; the launch traced here: 146 us
  waiting for transfers between devices  70.7 us (48%)
  starting transfers between devices  48.5 us (33%)
  Pallas kernels  18.6 us (13%)
  local copies, waits for them, and re-layouts  7.11 us (5%)
    ppermute x35, waiting for transfers between devices, move(): return lax.ppermute(block, ('section', 'dp'), pairs)  70.7 us
    ppermute x35, starting transfers between devices, move(): return lax.ppermute(block, ('section', 'dp'), pairs)  48.5 us
    pallas_call x14, Pallas kernels, run_stage(): pl.pallas_call(functools.partial(stage_kernel, stage, piece, size, down_l...  13 us
    unnamed x28, local copies, waits for them, and re-layouts  6.96 us
  transfers between devices with their start and end apart: 35, of which 10 were waited for; matrix products, arithmetic and copies ran while one was open for 1% of the time, Pallas kernels for 12%

profile of v3, /device:TPU:0, one launch (start us, length us, event | category | flops | bytes accessed | tf_op | source)
XLA Modules:
  0.0 146.3 jit_solution(4673656564016923329)
XLA Ops:
  0.6 1.1 copy.457
  5.6 1.5 %collective-permute-start.1 = (bf16[1024,256]{1,0:T(8,128)(2,1)S(1)}, bf16[1024,256]{1,0:T(8,128)(2,1)}, u32[]{:S(2)}, u32[]{:S(2)}) collective-permute-start(bf16[1024,256]{1,0:T(8,128)(2,1)S(1)} %bitcast.11), channel_id=1, source_target_pairs={{28,30},{29,31},{30,28},{31,29}} | collective-permute-start | bytes 1572872 | tf_op jit(solution)/shard_map/ppermute | solution.py:41
  7.8 1.5 %collective-permute-start = (bf16[1024,256]{1,0:T(8,128)(2,1)S(1)}, bf16[1024,256]{1,0:T(8,128)(2,1)}, u32[]{:S(2)}, u32[]{:S(2)}) collective-permute-start(bf16[1024,256]{1,0:T(8,128)(2,1)S(1)} %bitcast.12), channel_id=1, source_target_pairs={{28,29},{29,28},{30,31},{31,30}} | collective-permute-start | bytes 1572872 | tf_op jit(solution)/shard_map/ppermute | solution.py:41
  10.0 5.8 %collective-permute-start.10 = (bf16[1024,256]{1,0:T(8,128)(2,1)S(1)}, bf16[1024,256]{1,0:T(8,128)(2,1)S(1)}, u32[]{:S(2)}, u32[]{:S(2)}) collective-permute-start(bf16[1024,256]{1,0:T(8,128)(2,1)S(1)} %bitcast.13), channel_id=1, source_target_pairs={{0,3},{1,2},{2,1},{3,0},{4,7},{5,6},{6,5},{7,4},{8,11},{9,10},{10,... | collective-permute-start | bytes 1572872 | tf_op jit(solution)/shard_map/ppermute | solution.py:41
  16.6 2.4 %collective-permute-start.9 = (bf16[1024,256]{1,0:T(8,128)(2,1)S(1)}, bf16[1024,256]{1,0:T(8,128)(2,1)S(1)}, u32[]{:S(2)}, u32[]{:S(2)}) collective-permute-start(bf16[1024,256]{1,0:T(8,128)(2,1)S(1)} %bitcast.14), channel_id=1, source_target_pairs={{0,2},{1,3},{2,0},{3,1},{4,6},{5,7},{6,4},{7,5},{8,10},{9,11},{10,... | collective-permute-start | bytes 1572872 | tf_op jit(solution)/shard_map/ppermute | solution.py:41
  19.0 2.0 %collective-permute-start.8 = (bf16[1024,256]{1,0:T(8,128)(2,1)S(1)}, bf16[1024,256]{1,0:T(8,128)(2,1)S(1)}, u32[]{:S(2)}, u32[]{:S(2)}) collective-permute-start(bf16[1024,256]{1,0:T(8,128)(2,1)S(1)} %bitcast.15), channel_id=1, source_target_pairs={{0,1},{1,0},{2,3},{3,2},{4,5},{5,4},{6,7},{7,6},{8,9},{9,8},{10,11... | collective-permute-start | bytes 1572872 | tf_op jit(solution)/shard_map/ppermute | solution.py:41
  21.8 1.2 copy-done
  23.8 4.8 %collective-permute-start.13 = (bf16[256,1024]{1,0:T(8,128)(2,1)S(1)}, bf16[256,1024]{1,0:T(8,128)(2,1)S(1)}, u32[]{:S(2)}, u32[]{:S(2)}) collective-permute-start(bf16[256,1024]{1,0:T(8,128)(2,1)S(1)} %bitcast.19), channel_id=1, source_target_pairs={{0,3},{1,2},{2,1},{3,0},{4,7},{5,6},{6,5},{7,4},{8,11},{9,10},{10,... | collective-permute-start | bytes 1572872 | tf_op jit(solution)/shard_map/ppermute | solution.py:41
  28.6 2.4 %collective-permute-start.12 = (bf16[256,1024]{1,0:T(8,128)(2,1)S(1)}, bf16[256,1024]{1,0:T(8,128)(2,1)S(1)}, u32[]{:S(2)}, u32[]{:S(2)}) collective-permute-start(bf16[256,1024]{1,0:T(8,128)(2,1)S(1)} %bitcast.20), channel_id=1, source_target_pairs={{0,2},{1,3},{2,0},{3,1},{4,6},{5,7},{6,4},{7,5},{8,10},{9,11},{10,... | collective-permute-start | bytes 1572872 | tf_op jit(solution)/shard_map/ppermute | solution.py:41
  31.2 1.2 shard_map.96
  32.4 2.0 %collective-permute-start.11 = (bf16[256,1024]{1,0:T(8,128)(2,1)S(1)}, bf16[256,1024]{1,0:T(8,128)(2,1)S(1)}, u32[]{:S(2)}, u32[]{:S(2)}) collective-permute-start(bf16[256,1024]{1,0:T(8,128)(2,1)S(1)} %bitcast.21), channel_id=1, source_target_pairs={{0,1},{1,0},{2,3},{3,2},{4,5},{5,4},{6,7},{7,6},{8,9},{9,8},{10,11... | collective-permute-start | bytes 1572872 | tf_op jit(solution)/shard_map/ppermute | solution.py:41
  34.4 5.5 %collective-permute-done.9.refs_5_ = bf16[1024,256]{1,0:T(8,128)(2,1)S(1)} collective-permute-done((bf16[1024,256]{1,0:T(8,128)(2,1)S(1)}, bf16[1024,256]{1,0:T(8,128)(2,1)S(1)}, u32[]{:S(2)}, u32[]{:S(2)}) %collective-permute-start.9) | collective-permute-done | bytes 524320 | tf_op jit(solution)/shard_map/ppermute | solution.py:41
  41.3 1.0 shard_map.97
  42.3 8.8 %collective-permute-done.13.refs_16_ = bf16[256,1024]{1,0:T(8,128)(2,1)S(1)} collective-permute-done((bf16[256,1024]{1,0:T(8,128)(2,1)S(1)}, bf16[256,1024]{1,0:T(8,128)(2,1)S(1)}, u32[]{:S(2)}, u32[]{:S(2)}) %collective-permute-start.13) | collective-permute-done | bytes 524320 | tf_op jit(solution)/shard_map/ppermute | solution.py:41
  51.1 10.3 %collective-permute-done.12.refs_15_ = bf16[256,1024]{1,0:T(8,128)(2,1)S(1)} collective-permute-done((bf16[256,1024]{1,0:T(8,128)(2,1)S(1)}, bf16[256,1024]{1,0:T(8,128)(2,1)S(1)}, u32[]{:S(2)}, u32[]{:S(2)}) %collective-permute-start.12) | collective-permute-done | bytes 524320 | tf_op jit(solution)/shard_map/ppermute | solution.py:41
  76.1 1.3 collective-permute-start.25
  78.0 1.3 collective-permute-start.24
  79.3 1.6 %collective-permute-start.26 = (bf16[128,1280]{1,0:T(8,128)(2,1)S(1)}, bf16[128,1280]{1,0:T(8,128)(2,1)S(1)}, u32[]{:S(2)}, u32[]{:S(2)}) collective-permute-start(bf16[128,1280]{1,0:T(8,128)(2,1)S(1)} %get-tuple-element.476), channel_id=1, source_target_pairs={{0,1},{1,0},{2,3},{3,2},{4,5},{5,4},{6,7},{7,6},{8,9},{9,8},{10,11... | collective-permute-start | bytes 983048 | tf_op jit(solution)/shard_map/ppermute | solution.py:41
  80.9 1.4 collective-permute-start.27
  82.9 32.3 %collective-permute-done.25.refs_1_ = bf16[64,4096]{1,0:T(8,128)(2,1)S(1)} collective-permute-done((bf16[64,4096]{1,0:T(8,128)(2,1)S(1)}, bf16[64,4096]{1,0:T(8,128)(2,1)S(1)}, u32[]{:S(2)}, u32[]{:S(2)}) %collective-permute-start.25) | collective-permute-done | bytes 524320 | tf_op jit(solution)/shard_map/ppermute | solution.py:41
  115.2 3.0 %shard_map.111 = (bf16[1,4096]{1,0:T(2,128)(2,1)S(1)}, f32[128,128]{1,0:T(8,128)S(1)}, f32[128,256]{1,0:T(8,128)S(1)}, bf16[128,4096]{1,0:T(8,128)(2,1)S(1)}, bf...) custom-call(s32[3]{0:T(128)S(1)} %pad_add_fusion.refs_0_, ...), custom_call_target="tpu_custom_call", output_to_operand_aliasing={{0}: (2, {}), {1}: (3, {}), {2}: (4, {}), {3}: (5, {}), {4}... | custom-call | tf_op jit(solution)/shard_map/pallas_call | solution.py:360
  118.2 2.8 %collective-permute-done.24.refs_1_ = bf16[64,4096]{1,0:T(8,128)(2,1)S(1)} collective-permute-done((bf16[64,4096]{1,0:T(8,128)(2,1)S(1)}, bf16[64,4096]{1,0:T(8,128)(2,1)S(1)}, u32[]{:S(2)}, u32[]{:S(2)}) %collective-permute-start.24) | collective-permute-done | bytes 524320 | tf_op jit(solution)/shard_map/ppermute | solution.py:41
  121.0 3.0 %shard_map.112 = (bf16[1,4096]{1,0:T(2,128)(2,1)S(1)}, f32[128,128]{1,0:T(8,128)S(1)}, f32[128,256]{1,0:T(8,128)S(1)}, bf16[128,4096]{1,0:T(8,128)(2,1)S(1)}, bf...) custom-call(s32[3]{0:T(128)S(1)} %pad_add_fusion.refs_0_, ...), custom_call_target="tpu_custom_call", output_to_operand_aliasing={{0}: (2, {}), {1}: (3, {}), {2}: (4, {}), {3}: (5, {}), {4}... | custom-call | tf_op jit(solution)/shard_map/pallas_call | solution.py:360
  123.9 1.6 %collective-permute-start.32 = (bf16[64,1280]{1,0:T(8,128)(2,1)S(1)}, bf16[64,1280]{1,0:T(8,128)(2,1)S(1)}, u32[]{:S(2)}, u32[]{:S(2)}) collective-permute-start(bf16[64,1280]{1,0:T(8,128)(2,1)S(1)} %get-tuple-element.484), channel_id=1, source_target_pairs={{0,1},{1,0},{2,3},{3,2},{4,5},{5,4},{6,7},{7,6},{8,9},{9,8},{10,11... | collective-permute-start | bytes 491528 | tf_op jit(solution)/shard_map/ppermute | solution.py:41
  125.5 1.5 %collective-permute-start.33 = (bf16[64,1280]{1,0:T(8,128)(2,1)S(1)}, bf16[64,1280]{1,0:T(8,128)(2,1)S(1)}, u32[]{:S(2)}, u32[]{:S(2)}) collective-permute-start(bf16[64,1280]{1,0:T(8,128)(2,1)S(1)} %get-tuple-element.485), channel_id=1, source_target_pairs={{0,2},{1,3},{2,0},{3,1},{4,6},{5,7},{6,4},{7,5},{8,10},{9,11},{10,... | collective-permute-start | bytes 491528 | tf_op jit(solution)/shard_map/ppermute | solution.py:41
  127.5 1.5 %collective-permute-start.29 = (bf16[64,1280]{1,0:T(8,128)(2,1)S(1)}, bf16[64,1280]{1,0:T(8,128)(2,1)S(1)}, u32[]{:S(2)}, u32[]{:S(2)}) collective-permute-start(bf16[64,1280]{1,0:T(8,128)(2,1)S(1)} %get-tuple-element.480), channel_id=1, source_target_pairs={{0,1},{1,0},{2,3},{3,2},{4,5},{5,4},{6,7},{7,6},{8,9},{9,8},{10,11... | collective-permute-start | bytes 491528 | tf_op jit(solution)/shard_map/ppermute | solution.py:41
  129.0 1.5 %collective-permute-start.30 = (bf16[64,1280]{1,0:T(8,128)(2,1)S(1)}, bf16[64,1280]{1,0:T(8,128)(2,1)S(1)}, u32[]{:S(2)}, u32[]{:S(2)}) collective-permute-start(bf16[64,1280]{1,0:T(8,128)(2,1)S(1)} %get-tuple-element.481), channel_id=1, source_target_pairs={{0,2},{1,3},{2,0},{3,1},{4,6},{5,7},{6,4},{7,5},{8,10},{9,11},{10,... | collective-permute-start | bytes 491528 | tf_op jit(solution)/shard_map/ppermute | solution.py:41
  131.1 2.4 %collective-permute-start.31 = (bf16[64,1280]{1,0:T(8,128)(2,1)S(1)}, bf16[64,1280]{1,0:T(8,128)(2,1)S(1)}, u32[]{:S(2)}, u32[]{:S(2)}) collective-permute-start(bf16[64,1280]{1,0:T(8,128)(2,1)S(1)} %get-tuple-element.482), channel_id=1, source_target_pairs={{0,3},{1,2},{2,1},{3,0},{4,7},{5,6},{6,5},{7,4},{8,11},{9,10},{10,... | collective-permute-start | bytes 491528 | tf_op jit(solution)/shard_map/ppermute | solution.py:41
  134.6 1.6 %collective-permute-done.33.refs_10_ = bf16[64,1280]{1,0:T(8,128)(2,1)S(1)} collective-permute-done((bf16[64,1280]{1,0:T(8,128)(2,1)S(1)}, bf16[64,1280]{1,0:T(8,128)(2,1)S(1)}, u32[]{:S(2)}, u32[]{:S(2)}) %collective-permute-start.33) | collective-permute-done | bytes 163872 | tf_op jit(solution)/shard_map/ppermute | solution.py:41
  136.2 2.0 %collective-permute-done.29.refs_5_ = bf16[64,1280]{1,0:T(8,128)(2,1)S(1)} collective-permute-done((bf16[64,1280]{1,0:T(8,128)(2,1)S(1)}, bf16[64,1280]{1,0:T(8,128)(2,1)S(1)}, u32[]{:S(2)}, u32[]{:S(2)}) %collective-permute-start.29) | collective-permute-done | bytes 163872 | tf_op jit(solution)/shard_map/ppermute | solution.py:41
  138.2 6.4 %collective-permute-done.30.refs_6_ = bf16[64,1280]{1,0:T(8,128)(2,1)S(1)} collective-permute-done((bf16[64,1280]{1,0:T(8,128)(2,1)S(1)}, bf16[64,1280]{1,0:T(8,128)(2,1)S(1)}, u32[]{:S(2)}, u32[]{:S(2)}) %collective-permute-start.30) | collective-permute-done | bytes 163872 | tf_op jit(solution)/shard_map/ppermute | solution.py:41
  144.5 1.7 %shard_map.113 = (bf16[1024,256]{1,0:T(8,128)(2,1)}, bf16[256,1024]{1,0:T(8,128)(2,1)}) custom-call(bf16[128,1280]{1,0:T(8,128)(2,1)S(1)} %get-tuple-element.475.refs_0_, bf16[128,1280]{1,0:T(8,128)(2,1)S(1)} %collective-permute-done.26.refs_1_, bf16[128,1280]{1,0:T(8,128)(2,1)S(1)} %collective-permute-done.27.refs_2_, ...), custom_call_target="tpu_custom_call" | custom-call | tf_op jit(solution)/shard_map/pallas_call | solution.py:397
  (90 shorter events, 26.8 us)
Async XLA Ops:
  2.6 16.4 %collective-permute-start.2 = (bf16[1024,256]{1,0:T(8,128)(2,1)S(1)}, bf16[1024,256]{1,0:T(8,128)(2,1)S(1)}, u32[]{:S(2)}, u32[]{:S(2)}) collective-permute-start(bf16[1024,256]{1,0:T(8,128)(2,1)S(1)} %bitcast.10), channel_id=1, source_target_pairs={{28,31},{29,30},{30,29},{31,28}} | collective-permute-start | bytes 1572872 | tf_op jit(solution)/shard_map/ppermute | solution.py:41
  3.6 3.5 %collective-permute-start.5 = (bf16[1280,128]{1,0:T(8,128)(2,1)S(1)}, bf16[1280,128]{1,0:T(8,128)(2,1)S(1)}, u32[]{:S(2)}, u32[]{:S(2)}) collective-permute-start(bf16[1280,128]{1,0:T(8,128)(2,1)S(1)} %shard_map.95.refs_11_), channel_id=1, source_target_pairs={{28,31},{29,30},{30,29},{31,28}} | collective-permute-start | bytes 983048 | tf_op jit(solution)/shard_map/ppermute | solution.py:41
  4.3 5.0 %collective-permute-start.4 = (bf16[1280,128]{1,0:T(8,128)(2,1)S(1)}, bf16[1280,128]{1,0:T(8,128)(2,1)S(1)}, u32[]{:S(2)}, u32[]{:S(2)}) collective-permute-start(bf16[1280,128]{1,0:T(8,128)(2,1)S(1)} %shard_map.95.refs_11_), channel_id=1, source_target_pairs={{28,30},{29,31},{30,28},{31,29}} | collective-permute-start | bytes 983048 | tf_op jit(solution)/shard_map/ppermute | solution.py:41
  5.0 10.9 %collective-permute-start.3 = (bf16[1280,128]{1,0:T(8,128)(2,1)S(1)}, bf16[1280,128]{1,0:T(8,128)(2,1)S(1)}, u32[]{:S(2)}, u32[]{:S(2)}) collective-permute-start(bf16[1280,128]{1,0:T(8,128)(2,1)S(1)} %shard_map.95.refs_11_), channel_id=1, source_target_pairs={{28,29},{29,28},{30,31},{31,30}} | collective-permute-start | bytes 983048 | tf_op jit(solution)/shard_map/ppermute | solution.py:41
  5.6 18.2 %collective-permute-start.1 = (bf16[1024,256]{1,0:T(8,128)(2,1)S(1)}, bf16[1024,256]{1,0:T(8,128)(2,1)}, u32[]{:S(2)}, u32[]{:S(2)}) collective-permute-start(bf16[1024,256]{1,0:T(8,128)(2,1)S(1)} %bitcast.11), channel_id=1, source_target_pairs={{28,30},{29,31},{30,28},{31,29}} | collective-permute-start | bytes 1572872 | tf_op jit(solution)/shard_map/ppermute | solution.py:41
  7.8 20.8 %collective-permute-start = (bf16[1024,256]{1,0:T(8,128)(2,1)S(1)}, bf16[1024,256]{1,0:T(8,128)(2,1)}, u32[]{:S(2)}, u32[]{:S(2)}) collective-permute-start(bf16[1024,256]{1,0:T(8,128)(2,1)S(1)} %bitcast.12), channel_id=1, source_target_pairs={{28,29},{29,28},{30,31},{31,30}} | collective-permute-start | bytes 1572872 | tf_op jit(solution)/shard_map/ppermute | solution.py:41
  10.0 22.4 %collective-permute-start.10 = (bf16[1024,256]{1,0:T(8,128)(2,1)S(1)}, bf16[1024,256]{1,0:T(8,128)(2,1)S(1)}, u32[]{:S(2)}, u32[]{:S(2)}) collective-permute-start(bf16[1024,256]{1,0:T(8,128)(2,1)S(1)} %bitcast.13), channel_id=1, source_target_pairs={{0,3},{1,2},{2,1},{3,0},{4,7},{5,6},{6,5},{7,4},{8,11},{9,10},{10,... | collective-permute-start | bytes 1572872 | tf_op jit(solution)/shard_map/ppermute | solution.py:41
  16.6 23.3 %collective-permute-start.9 = (bf16[1024,256]{1,0:T(8,128)(2,1)S(1)}, bf16[1024,256]{1,0:T(8,128)(2,1)S(1)}, u32[]{:S(2)}, u32[]{:S(2)}) collective-permute-start(bf16[1024,256]{1,0:T(8,128)(2,1)S(1)} %bitcast.14), channel_id=1, source_target_pairs={{0,2},{1,3},{2,0},{3,1},{4,6},{5,7},{6,4},{7,5},{8,10},{9,11},{10,... | collective-permute-start | bytes 1572872 | tf_op jit(solution)/shard_map/ppermute | solution.py:41
  19.0 21.6 %collective-permute-start.8 = (bf16[1024,256]{1,0:T(8,128)(2,1)S(1)}, bf16[1024,256]{1,0:T(8,128)(2,1)S(1)}, u32[]{:S(2)}, u32[]{:S(2)}) collective-permute-start(bf16[1024,256]{1,0:T(8,128)(2,1)S(1)} %bitcast.15), channel_id=1, source_target_pairs={{0,1},{1,0},{2,3},{3,2},{4,5},{5,4},{6,7},{7,6},{8,9},{9,8},{10,11... | collective-permute-start | bytes 1572872 | tf_op jit(solution)/shard_map/ppermute | solution.py:41
  23.8 27.3 %collective-permute-start.13 = (bf16[256,1024]{1,0:T(8,128)(2,1)S(1)}, bf16[256,1024]{1,0:T(8,128)(2,1)S(1)}, u32[]{:S(2)}, u32[]{:S(2)}) collective-permute-start(bf16[256,1024]{1,0:T(8,128)(2,1)S(1)} %bitcast.19), channel_id=1, source_target_pairs={{0,3},{1,2},{2,1},{3,0},{4,7},{5,6},{6,5},{7,4},{8,11},{9,10},{10,... | collective-permute-start | bytes 1572872 | tf_op jit(solution)/shard_map/ppermute | solution.py:41
  28.6 32.8 %collective-permute-start.12 = (bf16[256,1024]{1,0:T(8,128)(2,1)S(1)}, bf16[256,1024]{1,0:T(8,128)(2,1)S(1)}, u32[]{:S(2)}, u32[]{:S(2)}) collective-permute-start(bf16[256,1024]{1,0:T(8,128)(2,1)S(1)} %bitcast.20), channel_id=1, source_target_pairs={{0,2},{1,3},{2,0},{3,1},{4,6},{5,7},{6,4},{7,5},{8,10},{9,11},{10,... | collective-permute-start | bytes 1572872 | tf_op jit(solution)/shard_map/ppermute | solution.py:41
  32.4 29.4 %collective-permute-start.11 = (bf16[256,1024]{1,0:T(8,128)(2,1)S(1)}, bf16[256,1024]{1,0:T(8,128)(2,1)S(1)}, u32[]{:S(2)}, u32[]{:S(2)}) collective-permute-start(bf16[256,1024]{1,0:T(8,128)(2,1)S(1)} %bitcast.21), channel_id=1, source_target_pairs={{0,1},{1,0},{2,3},{3,2},{4,5},{5,4},{6,7},{7,6},{8,9},{9,8},{10,11... | collective-permute-start | bytes 1572872 | tf_op jit(solution)/shard_map/ppermute | solution.py:41
  39.9 21.9 %collective-permute-start.7 = (bf16[64,4096]{1,0:T(8,128)(2,1)S(1)}, bf16[64,4096]{1,0:T(8,128)(2,1)S(1)}, u32[]{:S(2)}, u32[]{:S(2)}) collective-permute-start(bf16[64,4096]{1,0:T(8,128)(2,1)S(1)} %get-tuple-element.250), channel_id=1, source_target_pairs={{28,24},{29,25},{30,26},{31,27}} | collective-permute-start | bytes 1572872 | tf_op jit(solution)/shard_map/ppermute | solution.py:41
  40.6 22.4 %collective-permute-start.6 = (bf16[64,4096]{1,0:T(8,128)(2,1)S(1)}, bf16[64,4096]{1,0:T(8,128)(2,1)S(1)}, u32[]{:S(2)}, u32[]{:S(2)}) collective-permute-start(bf16[64,4096]{1,0:T(8,128)(2,1)S(1)} %get-tuple-element.249), channel_id=1, source_target_pairs={{28,24},{29,25},{30,26},{31,27}} | collective-permute-start | bytes 1572872 | tf_op jit(solution)/shard_map/ppermute | solution.py:41
  62.3 2.6 %collective-permute-start.15 = (bf16[64,4096]{1,0:T(8,128)(2,1)S(1)}, bf16[64,4096]{1,0:T(8,128)(2,1)S(1)}, u32[]{:S(2)}, u32[]{:S(2)}) collective-permute-start(bf16[64,4096]{1,0:T(8,128)(2,1)S(1)} %get-tuple-element.281), channel_id=1, source_target_pairs={{24,20},{25,21},{26,22},{27,23}} | collective-permute-start | bytes 1572872 | tf_op jit(solution)/shard_map/ppermute | solution.py:41
  63.6 2.6 %collective-permute-start.14 = (bf16[64,4096]{1,0:T(8,128)(2,1)S(1)}, bf16[64,4096]{1,0:T(8,128)(2,1)S(1)}, u32[]{:S(2)}, u32[]{:S(2)}) collective-permute-start(bf16[64,4096]{1,0:T(8,128)(2,1)S(1)} %get-tuple-element.280), channel_id=1, source_target_pairs={{24,20},{25,21},{26,22},{27,23}} | collective-permute-start | bytes 1572872 | tf_op jit(solution)/shard_map/ppermute | solution.py:41
  66.9 2.0 %collective-permute-start.16 = (bf16[64,4096]{1,0:T(8,128)(2,1)S(1)}, bf16[64,4096]{1,0:T(8,128)(2,1)S(1)}, u32[]{:S(2)}, u32[]{:S(2)}) collective-permute-start(bf16[64,4096]{1,0:T(8,128)(2,1)S(1)} %get-tuple-element.314), channel_id=1, source_target_pairs={{20,16},{21,17},{22,18},{23,19}} | collective-permute-start | bytes 1572872 | tf_op jit(solution)/shard_map/ppermute | solution.py:41
  68.2 2.2 %collective-permute-start.19 = (bf16[64,4096]{1,0:T(8,128)(2,1)S(1)}, bf16[64,4096]{1,0:T(8,128)(2,1)S(1)}, u32[]{:S(2)}, u32[]{:S(2)}) collective-permute-start(bf16[64,4096]{1,0:T(8,128)(2,1)S(1)} %get-tuple-element.347), channel_id=1, source_target_pairs={{16,12},{17,13},{18,14},{19,15}} | collective-permute-start | bytes 1572872 | tf_op jit(solution)/shard_map/ppermute | solution.py:41
  69.6 2.0 %collective-permute-start.18 = (bf16[64,4096]{1,0:T(8,128)(2,1)S(1)}, bf16[64,4096]{1,0:T(8,128)(2,1)S(1)}, u32[]{:S(2)}, u32[]{:S(2)}) collective-permute-start(bf16[64,4096]{1,0:T(8,128)(2,1)S(1)} %get-tuple-element.346), channel_id=1, source_target_pairs={{16,12},{17,13},{18,14},{19,15}} | collective-permute-start | bytes 1572872 | tf_op jit(solution)/shard_map/ppermute | solution.py:41
  73.5 2.0 %collective-permute-start.23 = (bf16[64,4096]{1,0:T(8,128)(2,1)S(1)}, bf16[64,4096]{1,0:T(8,128)(2,1)S(1)}, u32[]{:S(2)}, u32[]{:S(2)}) collective-permute-start(bf16[64,4096]{1,0:T(8,128)(2,1)S(1)} %get-tuple-element.411), channel_id=1, source_target_pairs={{8,4},{9,5},{10,6},{11,7}} | collective-permute-start | bytes 1572872 | tf_op jit(solution)/shard_map/ppermute | solution.py:41
  74.8 2.6 %collective-permute-start.22 = (bf16[64,4096]{1,0:T(8,128)(2,1)S(1)}, bf16[64,4096]{1,0:T(8,128)(2,1)S(1)}, u32[]{:S(2)}, u32[]{:S(2)}) collective-permute-start(bf16[64,4096]{1,0:T(8,128)(2,1)S(1)} %get-tuple-element.410), channel_id=1, source_target_pairs={{8,4},{9,5},{10,6},{11,7}} | collective-permute-start | bytes 1572872 | tf_op jit(solution)/shard_map/ppermute | solution.py:41
  76.1 39.0 %collective-permute-start.25 = (bf16[64,4096]{1,0:T(8,128)(2,1)S(1)}, bf16[64,4096]{1,0:T(8,128)(2,1)S(1)}, u32[]{:S(2)}, u32[]{:S(2)}) collective-permute-start(bf16[64,4096]{1,0:T(8,128)(2,1)S(1)} %get-tuple-element.443), channel_id=1, source_target_pairs={{4,0},{5,1},{6,2},{7,3}} | collective-permute-start | bytes 1572872 | tf_op jit(solution)/shard_map/ppermute | solution.py:41
  78.0 42.9 %collective-permute-start.24 = (bf16[64,4096]{1,0:T(8,128)(2,1)S(1)}, bf16[64,4096]{1,0:T(8,128)(2,1)S(1)}, u32[]{:S(2)}, u32[]{:S(2)}) collective-permute-start(bf16[64,4096]{1,0:T(8,128)(2,1)S(1)} %get-tuple-element.442), channel_id=1, source_target_pairs={{4,0},{5,1},{6,2},{7,3}} | collective-permute-start | bytes 1572872 | tf_op jit(solution)/shard_map/ppermute | solution.py:41
  79.3 47.7 %collective-permute-start.26 = (bf16[128,1280]{1,0:T(8,128)(2,1)S(1)}, bf16[128,1280]{1,0:T(8,128)(2,1)S(1)}, u32[]{:S(2)}, u32[]{:S(2)}) collective-permute-start(bf16[128,1280]{1,0:T(8,128)(2,1)S(1)} %get-tuple-element.476), channel_id=1, source_target_pairs={{0,1},{1,0},{2,3},{3,2},{4,5},{5,4},{6,7},{7,6},{8,9},{9,8},{10,11... | collective-permute-start | bytes 983048 | tf_op jit(solution)/shard_map/ppermute | solution.py:41
  80.9 46.6 %collective-permute-start.27 = (bf16[128,1280]{1,0:T(8,128)(2,1)S(1)}, bf16[128,1280]{1,0:T(8,128)(2,1)S(1)}, u32[]{:S(2)}, u32[]{:S(2)}) collective-permute-start(bf16[128,1280]{1,0:T(8,128)(2,1)S(1)} %get-tuple-element.477), channel_id=1, source_target_pairs={{0,2},{1,3},{2,0},{3,1},{4,6},{5,7},{6,4},{7,5},{8,10},{9,11},{10,... | collective-permute-start | bytes 983048 | tf_op jit(solution)/shard_map/ppermute | solution.py:41
  82.3 46.7 %collective-permute-start.28 = (bf16[128,1280]{1,0:T(8,128)(2,1)S(1)}, bf16[128,1280]{1,0:T(8,128)(2,1)S(1)}, u32[]{:S(2)}, u32[]{:S(2)}) collective-permute-start(bf16[128,1280]{1,0:T(8,128)(2,1)S(1)} %get-tuple-element.478), channel_id=1, source_target_pairs={{0,3},{1,2},{2,1},{3,0},{4,7},{5,6},{6,5},{7,4},{8,11},{9,10},{10,... | collective-permute-start | bytes 983048 | tf_op jit(solution)/shard_map/ppermute | solution.py:41
  123.9 7.2 %collective-permute-start.32 = (bf16[64,1280]{1,0:T(8,128)(2,1)S(1)}, bf16[64,1280]{1,0:T(8,128)(2,1)S(1)}, u32[]{:S(2)}, u32[]{:S(2)}) collective-permute-start(bf16[64,1280]{1,0:T(8,128)(2,1)S(1)} %get-tuple-element.484), channel_id=1, source_target_pairs={{0,1},{1,0},{2,3},{3,2},{4,5},{5,4},{6,7},{7,6},{8,9},{9,8},{10,11... | collective-permute-start | bytes 491528 | tf_op jit(solution)/shard_map/ppermute | solution.py:41
  125.5 10.7 %collective-permute-start.33 = (bf16[64,1280]{1,0:T(8,128)(2,1)S(1)}, bf16[64,1280]{1,0:T(8,128)(2,1)S(1)}, u32[]{:S(2)}, u32[]{:S(2)}) collective-permute-start(bf16[64,1280]{1,0:T(8,128)(2,1)S(1)} %get-tuple-element.485), channel_id=1, source_target_pairs={{0,2},{1,3},{2,0},{3,1},{4,6},{5,7},{6,4},{7,5},{8,10},{9,11},{10,... | collective-permute-start | bytes 491528 | tf_op jit(solution)/shard_map/ppermute | solution.py:41
  127.0 9.2 %collective-permute-start.34 = (bf16[64,1280]{1,0:T(8,128)(2,1)S(1)}, bf16[64,1280]{1,0:T(8,128)(2,1)S(1)}, u32[]{:S(2)}, u32[]{:S(2)}) collective-permute-start(bf16[64,1280]{1,0:T(8,128)(2,1)S(1)} %get-tuple-element.486), channel_id=1, source_target_pairs={{0,3},{1,2},{2,1},{3,0},{4,7},{5,6},{6,5},{7,4},{8,11},{9,10},{10,... | collective-permute-start | bytes 491528 | tf_op jit(solution)/shard_map/ppermute | solution.py:41
  127.5 10.7 %collective-permute-start.29 = (bf16[64,1280]{1,0:T(8,128)(2,1)S(1)}, bf16[64,1280]{1,0:T(8,128)(2,1)S(1)}, u32[]{:S(2)}, u32[]{:S(2)}) collective-permute-start(bf16[64,1280]{1,0:T(8,128)(2,1)S(1)} %get-tuple-element.480), channel_id=1, source_target_pairs={{0,1},{1,0},{2,3},{3,2},{4,5},{5,4},{6,7},{7,6},{8,9},{9,8},{10,11... | collective-permute-start | bytes 491528 | tf_op jit(solution)/shard_map/ppermute | solution.py:41
  129.0 15.5 %collective-permute-start.30 = (bf16[64,1280]{1,0:T(8,128)(2,1)S(1)}, bf16[64,1280]{1,0:T(8,128)(2,1)S(1)}, u32[]{:S(2)}, u32[]{:S(2)}) collective-permute-start(bf16[64,1280]{1,0:T(8,128)(2,1)S(1)} %get-tuple-element.481), channel_id=1, source_target_pairs={{0,2},{1,3},{2,0},{3,1},{4,6},{5,7},{6,4},{7,5},{8,10},{9,11},{10,... | collective-permute-start | bytes 491528 | tf_op jit(solution)/shard_map/ppermute | solution.py:41
  131.1 13.4 %collective-permute-start.31 = (bf16[64,1280]{1,0:T(8,128)(2,1)S(1)}, bf16[64,1280]{1,0:T(8,128)(2,1)S(1)}, u32[]{:S(2)}, u32[]{:S(2)}) collective-permute-start(bf16[64,1280]{1,0:T(8,128)(2,1)S(1)} %get-tuple-element.482), channel_id=1, source_target_pairs={{0,3},{1,2},{2,1},{3,0},{4,7},{5,6},{6,5},{7,4},{8,11},{9,10},{10,... | collective-permute-start | bytes 491528 | tf_op jit(solution)/shard_map/ppermute | solution.py:41
  (15 other events, 45.2 us)

commit v4 on v3

v4 whole, which is shorter than its diff:
```python
import functools

import jax
import jax.numpy as jnp
from jax import lax
from jax.experimental import pallas as pl
from jax.experimental.pallas import tpu as pltpu
from jax.sharding import PartitionSpec as P

EPSILON = 1e-05
CHUNK_SHARES = (4, 4)
ANY = pl.BlockSpec(memory_space=pl.ANY)
VMEM = pl.BlockSpec(memory_space=pltpu.VMEM)
SMEM = pl.BlockSpec(memory_space=pltpu.SMEM)
PARAMS = pltpu.CompilerParams(vmem_limit_bytes=20 * 1024 * 1024)


def dot_nn(left, right):
    return lax.dot_general(
        left, right, (((1,), (0,)), ((), ())), preferred_element_type=jnp.float32
    )


def dot_nt(left, right):
    return lax.dot_general(
        left, right, (((1,), (1,)), ((), ())), preferred_element_type=jnp.float32
    )


def dot_tn(left, right):
    return lax.dot_general(
        left, right, (((0,), (0,)), ((), ())), preferred_element_type=jnp.float32
    )


def silu_slope(latent):
    sigmoid = jax.nn.sigmoid(latent)
    return sigmoid * (1.0 + latent * (1.0 - sigmoid))


def move(block, pairs):
    return lax.ppermute(block, ("section", "dp"), pairs)


def peers(sections, size, k):
    return [(s * size + i, s * size + (i ^ k)) for s in sections for i in range(size)]


def gather(block, sections, size):
    return [block] + [move(block, peers(sections, size, k)) for k in range(1, size)]


def gather_halves(low, high, sections, size):
    if size != 4:
        return list(zip(gather(low, sections, size), gather(high, sections, size)))
    across, along = peers(sections, size, 1), peers(sections, size, 2)
    low_along = move(low, along)
    high_across = move(high, across)
    high_along = move(high, along)
    low_across = move(low, across)
    low_far = move(low_along, across)
    high_far = move(high_across, along)
    return [(low, high), (low_across, high_across), (low_along, high_along), (low_far, high_far)]


def pin(block):
    return pltpu.with_memory_space_constraint(block, pltpu.VMEM)


def stay(block):
    return pltpu.with_memory_space_constraint(block, pltpu.HBM)


def held_like(block):
    return pltpu.VMEM(block.shape, block.dtype)


def columns(dp_index, k, width):
    return pl.ds(pl.multiple_of((dp_index ^ k) * width, width), width)


def half_columns(dp_index, k, half, width):
    start = (dp_index ^ k) * width + half * (width // 2)
    return pl.ds(pl.multiple_of(start, width // 2), width // 2)


def down_kernel(down, low, high, held, sem):
    copy = pltpu.make_async_copy(down, held, sem)
    copy.start()
    copy.wait()
    turned = held[0].T
    half = turned.shape[1] // 2
    low[...] = turned[:, :half]
    high[...] = turned[:, half:]


def up_kernel(up, readout, up_out, head, up_held, readout_held, sems):
    copies = [
        pltpu.make_async_copy(up, up_held, sems.at[0]),
        pltpu.make_async_copy(readout, readout_held, sems.at[1]),
    ]
    for copy in copies:
        copy.start()
    for copy in copies:
        copy.wait()
    latent_width, shard = up_held.shape[1:]
    horizon = readout_held.shape[1]
    values = up_held[0]
    product = dot_nn(values, readout_held[...]).astype(jnp.bfloat16)
    head[:horizon] = readout_held[...].T
    rows = latent_width * horizon // shard
    for at in range(0, shard, horizon):
        row = at // horizon * rows
        head[horizon:, at : at + horizon] = product[row : row + rows]
    block = min(latent_width, shard)
    for at in range(0, shard, block):
        up_out[:, at // block * latent_width : (at // block + 1) * latent_width] = values[
            :, at : at + block
        ].T


def norm_kernel(x, gain, x_out, normed_out, inverse_out, gain_out):
    values = x[...].astype(jnp.float32)
    inverse = lax.rsqrt(jnp.mean(values * values, axis=-1, keepdims=True) + EPSILON)
    x_out[...] = x[...]
    normed_out[...] = (values * inverse * gain[...].astype(jnp.float32)).astype(jnp.bfloat16)
    inverse_out[...] = jnp.broadcast_to(inverse, inverse_out.shape)
    gain_out[...] = gain[...]


def top_kernel(size, bounds, *refs):
    flags, truth, mask = refs[:3]
    down = refs[7 : 7 + 2 * size]
    head = refs[7 + 2 * size : 7 + 3 * size]
    gain, x, inverse, latent_ref, latent_grad_out, arriving_out, grads_out = refs[
        7 + 3 * size : 14 + 3 * size
    ]
    sends = refs[14 + 3 * size :]
    dp_index = flags[0]
    width = x.shape[1] // size
    horizon = truth.shape[1]

    @pl.when(flags[2] == 1)
    def _():
        latent = latent_ref[...]
        activated = jax.nn.silu(latent).astype(jnp.bfloat16)
        estimate = None
        product = None
        for k in range(size):
            part = dot_nt(x[:, columns(dp_index, k, width)], head[k][:horizon])
            extra = jnp.concatenate(
                [head[k][horizon:, at : at + horizon] for at in range(0, width, horizon)], axis=0
            ).astype(jnp.float32)
            estimate = part if estimate is None else estimate + part
            product = extra if product is None else product + extra
        product = product.astype(jnp.bfloat16)
        estimate = estimate + dot_nn(activated, product)
        error = (mask[:, :1] * (estimate - truth[...])).astype(jnp.bfloat16)
        hidden_grad = dot_nt(error, product)
        latent_grad = (hidden_grad * silu_slope(latent)).astype(jnp.bfloat16)
        latent_grad_out[...] = latent_grad
        scale = inverse[:, :1]
        mean = jnp.sum(latent_grad.astype(jnp.float32) * latent, axis=-1, keepdims=True) / (
            width * size
        )
        slope = scale * scale * mean
        for k in range(size):
            for half in range(2):
                at_k = half_columns(dp_index, k, half, width)
                here = slice(half * (width // 2), (half + 1) * (width // 2))
                arriving = dot_nn(error, head[k][:horizon, here]).astype(jnp.bfloat16)
                arriving_out[:, at_k] = arriving
                scaled = dot_nn(latent_grad, down[2 * k + half][...])
                grads = (
                    arriving.astype(jnp.float32)
                    + scale * (scaled * gain[:, at_k].astype(jnp.float32))
                    - x[:, at_k].astype(jnp.float32) * slope
                ).astype(jnp.bfloat16)
                grads_out[:, at_k] = grads
                for (row, end), send in zip(bounds, sends):
                    send[:, at_k] = grads[row:end]


def latent_kernel(size, *refs):
    flags, normed = refs[:2]
    down = refs[2 : 2 + 2 * size]
    latent = refs[3 + 2 * size]
    width = normed.shape[1] // size
    total = None
    for k in range(size):
        for half in range(2):
            block = normed[:, half_columns(flags[0], k, half, width)]
            part = dot_nt(block, down[2 * k + half][...])
            total = part if total is None else total + part
    latent[...] = total


def message_kernel(size, *refs):
    flags, normed = refs[:2]
    latent = refs[3 + 3 * size]
    shards = refs[3 : 3 + 3 * size]
    kept = refs[4 + 3 * size : 4 + 6 * size]
    messages = refs[4 + 6 * size :]
    shard = normed.shape[1] // size
    activated = jax.nn.silu(latent[...]).astype(jnp.bfloat16)
    for k in range(size):
        messages[k][:, :shard] = normed[:, columns(flags[0], k, shard)]
        messages[k][:, shard:] = activated
    for source, place in zip(shards, kept):
        place[...] = source[...]


def stage_kernel(stage, bounds, size, held, *refs):
    flags = refs[0]
    pieces = refs[1 : 1 + len(bounds)]
    at = 1 + len(bounds)
    if held == 7:
        shards = refs[at + 7 : at + 7 + 3 * size]
        state = refs[at + 7 + 3 * size : at + 14 + 3 * size]
        outs = refs[at + 14 + 3 * size :]
    else:
        state = refs[at + held : at + held + 7]
        shards = refs[at + held + 7 : at + 2 * held]
        outs = refs[at + 2 * held :]
    gain, inverse, latent, x, latent_grads, arrivals, grads = state
    down, up = shards[: 2 * size], shards[2 * size :]
    width = x.shape[1]
    shard = width // size
    latent_width = latent.shape[1]
    block = min(latent_width, shard)
    at_rows = slice(bounds[0][0], bounds[-1][1])

    def take(place):
        parts = [piece[:, place] for piece in pieces]
        return parts[0] if len(parts) == 1 else jnp.concatenate(parts, axis=0)

    @pl.when(flags[1] == stage)
    def _():
        hidden_grad = None
        for k in range(size):
            arriving = take(columns(flags[0], k, shard))
            for at in range(0, shard, block):
                lanes = at // block * latent_width
                part = dot_nn(arriving[:, at : at + block], up[k][:, lanes : lanes + latent_width])
                hidden_grad = part if hidden_grad is None else hidden_grad + part
        lat = latent[at_rows]
        latent_grad = (hidden_grad * silu_slope(lat)).astype(jnp.bfloat16)
        latent_grads[at_rows] = latent_grad
        scale = inverse[at_rows][:, :1]
        mean = jnp.sum(latent_grad.astype(jnp.float32) * lat, axis=-1, keepdims=True) / width
        slope = scale * scale * mean
        for k in range(size):
            for half in range(2):
                at_k = half_columns(flags[0], k, half, shard)
                arriving = take(at_k)
                arrivals[at_rows, at_k] = arriving
                scaled = dot_nn(latent_grad, down[2 * k + half][...])
                value = (
                    arriving.astype(jnp.float32)
                    + scale * (scaled * gain[:, at_k].astype(jnp.float32))
                    - x[at_rows, at_k].astype(jnp.float32) * slope
                ).astype(jnp.bfloat16)
                grads[at_rows, at_k] = value
                if stage:
                    outs[0][:, at_k] = value

    if stage == 0:
        for k in range(size):
            outs[k][:, :shard] = arrivals[:, columns(flags[0], k, shard)]
            outs[k][:, shard:] = latent_grads[...]


def touch_kernel(*refs):
    pass


def weight_kernel(size, *refs):
    early, late = refs[:size], refs[size : 2 * size]
    down_grads, up_grads, left, right = refs[2 * size :]
    tokens = early[0].shape[0]
    shard = down_grads.shape[0]
    for k in range(size):
        left[k * tokens : (k + 1) * tokens] = early[k][...]
        right[k * tokens : (k + 1) * tokens] = late[k][...]
    down_grads[...] = dot_tn(left[:, :shard], right[:, shard:]).astype(jnp.bfloat16)
    up_grads[...] = dot_tn(left[:, shard:], right[:, :shard]).astype(jnp.bfloat16)


def per_device(
    section_inputs, norm_gain, down_proj, up_proj, readout_matrix, ground_truth_series, valid_len
):
    size = lax.axis_size("dp")
    sections = lax.axis_size("section")
    top = sections - 1
    dp_index = lax.axis_index("dp")
    section = lax.axis_index("section")
    f32, bf16 = jnp.float32, jnp.bfloat16

    x = section_inputs[0]
    tokens, width = x.shape
    shard, latent_width = down_proj.shape[1:]
    horizon = readout_matrix.shape[1]
    share = tokens // sum(CHUNK_SHARES)
    ends = [share * sum(CHUNK_SHARES[: i + 1]) for i in range(len(CHUNK_SHARES))]
    bounds = list(zip([0] + ends, ends))

    flags = jnp.stack(
        [dp_index.astype(jnp.int32), section.astype(jnp.int32), (section == top).astype(jnp.int32)]
    )
    everyone, rest = list(range(sections)), list(range(top))
    low, high = pl.pallas_call(
        down_kernel,
        out_shape=(jax.ShapeDtypeStruct((latent_width, shard // 2), bf16),) * 2,
        in_specs=[ANY],
        out_specs=(VMEM,) * 2,
        scratch_shapes=[
            pltpu.VMEM((1, shard, latent_width), bf16),
            pltpu.SemaphoreType.DMA(()),
        ],
        compiler_params=PARAMS,
    )(stay(down_proj))
    down = gather_halves(low, high, everyone, size)
    up_block = min(latent_width, shard)
    up_own, head_own = pl.pallas_call(
        up_kernel,
        out_shape=(
            jax.ShapeDtypeStruct((up_block, latent_width * shard // up_block), bf16),
            jax.ShapeDtypeStruct((horizon + latent_width * horizon // shard, shard), bf16),
        ),
        in_specs=[ANY] * 2,
        out_specs=(VMEM,) * 2,
        scratch_shapes=[
            pltpu.VMEM((1, latent_width, shard), bf16),
            pltpu.VMEM((shard, horizon), bf16),
            pltpu.SemaphoreType.DMA((2,)),
        ],
        compiler_params=PARAMS,
    )(stay(up_proj), stay(readout_matrix))
    head = gather(head_own, [top], size)
    up_held, down_first = lax.optimization_barrier((up_own, down[2 % size][0]))
    down[2 % size] = (down_first, down[2 % size][1])
    up = gather(up_held, rest, size)
    down = [half for pair in down for half in pair]

    x, normed, inverse, gain = pl.pallas_call(
        norm_kernel,
        out_shape=(
            pltpu.VMEM((tokens, width), bf16),
            pltpu.VMEM((tokens, width), bf16),
            pltpu.VMEM((tokens, 128), f32),
            pltpu.VMEM((1, width), bf16),
        ),
        in_specs=[VMEM] * 2,
        out_specs=(VMEM,) * 4,
        compiler_params=PARAMS,
    )(x, norm_gain)
    per_micro = tokens // valid_len.shape[0]
    mask = (
        (jnp.arange(per_micro)[None, :] < valid_len[:, None]).astype(f32).reshape(tokens, 1)
    )
    mask = jnp.broadcast_to(mask, (tokens, 128))

    normed, latent = pl.pallas_call(
        functools.partial(latent_kernel, size),
        out_shape=(held_like(normed), pltpu.VMEM((tokens, latent_width), f32)),
        in_specs=[SMEM] + [VMEM] * (1 + 2 * size),
        out_specs=(VMEM,) * 2,
        input_output_aliases={1: 0},
        compiler_params=PARAMS,
    )(flags, pin(normed), *[pin(half) for half in down])

    gain, x, inverse, latent, latent_grads, arrivals, grads, *sends = pl.pallas_call(
        functools.partial(top_kernel, size, bounds),
        out_shape=(
            held_like(gain),
            held_like(x),
            held_like(inverse),
            held_like(latent),
            pltpu.VMEM((tokens, latent_width), bf16),
            pltpu.VMEM((tokens, width), bf16),
            pltpu.VMEM((tokens, width), bf16),
        )
        + tuple(jax.ShapeDtypeStruct((end - row, width), bf16) for row, end in bounds),
        in_specs=[SMEM] + [VMEM] * (6 + 3 * size),
        out_specs=(VMEM,) * (7 + len(bounds)),
        input_output_aliases={3: 0, 4: 1, 5: 2, 6: 3},
        compiler_params=PARAMS,
    )(
        flags, ground_truth_series, mask, pin(gain), pin(x), pin(inverse), pin(latent),
        *[pin(part) for part in down + head],
    )

    def hop(block, sender):
        return move(block, [(sender * size + i, (sender - 1) * size + i) for i in range(size)])

    received = [hop(send, top) for send in sends]

    message = jax.ShapeDtypeStruct((tokens, shard + latent_width), bf16)
    shards = (*down, *up)
    state = (gain, inverse, latent, x, latent_grads, arrivals, grads)

    def run_stage(stage, bounds, received, state, shards):
        rows = bounds[-1][1] - bounds[0][0]
        if stage:
            outs = (jax.ShapeDtypeStruct((rows, width), bf16),)
        else:
            outs = (message,) * size
        first = 1 + len(received)
        results = pl.pallas_call(
            functools.partial(stage_kernel, stage, bounds, size, len(state)),
            out_shape=tuple(held_like(part) for part in state) + outs,
            in_specs=[SMEM] + [VMEM] * (len(received) + len(state) + len(shards)),
            out_specs=(VMEM,) * (len(state) + len(outs)),
            input_output_aliases={first + i: i for i in range(len(state))},
            cost_estimate=pl.CostEstimate(
                flops=4 * rows * width * latent_width,
                bytes_accessed=8 * width * latent_width,
                transcendentals=rows * latent_width,
            ),
            compiler_params=PARAMS,
        )(flags, *received, *[pin(part) for part in state + shards])
        return tuple(results[: len(state)]), results[len(state) :]

    def send_messages(messages):
        return [messages[0]] + [
            move(messages[k], peers(range(sections), size, k)) for k in range(1, size)
        ]

    for stage in range(top - 1, 0, -1):
        sent = []
        for bound, block in zip(bounds, received):
            state, outs = run_stage(stage, [bound], [block], state, shards)
            sent.append(hop(outs[0], stage))
        received = sent
        if stage == top - 1:
            results = pl.pallas_call(
                functools.partial(message_kernel, size),
                out_shape=(held_like(state[2]),)
                + tuple(held_like(part) for part in shards)
                + (message,) * size,
                in_specs=[SMEM] + [VMEM] * (2 + len(shards)),
                out_specs=(VMEM,) * (1 + len(shards) + size),
                input_output_aliases={2: 0},
                compiler_params=PARAMS,
            )(flags, pin(normed), pin(state[2]), *[pin(part) for part in shards])
            state = state[:2] + (results[0],) + state[3:] + tuple(results[1 : 1 + len(shards)])
            shards = ()
            early = send_messages(results[-size:])
        if stage == max(top - 3, 1):
            latent, *early = pl.pallas_call(
                touch_kernel,
                out_shape=(held_like(state[2]),) + tuple(held_like(part) for part in early),
                in_specs=[VMEM] * (1 + size),
                out_specs=(VMEM,) * (1 + size),
                input_output_aliases={i: i for i in range(1 + size)},
                compiler_params=PARAMS,
            )(pin(state[2]), *[pin(part) for part in early])
            state = state[:2] + (latent,) + state[3:]

    state, outs = run_stage(0, bounds, received, state, shards)
    late = send_messages(outs)
    down_grads, up_grads = pl.pallas_call(
        functools.partial(weight_kernel, size),
        out_shape=(
            jax.ShapeDtypeStruct((shard, latent_width), bf16),
            jax.ShapeDtypeStruct((latent_width, shard), bf16),
        ),
        in_specs=[VMEM] * (2 * size),
        out_specs=(VMEM,) * 2,
        scratch_shapes=[pltpu.VMEM((size * tokens, shard + latent_width), bf16)] * 2,
        compiler_params=PARAMS,
    )(*early, *late)
    return (state[6][None], down_grads[None], up_grads[None])


def solution(mesh):
    placed = (
        P("section", "dp", None),
        P("section", None),
        P("section", "dp", None),
        P("section", None, "dp"),
        P("dp", None),
        P("dp", None),
        P("dp"),
    )
    return jax.shard_map(
        per_device,
        mesh=mesh,
        in_specs=placed,
        out_specs=(P("section", "dp", None), P("section", "dp", None), P("section", None, "dp")),
        check_vma=False,
    )
```

time: 147 us -> 126 us (0.86)
  starting transfers between devices: 48.5 us -> 39.3 us
  waiting for transfers between devices: 70.7 us -> 64.7 us
  local copies, waits for them, and re-layouts: 7.11 us -> 2.37 us
    ppermute x35 -> x32, starting transfers between devices: 48.5 us -> 39.3 us  [move(): return lax.ppermute(block, ('section', 'dp'), pairs)]
    ppermute x35 -> x32, waiting for transfers between devices: 70.7 us -> 64.7 us  [move(): return lax.ppermute(block, ('section', 'dp'), pairs)]
    unnamed x28 -> x9, local copies, waits for them, and re-layouts: 6.96 us -> 2.21 us
    pallas_call x17 -> x18, Pallas kernels: 15.6 us -> 14.2 us  [the longest x13 9.04 us: run_stage(): pl.pallas_call(functools.partial(stage_kernel, stage, bounds, size, len(s...]
  transfers between devices with their start and end apart: 35 -> 32, of which waited for: 10 -> 13; matrix products, arithmetic and copies ran while one was open for 1% -> 1% of each run, Pallas kernels for 12% -> 10%
where the time goes in v4:
time: 126 us; the launch traced here: 125 us
  waiting for transfers between devices  64.7 us (51%)
  starting transfers between devices  39.3 us (31%)
  Pallas kernels  17.5 us (14%)
  local copies, waits for them, and re-layouts  2.37 us (2%)
    ppermute x32, waiting for transfers between devices, move(): return lax.ppermute(block, ('section', 'dp'), pairs)  64.7 us
    ppermute x32, starting transfers between devices, move(): return lax.ppermute(block, ('section', 'dp'), pairs)  39.3 us
    pallas_call x13, Pallas kernels, run_stage(): pl.pallas_call(functools.partial(stage_kernel, stage, bounds, size, len(s...  9.04 us
  transfers between devices with their start and end apart: 32, of which 13 were waited for; matrix products, arithmetic and copies ran while one was open for 1% of the time, Pallas kernels for 10%

profile of v4, /device:TPU:0, one launch (start us, length us, event | category | flops | bytes accessed | tf_op | source)
XLA Modules:
  0.0 125.1 jit_solution(14834291241308478371)
XLA Ops:
  0.6 1.2 shard_map.95
  1.9 3.0 %collective-permute-start.2 = (bf16[256,512]{1,0:T(8,128)(2,1)S(1)}, bf16[256,512]{1,0:T(8,128)(2,1)S(1)}, u32[]{:S(2)}, u32[]{:S(2)}) collective-permute-start(bf16[256,512]{1,0:T(8,128)(2,1)S(1)} %get-tuple-element.273.refs_2_.refs_7_.refs_9_.refs_3_), channel_id=1, source_target_pairs={{0,2},{1,3},{2,0},{3,1},{4,6},{5,7},{6,4},{7,5},{8,10},{9,11},{10,... | collective-permute-start | bytes 786440 | tf_op jit(solution)/shard_map/ppermute | solution.py:42
  4.9 1.5 %collective-permute-start = (bf16[256,512]{1,0:T(8,128)(2,1)S(1)}, bf16[256,512]{1,0:T(8,128)(2,1)S(1)}, u32[]{:S(2)}, u32[]{:S(2)}) collective-permute-start(bf16[256,512]{1,0:T(8,128)(2,1)S(1)} %get-tuple-element.273.refs_2_.refs_7_.refs_9_.refs_3_), channel_id=1, source_target_pairs={{0,1},{1,0},{2,3},{3,2},{4,5},{5,4},{6,7},{7,6},{8,9},{9,8},{10,11... | collective-permute-start | bytes 786440 | tf_op jit(solution)/shard_map/ppermute | solution.py:42
  7.0 1.4 %shard_map.96 = (bf16[256,1024]{1,0:T(8,128)(2,1)S(1)}, bf16[160,1024]{1,0:T(8,128)(2,1)S(1)}) custom-call(bf16[1,256,1024]{2,1,0:T(8,128)(2,1)} %up.1, bf16[1024,128]{1,0:T(8,128)(2,1)} %readout.1), custom_call_target="tpu_custom_call" | custom-call | tf_op jit(solution)/shard_map/pallas_call | solution.py:324
  9.2 2.9 %collective-permute-done.2.refs_6_.refs_11_.refs_13_.refs_7_ = bf16[256,512]{1,0:T(8,128)(2,1)S(1)} collective-permute-done((bf16[256,512]{1,0:T(8,128)(2,1)S(1)}, bf16[256,512]{1,0:T(8,128)(2,1)S(1)}, u32[]{:S(2)}, u32[]{:S(2)}) %collective-permute-start.2) | collective-permute-done | bytes 262176 | tf_op jit(solution)/shard_map/ppermute | solution.py:42
  12.0 1.4 %collective-permute-start.7 = (bf16[160,1024]{1,0:T(8,128)(2,1)S(1)}, bf16[160,1024]{1,0:T(8,128)(2,1)}, u32[]{:S(2)}, u32[]{:S(2)}) collective-permute-start(bf16[160,1024]{1,0:T(8,128)(2,1)S(1)} %get-tuple-element.278.refs_15_), channel_id=1, source_target_pairs={{28,30},{29,31},{30,28},{31,29}} | collective-permute-start | bytes 983048 | tf_op jit(solution)/shard_map/ppermute | solution.py:42
  14.1 1.4 %collective-permute-start.6 = (bf16[160,1024]{1,0:T(8,128)(2,1)S(1)}, bf16[160,1024]{1,0:T(8,128)(2,1)}, u32[]{:S(2)}, u32[]{:S(2)}) collective-permute-start(bf16[160,1024]{1,0:T(8,128)(2,1)S(1)} %get-tuple-element.278.refs_15_), channel_id=1, source_target_pairs={{28,29},{29,28},{30,31},{31,30}} | collective-permute-start | bytes 983048 | tf_op jit(solution)/shard_map/ppermute | solution.py:42
  15.5 1.3 %collective-permute-done.3.refs_7_.refs_12_.refs_14_.refs_8_ = bf16[256,512]{1,0:T(8,128)(2,1)S(1)} collective-permute-done((bf16[256,512]{1,0:T(8,128)(2,1)S(1)}, bf16[256,512]{1,0:T(8,128)(2,1)S(1)}, u32[]{:S(2)}, u32[]{:S(2)}) %collective-permute-start.3) | collective-permute-done | bytes 262176 | tf_op jit(solution)/shard_map/ppermute | solution.py:42
  16.8 1.7 %collective-permute-start.4 = (bf16[256,512]{1,0:T(8,128)(2,1)S(1)}, bf16[256,512]{1,0:T(8,128)(2,1)S(1)}, u32[]{:S(2)}, u32[]{:S(2)}) collective-permute-start(bf16[256,512]{1,0:T(8,128)(2,1)S(1)} %collective-permute-done.2.refs_6_.refs_11_.refs_13_.refs_7_), channel_id=1, source_target_pairs={{0,1},{1,0},{2,3},{3,2},{4,5},{5,4},{6,7},{7,6},{8,9},{9,8},{10,11... | collective-permute-start | bytes 786440 | tf_op jit(solution)/shard_map/ppermute | solution.py:42
  18.5 1.5 %collective-permute-start.5 = (bf16[256,512]{1,0:T(8,128)(2,1)S(1)}, bf16[256,512]{1,0:T(8,128)(2,1)S(1)}, u32[]{:S(2)}, u32[]{:S(2)}) collective-permute-start(bf16[256,512]{1,0:T(8,128)(2,1)S(1)} %collective-permute-done.1.refs_5_.refs_10_.refs_12_.refs_6_), channel_id=1, source_target_pairs={{0,2},{1,3},{2,0},{3,1},{4,6},{5,7},{6,4},{7,5},{8,10},{9,11},{10,... | collective-permute-start | bytes 786440 | tf_op jit(solution)/shard_map/ppermute | solution.py:42
  20.2 1.2 copy-done
  22.2 2.1 %collective-permute-done.4.refs_8_.refs_13_.refs_15_.refs_9_ = bf16[256,512]{1,0:T(8,128)(2,1)S(1)} collective-permute-done((bf16[256,512]{1,0:T(8,128)(2,1)S(1)}, bf16[256,512]{1,0:T(8,128)(2,1)S(1)}, u32[]{:S(2)}, u32[]{:S(2)}) %collective-permute-start.4) | collective-permute-done | bytes 262176 | tf_op jit(solution)/shard_map/ppermute | solution.py:42
  24.3 4.2 %collective-permute-start.12 = (bf16[256,1024]{1,0:T(8,128)(2,1)S(1)}, bf16[256,1024]{1,0:T(8,128)(2,1)S(1)}, u32[]{:S(2)}, u32[]{:S(2)}) collective-permute-start(bf16[256,1024]{1,0:T(8,128)(2,1)S(1)} %get-tuple-element.287.refs_17_.refs_11_), channel_id=1, source_target_pairs={{0,3},{1,2},{2,1},{3,0},{4,7},{5,6},{6,5},{7,4},{8,11},{9,10},{10,... | collective-permute-start | bytes 1572872 | tf_op jit(solution)/shard_map/ppermute | solution.py:42
  28.6 2.4 %collective-permute-start.11 = (bf16[256,1024]{1,0:T(8,128)(2,1)S(1)}, bf16[256,1024]{1,0:T(8,128)(2,1)S(1)}, u32[]{:S(2)}, u32[]{:S(2)}) collective-permute-start(bf16[256,1024]{1,0:T(8,128)(2,1)S(1)} %get-tuple-element.287.refs_17_.refs_11_), channel_id=1, source_target_pairs={{0,2},{1,3},{2,0},{3,1},{4,6},{5,7},{6,4},{7,5},{8,10},{9,11},{10,... | collective-permute-start | bytes 1572872 | tf_op jit(solution)/shard_map/ppermute | solution.py:42
  31.0 1.4 %shard_map.97 = (bf16[128,4096]{1,0:T(8,128)(2,1)S(1)}, f32[128,256]{1,0:T(8,128)S(1)}) custom-call(s32[3]{0:T(128)S(1)} %pad_add_fusion.refs_0_, bf16[128,4096]{1,0:T(8,128)(2,1)S(1)} %get-tuple-element.272.refs_1_, bf16[256,512]{1,0:T(8,128)(2,1)S(1)} %get-tuple-element.273.refs_2_.refs_7_.refs_9_.refs_3_, ...), custom_call_target="tpu_custom_call", output_to_operand_aliasing={{0}: (1, {})} | custom-call | tf_op jit(solution)/shard_map/pallas_call | solution.py:363
  32.4 2.5 %collective-permute-start.10 = (bf16[256,1024]{1,0:T(8,128)(2,1)S(1)}, bf16[256,1024]{1,0:T(8,128)(2,1)S(1)}, u32[]{:S(2)}, u32[]{:S(2)}) collective-permute-start(bf16[256,1024]{1,0:T(8,128)(2,1)S(1)} %get-tuple-element.287.refs_17_.refs_11_), channel_id=1, source_target_pairs={{0,1},{1,0},{2,3},{3,2},{4,5},{5,4},{6,7},{7,6},{8,9},{9,8},{10,11... | collective-permute-start | bytes 1572872 | tf_op jit(solution)/shard_map/ppermute | solution.py:42
  37.6 4.4 %collective-permute-done.12.refs_20_.refs_14_ = bf16[256,1024]{1,0:T(8,128)(2,1)S(1)} collective-permute-done((bf16[256,1024]{1,0:T(8,128)(2,1)S(1)}, bf16[256,1024]{1,0:T(8,128)(2,1)S(1)}, u32[]{:S(2)}, u32[]{:S(2)}) %collective-permute-start.12) | collective-permute-done | bytes 524320 | tf_op jit(solution)/shard_map/ppermute | solution.py:42
  42.0 8.5 %collective-permute-done.11.refs_19_.refs_13_ = bf16[256,1024]{1,0:T(8,128)(2,1)S(1)} collective-permute-done((bf16[256,1024]{1,0:T(8,128)(2,1)S(1)}, bf16[256,1024]{1,0:T(8,128)(2,1)S(1)}, u32[]{:S(2)}, u32[]{:S(2)}) %collective-permute-start.11) | collective-permute-done | bytes 524320 | tf_op jit(solution)/shard_map/ppermute | solution.py:42
  59.4 1.2 collective-permute-start.19
  60.7 1.4 %collective-permute-start.20 = (bf16[128,1280]{1,0:T(8,128)(2,1)S(1)}, bf16[128,1280]{1,0:T(8,128)(2,1)S(1)}, u32[]{:S(2)}, u32[]{:S(2)}) collective-permute-start(bf16[128,1280]{1,0:T(8,128)(2,1)S(1)} %get-tuple-element.384), channel_id=1, source_target_pairs={{0,2},{1,3},{2,0},{3,1},{4,6},{5,7},{6,4},{7,5},{8,10},{9,11},{10,... | collective-permute-start | bytes 983048 | tf_op jit(solution)/shard_map/ppermute | solution.py:42
  63.0 7.1 %collective-permute-done.19.refs_2_ = bf16[128,1280]{1,0:T(8,128)(2,1)S(1)} collective-permute-done((bf16[128,1280]{1,0:T(8,128)(2,1)S(1)}, bf16[128,1280]{1,0:T(8,128)(2,1)S(1)}, u32[]{:S(2)}, u32[]{:S(2)}) %collective-permute-start.19) | collective-permute-done | bytes 327712 | tf_op jit(solution)/shard_map/ppermute | solution.py:42
  70.1 6.9 %collective-permute-done.20.refs_3_ = bf16[128,1280]{1,0:T(8,128)(2,1)S(1)} collective-permute-done((bf16[128,1280]{1,0:T(8,128)(2,1)S(1)}, bf16[128,1280]{1,0:T(8,128)(2,1)S(1)}, u32[]{:S(2)}, u32[]{:S(2)}) %collective-permute-start.20) | collective-permute-done | bytes 327712 | tf_op jit(solution)/shard_map/ppermute | solution.py:42
  82.8 1.3 %collective-permute-start.26 = (bf16[64,4096]{1,0:T(8,128)(2,1)S(1)}, bf16[64,4096]{1,0:T(8,128)(2,1)S(1)}, u32[]{:S(2)}, u32[]{:S(2)}) collective-permute-start(bf16[64,4096]{1,0:T(8,128)(2,1)S(1)} %get-tuple-element.483), channel_id=1, source_target_pairs={{4,0},{5,1},{6,2},{7,3}} | collective-permute-start | bytes 1572872 | tf_op jit(solution)/shard_map/ppermute | solution.py:42
  84.7 1.3 %collective-permute-start.28 = (bf16[64,4096]{1,0:T(8,128)(2,1)S(1)}, bf16[64,4096]{1,0:T(8,128)(2,1)S(1)}, u32[]{:S(2)}, u32[]{:S(2)}) collective-permute-start(bf16[64,4096]{1,0:T(8,128)(2,1)S(1)} %get-tuple-element.504), channel_id=1, source_target_pairs={{4,0},{5,1},{6,2},{7,3}} | collective-permute-start | bytes 1572872 | tf_op jit(solution)/shard_map/ppermute | solution.py:42
  86.0 13.3 %collective-permute-done.26.refs_1_ = bf16[64,4096]{1,0:T(8,128)(2,1)S(1)} collective-permute-done((bf16[64,4096]{1,0:T(8,128)(2,1)S(1)}, bf16[64,4096]{1,0:T(8,128)(2,1)S(1)}, u32[]{:S(2)}, u32[]{:S(2)}) %collective-permute-start.26) | collective-permute-done | bytes 524320 | tf_op jit(solution)/shard_map/ppermute | solution.py:42
  99.2 5.6 %collective-permute-done.28.refs_2_ = bf16[64,4096]{1,0:T(8,128)(2,1)S(1)} collective-permute-done((bf16[64,4096]{1,0:T(8,128)(2,1)S(1)}, bf16[64,4096]{1,0:T(8,128)(2,1)S(1)}, u32[]{:S(2)}, u32[]{:S(2)}) %collective-permute-start.28) | collective-permute-done | bytes 524320 | tf_op jit(solution)/shard_map/ppermute | solution.py:42
  104.9 2.1 %shard_map.113 = (bf16[1,4096]{1,0:T(2,128)(2,1)S(1)}, f32[128,128]{1,0:T(8,128)S(1)}, f32[128,256]{1,0:T(8,128)S(1)}, bf16[128,4096]{1,0:T(8,128)(2,1)S(1)}, bf...) custom-call(s32[3]{0:T(128)S(1)} %pad_add_fusion.refs_0_, ...), custom_call_target="tpu_custom_call", output_to_operand_aliasing={{0}: (3, {}), {1}: (4, {}), {2}: (5, {}), {3}: (6, {}), {4}... | custom-call | flops 536870912 | bytes 8388608 | tf_op jit(solution)/shard_map/pallas_call | solution.py:409
  108.0 1.5 %collective-permute-start.30 = (bf16[128,1280]{1,0:T(8,128)(2,1)S(1)}, bf16[128,1280]{1,0:T(8,128)(2,1)S(1)}, u32[]{:S(2)}, u32[]{:S(2)}) collective-permute-start(bf16[128,1280]{1,0:T(8,128)(2,1)S(1)} %get-tuple-element.531), channel_id=1, source_target_pairs={{0,2},{1,3},{2,0},{3,1},{4,6},{5,7},{6,4},{7,5},{8,10},{9,11},{10,... | collective-permute-start | bytes 983048 | tf_op jit(solution)/shard_map/ppermute | solution.py:42
  111.5 6.2 %collective-permute-done.29.refs_5_ = bf16[128,1280]{1,0:T(8,128)(2,1)S(1)} collective-permute-done((bf16[128,1280]{1,0:T(8,128)(2,1)S(1)}, bf16[128,1280]{1,0:T(8,128)(2,1)S(1)}, u32[]{:S(2)}, u32[]{:S(2)}) %collective-permute-start.29) | collective-permute-done | bytes 327712 | tf_op jit(solution)/shard_map/ppermute | solution.py:42
  117.7 4.4 %collective-permute-done.30.refs_6_ = bf16[128,1280]{1,0:T(8,128)(2,1)S(1)} collective-permute-done((bf16[128,1280]{1,0:T(8,128)(2,1)S(1)}, bf16[128,1280]{1,0:T(8,128)(2,1)S(1)}, u32[]{:S(2)}, u32[]{:S(2)}) %collective-permute-start.30) | collective-permute-done | bytes 327712 | tf_op jit(solution)/shard_map/ppermute | solution.py:42
  122.1 1.3 %collective-permute-done.31.refs_7_ = bf16[128,1280]{1,0:T(8,128)(2,1)S(1)} collective-permute-done((bf16[128,1280]{1,0:T(8,128)(2,1)S(1)}, bf16[128,1280]{1,0:T(8,128)(2,1)S(1)}, u32[]{:S(2)}, u32[]{:S(2)}) %collective-permute-start.31) | collective-permute-done | bytes 327712 | tf_op jit(solution)/shard_map/ppermute | solution.py:42
  123.4 1.7 %shard_map.114 = (bf16[1024,256]{1,0:T(8,128)(2,1)}, bf16[256,1024]{1,0:T(8,128)(2,1)}) custom-call(bf16[128,1280]{1,0:T(8,128)(2,1)S(1)} %get-tuple-element.525.refs_0_, bf16[128,1280]{1,0:T(8,128)(2,1)S(1)} %get-tuple-element.526.refs_1_, bf16[128,1280]{1,0:T(8,128)(2,1)S(1)} %get-tuple-element.527.refs_2_, ...), custom_call_target="tpu_custom_call" | custom-call | tf_op jit(solution)/shard_map/pallas_call | solution.py:462
  (66 shorter events, 24.4 us)
Async XLA Ops:
  1.9 10.2 %collective-permute-start.2 = (bf16[256,512]{1,0:T(8,128)(2,1)S(1)}, bf16[256,512]{1,0:T(8,128)(2,1)S(1)}, u32[]{:S(2)}, u32[]{:S(2)}) collective-permute-start(bf16[256,512]{1,0:T(8,128)(2,1)S(1)} %get-tuple-element.273.refs_2_.refs_7_.refs_9_.refs_3_), channel_id=1, source_target_pairs={{0,2},{1,3},{2,0},{3,1},{4,6},{5,7},{6,4},{7,5},{8,10},{9,11},{10,... | collective-permute-start | bytes 786440 | tf_op jit(solution)/shard_map/ppermute | solution.py:42
  4.9 9.2 %collective-permute-start = (bf16[256,512]{1,0:T(8,128)(2,1)S(1)}, bf16[256,512]{1,0:T(8,128)(2,1)S(1)}, u32[]{:S(2)}, u32[]{:S(2)}) collective-permute-start(bf16[256,512]{1,0:T(8,128)(2,1)S(1)} %get-tuple-element.273.refs_2_.refs_7_.refs_9_.refs_3_), channel_id=1, source_target_pairs={{0,1},{1,0},{2,3},{3,2},{4,5},{5,4},{6,7},{7,6},{8,9},{9,8},{10,11... | collective-permute-start | bytes 786440 | tf_op jit(solution)/shard_map/ppermute | solution.py:42
  6.4 10.4 %collective-permute-start.3 = (bf16[256,512]{1,0:T(8,128)(2,1)S(1)}, bf16[256,512]{1,0:T(8,128)(2,1)S(1)}, u32[]{:S(2)}, u32[]{:S(2)}) collective-permute-start(bf16[256,512]{1,0:T(8,128)(2,1)S(1)} %get-tuple-element.274.refs_3_.refs_8_.refs_10_.refs_4_), channel_id=1, source_target_pairs={{0,2},{1,3},{2,0},{3,1},{4,6},{5,7},{6,4},{7,5},{8,10},{9,11},{10,... | collective-permute-start | bytes 786440 | tf_op jit(solution)/shard_map/ppermute | solution.py:42
  6.9 11.6 %collective-permute-start.1 = (bf16[256,512]{1,0:T(8,128)(2,1)S(1)}, bf16[256,512]{1,0:T(8,128)(2,1)S(1)}, u32[]{:S(2)}, u32[]{:S(2)}) collective-permute-start(bf16[256,512]{1,0:T(8,128)(2,1)S(1)} %get-tuple-element.274.refs_3_.refs_8_.refs_10_.refs_4_), channel_id=1, source_target_pairs={{0,1},{1,0},{2,3},{3,2},{4,5},{5,4},{6,7},{7,6},{8,9},{9,8},{10,11... | collective-permute-start | bytes 786440 | tf_op jit(solution)/shard_map/ppermute | solution.py:42
  8.5 23.9 %collective-permute-start.8 = (bf16[160,1024]{1,0:T(8,128)(2,1)S(1)}, bf16[160,1024]{1,0:T(8,128)(2,1)S(1)}, u32[]{:S(2)}, u32[]{:S(2)}) collective-permute-start(bf16[160,1024]{1,0:T(8,128)(2,1)S(1)} %get-tuple-element.278.refs_15_), channel_id=1, source_target_pairs={{28,31},{29,30},{30,29},{31,28}} | collective-permute-start | bytes 983048 | tf_op jit(solution)/shard_map/ppermute | solution.py:42
  12.0 22.9 %collective-permute-start.7 = (bf16[160,1024]{1,0:T(8,128)(2,1)S(1)}, bf16[160,1024]{1,0:T(8,128)(2,1)}, u32[]{:S(2)}, u32[]{:S(2)}) collective-permute-start(bf16[160,1024]{1,0:T(8,128)(2,1)S(1)} %get-tuple-element.278.refs_15_), channel_id=1, source_target_pairs={{28,30},{29,31},{30,28},{31,29}} | collective-permute-start | bytes 983048 | tf_op jit(solution)/shard_map/ppermute | solution.py:42
  14.1 20.8 %collective-permute-start.6 = (bf16[160,1024]{1,0:T(8,128)(2,1)S(1)}, bf16[160,1024]{1,0:T(8,128)(2,1)}, u32[]{:S(2)}, u32[]{:S(2)}) collective-permute-start(bf16[160,1024]{1,0:T(8,128)(2,1)S(1)} %get-tuple-element.278.refs_15_), channel_id=1, source_target_pairs={{28,29},{29,28},{30,31},{31,30}} | collective-permute-start | bytes 983048 | tf_op jit(solution)/shard_map/ppermute | solution.py:42
  16.8 7.5 %collective-permute-start.4 = (bf16[256,512]{1,0:T(8,128)(2,1)S(1)}, bf16[256,512]{1,0:T(8,128)(2,1)S(1)}, u32[]{:S(2)}, u32[]{:S(2)}) collective-permute-start(bf16[256,512]{1,0:T(8,128)(2,1)S(1)} %collective-permute-done.2.refs_6_.refs_11_.refs_13_.refs_7_), channel_id=1, source_target_pairs={{0,1},{1,0},{2,3},{3,2},{4,5},{5,4},{6,7},{7,6},{8,9},{9,8},{10,11... | collective-permute-start | bytes 786440 | tf_op jit(solution)/shard_map/ppermute | solution.py:42
  18.5 10.0 %collective-permute-start.5 = (bf16[256,512]{1,0:T(8,128)(2,1)S(1)}, bf16[256,512]{1,0:T(8,128)(2,1)S(1)}, u32[]{:S(2)}, u32[]{:S(2)}) collective-permute-start(bf16[256,512]{1,0:T(8,128)(2,1)S(1)} %collective-permute-done.1.refs_5_.refs_10_.refs_12_.refs_6_), channel_id=1, source_target_pairs={{0,2},{1,3},{2,0},{3,1},{4,6},{5,7},{6,4},{7,5},{8,10},{9,11},{10,... | collective-permute-start | bytes 786440 | tf_op jit(solution)/shard_map/ppermute | solution.py:42
  24.3 17.7 %collective-permute-start.12 = (bf16[256,1024]{1,0:T(8,128)(2,1)S(1)}, bf16[256,1024]{1,0:T(8,128)(2,1)S(1)}, u32[]{:S(2)}, u32[]{:S(2)}) collective-permute-start(bf16[256,1024]{1,0:T(8,128)(2,1)S(1)} %get-tuple-element.287.refs_17_.refs_11_), channel_id=1, source_target_pairs={{0,3},{1,2},{2,1},{3,0},{4,7},{5,6},{6,5},{7,4},{8,11},{9,10},{10,... | collective-permute-start | bytes 1572872 | tf_op jit(solution)/shard_map/ppermute | solution.py:42
  28.6 21.9 %collective-permute-start.11 = (bf16[256,1024]{1,0:T(8,128)(2,1)S(1)}, bf16[256,1024]{1,0:T(8,128)(2,1)S(1)}, u32[]{:S(2)}, u32[]{:S(2)}) collective-permute-start(bf16[256,1024]{1,0:T(8,128)(2,1)S(1)} %get-tuple-element.287.refs_17_.refs_11_), channel_id=1, source_target_pairs={{0,2},{1,3},{2,0},{3,1},{4,6},{5,7},{6,4},{7,5},{8,10},{9,11},{10,... | collective-permute-start | bytes 1572872 | tf_op jit(solution)/shard_map/ppermute | solution.py:42
  32.4 18.1 %collective-permute-start.10 = (bf16[256,1024]{1,0:T(8,128)(2,1)S(1)}, bf16[256,1024]{1,0:T(8,128)(2,1)S(1)}, u32[]{:S(2)}, u32[]{:S(2)}) collective-permute-start(bf16[256,1024]{1,0:T(8,128)(2,1)S(1)} %get-tuple-element.287.refs_17_.refs_11_), channel_id=1, source_target_pairs={{0,1},{1,0},{2,3},{3,2},{4,5},{5,4},{6,7},{7,6},{8,9},{9,8},{10,11... | collective-permute-start | bytes 1572872 | tf_op jit(solution)/shard_map/ppermute | solution.py:42
  36.2 14.4 %collective-permute-start.9 = (bf16[64,4096]{1,0:T(8,128)(2,1)S(1)}, bf16[64,4096]{1,0:T(8,128)(2,1)S(1)}, u32[]{:S(2)}, u32[]{:S(2)}) collective-permute-start(bf16[64,4096]{1,0:T(8,128)(2,1)S(1)} %get-tuple-element.279), channel_id=1, source_target_pairs={{28,24},{29,25},{30,26},{31,27}} | collective-permute-start | bytes 1572872 | tf_op jit(solution)/shard_map/ppermute | solution.py:42
  36.9 14.9 %collective-permute-start.14 = (bf16[64,4096]{1,0:T(8,128)(2,1)S(1)}, bf16[64,4096]{1,0:T(8,128)(2,1)S(1)}, u32[]{:S(2)}, u32[]{:S(2)}) collective-permute-start(bf16[64,4096]{1,0:T(8,128)(2,1)S(1)} %get-tuple-element.289), channel_id=1, source_target_pairs={{28,24},{29,25},{30,26},{31,27}} | collective-permute-start | bytes 1572872 | tf_op jit(solution)/shard_map/ppermute | solution.py:42
  51.1 2.9 %collective-permute-start.13 = (bf16[64,4096]{1,0:T(8,128)(2,1)S(1)}, bf16[64,4096]{1,0:T(8,128)(2,1)S(1)}, u32[]{:S(2)}, u32[]{:S(2)}) collective-permute-start(bf16[64,4096]{1,0:T(8,128)(2,1)S(1)} %get-tuple-element.288), channel_id=1, source_target_pairs={{24,20},{25,21},{26,22},{27,23}} | collective-permute-start | bytes 1572872 | tf_op jit(solution)/shard_map/ppermute | solution.py:42
  52.4 3.0 %collective-permute-start.16 = (bf16[64,4096]{1,0:T(8,128)(2,1)S(1)}, bf16[64,4096]{1,0:T(8,128)(2,1)S(1)}, u32[]{:S(2)}, u32[]{:S(2)}) collective-permute-start(bf16[64,4096]{1,0:T(8,128)(2,1)S(1)} %get-tuple-element.319), channel_id=1, source_target_pairs={{24,20},{25,21},{26,22},{27,23}} | collective-permute-start | bytes 1572872 | tf_op jit(solution)/shard_map/ppermute | solution.py:42
  54.6 2.0 %collective-permute-start.15 = (bf16[64,4096]{1,0:T(8,128)(2,1)S(1)}, bf16[64,4096]{1,0:T(8,128)(2,1)S(1)}, u32[]{:S(2)}, u32[]{:S(2)}) collective-permute-start(bf16[64,4096]{1,0:T(8,128)(2,1)S(1)} %get-tuple-element.318), channel_id=1, source_target_pairs={{20,16},{21,17},{22,18},{23,19}} | collective-permute-start | bytes 1572872 | tf_op jit(solution)/shard_map/ppermute | solution.py:42
  55.9 2.0 %collective-permute-start.18 = (bf16[64,4096]{1,0:T(8,128)(2,1)S(1)}, bf16[64,4096]{1,0:T(8,128)(2,1)S(1)}, u32[]{:S(2)}, u32[]{:S(2)}) collective-permute-start(bf16[64,4096]{1,0:T(8,128)(2,1)S(1)} %get-tuple-element.359), channel_id=1, source_target_pairs={{20,16},{21,17},{22,18},{23,19}} | collective-permute-start | bytes 1572872 | tf_op jit(solution)/shard_map/ppermute | solution.py:42
  57.2 19.7 %collective-permute-start.17 = (bf16[64,4096]{1,0:T(8,128)(2,1)S(1)}, bf16[64,4096]{1,0:T(8,128)(2,1)S(1)}, u32[]{:S(2)}, u32[]{:S(2)}) collective-permute-start(bf16[64,4096]{1,0:T(8,128)(2,1)S(1)} %get-tuple-element.358), channel_id=1, source_target_pairs={{16,12},{17,13},{18,14},{19,15}} | collective-permute-start | bytes 1572872 | tf_op jit(solution)/shard_map/ppermute | solution.py:42
  58.6 19.7 %collective-permute-start.23 = (bf16[64,4096]{1,0:T(8,128)(2,1)S(1)}, bf16[64,4096]{1,0:T(8,128)(2,1)S(1)}, u32[]{:S(2)}, u32[]{:S(2)}) collective-permute-start(bf16[64,4096]{1,0:T(8,128)(2,1)S(1)} %get-tuple-element.404), channel_id=1, source_target_pairs={{16,12},{17,13},{18,14},{19,15}} | collective-permute-start | bytes 1572872 | tf_op jit(solution)/shard_map/ppermute | solution.py:42
  59.4 10.6 %collective-permute-start.19 = (bf16[128,1280]{1,0:T(8,128)(2,1)S(1)}, bf16[128,1280]{1,0:T(8,128)(2,1)S(1)}, u32[]{:S(2)}, u32[]{:S(2)}) collective-permute-start(bf16[128,1280]{1,0:T(8,128)(2,1)S(1)} %get-tuple-element.383), channel_id=1, source_target_pairs={{0,1},{1,0},{2,3},{3,2},{4,5},{5,4},{6,7},{7,6},{8,9},{9,8},{10,11... | collective-permute-start | bytes 983048 | tf_op jit(solution)/shard_map/ppermute | solution.py:42
  60.7 16.3 %collective-permute-start.20 = (bf16[128,1280]{1,0:T(8,128)(2,1)S(1)}, bf16[128,1280]{1,0:T(8,128)(2,1)S(1)}, u32[]{:S(2)}, u32[]{:S(2)}) collective-permute-start(bf16[128,1280]{1,0:T(8,128)(2,1)S(1)} %get-tuple-element.384), channel_id=1, source_target_pairs={{0,2},{1,3},{2,0},{3,1},{4,6},{5,7},{6,4},{7,5},{8,10},{9,11},{10,... | collective-permute-start | bytes 983048 | tf_op jit(solution)/shard_map/ppermute | solution.py:42
  62.1 14.9 %collective-permute-start.21 = (bf16[128,1280]{1,0:T(8,128)(2,1)S(1)}, bf16[128,1280]{1,0:T(8,128)(2,1)S(1)}, u32[]{:S(2)}, u32[]{:S(2)}) collective-permute-start(bf16[128,1280]{1,0:T(8,128)(2,1)S(1)} %get-tuple-element.385), channel_id=1, source_target_pairs={{0,3},{1,2},{2,1},{3,0},{4,7},{5,6},{6,5},{7,4},{8,11},{9,10},{10,... | collective-permute-start | bytes 983048 | tf_op jit(solution)/shard_map/ppermute | solution.py:42
  77.5 2.0 %collective-permute-start.22 = (bf16[64,4096]{1,0:T(8,128)(2,1)S(1)}, bf16[64,4096]{1,0:T(8,128)(2,1)S(1)}, u32[]{:S(2)}, u32[]{:S(2)}) collective-permute-start(bf16[64,4096]{1,0:T(8,128)(2,1)S(1)} %get-tuple-element.403), channel_id=1, source_target_pairs={{12,8},{13,9},{14,10},{15,11}} | collective-permute-start | bytes 1572872 | tf_op jit(solution)/shard_map/ppermute | solution.py:42
  78.9 2.0 %collective-permute-start.25 = (bf16[64,4096]{1,0:T(8,128)(2,1)S(1)}, bf16[64,4096]{1,0:T(8,128)(2,1)S(1)}, u32[]{:S(2)}, u32[]{:S(2)}) collective-permute-start(bf16[64,4096]{1,0:T(8,128)(2,1)S(1)} %get-tuple-element.444), channel_id=1, source_target_pairs={{12,8},{13,9},{14,10},{15,11}} | collective-permute-start | bytes 1572872 | tf_op jit(solution)/shard_map/ppermute | solution.py:42
  80.2 2.0 %collective-permute-start.24 = (bf16[64,4096]{1,0:T(8,128)(2,1)S(1)}, bf16[64,4096]{1,0:T(8,128)(2,1)S(1)}, u32[]{:S(2)}, u32[]{:S(2)}) collective-permute-start(bf16[64,4096]{1,0:T(8,128)(2,1)S(1)} %get-tuple-element.443), channel_id=1, source_target_pairs={{8,4},{9,5},{10,6},{11,7}} | collective-permute-start | bytes 1572872 | tf_op jit(solution)/shard_map/ppermute | solution.py:42
  81.5 2.6 %collective-permute-start.27 = (bf16[64,4096]{1,0:T(8,128)(2,1)S(1)}, bf16[64,4096]{1,0:T(8,128)(2,1)S(1)}, u32[]{:S(2)}, u32[]{:S(2)}) collective-permute-start(bf16[64,4096]{1,0:T(8,128)(2,1)S(1)} %get-tuple-element.484), channel_id=1, source_target_pairs={{8,4},{9,5},{10,6},{11,7}} | collective-permute-start | bytes 1572872 | tf_op jit(solution)/shard_map/ppermute | solution.py:42
  82.8 16.5 %collective-permute-start.26 = (bf16[64,4096]{1,0:T(8,128)(2,1)S(1)}, bf16[64,4096]{1,0:T(8,128)(2,1)S(1)}, u32[]{:S(2)}, u32[]{:S(2)}) collective-permute-start(bf16[64,4096]{1,0:T(8,128)(2,1)S(1)} %get-tuple-element.483), channel_id=1, source_target_pairs={{4,0},{5,1},{6,2},{7,3}} | collective-permute-start | bytes 1572872 | tf_op jit(solution)/shard_map/ppermute | solution.py:42
  84.7 20.2 %collective-permute-start.28 = (bf16[64,4096]{1,0:T(8,128)(2,1)S(1)}, bf16[64,4096]{1,0:T(8,128)(2,1)S(1)}, u32[]{:S(2)}, u32[]{:S(2)}) collective-permute-start(bf16[64,4096]{1,0:T(8,128)(2,1)S(1)} %get-tuple-element.504), channel_id=1, source_target_pairs={{4,0},{5,1},{6,2},{7,3}} | collective-permute-start | bytes 1572872 | tf_op jit(solution)/shard_map/ppermute | solution.py:42
  107.0 10.7 %collective-permute-start.29 = (bf16[128,1280]{1,0:T(8,128)(2,1)S(1)}, bf16[128,1280]{1,0:T(8,128)(2,1)S(1)}, u32[]{:S(2)}, u32[]{:S(2)}) collective-permute-start(bf16[128,1280]{1,0:T(8,128)(2,1)S(1)} %get-tuple-element.530), channel_id=1, source_target_pairs={{0,1},{1,0},{2,3},{3,2},{4,5},{5,4},{6,7},{7,6},{8,9},{9,8},{10,11... | collective-permute-start | bytes 983048 | tf_op jit(solution)/shard_map/ppermute | solution.py:42
  108.0 14.1 %collective-permute-start.30 = (bf16[128,1280]{1,0:T(8,128)(2,1)S(1)}, bf16[128,1280]{1,0:T(8,128)(2,1)S(1)}, u32[]{:S(2)}, u32[]{:S(2)}) collective-permute-start(bf16[128,1280]{1,0:T(8,128)(2,1)S(1)} %get-tuple-element.531), channel_id=1, source_target_pairs={{0,2},{1,3},{2,0},{3,1},{4,6},{5,7},{6,4},{7,5},{8,10},{9,11},{10,... | collective-permute-start | bytes 983048 | tf_op jit(solution)/shard_map/ppermute | solution.py:42
  109.5 13.9 %collective-permute-start.31 = (bf16[128,1280]{1,0:T(8,128)(2,1)S(1)}, bf16[128,1280]{1,0:T(8,128)(2,1)S(1)}, u32[]{:S(2)}, u32[]{:S(2)}) collective-permute-start(bf16[128,1280]{1,0:T(8,128)(2,1)S(1)} %get-tuple-element.532), channel_id=1, source_target_pairs={{0,3},{1,2},{2,1},{3,0},{4,7},{5,6},{6,5},{7,4},{8,11},{9,10},{10,... | collective-permute-start | bytes 983048 | tf_op jit(solution)/shard_map/ppermute | solution.py:42
  (4 other events, 26.6 us)

commit v5 on v4

v5 whole, which is shorter than its diff:
```python
import functools

import jax
import jax.numpy as jnp
from jax import lax
from jax.experimental import pallas as pl
from jax.experimental.pallas import tpu as pltpu
from jax.sharding import PartitionSpec as P

EPSILON = 1e-05
CHUNK_SHARES = (4, 4)
GAIN_ROWS = 16
ANY = pl.BlockSpec(memory_space=pl.ANY)
VMEM = pl.BlockSpec(memory_space=pltpu.VMEM)
SMEM = pl.BlockSpec(memory_space=pltpu.SMEM)
NOTHING = pl.CostEstimate(flops=0, bytes_accessed=0, transcendentals=0)
PARAMS = pltpu.CompilerParams(vmem_limit_bytes=20 * 1024 * 1024)


def dot_nn(left, right):
    return lax.dot_general(
        left, right, (((1,), (0,)), ((), ())), preferred_element_type=jnp.float32
    )


def dot_nt(left, right):
    return lax.dot_general(
        left, right, (((1,), (1,)), ((), ())), preferred_element_type=jnp.float32
    )


def dot_tn(left, right):
    return lax.dot_general(
        left, right, (((0,), (0,)), ((), ())), preferred_element_type=jnp.float32
    )


def silu_slope(latent):
    sigmoid = jax.nn.sigmoid(latent)
    return sigmoid * (1.0 + latent * (1.0 - sigmoid))


def move(block, pairs):
    return lax.ppermute(block, ("section", "dp"), pairs)


def peers(sections, size, k):
    return [(s * size + i, s * size + (i ^ k)) for s in sections for i in range(size)]


def gather(block, sections, size):
    return [block] + [move(block, peers(sections, size, k)) for k in range(1, size)]


def gather_halves(low, high, sections, size):
    if size != 4:
        return list(zip(gather(low, sections, size), gather(high, sections, size)))
    across, along = peers(sections, size, 1), peers(sections, size, 2)
    low_along = move(low, along)
    high_across = move(high, across)
    high_along = move(high, along)
    low_across = move(low, across)
    low_far = move(low_along, across)
    high_far = move(high_across, along)
    return [(low, high), (low_across, high_across), (low_along, high_along), (low_far, high_far)]


def pin(block):
    return pltpu.with_memory_space_constraint(block, pltpu.VMEM)


def stay(block):
    return pltpu.with_memory_space_constraint(block, pltpu.HBM)


def held_like(block):
    return pltpu.VMEM(block.shape, block.dtype)


def columns(dp_index, k, width):
    return pl.ds(pl.multiple_of((dp_index ^ k) * width, width), width)


def half_columns(dp_index, k, half, width):
    start = (dp_index ^ k) * width + half * (width // 2)
    return pl.ds(pl.multiple_of(start, width // 2), width // 2)


def prepare_kernel(flags, down, up, readout, *refs):
    low, high, *rest, down_held, up_held, readout_held, sems = refs
    copies = [
        pltpu.make_async_copy(down, down_held, sems.at[0]),
        pltpu.make_async_copy(up, up_held, sems.at[1]),
        pltpu.make_async_copy(readout, readout_held, sems.at[2]),
    ]
    for copy in copies:
        copy.start()
    latent_width, shard = up_held.shape[1:]
    horizon = readout_held.shape[1]
    half = shard // 2
    head_rows = low.shape[0] - latent_width
    copies[0].wait()
    turned = down_held[0].T
    low[:latent_width] = turned[:, :half]
    high[:latent_width] = turned[:, half:]
    copies[1].wait()
    copies[2].wait()
    values = up_held[0]

    @pl.when(flags[2] == 1)
    def _():
        product = dot_nn(values, readout_held[...]).astype(jnp.bfloat16)
        turned_readout = readout_held[...].T
        rows = latent_width * horizon // shard
        for out, start in ((low, 0), (high, half)):
            out[latent_width : latent_width + horizon] = turned_readout[:, start : start + half]
            for at in range(0, half, horizon):
                row = (start + at) // horizon * rows
                out[latent_width + horizon :, at : at + horizon] = product[row : row + rows]

    @pl.when(flags[2] == 0)
    def _():
        block = min(latent_width, shard)
        blocks = [values[:, at : at + block].T for at in range(0, shard, block)]
        whole = blocks[0] if len(blocks) == 1 else jnp.concatenate(blocks, axis=1)
        low[latent_width:] = whole[:head_rows, :half]
        high[latent_width:] = whole[:head_rows, half:]
        if rest:
            rest[0][...] = whole[head_rows:]


def norm_kernel(x, gain, x_out, normed_out, inverse_out, gain_out):
    values = x[...].astype(jnp.float32)
    inverse = lax.rsqrt(jnp.mean(values * values, axis=-1, keepdims=True) + EPSILON)
    x_out[...] = x[...]
    normed_out[...] = (values * inverse * gain[...].astype(jnp.float32)).astype(jnp.bfloat16)
    inverse_out[...] = jnp.broadcast_to(inverse, inverse_out.shape)
    gain_out[...] = gain[...]


def top_kernel(size, bounds, *refs):
    flags, truth, mask = refs[:3]
    halves = refs[7 : 7 + 2 * size]
    gain, x, inverse, latent_ref, latent_grad_out, arriving_out, grads_out = refs[
        7 + 2 * size : 14 + 2 * size
    ]
    sends = refs[14 + 2 * size :]
    dp_index = flags[0]
    width = x.shape[1] // size
    latent_width = latent_ref.shape[1]
    horizon = truth.shape[1]
    head = slice(latent_width, latent_width + horizon)

    @pl.when(flags[2] == 1)
    def _():
        latent = latent_ref[...]
        activated = jax.nn.silu(latent).astype(jnp.bfloat16)
        estimate = None
        product = None
        for k in range(size):
            extra = []
            for half in range(2):
                ref = halves[2 * k + half]
                part = dot_nt(x[:, half_columns(dp_index, k, half, width)], ref[head])
                estimate = part if estimate is None else estimate + part
                extra += [
                    ref[latent_width + horizon :, at : at + horizon]
                    for at in range(0, width // 2, horizon)
                ]
            extra = jnp.concatenate(extra, axis=0).astype(jnp.float32)
            product = extra if product is None else product + extra
        product = product.astype(jnp.bfloat16)
        estimate = estimate + dot_nn(activated, product)
        error = (mask[:, :1] * (estimate - truth[...])).astype(jnp.bfloat16)
        hidden_grad = dot_nt(error, product)
        latent_grad = (hidden_grad * silu_slope(latent)).astype(jnp.bfloat16)
        latent_grad_out[...] = latent_grad
        scale = inverse[:, :1]
        mean = jnp.sum(latent_grad.astype(jnp.float32) * latent, axis=-1, keepdims=True) / (
            width * size
        )
        slope = scale * scale * mean
        for k in range(size):
            for half in range(2):
                at_k = half_columns(dp_index, k, half, width)
                ref = halves[2 * k + half]
                arriving = dot_nn(error, ref[head]).astype(jnp.bfloat16)
                arriving_out[:, at_k] = arriving
                scaled = dot_nn(latent_grad, ref[:latent_width])
                grads = (
                    arriving.astype(jnp.float32)
                    + scale * (scaled * gain[:, at_k].astype(jnp.float32))
                    - x[:, at_k].astype(jnp.float32) * slope
                ).astype(jnp.bfloat16)
                grads_out[:, at_k] = grads
                for (row, end), send in zip(bounds, sends):
                    send[:, at_k] = grads[row:end]


def latent_kernel(size, *refs):
    flags, normed = refs[:2]
    down = refs[2 : 2 + 2 * size]
    latent = refs[3 + 2 * size]
    width = normed.shape[1] // size
    total = None
    for k in range(size):
        for half in range(2):
            block = normed[:, half_columns(flags[0], k, half, width)]
            part = dot_nt(block, down[2 * k + half][: latent.shape[1]])
            total = part if total is None else total + part
    latent[...] = total


def shard_of(raw, size, latent_width, rows):
    def down(k, half):
        return raw[2 * k + half][:latent_width]

    def up(k, lanes):
        half = raw[0].shape[1]
        parts = []
        for which in range(2):
            start, end = max(lanes.start - which * half, 0), min(lanes.stop - which * half, half)
            if start < end:
                parts.append(raw[2 * k + which][latent_width:, start:end])
        first = parts[0] if len(parts) == 1 else jnp.concatenate(parts, axis=1)
        if len(raw) == 2 * size:
            return first
        return jnp.concatenate([first, raw[2 * size + k][:, lanes]], axis=0)

    return down, up


def keep_kernel(size, count, *refs):
    flags = refs[0]
    gain, inverse, latent, x = refs[1:5]
    raw = refs[8 : 8 + count]
    kept = refs[15 + count : 15 + count + 2 * size]
    (bundle,) = refs[15 + count + 2 * size :]
    tokens, width = x.shape
    latent_width = latent.shape[1]
    shard = width // size
    block, lanes = kept[-1].shape
    down, up = shard_of(raw, size, latent_width, block)

    @pl.when(flags[3] == 1)
    def _():
        for k in range(size):
            for half in range(2):
                here = slice(half * (shard // 2), (half + 1) * (shard // 2))
                kept[k][:, here] = down(k, half)
            step = lanes // 2
            for at in range(0, lanes, step):
                kept[size + k][:, at : at + step] = up(k, slice(at, at + step))

    @pl.when((flags[1] % 2 == 0) & (flags[3] == 1))
    def _():
        for k in range(size):
            bundle[k * latent_width : (k + 1) * latent_width] = kept[k][...]
            row = size * latent_width + k * block
            bundle[row : row + block] = kept[size + k][...]
        at = size * (latent_width + block)
        for k in range(size):
            here = slice(k * shard, (k + 1) * shard)
            bundle[at + k * tokens : at + (k + 1) * tokens] = x[:, here]
            row = at + size * tokens + k * GAIN_ROWS
            bundle[row : row + GAIN_ROWS] = jnp.broadcast_to(gain[:, here], (GAIN_ROWS, shard))
        at += size * (tokens + GAIN_ROWS)
        for values in (latent[...], inverse[...]):
            high = values.astype(jnp.bfloat16)
            low = (values - high.astype(jnp.float32)).astype(jnp.bfloat16)
            for part in (high, low):
                bundle[at : at + tokens, : part.shape[1]] = part
                at += tokens


def message_kernel(size, *refs):
    flags, normed = refs[:2]
    latent = refs[3]
    messages = refs[4:]
    shard = normed.shape[1] // size
    activated = jax.nn.silu(latent[...]).astype(jnp.bfloat16)
    for k in range(size):
        messages[k][:, :shard] = normed[:, columns(flags[0], k, shard)]
        messages[k][:, shard:] = activated


def step_back(dp_index, size, width, take, down, up, lat, scale, gain, x, write):
    latent_width = lat.shape[1]
    shard = width // size
    block = min(latent_width, shard)
    hidden_grad = None
    for k in range(size):
        arriving = take(columns(dp_index, k, shard))
        for at in range(0, shard, block):
            lanes = at // block * latent_width
            part = dot_nn(arriving[:, at : at + block], up(k, slice(lanes, lanes + latent_width)))
            hidden_grad = part if hidden_grad is None else hidden_grad + part
    latent_grad = (hidden_grad * silu_slope(lat)).astype(jnp.bfloat16)
    mean = jnp.sum(latent_grad.astype(jnp.float32) * lat, axis=-1, keepdims=True) / width
    slope = scale * scale * mean
    for k in range(size):
        for half in range(2):
            place = half_columns(dp_index, k, half, shard)
            arriving = take(place)
            scaled = dot_nn(latent_grad, down(k, half))
            value = (
                arriving.astype(jnp.float32)
                + scale * (scaled * gain(k, half).astype(jnp.float32))
                - x(k, half).astype(jnp.float32) * slope
            ).astype(jnp.bfloat16)
            write(place, arriving, value)
    return latent_grad


def kept_of(kept, size, shard):
    def down(k, half):
        return kept[k][:, half * (shard // 2) : (half + 1) * (shard // 2)]

    return down, lambda k, lanes: kept[size + k][:, lanes]


def stage_kernel(stage, bounds, size, held, count, *refs):
    flags = refs[0]
    pieces = refs[1 : 1 + len(bounds)]
    at = 1 + len(bounds)
    raw = refs[at + held : at + held + count]
    state = refs[at + held + count : at + 2 * held + count]
    outs = refs[at + 2 * held + count :]
    shard = state[3].shape[1] // size
    if raw:
        down, up = shard_of(raw, size, state[2].shape[1], None)
    else:
        down, up = kept_of(state[7:], size, shard)
    state = state[:7]
    gain, inverse, latent, x, latent_grads, arrivals, grads = state
    at_rows = slice(bounds[0][0], bounds[-1][1])

    def take(place):
        parts = [piece[:, place] for piece in pieces]
        return parts[0] if len(parts) == 1 else jnp.concatenate(parts, axis=0)

    def write(place, arriving, value):
        arrivals[at_rows, place] = arriving
        grads[at_rows, place] = value
        if stage and outs:
            outs[0][:, place] = value

    @pl.when(flags[1] == stage)
    def _():
        latent_grads[at_rows] = step_back(
            flags[0],
            size,
            x.shape[1],
            take,
            down,
            up,
            latent[at_rows],
            inverse[at_rows][:, :1],
            lambda k, half: gain[:, half_columns(flags[0], k, half, shard)],
            lambda k, half: x[at_rows, half_columns(flags[0], k, half, shard)],
            write,
        )

    if stage == 0:
        for k in range(size):
            outs[k][:, :shard] = arrivals[:, columns(flags[0], k, shard)]
            outs[k][:, shard:] = latent_grads[...]


def pair_kernel(stage, bound, size, held, *refs):
    flags, received = refs[:2]
    state = refs[2 + held : 9 + held]
    kept = refs[9 + held : 9 + held + 2 * size]
    bundle = refs[1 + 2 * held]
    middle, last = refs[2 + 2 * held :]
    gain, inverse, latent, x, latent_grads, arrivals, grads = state
    tokens = x.shape[0]
    latent_width = latent.shape[1]
    shard = x.shape[1] // size
    down, up = kept_of(kept, size, shard)
    block = kept[-1].shape[0]
    at_rows = slice(*bound)

    def write(place, arriving, value):
        arrivals[at_rows, place] = arriving
        grads[at_rows, place] = value
        middle[:, place] = value

    def write_last(place, arriving, value):
        last[:, place] = value

    def next_down(k, half):
        here = slice(half * (shard // 2), (half + 1) * (shard // 2))
        return bundle[k * latent_width : (k + 1) * latent_width, here]

    def both(index, lanes):
        row = size * (latent_width + block + tokens + GAIN_ROWS) + index * tokens + bound[0]
        end = row + bound[1] - bound[0]
        high = bundle[row:end, :lanes].astype(jnp.float32)
        return high + bundle[row + tokens : end + tokens, :lanes].astype(jnp.float32)

    def next_x(k, half):
        here = slice(half * (shard // 2), (half + 1) * (shard // 2))
        start = size * (latent_width + block) + (flags[0] ^ k) * tokens + bound[0]
        return bundle[pl.ds(pl.multiple_of(start, 16), bound[1] - bound[0]), here]

    def next_gain(k, half):
        here = slice(half * (shard // 2), (half + 1) * (shard // 2))
        start = size * (latent_width + block + tokens) + (flags[0] ^ k) * GAIN_ROWS
        return bundle[pl.ds(pl.multiple_of(start, 16), GAIN_ROWS), here][:1]

    def next_up(k, lanes):
        row = size * latent_width + k * block
        return bundle[row : row + block, lanes]

    @pl.when(flags[1] == stage)
    def _():
        latent_grads[at_rows] = step_back(
            flags[0],
            size,
            x.shape[1],
            lambda place: received[:, place],
            down,
            up,
            latent[at_rows],
            inverse[at_rows][:, :1],
            lambda k, half: gain[:, half_columns(flags[0], k, half, shard)],
            lambda k, half: x[at_rows, half_columns(flags[0], k, half, shard)],
            write,
        )
        step_back(
            flags[0],
            size,
            x.shape[1],
            lambda place: middle[:, place],
            next_down,
            next_up,
            both(0, latent_width),
            both(2, 128)[:, :1],
            next_gain,
            next_x,
            write_last,
        )


def touch_kernel(*refs):
    pass


def weight_kernel(size, *refs):
    early, late = refs[:size], refs[size : 2 * size]
    down_grads, up_grads, left, right = refs[2 * size :]
    tokens = early[0].shape[0]
    shard = down_grads.shape[0]
    for k in range(size):
        left[k * tokens : (k + 1) * tokens] = early[k][...]
        right[k * tokens : (k + 1) * tokens] = late[k][...]
    down_grads[...] = dot_tn(left[:, :shard], right[:, shard:]).astype(jnp.bfloat16)
    up_grads[...] = dot_tn(left[:, shard:], right[:, :shard]).astype(jnp.bfloat16)


def per_device(
    section_inputs, norm_gain, down_proj, up_proj, readout_matrix, ground_truth_series, valid_len
):
    size = lax.axis_size("dp")
    sections = lax.axis_size("section")
    top = sections - 1
    dp_index = lax.axis_index("dp")
    section = lax.axis_index("section")
    f32, bf16 = jnp.float32, jnp.bfloat16

    x = section_inputs[0]
    tokens, width = x.shape
    shard, latent_width = down_proj.shape[1:]
    horizon = readout_matrix.shape[1]
    share = tokens // sum(CHUNK_SHARES)
    ends = [share * sum(CHUNK_SHARES[: i + 1]) for i in range(len(CHUNK_SHARES))]
    bounds = list(zip([0] + ends, ends))

    flags = jnp.stack(
        [
            dp_index.astype(jnp.int32),
            section.astype(jnp.int32),
            (section == top).astype(jnp.int32),
            (section < top - 1).astype(jnp.int32),
        ]
    )
    everyone, rest = list(range(sections)), list(range(top))
    up_block = min(latent_width, shard)
    up_lanes = latent_width * shard // up_block
    head_rows = horizon + latent_width * horizon // shard
    more = max(up_block - head_rows, 0)
    low, high, *up_rest = pl.pallas_call(
        prepare_kernel,
        out_shape=(jax.ShapeDtypeStruct((latent_width + head_rows, shard // 2), bf16),) * 2
        + (jax.ShapeDtypeStruct((more, up_lanes), bf16),) * (more > 0),
        in_specs=[SMEM] + [ANY] * 3,
        out_specs=(VMEM,) * (2 + (more > 0)),
        scratch_shapes=[
            pltpu.VMEM((1, shard, latent_width), bf16),
            pltpu.VMEM((1, latent_width, shard), bf16),
            pltpu.VMEM((shard, horizon), bf16),
            pltpu.SemaphoreType.DMA((3,)),
        ],
        cost_estimate=NOTHING,
        compiler_params=PARAMS,
    )(flags, stay(down_proj), stay(up_proj), stay(readout_matrix))
    halves = gather_halves(low, high, everyone, size)
    if more:
        up_rest, first = lax.optimization_barrier((up_rest[0], halves[2 % size][0]))
        halves[2 % size] = (first, halves[2 % size][1])
        up_rest = gather(up_rest, rest, size)
    halves = [half for pair in halves for half in pair]

    x, normed, inverse, gain = pl.pallas_call(
        norm_kernel,
        out_shape=(
            pltpu.VMEM((tokens, width), bf16),
            pltpu.VMEM((tokens, width), bf16),
            pltpu.VMEM((tokens, 128), f32),
            pltpu.VMEM((1, width), bf16),
        ),
        in_specs=[VMEM] * 2,
        out_specs=(VMEM,) * 4,
        cost_estimate=NOTHING,
        compiler_params=PARAMS,
    )(x, norm_gain)
    per_micro = tokens // valid_len.shape[0]
    mask = (
        (jnp.arange(per_micro)[None, :] < valid_len[:, None]).astype(f32).reshape(tokens, 1)
    )
    mask = jnp.broadcast_to(mask, (tokens, 128))

    normed, latent = pl.pallas_call(
        functools.partial(latent_kernel, size),
        out_shape=(held_like(normed), pltpu.VMEM((tokens, latent_width), f32)),
        in_specs=[SMEM] + [VMEM] * (1 + 2 * size),
        out_specs=(VMEM,) * 2,
        input_output_aliases={1: 0},
        cost_estimate=NOTHING,
        compiler_params=PARAMS,
    )(flags, pin(normed), *[pin(half) for half in halves])

    gain, x, inverse, latent, latent_grads, arrivals, grads, *sends = pl.pallas_call(
        functools.partial(top_kernel, size, bounds),
        out_shape=(
            held_like(gain),
            held_like(x),
            held_like(inverse),
            held_like(latent),
            pltpu.VMEM((tokens, latent_width), bf16),
            pltpu.VMEM((tokens, width), bf16),
            pltpu.VMEM((tokens, width), bf16),
        )
        + tuple(jax.ShapeDtypeStruct((end - row, width), bf16) for row, end in bounds),
        in_specs=[SMEM] + [VMEM] * (6 + 2 * size),
        out_specs=(VMEM,) * (7 + len(bounds)),
        input_output_aliases={3: 0, 4: 1, 5: 2, 6: 3},
        cost_estimate=NOTHING,
        compiler_params=PARAMS,
    )(
        flags, ground_truth_series, mask, pin(gain), pin(x), pin(inverse), pin(latent),
        *[pin(part) for part in halves],
    )

    def hop(block, sender, distance=1):
        return move(
            block, [(sender * size + i, (sender - distance) * size + i) for i in range(size)]
        )

    received = [hop(send, top) for send in sends]

    message = jax.ShapeDtypeStruct((tokens, shard + latent_width), bf16)
    shards = (*halves, *up_rest)
    state = (gain, inverse, latent, x, latent_grads, arrivals, grads)

    def run_stage(stage, bounds, received, state, shards, sends=True):
        rows = bounds[-1][1] - bounds[0][0]
        if not stage:
            outs = (message,) * size
        else:
            outs = (jax.ShapeDtypeStruct((rows, width), bf16),) * sends
        first = 1 + len(received)
        results = pl.pallas_call(
            functools.partial(stage_kernel, stage, bounds, size, len(state), len(shards)),
            out_shape=tuple(held_like(part) for part in state) + outs,
            in_specs=[SMEM] + [VMEM] * (len(received) + len(state) + len(shards)),
            out_specs=(VMEM,) * (len(state) + len(outs)),
            input_output_aliases={first + i: i for i in range(len(state))},
            cost_estimate=NOTHING,
            compiler_params=PARAMS,
        )(flags, *received, *[pin(part) for part in state + shards])
        return tuple(results[: len(state)]), results[len(state) :]

    def run_pair(stage, bound, received, state):
        rows = bound[1] - bound[0]
        results = pl.pallas_call(
            functools.partial(pair_kernel, stage, bound, size, len(state)),
            out_shape=tuple(held_like(part) for part in state)
            + (jax.ShapeDtypeStruct((rows, width), bf16),) * 2,
            in_specs=[SMEM] + [VMEM] * (1 + len(state)),
            out_specs=(VMEM,) * (len(state) + 2),
            input_output_aliases={2 + i: i for i in range(len(state))},
            cost_estimate=NOTHING,
            compiler_params=PARAMS,
        )(flags, received, *[pin(part) for part in state])
        return tuple(results[: len(state)]), results[len(state) :]

    def send_messages(messages):
        return [messages[0]] + [
            move(messages[k], peers(range(sections), size, k)) for k in range(1, size)
        ]

    state_kept = pl.pallas_call(
        functools.partial(keep_kernel, size, len(shards)),
        out_shape=tuple(held_like(part) for part in state)
        + (pltpu.VMEM((latent_width, shard), bf16),) * size
        + (pltpu.VMEM((up_block, up_lanes), bf16),) * size
        + (
            jax.ShapeDtypeStruct(
                (size * (latent_width + up_block + tokens + GAIN_ROWS) + 4 * tokens, shard), bf16
            ),
        ),
        in_specs=[SMEM] + [VMEM] * (len(state) + len(shards)),
        out_specs=(VMEM,) * (len(state) + 2 * size + 1),
        input_output_aliases={1 + i: i for i in range(len(state))},
        cost_estimate=NOTHING,
        compiler_params=PARAMS,
    )(flags, *[pin(part) for part in state + shards])
    state, kept, bundle = tuple(state_kept[:7]), tuple(state_kept[7:-1]), state_kept[-1:]
    pairs = list(range(3, top - 1, 2))
    bundle = tuple(
        move(part, [((s - 1) * size + i, s * size + i) for s in pairs for i in range(size)])
        for part in bundle
    )

    sent = []
    for bound, block in zip(bounds, received):
        state, outs = run_stage(top - 1, [bound], [block], state, shards)
        sent.append(hop(outs[0], top - 1))
    received = sent

    state = state + kept + bundle

    waiting = []
    for stage in reversed(pairs):
        sent, side = [], []
        for bound, block in zip(bounds, received):
            state, outs = run_pair(stage, bound, block, state)
            sent.append(hop(outs[1], stage, 2))
            side.append(hop(outs[0], stage))
        received = sent
        for asides, bound, block in waiting:
            base, _ = run_stage(asides, [bound], [block], state[:-1], (), False)
            state = base + state[-1:]
        waiting = [(stage - 1, bound, block) for bound, block in zip(bounds, side)]
    latent, *messages = pl.pallas_call(
        functools.partial(message_kernel, size),
        out_shape=(held_like(state[2]),) + (message,) * size,
        in_specs=[SMEM] + [VMEM] * 2,
        out_specs=(VMEM,) * (1 + size),
        input_output_aliases={2: 0},
        cost_estimate=NOTHING,
        compiler_params=PARAMS,
    )(flags, pin(normed), pin(state[2]))
    early = send_messages(messages)
    latent, *early = pl.pallas_call(
        touch_kernel,
        out_shape=(held_like(latent),) + tuple(held_like(part) for part in early),
        in_specs=[VMEM] * (1 + size),
        out_specs=(VMEM,) * (1 + size),
        input_output_aliases={i: i for i in range(1 + size)},
        cost_estimate=NOTHING,
        compiler_params=PARAMS,
    )(pin(latent), *[pin(part) for part in early])
    state = state[:2] + (latent,) + state[3:]
    state = state[:-1]

    sent = []
    for bound, block in zip(bounds, received):
        state, outs = run_stage(1, [bound], [block], state, ())
        sent.append(hop(outs[0], 1))
    received = sent
    for asides, bound, block in waiting:
        state, _ = run_stage(asides, [bound], [block], state, (), False)
    shards = ()
    state, outs = run_stage(0, bounds, received, state, shards)
    late = send_messages(outs)
    down_grads, up_grads = pl.pallas_call(
        functools.partial(weight_kernel, size),
        out_shape=(
            jax.ShapeDtypeStruct((shard, latent_width), bf16),
            jax.ShapeDtypeStruct((latent_width, shard), bf16),
        ),
        in_specs=[VMEM] * (2 * size),
        out_specs=(VMEM,) * 2,
        scratch_shapes=[pltpu.VMEM((size * tokens, shard + latent_width), bf16)] * 2,
        cost_estimate=NOTHING,
        compiler_params=PARAMS,
    )(*early, *late)
    return (state[6][None], down_grads[None], up_grads[None])


def solution(mesh):
    placed = (
        P("section", "dp", None),
        P("section", None),
        P("section", "dp", None),
        P("section", None, "dp"),
        P("dp", None),
        P("dp", None),
        P("dp"),
    )
    return jax.shard_map(
        per_device,
        mesh=mesh,
        in_specs=placed,
        out_specs=(P("section", "dp", None), P("section", "dp", None), P("section", None, "dp")),
        check_vma=False,
    )
```

time: 126 us -> 119 us (0.944)
  the two profiles are of different devices: /device:TPU:0 before, /device:TPU:16 now
where the time goes in v5:
time: 119 us
  waiting for transfers between devices  56.1 us (47%)
  starting transfers between devices  36 us (30%)
  Pallas kernels  21.7 us (18%)
  local copies, waits for them, and re-layouts  3.07 us (3%)
    ppermute x30, waiting for transfers between devices, move(): return lax.ppermute(block, ('section', 'dp'), pairs)  56.1 us
    ppermute x30, starting transfers between devices, move(): return lax.ppermute(block, ('section', 'dp'), pairs)  36 us
    pallas_call x9, Pallas kernels, run_stage(): pl.pallas_call(functools.partial(stage_kernel, stage, bounds, size, len(s...  9.68 us
    unnamed x7, local copies, waits for them, and re-layouts  2.92 us
    pallas_call x1, Pallas kernels, per_device(): pl.pallas_call(prepare_kernel, out_shape=(jax.ShapeDtypeStruct((latent_wi...  2.73 us
    pallas_call x4, Pallas kernels, run_pair(): pl.pallas_call(functools.partial(pair_kernel, stage, bound, size, len(sta...  2.47 us
  transfers between devices with their start and end apart: 30, of which 12 were waited for; matrix products, arithmetic and copies ran while one was open for 2% of the time, Pallas kernels for 12%

profile of v5, /device:TPU:16, one launch (start us, length us, event | category | flops | bytes accessed | tf_op | source)
XLA Modules:
  0.0 118.8 jit_solution(532973897007697772)
XLA Ops:
  0.7 2.7 %shard_map.95 = (bf16[416,512]{1,0:T(8,128)(2,1)S(1)}, bf16[416,512]{1,0:T(8,128)(2,1)S(1)}, bf16[96,1024]{1,0:T(8,128)(2,1)}) custom-call(s32[4]{0:T(128)S(1)} %pad_add_fusion.flags.refs_0_, bf16[1,1024,256]{2,1,0:T(8,128)(2,1)} %down.1, bf16[1,256,1024]{2,1,0:T(8,128)(2,1)} %up.1, bf16[1024,128]{1,0:T(8,128)(2,1)} %readout.1), custom_call_target="tpu_custom_call" | custom-call | tf_op jit(solution)/shard_map/pallas_call | solution.py:493
  3.5 1.6 %collective-permute-start.2 = (bf16[416,512]{1,0:T(8,128)(2,1)S(1)}, bf16[416,512]{1,0:T(8,128)(2,1)S(1)}, u32[]{:S(2)}, u32[]{:S(2)}) collective-permute-start(bf16[416,512]{1,0:T(8,128)(2,1)S(1)} %get-tuple-element.239.refs_2_.refs_7_.refs_8_.refs_9_), channel_id=1, source_target_pairs={{0,2},{1,3},{2,0},{3,1},{4,6},{5,7},{6,4},{7,5},{8,10},{9,11},{10,... | collective-permute-start | bytes 1277960 | tf_op jit(solution)/shard_map/ppermute | solution.py:44
  5.1 1.5 %collective-permute-start.1 = (bf16[416,512]{1,0:T(8,128)(2,1)S(1)}, bf16[416,512]{1,0:T(8,128)(2,1)S(1)}, u32[]{:S(2)}, u32[]{:S(2)}) collective-permute-start(bf16[416,512]{1,0:T(8,128)(2,1)S(1)} %get-tuple-element.240.refs_3_.refs_8_.refs_9_.refs_10_), channel_id=1, source_target_pairs={{0,1},{1,0},{2,3},{3,2},{4,5},{5,4},{6,7},{7,6},{8,9},{9,8},{10,11... | collective-permute-start | bytes 1277960 | tf_op jit(solution)/shard_map/ppermute | solution.py:44
  7.6 8.7 %collective-permute-done.2.refs_6_.refs_11_.refs_12_.refs_13_ = bf16[416,512]{1,0:T(8,128)(2,1)S(1)} collective-permute-done((bf16[416,512]{1,0:T(8,128)(2,1)S(1)}, bf16[416,512]{1,0:T(8,128)(2,1)S(1)}, u32[]{:S(2)}, u32[]{:S(2)}) %collective-permute-start.2) | collective-permute-done | bytes 426016 | tf_op jit(solution)/shard_map/ppermute | solution.py:44
  16.2 1.5 %collective-permute-start.4 = (bf16[416,512]{1,0:T(8,128)(2,1)S(1)}, bf16[416,512]{1,0:T(8,128)(2,1)S(1)}, u32[]{:S(2)}, u32[]{:S(2)}) collective-permute-start(bf16[416,512]{1,0:T(8,128)(2,1)S(1)} %collective-permute-done.2.refs_6_.refs_11_.refs_12_.refs_13_), channel_id=1, source_target_pairs={{0,1},{1,0},{2,3},{3,2},{4,5},{5,4},{6,7},{7,6},{8,9},{9,8},{10,11... | collective-permute-start | bytes 1277960 | tf_op jit(solution)/shard_map/ppermute | solution.py:44
  17.8 1.5 %collective-permute-start.5 = (bf16[416,512]{1,0:T(8,128)(2,1)S(1)}, bf16[416,512]{1,0:T(8,128)(2,1)S(1)}, u32[]{:S(2)}, u32[]{:S(2)}) collective-permute-start(bf16[416,512]{1,0:T(8,128)(2,1)S(1)} %collective-permute-done.1.refs_5_.refs_10_.refs_11_.refs_12_), channel_id=1, source_target_pairs={{0,2},{1,3},{2,0},{3,1},{4,6},{5,7},{6,4},{7,5},{8,10},{9,11},{10,... | collective-permute-start | bytes 1277960 | tf_op jit(solution)/shard_map/ppermute | solution.py:44
  19.2 3.4 %collective-permute-start.9 = (bf16[96,1024]{1,0:T(8,128)(2,1)}, bf16[96,1024]{1,0:T(8,128)(2,1)}, u32[]{:S(2)}, u32[]{:S(2)}) collective-permute-start(bf16[96,1024]{1,0:T(8,128)(2,1)} %get-tuple-element.252.refs_16_.refs_17_), channel_id=1, source_target_pairs={{0,3},{1,2},{2,1},{3,0},{4,7},{5,6},{6,5},{7,4},{8,11},{9,10},{10,... | collective-permute-start | bytes 589832 | tf_op jit(solution)/shard_map/ppermute | solution.py:44
  22.7 4.3 %collective-permute-done.refs_4_.refs_9_.refs_10_.refs_11_ = bf16[416,512]{1,0:T(8,128)(2,1)S(1)} collective-permute-done((bf16[416,512]{1,0:T(8,128)(2,1)S(1)}, bf16[416,512]{1,0:T(8,128)(2,1)S(1)}, u32[]{:S(2)}, u32[]{:S(2)}) %collective-permute-start) | collective-permute-done | bytes 426016 | tf_op jit(solution)/shard_map/ppermute | solution.py:44
  26.9 2.4 %collective-permute-start.8 = (bf16[96,1024]{1,0:T(8,128)(2,1)}, bf16[96,1024]{1,0:T(8,128)(2,1)}, u32[]{:S(2)}, u32[]{:S(2)}) collective-permute-start(bf16[96,1024]{1,0:T(8,128)(2,1)} %get-tuple-element.252.refs_16_.refs_17_), channel_id=1, source_target_pairs={{0,2},{1,3},{2,0},{3,1},{4,6},{5,7},{6,4},{7,5},{8,10},{9,11},{10,... | collective-permute-start | bytes 589832 | tf_op jit(solution)/shard_map/ppermute | solution.py:44
  29.3 3.4 %collective-permute-start.7 = (bf16[96,1024]{1,0:T(8,128)(2,1)}, bf16[96,1024]{1,0:T(8,128)(2,1)}, u32[]{:S(2)}, u32[]{:S(2)}) collective-permute-start(bf16[96,1024]{1,0:T(8,128)(2,1)} %get-tuple-element.252.refs_16_.refs_17_), channel_id=1, source_target_pairs={{0,1},{1,0},{2,3},{3,2},{4,5},{5,4},{6,7},{7,6},{8,9},{9,8},{10,11... | collective-permute-start | bytes 589832 | tf_op jit(solution)/shard_map/ppermute | solution.py:44
  36.2 1.4 %shard_map.96 = (bf16[128,4096]{1,0:T(8,128)(2,1)S(1)}, f32[128,256]{1,0:T(8,128)S(1)}) custom-call(s32[4]{0:T(128)S(1)} %pad_add_fusion.flags.refs_0_, bf16[128,4096]{1,0:T(8,128)(2,1)S(1)} %get-tuple-element.238.refs_1_, bf16[416,512]{1,0:T(8,128)(2,1)S(1)} %get-tuple-element.239.refs_2_.refs_7_.refs_8_.refs_9_, ...), custom_call_target="tpu_custom_call", output_to_operand_aliasing={{0}: (1, {})} | custom-call | tf_op jit(solution)/shard_map/pallas_call | solution.py:534
  38.2 2.1 %collective-permute-done.9.refs_19_.refs_20_ = bf16[96,1024]{1,0:T(8,128)(2,1)} collective-permute-done((bf16[96,1024]{1,0:T(8,128)(2,1)}, bf16[96,1024]{1,0:T(8,128)(2,1)}, u32[]{:S(2)}, u32[]{:S(2)}) %collective-permute-start.9) | collective-permute-done | bytes 196640 | tf_op jit(solution)/shard_map/ppermute | solution.py:44
  40.4 1.5 %collective-permute-done.8.refs_18_.refs_19_ = bf16[96,1024]{1,0:T(8,128)(2,1)} collective-permute-done((bf16[96,1024]{1,0:T(8,128)(2,1)}, bf16[96,1024]{1,0:T(8,128)(2,1)}, u32[]{:S(2)}, u32[]{:S(2)}) %collective-permute-start.8) | collective-permute-done | bytes 196640 | tf_op jit(solution)/shard_map/ppermute | solution.py:44
  41.9 1.3 %collective-permute-done.7.refs_17_.refs_18_ = bf16[96,1024]{1,0:T(8,128)(2,1)} collective-permute-done((bf16[96,1024]{1,0:T(8,128)(2,1)}, bf16[96,1024]{1,0:T(8,128)(2,1)}, u32[]{:S(2)}, u32[]{:S(2)}) %collective-permute-start.7) | collective-permute-done | bytes 196640 | tf_op jit(solution)/shard_map/ppermute | solution.py:44
  43.2 1.9 %shard_map.98 = (bf16[1,4096]{1,0:T(2,128)(2,1)S(1)}, f32[128,128]{1,0:T(8,128)S(1)}, f32[128,256]{1,0:T(8,128)S(1)}, bf16[128,4096]{1,0:T(8,128)(2,1)S(1)}, bf1...) custom-call(s32[4]{0:T(128)S(1)} %pad_add_fusion.flags.refs_0_, ...), custom_call_target="tpu_custom_call", output_to_operand_aliasing={{0}: (1, {}), {1}: (2, {}), {2}: (3, {}), {3}: (4, {}), {4}... | custom-call | tf_op jit(solution)/shard_map/pallas_call | solution.py:614
  45.1 1.7 %collective-permute-start.12 = (bf16[3136,1024]{1,0:T(8,128)(2,1)S(1)}, bf16[3136,1024]{1,0:T(8,128)(2,1)S(1)}, u32[]{:S(2)}, u32[]{:S(2)}) collective-permute-start(bf16[3136,1024]{1,0:T(8,128)(2,1)S(1)} %get-tuple-element.284), channel_id=1, source_target_pairs={{8,12},{9,13},{10,14},{11,15},{16,20},{17,21},{18,22},{19,23}} | collective-permute-start | bytes 19267592 | tf_op jit(solution)/shard_map/ppermute | solution.py:44
  48.2 1.2 %shard_map.99 = (bf16[1,4096]{1,0:T(2,128)(2,1)S(1)}, f32[128,128]{1,0:T(8,128)S(1)}, f32[128,256]{1,0:T(8,128)S(1)}, bf16[128,4096]{1,0:T(8,128)(2,1)S(1)}, bf1...) custom-call(s32[4]{0:T(128)S(1)} %pad_add_fusion.flags.refs_0_, ...), custom_call_target="tpu_custom_call", output_to_operand_aliasing={{0}: (2, {}), {1}: (3, {}), {2}: (4, {}), {3}: (5, {}), {4}... | custom-call | tf_op jit(solution)/shard_map/pallas_call | solution.py:584
  50.2 1.2 %shard_map.100 = (bf16[1,4096]{1,0:T(2,128)(2,1)S(1)}, f32[128,128]{1,0:T(8,128)S(1)}, f32[128,256]{1,0:T(8,128)S(1)}, bf16[128,4096]{1,0:T(8,128)(2,1)S(1)}, bf...) custom-call(s32[4]{0:T(128)S(1)} %pad_add_fusion.flags.refs_0_, ...), custom_call_target="tpu_custom_call", output_to_operand_aliasing={{0}: (2, {}), {1}: (3, {}), {2}: (4, {}), {3}: (5, {}), {4}... | custom-call | tf_op jit(solution)/shard_map/pallas_call | solution.py:584
  52.1 4.2 %collective-permute-done.12.refs_17_ = bf16[3136,1024]{1,0:T(8,128)(2,1)S(1)} collective-permute-done((bf16[3136,1024]{1,0:T(8,128)(2,1)S(1)}, bf16[3136,1024]{1,0:T(8,128)(2,1)S(1)}, u32[]{:S(2)}, u32[]{:S(2)}) %collective-permute-start.12) | collective-permute-done | bytes 6422560 | tf_op jit(solution)/shard_map/ppermute | solution.py:44
  59.1 1.3 %collective-permute-start.17 = (bf16[64,4096]{1,0:T(8,128)(2,1)S(1)}, bf16[64,4096]{1,0:T(8,128)(2,1)S(1)}, u32[]{:S(2)}, u32[]{:S(2)}) collective-permute-start(bf16[64,4096]{1,0:T(8,128)(2,1)S(1)} %get-tuple-element.321), channel_id=1, source_target_pairs={{20,16},{21,17},{22,18},{23,19}} | collective-permute-start | bytes 1572872 | tf_op jit(solution)/shard_map/ppermute | solution.py:44
  60.4 1.3 %collective-permute-start.16 = (bf16[64,4096]{1,0:T(8,128)(2,1)S(1)}, bf16[64,4096]{1,0:T(8,128)(2,1)S(1)}, u32[]{:S(2)}, u32[]{:S(2)}) collective-permute-start(bf16[64,4096]{1,0:T(8,128)(2,1)S(1)} %get-tuple-element.320), channel_id=1, source_target_pairs={{20,16},{21,17},{22,18},{23,19}} | collective-permute-start | bytes 1572872 | tf_op jit(solution)/shard_map/ppermute | solution.py:44
  64.3 6.8 %collective-permute-done.17.refs_1_ = bf16[64,4096]{1,0:T(8,128)(2,1)S(1)} collective-permute-done((bf16[64,4096]{1,0:T(8,128)(2,1)S(1)}, bf16[64,4096]{1,0:T(8,128)(2,1)S(1)}, u32[]{:S(2)}, u32[]{:S(2)}) %collective-permute-start.17) | collective-permute-done | bytes 524320 | tf_op jit(solution)/shard_map/ppermute | solution.py:44
  71.0 2.0 %shard_map.105 = (bf16[1,4096]{1,0:T(2,128)(2,1)S(1)}, f32[128,128]{1,0:T(8,128)S(1)}, f32[128,256]{1,0:T(8,128)S(1)}, bf16[128,4096]{1,0:T(8,128)(2,1)S(1)}, bf...) custom-call(s32[4]{0:T(128)S(1)} %pad_add_fusion.flags.refs_0_, ...), custom_call_target="tpu_custom_call", output_to_operand_aliasing={{0}: (2, {}), {1}: (3, {}), {2}: (4, {}), {3}: (5, {}), {4}... | custom-call | tf_op jit(solution)/shard_map/pallas_call | solution.py:584
  73.0 2.0 %shard_map.106 = (bf16[1,4096]{1,0:T(2,128)(2,1)S(1)}, f32[128,128]{1,0:T(8,128)S(1)}, f32[128,256]{1,0:T(8,128)S(1)}, bf16[128,4096]{1,0:T(8,128)(2,1)S(1)}, bf...) custom-call(s32[4]{0:T(128)S(1)} %pad_add_fusion.flags.refs_0_, ...), custom_call_target="tpu_custom_call", output_to_operand_aliasing={{0}: (2, {}), {1}: (3, {}), {2}: (4, {}), {3}: (5, {}), {4}... | custom-call | tf_op jit(solution)/shard_map/pallas_call | solution.py:584
  75.7 1.6 %collective-permute-start.19 = (bf16[128,1280]{1,0:T(8,128)(2,1)S(1)}, bf16[128,1280]{1,0:T(8,128)(2,1)S(1)}, u32[]{:S(2)}, u32[]{:S(2)}) collective-permute-start(bf16[128,1280]{1,0:T(8,128)(2,1)S(1)} %get-tuple-element.375), channel_id=1, source_target_pairs={{0,1},{1,0},{2,3},{3,2},{4,5},{5,4},{6,7},{7,6},{8,9},{9,8},{10,11... | collective-permute-start | bytes 983048 | tf_op jit(solution)/shard_map/ppermute | solution.py:44
  77.8 1.4 %collective-permute-start.21 = (bf16[128,1280]{1,0:T(8,128)(2,1)S(1)}, bf16[128,1280]{1,0:T(8,128)(2,1)S(1)}, u32[]{:S(2)}, u32[]{:S(2)}) collective-permute-start(bf16[128,1280]{1,0:T(8,128)(2,1)S(1)} %get-tuple-element.377), channel_id=1, source_target_pairs={{0,3},{1,2},{2,1},{3,0},{4,7},{5,6},{6,5},{7,4},{8,11},{9,10},{10,... | collective-permute-start | bytes 983048 | tf_op jit(solution)/shard_map/ppermute | solution.py:44
  79.2 6.3 %collective-permute-done.19.refs_2_ = bf16[128,1280]{1,0:T(8,128)(2,1)S(1)} collective-permute-done((bf16[128,1280]{1,0:T(8,128)(2,1)S(1)}, bf16[128,1280]{1,0:T(8,128)(2,1)S(1)}, u32[]{:S(2)}, u32[]{:S(2)}) %collective-permute-start.19) | collective-permute-done | bytes 327712 | tf_op jit(solution)/shard_map/ppermute | solution.py:44
  86.2 8.1 %collective-permute-done.20.refs_3_ = bf16[128,1280]{1,0:T(8,128)(2,1)S(1)} collective-permute-done((bf16[128,1280]{1,0:T(8,128)(2,1)S(1)}, bf16[128,1280]{1,0:T(8,128)(2,1)S(1)}, u32[]{:S(2)}, u32[]{:S(2)}) %collective-permute-start.20) | collective-permute-done | bytes 327712 | tf_op jit(solution)/shard_map/ppermute | solution.py:44
  100.2 3.1 %collective-permute-start.29 = (bf16[128,1280]{1,0:T(8,128)(2,1)S(1)}, bf16[128,1280]{1,0:T(8,128)(2,1)S(1)}, u32[]{:S(2)}, u32[]{:S(2)}) collective-permute-start(bf16[128,1280]{1,0:T(8,128)(2,1)S(1)} %get-tuple-element.464), channel_id=1, source_target_pairs={{0,3},{1,2},{2,1},{3,0},{4,7},{5,6},{6,5},{7,4},{8,11},{9,10},{10,... | collective-permute-start | bytes 983048 | tf_op jit(solution)/shard_map/ppermute | solution.py:44
  104.3 6.1 %collective-permute-done.27.refs_5_ = bf16[128,1280]{1,0:T(8,128)(2,1)S(1)} collective-permute-done((bf16[128,1280]{1,0:T(8,128)(2,1)S(1)}, bf16[128,1280]{1,0:T(8,128)(2,1)S(1)}, u32[]{:S(2)}, u32[]{:S(2)}) %collective-permute-start.27) | collective-permute-done | bytes 327712 | tf_op jit(solution)/shard_map/ppermute | solution.py:44
  110.3 6.7 %collective-permute-done.28.refs_6_ = bf16[128,1280]{1,0:T(8,128)(2,1)S(1)} collective-permute-done((bf16[128,1280]{1,0:T(8,128)(2,1)S(1)}, bf16[128,1280]{1,0:T(8,128)(2,1)S(1)}, u32[]{:S(2)}, u32[]{:S(2)}) %collective-permute-start.28) | collective-permute-done | bytes 327712 | tf_op jit(solution)/shard_map/ppermute | solution.py:44
  117.0 1.7 %shard_map.114 = (bf16[1024,256]{1,0:T(8,128)(2,1)}, bf16[256,1024]{1,0:T(8,128)(2,1)}) custom-call(bf16[128,1280]{1,0:T(8,128)(2,1)S(1)} %get-tuple-element.457.refs_0_, bf16[128,1280]{1,0:T(8,128)(2,1)S(1)} %get-tuple-element.458.refs_1_, bf16[128,1280]{1,0:T(8,128)(2,1)S(1)} %get-tuple-element.459.refs_2_, ...), custom_call_target="tpu_custom_call" | custom-call | tf_op jit(solution)/shard_map/pallas_call | solution.py:689
  (60 shorter events, 21.9 us)
Async XLA Ops:
  0.6 37.0 %copy-start.1 = (f32[128,128]{1,0:T(8,128)S(1)}, f32[128,128]{1,0:T(8,128)}, u32[]{:S(2)}) copy-start(f32[128,128]{1,0:T(8,128)} %refs_1_.1) | copy-start | bytes 196612
  3.5 12.8 %collective-permute-start.2 = (bf16[416,512]{1,0:T(8,128)(2,1)S(1)}, bf16[416,512]{1,0:T(8,128)(2,1)S(1)}, u32[]{:S(2)}, u32[]{:S(2)}) collective-permute-start(bf16[416,512]{1,0:T(8,128)(2,1)S(1)} %get-tuple-element.239.refs_2_.refs_7_.refs_8_.refs_9_), channel_id=1, source_target_pairs={{0,2},{1,3},{2,0},{3,1},{4,6},{5,7},{6,4},{7,5},{8,10},{9,11},{10,... | collective-permute-start | bytes 1277960 | tf_op jit(solution)/shard_map/ppermute | solution.py:44
  5.1 12.7 %collective-permute-start.1 = (bf16[416,512]{1,0:T(8,128)(2,1)S(1)}, bf16[416,512]{1,0:T(8,128)(2,1)S(1)}, u32[]{:S(2)}, u32[]{:S(2)}) collective-permute-start(bf16[416,512]{1,0:T(8,128)(2,1)S(1)} %get-tuple-element.240.refs_3_.refs_8_.refs_9_.refs_10_), channel_id=1, source_target_pairs={{0,1},{1,0},{2,3},{3,2},{4,5},{5,4},{6,7},{7,6},{8,9},{9,8},{10,11... | collective-permute-start | bytes 1277960 | tf_op jit(solution)/shard_map/ppermute | solution.py:44
  6.5 20.4 %collective-permute-start = (bf16[416,512]{1,0:T(8,128)(2,1)S(1)}, bf16[416,512]{1,0:T(8,128)(2,1)S(1)}, u32[]{:S(2)}, u32[]{:S(2)}) collective-permute-start(bf16[416,512]{1,0:T(8,128)(2,1)S(1)} %get-tuple-element.239.refs_2_.refs_7_.refs_8_.refs_9_), channel_id=1, source_target_pairs={{0,1},{1,0},{2,3},{3,2},{4,5},{5,4},{6,7},{7,6},{8,9},{9,8},{10,11... | collective-permute-start | bytes 1277960 | tf_op jit(solution)/shard_map/ppermute | solution.py:44
  7.1 22.3 %collective-permute-start.3 = (bf16[416,512]{1,0:T(8,128)(2,1)S(1)}, bf16[416,512]{1,0:T(8,128)(2,1)S(1)}, u32[]{:S(2)}, u32[]{:S(2)}) collective-permute-start(bf16[416,512]{1,0:T(8,128)(2,1)S(1)} %get-tuple-element.240.refs_3_.refs_8_.refs_9_.refs_10_), channel_id=1, source_target_pairs={{0,2},{1,3},{2,0},{3,1},{4,6},{5,7},{6,4},{7,5},{8,10},{9,11},{10,... | collective-permute-start | bytes 1277960 | tf_op jit(solution)/shard_map/ppermute | solution.py:44
  16.2 19.9 %collective-permute-start.4 = (bf16[416,512]{1,0:T(8,128)(2,1)S(1)}, bf16[416,512]{1,0:T(8,128)(2,1)S(1)}, u32[]{:S(2)}, u32[]{:S(2)}) collective-permute-start(bf16[416,512]{1,0:T(8,128)(2,1)S(1)} %collective-permute-done.2.refs_6_.refs_11_.refs_12_.refs_13_), channel_id=1, source_target_pairs={{0,1},{1,0},{2,3},{3,2},{4,5},{5,4},{6,7},{7,6},{8,9},{9,8},{10,11... | collective-permute-start | bytes 1277960 | tf_op jit(solution)/shard_map/ppermute | solution.py:44
  17.8 18.4 %collective-permute-start.5 = (bf16[416,512]{1,0:T(8,128)(2,1)S(1)}, bf16[416,512]{1,0:T(8,128)(2,1)S(1)}, u32[]{:S(2)}, u32[]{:S(2)}) collective-permute-start(bf16[416,512]{1,0:T(8,128)(2,1)S(1)} %collective-permute-done.1.refs_5_.refs_10_.refs_11_.refs_12_), channel_id=1, source_target_pairs={{0,2},{1,3},{2,0},{3,1},{4,6},{5,7},{6,4},{7,5},{8,10},{9,11},{10,... | collective-permute-start | bytes 1277960 | tf_op jit(solution)/shard_map/ppermute | solution.py:44
  19.2 21.1 %collective-permute-start.9 = (bf16[96,1024]{1,0:T(8,128)(2,1)}, bf16[96,1024]{1,0:T(8,128)(2,1)}, u32[]{:S(2)}, u32[]{:S(2)}) collective-permute-start(bf16[96,1024]{1,0:T(8,128)(2,1)} %get-tuple-element.252.refs_16_.refs_17_), channel_id=1, source_target_pairs={{0,3},{1,2},{2,1},{3,0},{4,7},{5,6},{6,5},{7,4},{8,11},{9,10},{10,... | collective-permute-start | bytes 589832 | tf_op jit(solution)/shard_map/ppermute | solution.py:44
  26.9 15.0 %collective-permute-start.8 = (bf16[96,1024]{1,0:T(8,128)(2,1)}, bf16[96,1024]{1,0:T(8,128)(2,1)}, u32[]{:S(2)}, u32[]{:S(2)}) collective-permute-start(bf16[96,1024]{1,0:T(8,128)(2,1)} %get-tuple-element.252.refs_16_.refs_17_), channel_id=1, source_target_pairs={{0,2},{1,3},{2,0},{3,1},{4,6},{5,7},{6,4},{7,5},{8,10},{9,11},{10,... | collective-permute-start | bytes 589832 | tf_op jit(solution)/shard_map/ppermute | solution.py:44
  29.3 13.8 %collective-permute-start.7 = (bf16[96,1024]{1,0:T(8,128)(2,1)}, bf16[96,1024]{1,0:T(8,128)(2,1)}, u32[]{:S(2)}, u32[]{:S(2)}) collective-permute-start(bf16[96,1024]{1,0:T(8,128)(2,1)} %get-tuple-element.252.refs_16_.refs_17_), channel_id=1, source_target_pairs={{0,1},{1,0},{2,3},{3,2},{4,5},{5,4},{6,7},{7,6},{8,9},{9,8},{10,11... | collective-permute-start | bytes 589832 | tf_op jit(solution)/shard_map/ppermute | solution.py:44
  33.6 1.2 %copy-start = (bf16[1,128,4096]{2,1,0:T(8,128)(2,1)S(1)}, bf16[1,128,4096]{2,1,0:T(8,128)(2,1)}, u32[]{:S(2)}) copy-start(bf16[1,128,4096]{2,1,0:T(8,128)(2,1)} %param.7) | copy-start | bytes 3145732
  45.1 11.3 %collective-permute-start.12 = (bf16[3136,1024]{1,0:T(8,128)(2,1)S(1)}, bf16[3136,1024]{1,0:T(8,128)(2,1)S(1)}, u32[]{:S(2)}, u32[]{:S(2)}) collective-permute-start(bf16[3136,1024]{1,0:T(8,128)(2,1)S(1)} %get-tuple-element.284), channel_id=1, source_target_pairs={{8,12},{9,13},{10,14},{11,15},{16,20},{17,21},{18,22},{19,23}} | collective-permute-start | bytes 19267592 | tf_op jit(solution)/shard_map/ppermute | solution.py:44
  46.8 1.4 %collective-permute-start.6 = (bf16[64,4096]{1,0:T(8,128)(2,1)S(1)}, bf16[64,4096]{1,0:T(8,128)(2,1)S(1)}, u32[]{:S(2)}, u32[]{:S(2)}) collective-permute-start(bf16[64,4096]{1,0:T(8,128)(2,1)S(1)} %get-tuple-element.244), channel_id=1, source_target_pairs={{28,24},{29,25},{30,26},{31,27}} | collective-permute-start | bytes 1572872 | tf_op jit(solution)/shard_map/ppermute | solution.py:44
  47.5 2.7 %collective-permute-start.11 = (bf16[64,4096]{1,0:T(8,128)(2,1)S(1)}, bf16[64,4096]{1,0:T(8,128)(2,1)S(1)}, u32[]{:S(2)}, u32[]{:S(2)}) collective-permute-start(bf16[64,4096]{1,0:T(8,128)(2,1)S(1)} %get-tuple-element.261), channel_id=1, source_target_pairs={{28,24},{29,25},{30,26},{31,27}} | collective-permute-start | bytes 1572872 | tf_op jit(solution)/shard_map/ppermute | solution.py:44
  49.5 2.7 %collective-permute-start.10 = (bf16[64,4096]{1,0:T(8,128)(2,1)S(1)}, bf16[64,4096]{1,0:T(8,128)(2,1)S(1)}, u32[]{:S(2)}, u32[]{:S(2)}) collective-permute-start(bf16[64,4096]{1,0:T(8,128)(2,1)S(1)} %get-tuple-element.260), channel_id=1, source_target_pairs={{24,20},{25,21},{26,22},{27,23}} | collective-permute-start | bytes 1572872 | tf_op jit(solution)/shard_map/ppermute | solution.py:44
  51.4 6.2 %collective-permute-start.14 = (bf16[64,4096]{1,0:T(8,128)(2,1)S(1)}, bf16[64,4096]{1,0:T(8,128)(2,1)S(1)}, u32[]{:S(2)}, u32[]{:S(2)}) collective-permute-start(bf16[64,4096]{1,0:T(8,128)(2,1)S(1)} %get-tuple-element.286), channel_id=1, source_target_pairs={{24,20},{25,21},{26,22},{27,23}} | collective-permute-start | bytes 1572872 | tf_op jit(solution)/shard_map/ppermute | solution.py:44
  56.9 4.8 %collective-permute-start.13 = (bf16[64,4096]{1,0:T(8,128)(2,1)S(1)}, bf16[64,4096]{1,0:T(8,128)(2,1)S(1)}, u32[]{:S(2)}, u32[]{:S(2)}) collective-permute-start(bf16[64,4096]{1,0:T(8,128)(2,1)S(1)} %get-tuple-element.285), channel_id=1, source_target_pairs={{20,12},{21,13},{22,14},{23,15}} | collective-permute-start | bytes 1572872 | tf_op jit(solution)/shard_map/ppermute | solution.py:44
  58.4 4.6 %collective-permute-start.18 = (bf16[64,4096]{1,0:T(8,128)(2,1)S(1)}, bf16[64,4096]{1,0:T(8,128)(2,1)S(1)}, u32[]{:S(2)}, u32[]{:S(2)}) collective-permute-start(bf16[64,4096]{1,0:T(8,128)(2,1)S(1)} %get-tuple-element.322), channel_id=1, source_target_pairs={{20,12},{21,13},{22,14},{23,15}} | collective-permute-start | bytes 1572872 | tf_op jit(solution)/shard_map/ppermute | solution.py:44
  59.1 12.0 %collective-permute-start.17 = (bf16[64,4096]{1,0:T(8,128)(2,1)S(1)}, bf16[64,4096]{1,0:T(8,128)(2,1)S(1)}, u32[]{:S(2)}, u32[]{:S(2)}) collective-permute-start(bf16[64,4096]{1,0:T(8,128)(2,1)S(1)} %get-tuple-element.321), channel_id=1, source_target_pairs={{20,16},{21,17},{22,18},{23,19}} | collective-permute-start | bytes 1572872 | tf_op jit(solution)/shard_map/ppermute | solution.py:44
  60.4 12.6 %collective-permute-start.16 = (bf16[64,4096]{1,0:T(8,128)(2,1)S(1)}, bf16[64,4096]{1,0:T(8,128)(2,1)S(1)}, u32[]{:S(2)}, u32[]{:S(2)}) collective-permute-start(bf16[64,4096]{1,0:T(8,128)(2,1)S(1)} %get-tuple-element.320), channel_id=1, source_target_pairs={{20,16},{21,17},{22,18},{23,19}} | collective-permute-start | bytes 1572872 | tf_op jit(solution)/shard_map/ppermute | solution.py:44
  62.3 32.8 %collective-permute-start.15 = (bf16[64,4096]{1,0:T(8,128)(2,1)S(1)}, bf16[64,4096]{1,0:T(8,128)(2,1)S(1)}, u32[]{:S(2)}, u32[]{:S(2)}) collective-permute-start(bf16[64,4096]{1,0:T(8,128)(2,1)S(1)} %get-tuple-element.319), channel_id=1, source_target_pairs={{12,4},{13,5},{14,6},{15,7}} | collective-permute-start | bytes 1572872 | tf_op jit(solution)/shard_map/ppermute | solution.py:44
  63.6 32.8 %collective-permute-start.23 = (bf16[64,4096]{1,0:T(8,128)(2,1)S(1)}, bf16[64,4096]{1,0:T(8,128)(2,1)S(1)}, u32[]{:S(2)}, u32[]{:S(2)}) collective-permute-start(bf16[64,4096]{1,0:T(8,128)(2,1)S(1)} %get-tuple-element.392), channel_id=1, source_target_pairs={{12,4},{13,5},{14,6},{15,7}} | collective-permute-start | bytes 1572872 | tf_op jit(solution)/shard_map/ppermute | solution.py:44
  75.7 9.8 %collective-permute-start.19 = (bf16[128,1280]{1,0:T(8,128)(2,1)S(1)}, bf16[128,1280]{1,0:T(8,128)(2,1)S(1)}, u32[]{:S(2)}, u32[]{:S(2)}) collective-permute-start(bf16[128,1280]{1,0:T(8,128)(2,1)S(1)} %get-tuple-element.375), channel_id=1, source_target_pairs={{0,1},{1,0},{2,3},{3,2},{4,5},{5,4},{6,7},{7,6},{8,9},{9,8},{10,11... | collective-permute-start | bytes 983048 | tf_op jit(solution)/shard_map/ppermute | solution.py:44
  77.2 17.1 %collective-permute-start.20 = (bf16[128,1280]{1,0:T(8,128)(2,1)S(1)}, bf16[128,1280]{1,0:T(8,128)(2,1)S(1)}, u32[]{:S(2)}, u32[]{:S(2)}) collective-permute-start(bf16[128,1280]{1,0:T(8,128)(2,1)S(1)} %get-tuple-element.376), channel_id=1, source_target_pairs={{0,2},{1,3},{2,0},{3,1},{4,6},{5,7},{6,4},{7,5},{8,10},{9,11},{10,... | collective-permute-start | bytes 983048 | tf_op jit(solution)/shard_map/ppermute | solution.py:44
  77.8 17.2 %collective-permute-start.21 = (bf16[128,1280]{1,0:T(8,128)(2,1)S(1)}, bf16[128,1280]{1,0:T(8,128)(2,1)S(1)}, u32[]{:S(2)}, u32[]{:S(2)}) collective-permute-start(bf16[128,1280]{1,0:T(8,128)(2,1)S(1)} %get-tuple-element.377), channel_id=1, source_target_pairs={{0,3},{1,2},{2,1},{3,0},{4,7},{5,6},{6,5},{7,4},{8,11},{9,10},{10,... | collective-permute-start | bytes 983048 | tf_op jit(solution)/shard_map/ppermute | solution.py:44
  85.5 12.1 %collective-permute-start.26 = (bf16[64,4096]{1,0:T(8,128)(2,1)S(1)}, bf16[64,4096]{1,0:T(8,128)(2,1)S(1)}, u32[]{:S(2)}, u32[]{:S(2)}) collective-permute-start(bf16[64,4096]{1,0:T(8,128)(2,1)S(1)} %get-tuple-element.410), channel_id=1, source_target_pairs={{12,8},{13,9},{14,10},{15,11}} | collective-permute-start | bytes 1572872 | tf_op jit(solution)/shard_map/ppermute | solution.py:44
  94.3 4.1 %collective-permute-start.25 = (bf16[64,4096]{1,0:T(8,128)(2,1)S(1)}, bf16[64,4096]{1,0:T(8,128)(2,1)S(1)}, u32[]{:S(2)}, u32[]{:S(2)}) collective-permute-start(bf16[64,4096]{1,0:T(8,128)(2,1)S(1)} %get-tuple-element.409), channel_id=1, source_target_pairs={{12,8},{13,9},{14,10},{15,11}} | collective-permute-start | bytes 1572872 | tf_op jit(solution)/shard_map/ppermute | solution.py:44
  95.6 3.4 %collective-permute-start.22 = (bf16[64,4096]{1,0:T(8,128)(2,1)S(1)}, bf16[64,4096]{1,0:T(8,128)(2,1)S(1)}, u32[]{:S(2)}, u32[]{:S(2)}) collective-permute-start(bf16[64,4096]{1,0:T(8,128)(2,1)S(1)} %get-tuple-element.391), channel_id=1, source_target_pairs={{4,0},{5,1},{6,2},{7,3}} | collective-permute-start | bytes 1572872 | tf_op jit(solution)/shard_map/ppermute | solution.py:44
  96.9 2.1 %collective-permute-start.24 = (bf16[64,4096]{1,0:T(8,128)(2,1)S(1)}, bf16[64,4096]{1,0:T(8,128)(2,1)S(1)}, u32[]{:S(2)}, u32[]{:S(2)}) collective-permute-start(bf16[64,4096]{1,0:T(8,128)(2,1)S(1)} %get-tuple-element.408), channel_id=1, source_target_pairs={{4,0},{5,1},{6,2},{7,3}} | collective-permute-start | bytes 1572872 | tf_op jit(solution)/shard_map/ppermute | solution.py:44
  99.7 10.6 %collective-permute-start.27 = (bf16[128,1280]{1,0:T(8,128)(2,1)S(1)}, bf16[128,1280]{1,0:T(8,128)(2,1)S(1)}, u32[]{:S(2)}, u32[]{:S(2)}) collective-permute-start(bf16[128,1280]{1,0:T(8,128)(2,1)S(1)} %get-tuple-element.462), channel_id=1, source_target_pairs={{0,1},{1,0},{2,3},{3,2},{4,5},{5,4},{6,7},{7,6},{8,9},{9,8},{10,11... | collective-permute-start | bytes 983048 | tf_op jit(solution)/shard_map/ppermute | solution.py:44
  99.8 17.2 %collective-permute-start.28 = (bf16[128,1280]{1,0:T(8,128)(2,1)S(1)}, bf16[128,1280]{1,0:T(8,128)(2,1)S(1)}, u32[]{:S(2)}, u32[]{:S(2)}) collective-permute-start(bf16[128,1280]{1,0:T(8,128)(2,1)S(1)} %get-tuple-element.463), channel_id=1, source_target_pairs={{0,2},{1,3},{2,0},{3,1},{4,6},{5,7},{6,4},{7,5},{8,10},{9,11},{10,... | collective-permute-start | bytes 983048 | tf_op jit(solution)/shard_map/ppermute | solution.py:44
  100.2 16.8 %collective-permute-start.29 = (bf16[128,1280]{1,0:T(8,128)(2,1)S(1)}, bf16[128,1280]{1,0:T(8,128)(2,1)S(1)}, u32[]{:S(2)}, u32[]{:S(2)}) collective-permute-start(bf16[128,1280]{1,0:T(8,128)(2,1)S(1)} %get-tuple-element.464), channel_id=1, source_target_pairs={{0,3},{1,2},{2,1},{3,0},{4,7},{5,6},{6,5},{7,4},{8,11},{9,10},{10,... | collective-permute-start | bytes 983048 | tf_op jit(solution)/shard_map/ppermute | solution.py:44
  (1 other events, 0.7 us)

commit v6 on v5

--- a/solution.py
+++ b/solution.py
@@ -211,49 +211,37 @@
     latent[...] = total
 
 
-def shard_of(raw, size, latent_width, rows):
-    def down(k, half):
-        return raw[2 * k + half][:latent_width]
-
-    def up(k, lanes):
-        half = raw[0].shape[1]
-        parts = []
-        for which in range(2):
-            start, end = max(lanes.start - which * half, 0), min(lanes.stop - which * half, half)
-            if start < end:
-                parts.append(raw[2 * k + which][latent_width:, start:end])
-        first = parts[0] if len(parts) == 1 else jnp.concatenate(parts, axis=1)
-        if len(raw) == 2 * size:
-            return first
-        return jnp.concatenate([first, raw[2 * size + k][:, lanes]], axis=0)
-
-    return down, up
-
-
-def keep_kernel(size, count, *refs):
+def keep_kernel(size, count, more, *refs):
     flags = refs[0]
     gain, inverse, latent, x = refs[1:5]
     raw = refs[8 : 8 + count]
     kept = refs[15 + count : 15 + count + 2 * size]
-    (bundle,) = refs[15 + count + 2 * size :]
+    bundle, sems = refs[15 + count + 2 * size :]
     tokens, width = x.shape
     latent_width = latent.shape[1]
     shard = width // size
-    block, lanes = kept[-1].shape
-    down, up = shard_of(raw, size, latent_width, block)
+    rows = raw[0].shape[0] - latent_width
 
     @pl.when(flags[3] == 1)
     def _():
+        copies = [
+            pltpu.make_async_copy(raw[2 * size + k], kept[size + k].at[pl.ds(rows, more)], sems.at[k])
+            for k in range(size)
+            if more
+        ]
+        for copy in copies:
+            copy.start()
         for k in range(size):
             for half in range(2):
                 here = slice(half * (shard // 2), (half + 1) * (shard // 2))
-                kept[k][:, here] = down(k, half)
-            step = lanes // 2
-            for at in range(0, lanes, step):
-                kept[size + k][:, at : at + step] = up(k, slice(at, at + step))
-
-    @pl.when((flags[1] % 2 == 0) & (flags[3] == 1))
+                kept[k][:, here] = raw[2 * k + half][:latent_width]
+                kept[size + k][:rows, here] = raw[2 * k + half][latent_width:]
+        for copy in copies:
+            copy.wait()
+
+    @pl.when(flags[4] == 1)
     def _():
+        block = kept[-1].shape[0]
         for k in range(size):
             bundle[k * latent_width : (k + 1) * latent_width] = kept[k][...]
             row = size * latent_width + k * block
@@ -319,18 +307,14 @@
     return down, lambda k, lanes: kept[size + k][:, lanes]
 
 
-def stage_kernel(stage, bounds, size, held, count, *refs):
+def stage_kernel(stage, bounds, size, held, *refs):
     flags = refs[0]
     pieces = refs[1 : 1 + len(bounds)]
     at = 1 + len(bounds)
-    raw = refs[at + held : at + held + count]
-    state = refs[at + held + count : at + 2 * held + count]
-    outs = refs[at + 2 * held + count :]
+    state = refs[at + held : at + 2 * held]
+    outs = refs[at + 2 * held :]
     shard = state[3].shape[1] // size
-    if raw:
-        down, up = shard_of(raw, size, state[2].shape[1], None)
-    else:
-        down, up = kept_of(state[7:], size, shard)
+    down, up = kept_of(state[7:], size, shard)
     state = state[:7]
     gain, inverse, latent, x, latent_grads, arrivals, grads = state
     at_rows = slice(bounds[0][0], bounds[-1][1])
@@ -447,16 +431,29 @@
     pass
 
 
-def weight_kernel(size, *refs):
-    early, late = refs[:size], refs[size : 2 * size]
-    down_grads, up_grads, left, right = refs[2 * size :]
+def merge_kernel(size, split, *refs):
+    flags, latent, early = refs[0], refs[1], refs[2 : 2 + size]
+    above = (early[0],) + refs[2 + size : 1 + 2 * size]
+    left = refs[2 + 2 * size]
     tokens = early[0].shape[0]
+
+    def fill(sources):
+        for k in range(size):
+            left[:, k * tokens : (k + 1) * tokens] = sources[k][...].T
+
+    pl.when(flags[1] < split)(lambda: fill(early))
+    pl.when(flags[1] >= split)(lambda: fill(above))
+
+
+def weight_kernel(size, left, *refs):
+    late = refs[:size]
+    down_grads, up_grads, right = refs[size:]
+    tokens = late[0].shape[0]
     shard = down_grads.shape[0]
     for k in range(size):
-        left[k * tokens : (k + 1) * tokens] = early[k][...]
         right[k * tokens : (k + 1) * tokens] = late[k][...]
-    down_grads[...] = dot_tn(left[:, :shard], right[:, shard:]).astype(jnp.bfloat16)
-    up_grads[...] = dot_tn(left[:, shard:], right[:, :shard]).astype(jnp.bfloat16)
+    down_grads[...] = dot_nn(left[:shard], right[:, shard:]).astype(jnp.bfloat16)
+    up_grads[...] = dot_nn(left[shard:], right[:, :shard]).astype(jnp.bfloat16)
 
 
 def per_device(
@@ -482,7 +479,8 @@
             dp_index.astype(jnp.int32),
             section.astype(jnp.int32),
             (section == top).astype(jnp.int32),
-            (section < top - 1).astype(jnp.int32),
+            (section < top).astype(jnp.int32),
+            ((section < top - 1) & (section % 2 == 0)).astype(jnp.int32),
         ]
     )
     everyone, rest = list(range(sections)), list(range(top))
@@ -574,7 +572,7 @@
     shards = (*halves, *up_rest)
     state = (gain, inverse, latent, x, latent_grads, arrivals, grads)
 
-    def run_stage(stage, bounds, received, state, shards, sends=True):
+    def run_stage(stage, bounds, received, state, sends=True):
         rows = bounds[-1][1] - bounds[0][0]
         if not stage:
             outs = (message,) * size
@@ -582,14 +580,14 @@
             outs = (jax.ShapeDtypeStruct((rows, width), bf16),) * sends
         first = 1 + len(received)
         results = pl.pallas_call(
-            functools.partial(stage_kernel, stage, bounds, size, len(state), len(shards)),
+            functools.partial(stage_kernel, stage, bounds, size, len(state)),
             out_shape=tuple(held_like(part) for part in state) + outs,
-            in_specs=[SMEM] + [VMEM] * (len(received) + len(state) + len(shards)),
+            in_specs=[SMEM] + [VMEM] * (len(received) + len(state)),
             out_specs=(VMEM,) * (len(state) + len(outs)),
             input_output_aliases={first + i: i for i in range(len(state))},
             cost_estimate=NOTHING,
             compiler_params=PARAMS,
-        )(flags, *received, *[pin(part) for part in state + shards])
+        )(flags, *received, *[pin(part) for part in state])
         return tuple(results[: len(state)]), results[len(state) :]
 
     def run_pair(stage, bound, received, state):
@@ -606,13 +604,23 @@
         )(flags, received, *[pin(part) for part in state])
         return tuple(results[: len(state)]), results[len(state) :]
 
-    def send_messages(messages):
-        return [messages[0]] + [
-            move(messages[k], peers(range(sections), size, k)) for k in range(1, size)
-        ]
+    def send_messages(messages, among):
+        return [messages[0]] + [move(messages[k], peers(among, size, k)) for k in range(1, size)]
+
+    def hold(state, blocks):
+        latent, *blocks = pl.pallas_call(
+            touch_kernel,
+            out_shape=(held_like(state[2]),) + tuple(held_like(part) for part in blocks),
+            in_specs=[VMEM] * (1 + len(blocks)),
+            out_specs=(VMEM,) * (1 + len(blocks)),
+            input_output_aliases={i: i for i in range(1 + len(blocks))},
+            cost_estimate=NOTHING,
+            compiler_params=PARAMS,
+        )(pin(state[2]), *[pin(part) for part in blocks])
+        return state[:2] + (latent,) + state[3:], blocks
 
     state_kept = pl.pallas_call(
-        functools.partial(keep_kernel, size, len(shards)),
+        functools.partial(keep_kernel, size, len(shards), more),
         out_shape=tuple(held_like(part) for part in state)
         + (pltpu.VMEM((latent_width, shard), bf16),) * size
         + (pltpu.VMEM((up_block, up_lanes), bf16),) * size
@@ -621,12 +629,15 @@
                 (size * (latent_width + up_block + tokens + GAIN_ROWS) + 4 * tokens, shard), bf16
             ),
         ),
-        in_specs=[SMEM] + [VMEM] * (len(state) + len(shards)),
+        in_specs=[SMEM]
+        + [VMEM] * (len(state) + 2 * size)
+        + [ANY] * (len(shards) - 2 * size),
         out_specs=(VMEM,) * (len(state) + 2 * size + 1),
+        scratch_shapes=[pltpu.SemaphoreType.DMA((size,))],
         input_output_aliases={1 + i: i for i in range(len(state))},
         cost_estimate=NOTHING,
         compiler_params=PARAMS,
-    )(flags, *[pin(part) for part in state + shards])
+    )(flags, *[pin(part) for part in (*state, *halves)], *up_rest)
     state, kept, bundle = tuple(state_kept[:7]), tuple(state_kept[7:-1]), state_kept[-1:]
     pairs = list(range(3, top - 1, 2))
     bundle = tuple(
@@ -634,26 +645,15 @@
         for part in bundle
     )
 
+    state = state + kept
     sent = []
     for bound, block in zip(bounds, received):
-        state, outs = run_stage(top - 1, [bound], [block], state, shards)
+        state, outs = run_stage(top - 1, [bound], [block], state)
         sent.append(hop(outs[0], top - 1))
     received = sent
 
-    state = state + kept + bundle
-
-    waiting = []
-    for stage in reversed(pairs):
-        sent, side = [], []
-        for bound, block in zip(bounds, received):
-            state, outs = run_pair(stage, bound, block, state)
-            sent.append(hop(outs[1], stage, 2))
-            side.append(hop(outs[0], stage))
-        received = sent
-        for asides, bound, block in waiting:
-            base, _ = run_stage(asides, [bound], [block], state[:-1], (), False)
-            state = base + state[-1:]
-        waiting = [(stage - 1, bound, block) for bound, block in zip(bounds, side)]
+    state = state + bundle
+
     latent, *messages = pl.pallas_call(
         functools.partial(message_kernel, size),
         out_shape=(held_like(state[2]),) + (message,) * size,
@@ -663,41 +663,61 @@
         cost_estimate=NOTHING,
         compiler_params=PARAMS,
     )(flags, pin(normed), pin(state[2]))
-    early = send_messages(messages)
-    latent, *early = pl.pallas_call(
-        touch_kernel,
-        out_shape=(held_like(latent),) + tuple(held_like(part) for part in early),
-        in_specs=[VMEM] * (1 + size),
-        out_specs=(VMEM,) * (1 + size),
-        input_output_aliases={i: i for i in range(1 + size)},
-        cost_estimate=NOTHING,
-        compiler_params=PARAMS,
-    )(pin(latent), *[pin(part) for part in early])
     state = state[:2] + (latent,) + state[3:]
+    split = pairs[-1] - 1
+    early = send_messages(messages, range(split))
+    above = send_messages(messages, range(split, sections))
+
+    waiting = []
+    for stage in reversed(pairs):
+        sent, side = [], []
+        for bound, block in zip(bounds, received):
+            state, outs = run_pair(stage, bound, block, state)
+            sent.append(hop(outs[1], stage, 2))
+            side.append(hop(outs[0], stage))
+            if stage == pairs[-1] and len(sent) == 1:
+                state, early = hold(state, early)
+        received = sent
+        for asides, bound, block in waiting:
+            base, _ = run_stage(asides, [bound], [block], state[:-1], False)
+            state = base + state[-1:]
+        waiting = [(stage - 1, bound, block) for bound, block in zip(bounds, side)]
+        if stage == pairs[0]:
+            latent, left = pl.pallas_call(
+                functools.partial(merge_kernel, size, split),
+                out_shape=(
+                    held_like(state[2]),
+                    pltpu.VMEM((shard + latent_width, size * tokens), bf16),
+                ),
+                in_specs=[SMEM] + [VMEM] * (2 * size),
+                out_specs=(VMEM,) * 2,
+                input_output_aliases={1: 0},
+                cost_estimate=NOTHING,
+                compiler_params=PARAMS,
+            )(flags, pin(state[2]), *early, *above[1:])
+            state = state[:2] + (latent,) + state[3:]
     state = state[:-1]
 
     sent = []
     for bound, block in zip(bounds, received):
-        state, outs = run_stage(1, [bound], [block], state, ())
+        state, outs = run_stage(1, [bound], [block], state)
         sent.append(hop(outs[0], 1))
     received = sent
     for asides, bound, block in waiting:
-        state, _ = run_stage(asides, [bound], [block], state, (), False)
-    shards = ()
-    state, outs = run_stage(0, bounds, received, state, shards)
-    late = send_messages(outs)
+        state, _ = run_stage(asides, [bound], [block], state, False)
+    state, outs = run_stage(0, bounds, received, state)
+    late = send_messages(outs, everyone)
     down_grads, up_grads = pl.pallas_call(
         functools.partial(weight_kernel, size),
         out_shape=(
             jax.ShapeDtypeStruct((shard, latent_width), bf16),
             jax.ShapeDtypeStruct((latent_width, shard), bf16),
         ),
-        in_specs=[VMEM] * (2 * size),
+        in_specs=[VMEM] * (1 + size),
         out_specs=(VMEM,) * 2,
-        scratch_shapes=[pltpu.VMEM((size * tokens, shard + latent_width), bf16)] * 2,
-        cost_estimate=NOTHING,
+        scratch_shapes=[pltpu.VMEM((size * tokens, shard + latent_width), bf16)],
         compiler_params=PARAMS,
-    )(*early, *late)
+    )(pin(left), *late)
     return (state[6][None], down_grads[None], up_grads[None])
 
 

time: 119 us -> 117 us (0.983)
  the two profiles are of different devices: /device:TPU:16 before, /device:TPU:0 now
where the time goes in v6:
time: 117 us; the launch traced here: 116 us
  waiting for transfers between devices  46.3 us (40%)
  starting transfers between devices  44.6 us (38%)
  Pallas kernels  20.2 us (17%)
  local copies, waits for them, and re-layouts  3.16 us (3%)
  between operations  1.18 us (1%)
    ppermute x33, waiting for transfers between devices, move(): return lax.ppermute(block, ('section', 'dp'), pairs)  46.3 us
    ppermute x33, starting transfers between devices, move(): return lax.ppermute(block, ('section', 'dp'), pairs)  44.6 us
    pallas_call x9, Pallas kernels, run_stage(): pl.pallas_call(functools.partial(stage_kernel, stage, bounds, size, len(s...  6.95 us
    unnamed x7, local copies, waits for them, and re-layouts  2.92 us
    pallas_call x1, Pallas kernels, per_device(): pl.pallas_call(prepare_kernel, out_shape=(jax.ShapeDtypeStruct((latent_wi...  2.73 us
    pallas_call x4, Pallas kernels, run_pair(): pl.pallas_call(functools.partial(pair_kernel, stage, bound, size, len(sta...  2.49 us
  transfers between devices with their start and end apart: 33, of which 11 were waited for; matrix products, arithmetic and copies ran while one was open for 2% of the time, Pallas kernels for 10%

profile of v6, /device:TPU:0, one launch (start us, length us, event | category | flops | bytes accessed | tf_op | source)
XLA Modules:
  0.0 116.2 jit_solution(8542043452735402615)
XLA Ops:
  0.7 2.7 %shard_map.95 = (bf16[416,512]{1,0:T(8,128)(2,1)S(1)}, bf16[416,512]{1,0:T(8,128)(2,1)S(1)}, bf16[96,1024]{1,0:T(8,128)(2,1)}) custom-call(s32[5]{0:T(128)S(1)} %stack.35.flags.refs_0_, bf16[1,1024,256]{2,1,0:T(8,128)(2,1)} %down.1, bf16[1,256,1024]{2,1,0:T(8,128)(2,1)} %up.1, bf16[1024,128]{1,0:T(8,128)(2,1)} %readout.1), custom_call_target="tpu_custom_call" | custom-call | tf_op jit(solution)/shard_map/pallas_call | solution.py:491
  3.5 3.0 %collective-permute-start.2 = (bf16[416,512]{1,0:T(8,128)(2,1)S(1)}, bf16[416,512]{1,0:T(8,128)(2,1)S(1)}, u32[]{:S(2)}, u32[]{:S(2)}) collective-permute-start(bf16[416,512]{1,0:T(8,128)(2,1)S(1)} %get-tuple-element.257.refs_2_.refs_7_.refs_8_), channel_id=1, source_target_pairs={{0,2},{1,3},{2,0},{3,1},{4,6},{5,7},{6,4},{7,5},{8,10},{9,11},{10,... | collective-permute-start | bytes 1277960 | tf_op jit(solution)/shard_map/ppermute | solution.py:44
  6.5 1.5 %collective-permute-start.1 = (bf16[416,512]{1,0:T(8,128)(2,1)S(1)}, bf16[416,512]{1,0:T(8,128)(2,1)S(1)}, u32[]{:S(2)}, u32[]{:S(2)}) collective-permute-start(bf16[416,512]{1,0:T(8,128)(2,1)S(1)} %get-tuple-element.258.refs_3_.refs_8_.refs_9_), channel_id=1, source_target_pairs={{0,1},{1,0},{2,3},{3,2},{4,5},{5,4},{6,7},{7,6},{8,9},{9,8},{10,11... | collective-permute-start | bytes 1277960 | tf_op jit(solution)/shard_map/ppermute | solution.py:44
  8.6 8.5 %collective-permute-done.2.refs_6_.refs_11_.refs_12_ = bf16[416,512]{1,0:T(8,128)(2,1)S(1)} collective-permute-done((bf16[416,512]{1,0:T(8,128)(2,1)S(1)}, bf16[416,512]{1,0:T(8,128)(2,1)S(1)}, u32[]{:S(2)}, u32[]{:S(2)}) %collective-permute-start.2) | collective-permute-done | bytes 426016 | tf_op jit(solution)/shard_map/ppermute | solution.py:44
  17.2 2.0 %collective-permute-start.4 = (bf16[416,512]{1,0:T(8,128)(2,1)S(1)}, bf16[416,512]{1,0:T(8,128)(2,1)S(1)}, u32[]{:S(2)}, u32[]{:S(2)}) collective-permute-start(bf16[416,512]{1,0:T(8,128)(2,1)S(1)} %collective-permute-done.2.refs_6_.refs_11_.refs_12_), channel_id=1, source_target_pairs={{0,1},{1,0},{2,3},{3,2},{4,5},{5,4},{6,7},{7,6},{8,9},{9,8},{10,11... | collective-permute-start | bytes 1277960 | tf_op jit(solution)/shard_map/ppermute | solution.py:44
  19.3 1.5 %collective-permute-start.5 = (bf16[416,512]{1,0:T(8,128)(2,1)S(1)}, bf16[416,512]{1,0:T(8,128)(2,1)S(1)}, u32[]{:S(2)}, u32[]{:S(2)}) collective-permute-start(bf16[416,512]{1,0:T(8,128)(2,1)S(1)} %collective-permute-done.1.refs_5_.refs_10_.refs_11_), channel_id=1, source_target_pairs={{0,2},{1,3},{2,0},{3,1},{4,6},{5,7},{6,4},{7,5},{8,10},{9,11},{10,... | collective-permute-start | bytes 1277960 | tf_op jit(solution)/shard_map/ppermute | solution.py:44
  20.7 3.4 %collective-permute-start.9 = (bf16[96,1024]{1,0:T(8,128)(2,1)}, bf16[96,1024]{1,0:T(8,128)(2,1)}, u32[]{:S(2)}, u32[]{:S(2)}) collective-permute-start(bf16[96,1024]{1,0:T(8,128)(2,1)} %get-tuple-element.270.refs_16_), channel_id=1, source_target_pairs={{0,3},{1,2},{2,1},{3,0},{4,7},{5,6},{6,5},{7,4},{8,11},{9,10},{10,... | collective-permute-start | bytes 589832 | tf_op jit(solution)/shard_map/ppermute | solution.py:44
  24.1 4.3 %collective-permute-done.refs_4_.refs_9_.refs_10_ = bf16[416,512]{1,0:T(8,128)(2,1)S(1)} collective-permute-done((bf16[416,512]{1,0:T(8,128)(2,1)S(1)}, bf16[416,512]{1,0:T(8,128)(2,1)S(1)}, u32[]{:S(2)}, u32[]{:S(2)}) %collective-permute-start) | collective-permute-done | bytes 426016 | tf_op jit(solution)/shard_map/ppermute | solution.py:44
  28.4 1.9 %collective-permute-start.8 = (bf16[96,1024]{1,0:T(8,128)(2,1)}, bf16[96,1024]{1,0:T(8,128)(2,1)}, u32[]{:S(2)}, u32[]{:S(2)}) collective-permute-start(bf16[96,1024]{1,0:T(8,128)(2,1)} %get-tuple-element.270.refs_16_), channel_id=1, source_target_pairs={{0,2},{1,3},{2,0},{3,1},{4,6},{5,7},{6,4},{7,5},{8,10},{9,11},{10,... | collective-permute-start | bytes 589832 | tf_op jit(solution)/shard_map/ppermute | solution.py:44
  30.3 3.9 %collective-permute-start.7 = (bf16[96,1024]{1,0:T(8,128)(2,1)}, bf16[96,1024]{1,0:T(8,128)(2,1)}, u32[]{:S(2)}, u32[]{:S(2)}) collective-permute-start(bf16[96,1024]{1,0:T(8,128)(2,1)} %get-tuple-element.270.refs_16_), channel_id=1, source_target_pairs={{0,1},{1,0},{2,3},{3,2},{4,5},{5,4},{6,7},{7,6},{8,9},{9,8},{10,11... | collective-permute-start | bytes 589832 | tf_op jit(solution)/shard_map/ppermute | solution.py:44
  35.0 1.2 %copy-done = bf16[1,128,4096]{2,1,0:T(8,128)(2,1)S(1)} copy-done((bf16[1,128,4096]{2,1,0:T(8,128)(2,1)S(1)}, bf16[1,128,4096]{2,1,0:T(8,128)(2,1)}, u32[]{:S(2)}) %copy-start) | copy-done | bytes 1048600
  37.7 1.4 %shard_map.96 = (bf16[128,4096]{1,0:T(8,128)(2,1)S(1)}, f32[128,256]{1,0:T(8,128)S(1)}) custom-call(s32[5]{0:T(128)S(1)} %stack.35.flags.refs_0_, bf16[128,4096]{1,0:T(8,128)(2,1)S(1)} %get-tuple-element.256.refs_1_, bf16[416,512]{1,0:T(8,128)(2,1)S(1)} %get-tuple-element.257.refs_2_.refs_7_.refs_8_, ...), custom_call_target="tpu_custom_call", output_to_operand_aliasing={{0}: (1, {})} | custom-call | tf_op jit(solution)/shard_map/pallas_call | solution.py:532
  39.7 1.7 %collective-permute-done.9.refs_19_ = bf16[96,1024]{1,0:T(8,128)(2,1)} collective-permute-done((bf16[96,1024]{1,0:T(8,128)(2,1)}, bf16[96,1024]{1,0:T(8,128)(2,1)}, u32[]{:S(2)}, u32[]{:S(2)}) %collective-permute-start.9) | collective-permute-done | bytes 196640 | tf_op jit(solution)/shard_map/ppermute | solution.py:44
  41.4 1.8 %collective-permute-done.8.refs_18_ = bf16[96,1024]{1,0:T(8,128)(2,1)} collective-permute-done((bf16[96,1024]{1,0:T(8,128)(2,1)}, bf16[96,1024]{1,0:T(8,128)(2,1)}, u32[]{:S(2)}, u32[]{:S(2)}) %collective-permute-start.8) | collective-permute-done | bytes 196640 | tf_op jit(solution)/shard_map/ppermute | solution.py:44
  43.1 1.5 %collective-permute-done.7.refs_17_ = bf16[96,1024]{1,0:T(8,128)(2,1)} collective-permute-done((bf16[96,1024]{1,0:T(8,128)(2,1)}, bf16[96,1024]{1,0:T(8,128)(2,1)}, u32[]{:S(2)}, u32[]{:S(2)}) %collective-permute-start.7) | collective-permute-done | bytes 196640 | tf_op jit(solution)/shard_map/ppermute | solution.py:44
  44.6 2.2 %shard_map.98 = (bf16[1,4096]{1,0:T(2,128)(2,1)S(1)}, f32[128,128]{1,0:T(8,128)S(1)}, f32[128,256]{1,0:T(8,128)S(1)}, bf16[128,4096]{1,0:T(8,128)(2,1)S(1)}, bf1...) custom-call(s32[5]{0:T(128)S(1)} %stack.35.flags.refs_0_, ...), custom_call_target="tpu_custom_call", output_to_operand_aliasing={{0}: (1, {}), {1}: (2, {}), {2}: (3, {}), {3}: (4, {}), {4}... | custom-call | tf_op jit(solution)/shard_map/pallas_call | solution.py:622
  46.8 1.1 collective-permute-start.12
  52.5 3.4 %collective-permute-start.15 = (bf16[128,1280]{1,0:T(8,128)(2,1)S(1)}, bf16[128,1280]{1,0:T(8,128)(2,1)S(1)}, u32[]{:S(2)}, u32[]{:S(2)}) collective-permute-start(bf16[128,1280]{1,0:T(8,128)(2,1)S(1)} %get-tuple-element.327), channel_id=1, source_target_pairs={{0,1},{1,0},{2,3},{3,2},{4,5},{5,4},{6,7},{7,6},{8,9},{9,8},{10,11... | collective-permute-start | bytes 983048 | tf_op jit(solution)/shard_map/ppermute | solution.py:44
  55.9 2.4 %collective-permute-start.16 = (bf16[128,1280]{1,0:T(8,128)(2,1)S(1)}, bf16[128,1280]{1,0:T(8,128)(2,1)S(1)}, u32[]{:S(2)}, u32[]{:S(2)}) collective-permute-start(bf16[128,1280]{1,0:T(8,128)(2,1)S(1)} %get-tuple-element.328), channel_id=1, source_target_pairs={{0,2},{1,3},{2,0},{3,1},{4,6},{5,7},{6,4},{7,5},{8,10},{9,11},{10,... | collective-permute-start | bytes 983048 | tf_op jit(solution)/shard_map/ppermute | solution.py:44
  58.4 3.4 %collective-permute-start.17 = (bf16[128,1280]{1,0:T(8,128)(2,1)S(1)}, bf16[128,1280]{1,0:T(8,128)(2,1)S(1)}, u32[]{:S(2)}, u32[]{:S(2)}) collective-permute-start(bf16[128,1280]{1,0:T(8,128)(2,1)S(1)} %get-tuple-element.329), channel_id=1, source_target_pairs={{0,3},{1,2},{2,1},{3,0},{4,7},{5,6},{6,5},{7,4},{8,11},{9,10},{10,... | collective-permute-start | bytes 983048 | tf_op jit(solution)/shard_map/ppermute | solution.py:44
  63.1 9.4 %collective-permute-done.16.refs_3_ = bf16[128,1280]{1,0:T(8,128)(2,1)S(1)} collective-permute-done((bf16[128,1280]{1,0:T(8,128)(2,1)S(1)}, bf16[128,1280]{1,0:T(8,128)(2,1)S(1)}, u32[]{:S(2)}, u32[]{:S(2)}) %collective-permute-start.16) | collective-permute-done | bytes 327712 | tf_op jit(solution)/shard_map/ppermute | solution.py:44
  84.2 1.3 %collective-permute-start.25 = (bf16[64,4096]{1,0:T(8,128)(2,1)S(1)}, bf16[64,4096]{1,0:T(8,128)(2,1)S(1)}, u32[]{:S(2)}, u32[]{:S(2)}) collective-permute-start(bf16[64,4096]{1,0:T(8,128)(2,1)S(1)} %get-tuple-element.430), channel_id=1, source_target_pairs={{4,0},{5,1},{6,2},{7,3}} | collective-permute-start | bytes 1572872 | tf_op jit(solution)/shard_map/ppermute | solution.py:44
  86.3 1.3 %collective-permute-start.27 = (bf16[64,4096]{1,0:T(8,128)(2,1)S(1)}, bf16[64,4096]{1,0:T(8,128)(2,1)S(1)}, u32[]{:S(2)}, u32[]{:S(2)}) collective-permute-start(bf16[64,4096]{1,0:T(8,128)(2,1)S(1)} %get-tuple-element.447), channel_id=1, source_target_pairs={{4,0},{5,1},{6,2},{7,3}} | collective-permute-start | bytes 1572872 | tf_op jit(solution)/shard_map/ppermute | solution.py:44
  88.8 1.0 collective-permute-done.25.refs_1_
  89.8 5.8 %collective-permute-done.27.refs_2_ = bf16[64,4096]{1,0:T(8,128)(2,1)S(1)} collective-permute-done((bf16[64,4096]{1,0:T(8,128)(2,1)S(1)}, bf16[64,4096]{1,0:T(8,128)(2,1)S(1)}, u32[]{:S(2)}, u32[]{:S(2)}) %collective-permute-start.27) | collective-permute-done | bytes 524320 | tf_op jit(solution)/shard_map/ppermute | solution.py:44
  95.6 2.1 %shard_map.114 = (bf16[1,4096]{1,0:T(2,128)(2,1)S(1)}, f32[128,128]{1,0:T(8,128)S(1)}, f32[128,256]{1,0:T(8,128)S(1)}, bf16[128,4096]{1,0:T(8,128)(2,1)S(1)}, bf...) custom-call(s32[5]{0:T(128)S(1)} %stack.35.flags.refs_0_, ...), custom_call_target="tpu_custom_call", output_to_operand_aliasing={{0}: (3, {}), {1}: (4, {}), {2}: (5, {}), {3}: (6, {}), {4}... | custom-call | tf_op jit(solution)/shard_map/pallas_call | solution.py:582
  97.8 1.8 %collective-permute-start.30 = (bf16[128,1280]{1,0:T(8,128)(2,1)S(1)}, bf16[128,1280]{1,0:T(8,128)(2,1)S(1)}, u32[]{:S(2)}, u32[]{:S(2)}) collective-permute-start(bf16[128,1280]{1,0:T(8,128)(2,1)S(1)} %get-tuple-element.498), channel_id=1, source_target_pairs={{0,1},{1,0},{2,3},{3,2},{4,5},{5,4},{6,7},{7,6},{8,9},{9,8},{10,11... | collective-permute-start | bytes 983048 | tf_op jit(solution)/shard_map/ppermute | solution.py:44
  99.5 1.4 %collective-permute-start.31 = (bf16[128,1280]{1,0:T(8,128)(2,1)S(1)}, bf16[128,1280]{1,0:T(8,128)(2,1)S(1)}, u32[]{:S(2)}, u32[]{:S(2)}) collective-permute-start(bf16[128,1280]{1,0:T(8,128)(2,1)S(1)} %get-tuple-element.499), channel_id=1, source_target_pairs={{0,2},{1,3},{2,0},{3,1},{4,6},{5,7},{6,4},{7,5},{8,10},{9,11},{10,... | collective-permute-start | bytes 983048 | tf_op jit(solution)/shard_map/ppermute | solution.py:44
  101.3 1.0 copy.446
  102.3 6.2 %collective-permute-done.30.refs_1_ = bf16[128,1280]{1,0:T(8,128)(2,1)S(1)} collective-permute-done((bf16[128,1280]{1,0:T(8,128)(2,1)S(1)}, bf16[128,1280]{1,0:T(8,128)(2,1)S(1)}, u32[]{:S(2)}, u32[]{:S(2)}) %collective-permute-start.30) | collective-permute-done | bytes 327712 | tf_op jit(solution)/shard_map/ppermute | solution.py:44
  108.5 6.0 %collective-permute-done.31.refs_2_ = bf16[128,1280]{1,0:T(8,128)(2,1)S(1)} collective-permute-done((bf16[128,1280]{1,0:T(8,128)(2,1)S(1)}, bf16[128,1280]{1,0:T(8,128)(2,1)S(1)}, u32[]{:S(2)}, u32[]{:S(2)}) %collective-permute-start.31) | collective-permute-done | bytes 327712 | tf_op jit(solution)/shard_map/ppermute | solution.py:44
  114.5 1.7 %shard_map.115 = (bf16[1024,256]{1,0:T(8,128)(2,1)}, bf16[256,1024]{1,0:T(8,128)(2,1)}) custom-call(bf16[1280,512]{1,0:T(8,128)(2,1)S(1)} %get-tuple-element.496.left, bf16[128,1280]{1,0:T(8,128)(2,1)S(1)} %get-tuple-element.497.refs_0_, bf16[128,1280]{1,0:T(8,128)(2,1)S(1)} %collective-permute-done.30.refs_1_, ...), custom_call_target="tpu_custom_call" | custom-call | tf_op jit(solution)/shard_map/pallas_call | solution.py:710
  (67 shorter events, 23.3 us)
Async XLA Ops:
  3.5 13.7 %collective-permute-start.2 = (bf16[416,512]{1,0:T(8,128)(2,1)S(1)}, bf16[416,512]{1,0:T(8,128)(2,1)S(1)}, u32[]{:S(2)}, u32[]{:S(2)}) collective-permute-start(bf16[416,512]{1,0:T(8,128)(2,1)S(1)} %get-tuple-element.257.refs_2_.refs_7_.refs_8_), channel_id=1, source_target_pairs={{0,2},{1,3},{2,0},{3,1},{4,6},{5,7},{6,4},{7,5},{8,10},{9,11},{10,... | collective-permute-start | bytes 1277960 | tf_op jit(solution)/shard_map/ppermute | solution.py:44
  6.5 12.7 %collective-permute-start.1 = (bf16[416,512]{1,0:T(8,128)(2,1)S(1)}, bf16[416,512]{1,0:T(8,128)(2,1)S(1)}, u32[]{:S(2)}, u32[]{:S(2)}) collective-permute-start(bf16[416,512]{1,0:T(8,128)(2,1)S(1)} %get-tuple-element.258.refs_3_.refs_8_.refs_9_), channel_id=1, source_target_pairs={{0,1},{1,0},{2,3},{3,2},{4,5},{5,4},{6,7},{7,6},{8,9},{9,8},{10,11... | collective-permute-start | bytes 1277960 | tf_op jit(solution)/shard_map/ppermute | solution.py:44
  8.0 20.4 %collective-permute-start = (bf16[416,512]{1,0:T(8,128)(2,1)S(1)}, bf16[416,512]{1,0:T(8,128)(2,1)S(1)}, u32[]{:S(2)}, u32[]{:S(2)}) collective-permute-start(bf16[416,512]{1,0:T(8,128)(2,1)S(1)} %get-tuple-element.257.refs_2_.refs_7_.refs_8_), channel_id=1, source_target_pairs={{0,1},{1,0},{2,3},{3,2},{4,5},{5,4},{6,7},{7,6},{8,9},{9,8},{10,11... | collective-permute-start | bytes 1277960 | tf_op jit(solution)/shard_map/ppermute | solution.py:44
  8.5 21.8 %collective-permute-start.3 = (bf16[416,512]{1,0:T(8,128)(2,1)S(1)}, bf16[416,512]{1,0:T(8,128)(2,1)S(1)}, u32[]{:S(2)}, u32[]{:S(2)}) collective-permute-start(bf16[416,512]{1,0:T(8,128)(2,1)S(1)} %get-tuple-element.258.refs_3_.refs_8_.refs_9_), channel_id=1, source_target_pairs={{0,2},{1,3},{2,0},{3,1},{4,6},{5,7},{6,4},{7,5},{8,10},{9,11},{10,... | collective-permute-start | bytes 1277960 | tf_op jit(solution)/shard_map/ppermute | solution.py:44
  17.2 20.5 %collective-permute-start.4 = (bf16[416,512]{1,0:T(8,128)(2,1)S(1)}, bf16[416,512]{1,0:T(8,128)(2,1)S(1)}, u32[]{:S(2)}, u32[]{:S(2)}) collective-permute-start(bf16[416,512]{1,0:T(8,128)(2,1)S(1)} %collective-permute-done.2.refs_6_.refs_11_.refs_12_), channel_id=1, source_target_pairs={{0,1},{1,0},{2,3},{3,2},{4,5},{5,4},{6,7},{7,6},{8,9},{9,8},{10,11... | collective-permute-start | bytes 1277960 | tf_op jit(solution)/shard_map/ppermute | solution.py:44
  19.3 18.4 %collective-permute-start.5 = (bf16[416,512]{1,0:T(8,128)(2,1)S(1)}, bf16[416,512]{1,0:T(8,128)(2,1)S(1)}, u32[]{:S(2)}, u32[]{:S(2)}) collective-permute-start(bf16[416,512]{1,0:T(8,128)(2,1)S(1)} %collective-permute-done.1.refs_5_.refs_10_.refs_11_), channel_id=1, source_target_pairs={{0,2},{1,3},{2,0},{3,1},{4,6},{5,7},{6,4},{7,5},{8,10},{9,11},{10,... | collective-permute-start | bytes 1277960 | tf_op jit(solution)/shard_map/ppermute | solution.py:44
  20.7 20.6 %collective-permute-start.9 = (bf16[96,1024]{1,0:T(8,128)(2,1)}, bf16[96,1024]{1,0:T(8,128)(2,1)}, u32[]{:S(2)}, u32[]{:S(2)}) collective-permute-start(bf16[96,1024]{1,0:T(8,128)(2,1)} %get-tuple-element.270.refs_16_), channel_id=1, source_target_pairs={{0,3},{1,2},{2,1},{3,0},{4,7},{5,6},{6,5},{7,4},{8,11},{9,10},{10,... | collective-permute-start | bytes 589832 | tf_op jit(solution)/shard_map/ppermute | solution.py:44
  28.4 14.7 %collective-permute-start.8 = (bf16[96,1024]{1,0:T(8,128)(2,1)}, bf16[96,1024]{1,0:T(8,128)(2,1)}, u32[]{:S(2)}, u32[]{:S(2)}) collective-permute-start(bf16[96,1024]{1,0:T(8,128)(2,1)} %get-tuple-element.270.refs_16_), channel_id=1, source_target_pairs={{0,2},{1,3},{2,0},{3,1},{4,6},{5,7},{6,4},{7,5},{8,10},{9,11},{10,... | collective-permute-start | bytes 589832 | tf_op jit(solution)/shard_map/ppermute | solution.py:44
  30.3 14.3 %collective-permute-start.7 = (bf16[96,1024]{1,0:T(8,128)(2,1)}, bf16[96,1024]{1,0:T(8,128)(2,1)}, u32[]{:S(2)}, u32[]{:S(2)}) collective-permute-start(bf16[96,1024]{1,0:T(8,128)(2,1)} %get-tuple-element.270.refs_16_), channel_id=1, source_target_pairs={{0,1},{1,0},{2,3},{3,2},{4,5},{5,4},{6,7},{7,6},{8,9},{9,8},{10,11... | collective-permute-start | bytes 589832 | tf_op jit(solution)/shard_map/ppermute | solution.py:44
  46.8 15.0 %collective-permute-start.12 = (bf16[3136,1024]{1,0:T(8,128)(2,1)S(1)}, bf16[3136,1024]{1,0:T(8,128)(2,1)S(1)}, u32[]{:S(2)}, u32[]{:S(2)}) collective-permute-start(bf16[3136,1024]{1,0:T(8,128)(2,1)S(1)} %get-tuple-element.320), channel_id=1, source_target_pairs={{8,12},{9,13},{10,14},{11,15},{16,20},{17,21},{18,22},{19,23}} | collective-permute-start | bytes 19267592 | tf_op jit(solution)/shard_map/ppermute | solution.py:44
  48.6 2.0 %collective-permute-start.11 = (bf16[64,4096]{1,0:T(8,128)(2,1)S(1)}, bf16[64,4096]{1,0:T(8,128)(2,1)S(1)}, u32[]{:S(2)}, u32[]{:S(2)}) collective-permute-start(bf16[64,4096]{1,0:T(8,128)(2,1)S(1)} %get-tuple-element.287), channel_id=1, source_target_pairs={{28,24},{29,25},{30,26},{31,27}} | collective-permute-start | bytes 1572872 | tf_op jit(solution)/shard_map/ppermute | solution.py:44
  49.9 8.5 %collective-permute-start.10 = (bf16[64,4096]{1,0:T(8,128)(2,1)S(1)}, bf16[64,4096]{1,0:T(8,128)(2,1)S(1)}, u32[]{:S(2)}, u32[]{:S(2)}) collective-permute-start(bf16[64,4096]{1,0:T(8,128)(2,1)S(1)} %get-tuple-element.286), channel_id=1, source_target_pairs={{24,20},{25,21},{26,22},{27,23}} | collective-permute-start | bytes 1572872 | tf_op jit(solution)/shard_map/ppermute | solution.py:44
  51.2 21.3 %collective-permute-start.14 = (bf16[64,4096]{1,0:T(8,128)(2,1)S(1)}, bf16[64,4096]{1,0:T(8,128)(2,1)S(1)}, u32[]{:S(2)}, u32[]{:S(2)}) collective-permute-start(bf16[64,4096]{1,0:T(8,128)(2,1)S(1)} %get-tuple-element.322), channel_id=1, source_target_pairs={{24,20},{25,21},{26,22},{27,23}} | collective-permute-start | bytes 1572872 | tf_op jit(solution)/shard_map/ppermute | solution.py:44
  52.5 10.6 %collective-permute-start.15 = (bf16[128,1280]{1,0:T(8,128)(2,1)S(1)}, bf16[128,1280]{1,0:T(8,128)(2,1)S(1)}, u32[]{:S(2)}, u32[]{:S(2)}) collective-permute-start(bf16[128,1280]{1,0:T(8,128)(2,1)S(1)} %get-tuple-element.327), channel_id=1, source_target_pairs={{0,1},{1,0},{2,3},{3,2},{4,5},{5,4},{6,7},{7,6},{8,9},{9,8},{10,11... | collective-permute-start | bytes 983048 | tf_op jit(solution)/shard_map/ppermute | solution.py:44
  55.9 16.5 %collective-permute-start.16 = (bf16[128,1280]{1,0:T(8,128)(2,1)S(1)}, bf16[128,1280]{1,0:T(8,128)(2,1)S(1)}, u32[]{:S(2)}, u32[]{:S(2)}) collective-permute-start(bf16[128,1280]{1,0:T(8,128)(2,1)S(1)} %get-tuple-element.328), channel_id=1, source_target_pairs={{0,2},{1,3},{2,0},{3,1},{4,6},{5,7},{6,4},{7,5},{8,10},{9,11},{10,... | collective-permute-start | bytes 983048 | tf_op jit(solution)/shard_map/ppermute | solution.py:44
  58.4 14.1 %collective-permute-start.17 = (bf16[128,1280]{1,0:T(8,128)(2,1)S(1)}, bf16[128,1280]{1,0:T(8,128)(2,1)S(1)}, u32[]{:S(2)}, u32[]{:S(2)}) collective-permute-start(bf16[128,1280]{1,0:T(8,128)(2,1)S(1)} %get-tuple-element.329), channel_id=1, source_target_pairs={{0,3},{1,2},{2,1},{3,0},{4,7},{5,6},{6,5},{7,4},{8,11},{9,10},{10,... | collective-permute-start | bytes 983048 | tf_op jit(solution)/shard_map/ppermute | solution.py:44
  62.4 13.0 %collective-permute-start.13 = (bf16[64,4096]{1,0:T(8,128)(2,1)S(1)}, bf16[64,4096]{1,0:T(8,128)(2,1)S(1)}, u32[]{:S(2)}, u32[]{:S(2)}) collective-permute-start(bf16[64,4096]{1,0:T(8,128)(2,1)S(1)} %get-tuple-element.321), channel_id=1, source_target_pairs={{20,12},{21,13},{22,14},{23,15}} | collective-permute-start | bytes 1572872 | tf_op jit(solution)/shard_map/ppermute | solution.py:44
  73.2 3.4 %collective-permute-start.21 = (bf16[64,4096]{1,0:T(8,128)(2,1)S(1)}, bf16[64,4096]{1,0:T(8,128)(2,1)S(1)}, u32[]{:S(2)}, u32[]{:S(2)}) collective-permute-start(bf16[64,4096]{1,0:T(8,128)(2,1)S(1)} %get-tuple-element.363), channel_id=1, source_target_pairs={{20,12},{21,13},{22,14},{23,15}} | collective-permute-start | bytes 1572872 | tf_op jit(solution)/shard_map/ppermute | solution.py:44
  73.9 4.7 %collective-permute-start.20 = (bf16[64,4096]{1,0:T(8,128)(2,1)S(1)}, bf16[64,4096]{1,0:T(8,128)(2,1)S(1)}, u32[]{:S(2)}, u32[]{:S(2)}) collective-permute-start(bf16[64,4096]{1,0:T(8,128)(2,1)S(1)} %get-tuple-element.362), channel_id=1, source_target_pairs={{20,16},{21,17},{22,18},{23,19}} | collective-permute-start | bytes 1572872 | tf_op jit(solution)/shard_map/ppermute | solution.py:44
  74.6 4.7 %collective-permute-start.19 = (bf16[64,4096]{1,0:T(8,128)(2,1)S(1)}, bf16[64,4096]{1,0:T(8,128)(2,1)S(1)}, u32[]{:S(2)}, u32[]{:S(2)}) collective-permute-start(bf16[64,4096]{1,0:T(8,128)(2,1)S(1)} %get-tuple-element.361), channel_id=1, source_target_pairs={{20,16},{21,17},{22,18},{23,19}} | collective-permute-start | bytes 1572872 | tf_op jit(solution)/shard_map/ppermute | solution.py:44
  75.9 7.6 %collective-permute-start.18 = (bf16[64,4096]{1,0:T(8,128)(2,1)S(1)}, bf16[64,4096]{1,0:T(8,128)(2,1)S(1)}, u32[]{:S(2)}, u32[]{:S(2)}) collective-permute-start(bf16[64,4096]{1,0:T(8,128)(2,1)S(1)} %get-tuple-element.360), channel_id=1, source_target_pairs={{12,4},{13,5},{14,6},{15,7}} | collective-permute-start | bytes 1572872 | tf_op jit(solution)/shard_map/ppermute | solution.py:44
  77.2 8.2 %collective-permute-start.26 = (bf16[64,4096]{1,0:T(8,128)(2,1)S(1)}, bf16[64,4096]{1,0:T(8,128)(2,1)S(1)}, u32[]{:S(2)}, u32[]{:S(2)}) collective-permute-start(bf16[64,4096]{1,0:T(8,128)(2,1)S(1)} %get-tuple-element.431), channel_id=1, source_target_pairs={{12,4},{13,5},{14,6},{15,7}} | collective-permute-start | bytes 1572872 | tf_op jit(solution)/shard_map/ppermute | solution.py:44
  77.9 3.3 %collective-permute-start.22 = (bf16[128,1280]{1,0:T(8,128)(2,1)S(1)}, bf16[128,1280]{1,0:T(8,128)(2,1)S(1)}, u32[]{:S(2)}, u32[]{:S(2)}) collective-permute-start(bf16[128,1280]{1,0:T(8,128)(2,1)S(1)} %get-tuple-element.327), channel_id=1, source_target_pairs={{16,17},{17,16},{18,19},{19,18},{20,21},{21,20},{22,23},{23,22},{2... | collective-permute-start | bytes 983048 | tf_op jit(solution)/shard_map/ppermute | solution.py:44
  78.6 3.3 %collective-permute-start.23 = (bf16[128,1280]{1,0:T(8,128)(2,1)S(1)}, bf16[128,1280]{1,0:T(8,128)(2,1)S(1)}, u32[]{:S(2)}, u32[]{:S(2)}) collective-permute-start(bf16[128,1280]{1,0:T(8,128)(2,1)S(1)} %get-tuple-element.328), channel_id=1, source_target_pairs={{16,18},{17,19},{18,16},{19,17},{20,22},{21,23},{22,20},{23,21},{2... | collective-permute-start | bytes 983048 | tf_op jit(solution)/shard_map/ppermute | solution.py:44
  79.3 3.3 %collective-permute-start.24 = (bf16[128,1280]{1,0:T(8,128)(2,1)S(1)}, bf16[128,1280]{1,0:T(8,128)(2,1)S(1)}, u32[]{:S(2)}, u32[]{:S(2)}) collective-permute-start(bf16[128,1280]{1,0:T(8,128)(2,1)S(1)} %get-tuple-element.329), channel_id=1, source_target_pairs={{16,19},{17,18},{18,17},{19,16},{20,23},{21,22},{22,21},{23,20},{2... | collective-permute-start | bytes 983048 | tf_op jit(solution)/shard_map/ppermute | solution.py:44
  81.2 6.4 %collective-permute-start.29 = (bf16[64,4096]{1,0:T(8,128)(2,1)S(1)}, bf16[64,4096]{1,0:T(8,128)(2,1)S(1)}, u32[]{:S(2)}, u32[]{:S(2)}) collective-permute-start(bf16[64,4096]{1,0:T(8,128)(2,1)S(1)} %get-tuple-element.449), channel_id=1, source_target_pairs={{12,8},{13,9},{14,10},{15,11}} | collective-permute-start | bytes 1572872 | tf_op jit(solution)/shard_map/ppermute | solution.py:44
  81.9 6.3 %collective-permute-start.28 = (bf16[64,4096]{1,0:T(8,128)(2,1)S(1)}, bf16[64,4096]{1,0:T(8,128)(2,1)S(1)}, u32[]{:S(2)}, u32[]{:S(2)}) collective-permute-start(bf16[64,4096]{1,0:T(8,128)(2,1)S(1)} %get-tuple-element.448), channel_id=1, source_target_pairs={{12,8},{13,9},{14,10},{15,11}} | collective-permute-start | bytes 1572872 | tf_op jit(solution)/shard_map/ppermute | solution.py:44
  84.2 5.6 %collective-permute-start.25 = (bf16[64,4096]{1,0:T(8,128)(2,1)S(1)}, bf16[64,4096]{1,0:T(8,128)(2,1)S(1)}, u32[]{:S(2)}, u32[]{:S(2)}) collective-permute-start(bf16[64,4096]{1,0:T(8,128)(2,1)S(1)} %get-tuple-element.430), channel_id=1, source_target_pairs={{4,0},{5,1},{6,2},{7,3}} | collective-permute-start | bytes 1572872 | tf_op jit(solution)/shard_map/ppermute | solution.py:44
  86.3 9.4 %collective-permute-start.27 = (bf16[64,4096]{1,0:T(8,128)(2,1)S(1)}, bf16[64,4096]{1,0:T(8,128)(2,1)S(1)}, u32[]{:S(2)}, u32[]{:S(2)}) collective-permute-start(bf16[64,4096]{1,0:T(8,128)(2,1)S(1)} %get-tuple-element.447), channel_id=1, source_target_pairs={{4,0},{5,1},{6,2},{7,3}} | collective-permute-start | bytes 1572872 | tf_op jit(solution)/shard_map/ppermute | solution.py:44
  97.8 10.7 %collective-permute-start.30 = (bf16[128,1280]{1,0:T(8,128)(2,1)S(1)}, bf16[128,1280]{1,0:T(8,128)(2,1)S(1)}, u32[]{:S(2)}, u32[]{:S(2)}) collective-permute-start(bf16[128,1280]{1,0:T(8,128)(2,1)S(1)} %get-tuple-element.498), channel_id=1, source_target_pairs={{0,1},{1,0},{2,3},{3,2},{4,5},{5,4},{6,7},{7,6},{8,9},{9,8},{10,11... | collective-permute-start | bytes 983048 | tf_op jit(solution)/shard_map/ppermute | solution.py:44
  99.5 15.0 %collective-permute-start.31 = (bf16[128,1280]{1,0:T(8,128)(2,1)S(1)}, bf16[128,1280]{1,0:T(8,128)(2,1)S(1)}, u32[]{:S(2)}, u32[]{:S(2)}) collective-permute-start(bf16[128,1280]{1,0:T(8,128)(2,1)S(1)} %get-tuple-element.499), channel_id=1, source_target_pairs={{0,2},{1,3},{2,0},{3,1},{4,6},{5,7},{6,4},{7,5},{8,10},{9,11},{10,... | collective-permute-start | bytes 983048 | tf_op jit(solution)/shard_map/ppermute | solution.py:44
  101.0 13.6 %collective-permute-start.32 = (bf16[128,1280]{1,0:T(8,128)(2,1)S(1)}, bf16[128,1280]{1,0:T(8,128)(2,1)S(1)}, u32[]{:S(2)}, u32[]{:S(2)}) collective-permute-start(bf16[128,1280]{1,0:T(8,128)(2,1)S(1)} %get-tuple-element.500), channel_id=1, source_target_pairs={{0,3},{1,2},{2,1},{3,0},{4,7},{5,6},{6,5},{7,4},{8,11},{9,10},{10,... | collective-permute-start | bytes 983048 | tf_op jit(solution)/shard_map/ppermute | solution.py:44
  (4 other events, 41.8 us)

commit v7 on v6

--- a/solution.py
+++ b/solution.py
@@ -129,7 +129,8 @@
             rest[0][...] = whole[head_rows:]
 
 
-def norm_kernel(x, gain, x_out, normed_out, inverse_out, gain_out):
+def norm_kernel(x, gain, truth, x_out, normed_out, inverse_out, gain_out, truth_out):
+    truth_out[...] = truth[...]
     values = x[...].astype(jnp.float32)
     inverse = lax.rsqrt(jnp.mean(values * values, axis=-1, keepdims=True) + EPSILON)
     x_out[...] = x[...]
@@ -141,10 +142,10 @@
 def top_kernel(size, bounds, *refs):
     flags, truth, mask = refs[:3]
     halves = refs[7 : 7 + 2 * size]
-    gain, x, inverse, latent_ref, latent_grad_out, arriving_out, grads_out = refs[
-        7 + 2 * size : 14 + 2 * size
+    gain, x, inverse, normed, latent_ref, latent_grad_out, arriving_out, grads_out = refs[
+        7 + 2 * size : 15 + 2 * size
     ]
-    sends = refs[14 + 2 * size :]
+    sends = refs[15 + 2 * size :]
     dp_index = flags[0]
     width = x.shape[1] // size
     latent_width = latent_ref.shape[1]
@@ -153,7 +154,8 @@
 
     @pl.when(flags[2] == 1)
     def _():
-        latent = latent_ref[...]
+        latent = latent_of(dp_index, size, normed, halves, latent_width)
+        latent_ref[...] = latent
         activated = jax.nn.silu(latent).astype(jnp.bfloat16)
         estimate = None
         product = None
@@ -197,26 +199,24 @@
                     send[:, at_k] = grads[row:end]
 
 
-def latent_kernel(size, *refs):
-    flags, normed = refs[:2]
-    down = refs[2 : 2 + 2 * size]
-    latent = refs[3 + 2 * size]
+def latent_of(dp_index, size, normed, halves, latent_width):
     width = normed.shape[1] // size
     total = None
     for k in range(size):
         for half in range(2):
-            block = normed[:, half_columns(flags[0], k, half, width)]
-            part = dot_nt(block, down[2 * k + half][: latent.shape[1]])
+            block = normed[:, half_columns(dp_index, k, half, width)]
+            part = dot_nt(block, halves[2 * k + half][:latent_width])
             total = part if total is None else total + part
-    latent[...] = total
+    return total
 
 
 def keep_kernel(size, count, more, *refs):
     flags = refs[0]
-    gain, inverse, latent, x = refs[1:5]
-    raw = refs[8 : 8 + count]
-    kept = refs[15 + count : 15 + count + 2 * size]
-    bundle, sems = refs[15 + count + 2 * size :]
+    gain, inverse, _, x = refs[1:5]
+    raw = refs[9 : 9 + count]
+    latent, normed = refs[11 + count], refs[16 + count]
+    kept = refs[17 + count : 17 + count + 2 * size]
+    bundle, sems = refs[17 + count + 2 * size :]
     tokens, width = x.shape
     latent_width = latent.shape[1]
     shard = width // size
@@ -224,13 +224,16 @@
 
     @pl.when(flags[3] == 1)
     def _():
+        sources = list(raw[2 * size :])
+        if len(sources) < size and more:
+            sources[2:] = [raw[-1].at[pl.ds(0, more)], raw[-1].at[pl.ds(more, more)]]
         copies = [
-            pltpu.make_async_copy(raw[2 * size + k], kept[size + k].at[pl.ds(rows, more)], sems.at[k])
-            for k in range(size)
-            if more
+            pltpu.make_async_copy(source, kept[size + k].at[pl.ds(rows, more)], sems.at[k])
+            for k, source in enumerate(sources)
         ]
         for copy in copies:
             copy.start()
+        latent[...] = latent_of(flags[0], size, normed, raw, latent_width)
         for k in range(size):
             for half in range(2):
                 here = slice(half * (shard // 2), (half + 1) * (shard // 2))
@@ -317,10 +320,14 @@
     down, up = kept_of(state[7:], size, shard)
     state = state[:7]
     gain, inverse, latent, x, latent_grads, arrivals, grads = state
+    tokens = x.shape[0]
     at_rows = slice(bounds[0][0], bounds[-1][1])
 
     def take(place):
-        parts = [piece[:, place] for piece in pieces]
+        parts = [
+            piece[slice(*bound) if piece.shape[0] == tokens else slice(None), place]
+            for bound, piece in zip(bounds, pieces)
+        ]
         return parts[0] if len(parts) == 1 else jnp.concatenate(parts, axis=0)
 
     def write(place, arriving, value):
@@ -505,59 +512,55 @@
     )(flags, stay(down_proj), stay(up_proj), stay(readout_matrix))
     halves = gather_halves(low, high, everyone, size)
     if more:
-        up_rest, first = lax.optimization_barrier((up_rest[0], halves[2 % size][0]))
-        halves[2 % size] = (first, halves[2 % size][1])
-        up_rest = gather(up_rest, rest, size)
+        up_rest = up_rest[0]
+        if size == 4:
+            across = move(up_rest, peers(rest, size, 1))
+            along = move(jnp.concatenate([up_rest, across]), peers(rest, size, 2))
+            up_rest = [up_rest, across, along]
+        else:
+            up_rest = gather(up_rest, rest, size)
     halves = [half for pair in halves for half in pair]
 
-    x, normed, inverse, gain = pl.pallas_call(
+    x, normed, inverse, gain, truth = pl.pallas_call(
         norm_kernel,
         out_shape=(
             pltpu.VMEM((tokens, width), bf16),
             pltpu.VMEM((tokens, width), bf16),
             pltpu.VMEM((tokens, 128), f32),
             pltpu.VMEM((1, width), bf16),
+            held_like(ground_truth_series),
         ),
-        in_specs=[VMEM] * 2,
-        out_specs=(VMEM,) * 4,
+        in_specs=[VMEM] * 3,
+        out_specs=(VMEM,) * 5,
         cost_estimate=NOTHING,
         compiler_params=PARAMS,
-    )(x, norm_gain)
+    )(x, norm_gain, ground_truth_series)
     per_micro = tokens // valid_len.shape[0]
     mask = (
         (jnp.arange(per_micro)[None, :] < valid_len[:, None]).astype(f32).reshape(tokens, 1)
     )
     mask = jnp.broadcast_to(mask, (tokens, 128))
 
-    normed, latent = pl.pallas_call(
-        functools.partial(latent_kernel, size),
-        out_shape=(held_like(normed), pltpu.VMEM((tokens, latent_width), f32)),
-        in_specs=[SMEM] + [VMEM] * (1 + 2 * size),
-        out_specs=(VMEM,) * 2,
-        input_output_aliases={1: 0},
-        cost_estimate=NOTHING,
-        compiler_params=PARAMS,
-    )(flags, pin(normed), *[pin(half) for half in halves])
-
-    gain, x, inverse, latent, latent_grads, arrivals, grads, *sends = pl.pallas_call(
-        functools.partial(top_kernel, size, bounds),
+    gain, x, inverse, normed, latent, latent_grads, arrivals, grads, *sends = pl.pallas_call(
+        functools.partial(top_kernel, size, [(0, tokens)]),
         out_shape=(
             held_like(gain),
             held_like(x),
             held_like(inverse),
-            held_like(latent),
+            held_like(normed),
+            pltpu.VMEM((tokens, latent_width), f32),
             pltpu.VMEM((tokens, latent_width), bf16),
             pltpu.VMEM((tokens, width), bf16),
             pltpu.VMEM((tokens, width), bf16),
         )
-        + tuple(jax.ShapeDtypeStruct((end - row, width), bf16) for row, end in bounds),
+        + (jax.ShapeDtypeStruct((tokens, width), bf16),),
         in_specs=[SMEM] + [VMEM] * (6 + 2 * size),
-        out_specs=(VMEM,) * (7 + len(bounds)),
+        out_specs=(VMEM,) * 9,
         input_output_aliases={3: 0, 4: 1, 5: 2, 6: 3},
         cost_estimate=NOTHING,
         compiler_params=PARAMS,
     )(
-        flags, ground_truth_series, mask, pin(gain), pin(x), pin(inverse), pin(latent),
+        flags, pin(truth), mask, pin(gain), pin(x), pin(inverse), pin(normed),
         *[pin(part) for part in halves],
     )
 
@@ -566,7 +569,7 @@
             block, [(sender * size + i, (sender - distance) * size + i) for i in range(size)]
         )
 
-    received = [hop(send, top) for send in sends]
+    received = [hop(sends[0], top)] * len(bounds)
 
     message = jax.ShapeDtypeStruct((tokens, shard + latent_width), bf16)
     shards = (*halves, *up_rest)
@@ -621,7 +624,7 @@
 
     state_kept = pl.pallas_call(
         functools.partial(keep_kernel, size, len(shards), more),
-        out_shape=tuple(held_like(part) for part in state)
+        out_shape=tuple(held_like(part) for part in (*state, normed))
         + (pltpu.VMEM((latent_width, shard), bf16),) * size
         + (pltpu.VMEM((up_block, up_lanes), bf16),) * size
         + (
@@ -630,15 +633,16 @@
             ),
         ),
         in_specs=[SMEM]
-        + [VMEM] * (len(state) + 2 * size)
+        + [VMEM] * (len(state) + 1 + 2 * size)
         + [ANY] * (len(shards) - 2 * size),
-        out_specs=(VMEM,) * (len(state) + 2 * size + 1),
+        out_specs=(VMEM,) * (len(state) + 2 * size + 2),
         scratch_shapes=[pltpu.SemaphoreType.DMA((size,))],
-        input_output_aliases={1 + i: i for i in range(len(state))},
+        input_output_aliases={1 + i: i for i in range(len(state) + 1)},
         cost_estimate=NOTHING,
         compiler_params=PARAMS,
-    )(flags, *[pin(part) for part in (*state, *halves)], *up_rest)
-    state, kept, bundle = tuple(state_kept[:7]), tuple(state_kept[7:-1]), state_kept[-1:]
+    )(flags, *[pin(part) for part in (*state, normed, *halves)], *up_rest)
+    state, normed = tuple(state_kept[:7]), state_kept[7]
+    kept, bundle = tuple(state_kept[8:-1]), state_kept[-1:]
     pairs = list(range(3, top - 1, 2))
     bundle = tuple(
         move(part, [((s - 1) * size + i, s * size + i) for s in pairs for i in range(size)])

time: 117 us -> 116 us (level)
  starting transfers between devices: 44.6 us -> 40.7 us
  waiting for transfers between devices: 46.3 us -> 48.9 us
  local copies, waits for them, and re-layouts: 3.16 us -> 4.68 us
  Pallas kernels: 20.2 us -> 18.8 us
    ppermute x33 -> x31, starting transfers between devices: 44.6 us -> 40.7 us  [move(): return lax.ppermute(block, ('section', 'dp'), pairs)]
    ppermute x33 -> x31, waiting for transfers between devices: 46.3 us -> 48.9 us  [move(): return lax.ppermute(block, ('section', 'dp'), pairs)]
    unnamed x7 -> x15, local copies, waits for them, and re-layouts: 2.92 us -> 4.44 us
    pallas_call x2 -> x1, Pallas kernels: 1.92 us -> 0.56 us  [per_device(): pl.pallas_call(functools.partial(top_kernel, size, [(0, tokens)]), out_sh...]
  transfers between devices with their start and end apart: 33 -> 31, of which waited for: 11 -> 12; matrix products, arithmetic and copies ran while one was open for 2% -> 2% of each run, Pallas kernels for 10% -> 9%
where the time goes in v7:
time: 116 us
  waiting for transfers between devices  48.9 us (42%)
  starting transfers between devices  40.7 us (35%)
  Pallas kernels  18.8 us (16%)
  local copies, waits for them, and re-layouts  4.68 us (4%)
  other arithmetic  1.54 us (1%)
    ppermute x31, waiting for transfers between devices, move(): return lax.ppermute(block, ('section', 'dp'), pairs)  48.9 us
    ppermute x31, starting transfers between devices, move(): return lax.ppermute(block, ('section', 'dp'), pairs)  40.7 us
    pallas_call x9, Pallas kernels, run_stage(): pl.pallas_call(functools.partial(stage_kernel, stage, bounds, size, len(s...  6.95 us
    unnamed x15, local copies, waits for them, and re-layouts  4.44 us
    pallas_call x1, Pallas kernels, per_device(): pl.pallas_call(functools.partial(keep_kernel, size, len(shards), more), o...  2.83 us
    pallas_call x4, Pallas kernels, run_pair(): pl.pallas_call(functools.partial(pair_kernel, stage, bound, size, len(sta...  2.49 us
  transfers between devices with their start and end apart: 31, of which 12 were waited for; matrix products, arithmetic and copies ran while one was open for 2% of the time, Pallas kernels for 9%

profile of v7, /device:TPU:0, one launch (start us, length us, event | category | flops | bytes accessed | tf_op | source)
XLA Modules:
  0.0 115.8 jit_solution(5251483197815245927)
XLA Ops:
  0.7 2.1 %shard_map.95 = (bf16[416,512]{1,0:T(8,128)(2,1)S(1)}, bf16[416,512]{1,0:T(8,128)(2,1)S(1)}, bf16[96,1024]{1,0:T(8,128)(2,1)S(1)}) custom-call(s32[5]{0:T(128)S(1)} %stack.35.flags.refs_0_, bf16[1,1024,256]{2,1,0:T(8,128)(2,1)} %down.1, bf16[1,256,1024]{2,1,0:T(8,128)(2,1)} %up.1, bf16[1024,128]{1,0:T(8,128)(2,1)} %readout.1), custom_call_target="tpu_custom_call" | custom-call | tf_op jit(solution)/shard_map/pallas_call | solution.py:498
  2.8 3.0 %collective-permute-start.2 = (bf16[416,512]{1,0:T(8,128)(2,1)S(1)}, bf16[416,512]{1,0:T(8,128)(2,1)S(1)}, u32[]{:S(2)}, u32[]{:S(2)}) collective-permute-start(bf16[416,512]{1,0:T(8,128)(2,1)S(1)} %get-tuple-element.256.refs_7_.refs_9_), channel_id=1, source_target_pairs={{0,2},{1,3},{2,0},{3,1},{4,6},{5,7},{6,4},{7,5},{8,10},{9,11},{10,... | collective-permute-start | bytes 1277960 | tf_op jit(solution)/shard_map/ppermute | solution.py:44
  5.8 1.5 %collective-permute-start.1 = (bf16[416,512]{1,0:T(8,128)(2,1)S(1)}, bf16[416,512]{1,0:T(8,128)(2,1)S(1)}, u32[]{:S(2)}, u32[]{:S(2)}) collective-permute-start(bf16[416,512]{1,0:T(8,128)(2,1)S(1)} %get-tuple-element.257.refs_8_.refs_10_), channel_id=1, source_target_pairs={{0,1},{1,0},{2,3},{3,2},{4,5},{5,4},{6,7},{7,6},{8,9},{9,8},{10,11... | collective-permute-start | bytes 1277960 | tf_op jit(solution)/shard_map/ppermute | solution.py:44
  7.3 2.4 %collective-permute-start.7 = (bf16[96,1024]{1,0:T(8,128)(2,1)S(1)}, bf16[96,1024]{1,0:T(8,128)(2,1)S(1)}, u32[]{:S(2)}, u32[]{:S(2)}) collective-permute-start(bf16[96,1024]{1,0:T(8,128)(2,1)S(1)} %get-tuple-element.267.refs_17_), channel_id=1, source_target_pairs={{0,1},{1,0},{2,3},{3,2},{4,5},{5,4},{6,7},{7,6},{8,9},{9,8},{10,11... | collective-permute-start | bytes 589832 | tf_op jit(solution)/shard_map/ppermute | solution.py:44
  9.8 1.6 %collective-permute-start = (bf16[416,512]{1,0:T(8,128)(2,1)S(1)}, bf16[416,512]{1,0:T(8,128)(2,1)S(1)}, u32[]{:S(2)}, u32[]{:S(2)}) collective-permute-start(bf16[416,512]{1,0:T(8,128)(2,1)S(1)} %get-tuple-element.256.refs_7_.refs_9_), channel_id=1, source_target_pairs={{0,1},{1,0},{2,3},{3,2},{4,5},{5,4},{6,7},{7,6},{8,9},{9,8},{10,11... | collective-permute-start | bytes 1277960 | tf_op jit(solution)/shard_map/ppermute | solution.py:44
  11.8 4.7 %collective-permute-done.2.refs_11_.refs_13_ = bf16[416,512]{1,0:T(8,128)(2,1)S(1)} collective-permute-done((bf16[416,512]{1,0:T(8,128)(2,1)S(1)}, bf16[416,512]{1,0:T(8,128)(2,1)S(1)}, u32[]{:S(2)}, u32[]{:S(2)}) %collective-permute-start.2) | collective-permute-done | bytes 426016 | tf_op jit(solution)/shard_map/ppermute | solution.py:44
  16.5 2.0 %collective-permute-start.4 = (bf16[416,512]{1,0:T(8,128)(2,1)S(1)}, bf16[416,512]{1,0:T(8,128)(2,1)S(1)}, u32[]{:S(2)}, u32[]{:S(2)}) collective-permute-start(bf16[416,512]{1,0:T(8,128)(2,1)S(1)} %collective-permute-done.2.refs_11_.refs_13_), channel_id=1, source_target_pairs={{0,1},{1,0},{2,3},{3,2},{4,5},{5,4},{6,7},{7,6},{8,9},{9,8},{10,11... | collective-permute-start | bytes 1277960 | tf_op jit(solution)/shard_map/ppermute | solution.py:44
  18.6 1.5 %collective-permute-start.5 = (bf16[416,512]{1,0:T(8,128)(2,1)S(1)}, bf16[416,512]{1,0:T(8,128)(2,1)S(1)}, u32[]{:S(2)}, u32[]{:S(2)}) collective-permute-start(bf16[416,512]{1,0:T(8,128)(2,1)S(1)} %collective-permute-done.1.refs_10_.refs_12_), channel_id=1, source_target_pairs={{0,2},{1,3},{2,0},{3,1},{4,6},{5,7},{6,4},{7,5},{8,10},{9,11},{10,... | collective-permute-start | bytes 1277960 | tf_op jit(solution)/shard_map/ppermute | solution.py:44
  20.0 2.8 %collective-permute-done.7.refs_18_ = bf16[96,1024]{1,0:T(8,128)(2,1)S(1)} collective-permute-done((bf16[96,1024]{1,0:T(8,128)(2,1)S(1)}, bf16[96,1024]{1,0:T(8,128)(2,1)S(1)}, u32[]{:S(2)}, u32[]{:S(2)}) %collective-permute-start.7) | collective-permute-done | bytes 196640 | tf_op jit(solution)/shard_map/ppermute | solution.py:44
  24.3 1.9 %collective-permute-start.8 = (bf16[192,1024]{1,0:T(8,128)(2,1)}, bf16[192,1024]{1,0:T(8,128)(2,1)}, u32[]{:S(2)}, u32[]{:S(2)}) collective-permute-start(bf16[192,1024]{1,0:T(8,128)(2,1)} %pad_maximum_fusion), channel_id=1, source_target_pairs={{0,2},{1,3},{2,0},{3,1},{4,6},{5,7},{6,4},{7,5},{8,10},{9,11},{10,... | collective-permute-start | bytes 1179656 | tf_op jit(solution)/shard_map/ppermute | solution.py:44
  27.0 1.2 %copy-done = bf16[1,128,4096]{2,1,0:T(8,128)(2,1)S(1)} copy-done((bf16[1,128,4096]{2,1,0:T(8,128)(2,1)S(1)}, bf16[1,128,4096]{2,1,0:T(8,128)(2,1)}, u32[]{:S(2)}) %copy-start) | copy-done | bytes 1048600
  30.5 1.4 %collective-permute-done.refs_9_.refs_11_ = bf16[416,512]{1,0:T(8,128)(2,1)S(1)} collective-permute-done((bf16[416,512]{1,0:T(8,128)(2,1)S(1)}, bf16[416,512]{1,0:T(8,128)(2,1)S(1)}, u32[]{:S(2)}, u32[]{:S(2)}) %collective-permute-start) | collective-permute-done | bytes 426016 | tf_op jit(solution)/shard_map/ppermute | solution.py:44
  31.9 7.7 %collective-permute-done.4.refs_13_.refs_15_ = bf16[416,512]{1,0:T(8,128)(2,1)S(1)} collective-permute-done((bf16[416,512]{1,0:T(8,128)(2,1)S(1)}, bf16[416,512]{1,0:T(8,128)(2,1)S(1)}, u32[]{:S(2)}, u32[]{:S(2)}) %collective-permute-start.4) | collective-permute-done | bytes 426016 | tf_op jit(solution)/shard_map/ppermute | solution.py:44
  40.2 2.2 %collective-permute-done.8.refs_19_ = bf16[192,1024]{1,0:T(8,128)(2,1)} collective-permute-done((bf16[192,1024]{1,0:T(8,128)(2,1)}, bf16[192,1024]{1,0:T(8,128)(2,1)}, u32[]{:S(2)}, u32[]{:S(2)}) %collective-permute-start.8) | collective-permute-done | bytes 393248 | tf_op jit(solution)/shard_map/ppermute | solution.py:44
  42.4 2.8 %shard_map.97 = (bf16[1,4096]{1,0:T(2,128)(2,1)S(1)}, f32[128,128]{1,0:T(8,128)S(1)}, f32[128,256]{1,0:T(8,128)S(1)}, bf16[128,4096]{1,0:T(8,128)(2,1)S(1)}, bf1...) custom-call(s32[5]{0:T(128)S(1)} %stack.35.flags.refs_0_, ...), custom_call_target="tpu_custom_call", output_to_operand_aliasing={{0}: (1, {}), {1}: (2, {}), {2}: (3, {}), {3}: (4, {}), {4}... | custom-call | tf_op jit(solution)/shard_map/pallas_call | solution.py:625
  45.3 1.1 collective-permute-start.10
  50.3 3.6 %collective-permute-start.13 = (bf16[128,1280]{1,0:T(8,128)(2,1)S(1)}, bf16[128,1280]{1,0:T(8,128)(2,1)S(1)}, u32[]{:S(2)}, u32[]{:S(2)}) collective-permute-start(bf16[128,1280]{1,0:T(8,128)(2,1)S(1)} %get-tuple-element.323), channel_id=1, source_target_pairs={{0,1},{1,0},{2,3},{3,2},{4,5},{5,4},{6,7},{7,6},{8,9},{9,8},{10,11... | collective-permute-start | bytes 983048 | tf_op jit(solution)/shard_map/ppermute | solution.py:44
  53.9 3.4 %collective-permute-start.14 = (bf16[128,1280]{1,0:T(8,128)(2,1)S(1)}, bf16[128,1280]{1,0:T(8,128)(2,1)S(1)}, u32[]{:S(2)}, u32[]{:S(2)}) collective-permute-start(bf16[128,1280]{1,0:T(8,128)(2,1)S(1)} %get-tuple-element.324), channel_id=1, source_target_pairs={{0,2},{1,3},{2,0},{3,1},{4,6},{5,7},{6,4},{7,5},{8,10},{9,11},{10,... | collective-permute-start | bytes 983048 | tf_op jit(solution)/shard_map/ppermute | solution.py:44
  57.4 2.2 %collective-permute-start.15 = (bf16[128,1280]{1,0:T(8,128)(2,1)S(1)}, bf16[128,1280]{1,0:T(8,128)(2,1)S(1)}, u32[]{:S(2)}, u32[]{:S(2)}) collective-permute-start(bf16[128,1280]{1,0:T(8,128)(2,1)S(1)} %get-tuple-element.325), channel_id=1, source_target_pairs={{0,3},{1,2},{2,1},{3,0},{4,7},{5,6},{6,5},{7,4},{8,11},{9,10},{10,... | collective-permute-start | bytes 983048 | tf_op jit(solution)/shard_map/ppermute | solution.py:44
  61.5 9.2 %collective-permute-done.14.refs_3_ = bf16[128,1280]{1,0:T(8,128)(2,1)S(1)} collective-permute-done((bf16[128,1280]{1,0:T(8,128)(2,1)S(1)}, bf16[128,1280]{1,0:T(8,128)(2,1)S(1)}, u32[]{:S(2)}, u32[]{:S(2)}) %collective-permute-start.14) | collective-permute-done | bytes 327712 | tf_op jit(solution)/shard_map/ppermute | solution.py:44
  80.9 0.9 shard_map.108
  82.5 1.3 %collective-permute-start.23 = (bf16[64,4096]{1,0:T(8,128)(2,1)S(1)}, bf16[64,4096]{1,0:T(8,128)(2,1)S(1)}, u32[]{:S(2)}, u32[]{:S(2)}) collective-permute-start(bf16[64,4096]{1,0:T(8,128)(2,1)S(1)} %get-tuple-element.426), channel_id=1, source_target_pairs={{4,0},{5,1},{6,2},{7,3}} | collective-permute-start | bytes 1572872 | tf_op jit(solution)/shard_map/ppermute | solution.py:44
  84.6 1.3 %collective-permute-start.25 = (bf16[64,4096]{1,0:T(8,128)(2,1)S(1)}, bf16[64,4096]{1,0:T(8,128)(2,1)S(1)}, u32[]{:S(2)}, u32[]{:S(2)}) collective-permute-start(bf16[64,4096]{1,0:T(8,128)(2,1)S(1)} %get-tuple-element.443), channel_id=1, source_target_pairs={{4,0},{5,1},{6,2},{7,3}} | collective-permute-start | bytes 1572872 | tf_op jit(solution)/shard_map/ppermute | solution.py:44
  87.1 1.8 %collective-permute-done.23.refs_1_ = bf16[64,4096]{1,0:T(8,128)(2,1)S(1)} collective-permute-done((bf16[64,4096]{1,0:T(8,128)(2,1)S(1)}, bf16[64,4096]{1,0:T(8,128)(2,1)S(1)}, u32[]{:S(2)}, u32[]{:S(2)}) %collective-permute-start.23) | collective-permute-done | bytes 524320 | tf_op jit(solution)/shard_map/ppermute | solution.py:44
  88.9 5.8 %collective-permute-done.25.refs_2_ = bf16[64,4096]{1,0:T(8,128)(2,1)S(1)} collective-permute-done((bf16[64,4096]{1,0:T(8,128)(2,1)S(1)}, bf16[64,4096]{1,0:T(8,128)(2,1)S(1)}, u32[]{:S(2)}, u32[]{:S(2)}) %collective-permute-start.25) | collective-permute-done | bytes 524320 | tf_op jit(solution)/shard_map/ppermute | solution.py:44
  94.8 2.1 %shard_map.113 = (bf16[1,4096]{1,0:T(2,128)(2,1)S(1)}, f32[128,128]{1,0:T(8,128)S(1)}, f32[128,256]{1,0:T(8,128)S(1)}, bf16[128,4096]{1,0:T(8,128)(2,1)S(1)}, bf...) custom-call(s32[5]{0:T(128)S(1)} %stack.35.flags.refs_0_, ...), custom_call_target="tpu_custom_call", output_to_operand_aliasing={{0}: (3, {}), {1}: (4, {}), {2}: (5, {}), {3}: (6, {}), {4}... | custom-call | tf_op jit(solution)/shard_map/pallas_call | solution.py:585
  96.9 2.2 %collective-permute-start.28 = (bf16[128,1280]{1,0:T(8,128)(2,1)S(1)}, bf16[128,1280]{1,0:T(8,128)(2,1)S(1)}, u32[]{:S(2)}, u32[]{:S(2)}) collective-permute-start(bf16[128,1280]{1,0:T(8,128)(2,1)S(1)} %get-tuple-element.494), channel_id=1, source_target_pairs={{0,1},{1,0},{2,3},{3,2},{4,5},{5,4},{6,7},{7,6},{8,9},{9,8},{10,11... | collective-permute-start | bytes 983048 | tf_op jit(solution)/shard_map/ppermute | solution.py:44
  99.1 0.9 collective-permute-start.29
  100.6 1.0 copy.446
  101.6 6.1 %collective-permute-done.28.refs_1_ = bf16[128,1280]{1,0:T(8,128)(2,1)S(1)} collective-permute-done((bf16[128,1280]{1,0:T(8,128)(2,1)S(1)}, bf16[128,1280]{1,0:T(8,128)(2,1)S(1)}, u32[]{:S(2)}, u32[]{:S(2)}) %collective-permute-start.28) | collective-permute-done | bytes 327712 | tf_op jit(solution)/shard_map/ppermute | solution.py:44
  107.7 6.4 %collective-permute-done.29.refs_2_ = bf16[128,1280]{1,0:T(8,128)(2,1)S(1)} collective-permute-done((bf16[128,1280]{1,0:T(8,128)(2,1)S(1)}, bf16[128,1280]{1,0:T(8,128)(2,1)S(1)}, u32[]{:S(2)}, u32[]{:S(2)}) %collective-permute-start.29) | collective-permute-done | bytes 327712 | tf_op jit(solution)/shard_map/ppermute | solution.py:44
  114.1 1.7 %shard_map.114 = (bf16[1024,256]{1,0:T(8,128)(2,1)}, bf16[256,1024]{1,0:T(8,128)(2,1)}) custom-call(bf16[1280,512]{1,0:T(8,128)(2,1)S(1)} %get-tuple-element.492.left, bf16[128,1280]{1,0:T(8,128)(2,1)S(1)} %get-tuple-element.493.refs_0_, bf16[128,1280]{1,0:T(8,128)(2,1)S(1)} %collective-permute-done.28.refs_1_, ...), custom_call_target="tpu_custom_call" | custom-call | tf_op jit(solution)/shard_map/pallas_call | solution.py:714
  (71 shorter events, 24.8 us)
Async XLA Ops:
  2.8 13.7 %collective-permute-start.2 = (bf16[416,512]{1,0:T(8,128)(2,1)S(1)}, bf16[416,512]{1,0:T(8,128)(2,1)S(1)}, u32[]{:S(2)}, u32[]{:S(2)}) collective-permute-start(bf16[416,512]{1,0:T(8,128)(2,1)S(1)} %get-tuple-element.256.refs_7_.refs_9_), channel_id=1, source_target_pairs={{0,2},{1,3},{2,0},{3,1},{4,6},{5,7},{6,4},{7,5},{8,10},{9,11},{10,... | collective-permute-start | bytes 1277960 | tf_op jit(solution)/shard_map/ppermute | solution.py:44
  5.8 12.7 %collective-permute-start.1 = (bf16[416,512]{1,0:T(8,128)(2,1)S(1)}, bf16[416,512]{1,0:T(8,128)(2,1)S(1)}, u32[]{:S(2)}, u32[]{:S(2)}) collective-permute-start(bf16[416,512]{1,0:T(8,128)(2,1)S(1)} %get-tuple-element.257.refs_8_.refs_10_), channel_id=1, source_target_pairs={{0,1},{1,0},{2,3},{3,2},{4,5},{5,4},{6,7},{7,6},{8,9},{9,8},{10,11... | collective-permute-start | bytes 1277960 | tf_op jit(solution)/shard_map/ppermute | solution.py:44
  7.3 15.5 %collective-permute-start.7 = (bf16[96,1024]{1,0:T(8,128)(2,1)S(1)}, bf16[96,1024]{1,0:T(8,128)(2,1)S(1)}, u32[]{:S(2)}, u32[]{:S(2)}) collective-permute-start(bf16[96,1024]{1,0:T(8,128)(2,1)S(1)} %get-tuple-element.267.refs_17_), channel_id=1, source_target_pairs={{0,1},{1,0},{2,3},{3,2},{4,5},{5,4},{6,7},{7,6},{8,9},{9,8},{10,11... | collective-permute-start | bytes 589832 | tf_op jit(solution)/shard_map/ppermute | solution.py:44
  9.8 22.2 %collective-permute-start = (bf16[416,512]{1,0:T(8,128)(2,1)S(1)}, bf16[416,512]{1,0:T(8,128)(2,1)S(1)}, u32[]{:S(2)}, u32[]{:S(2)}) collective-permute-start(bf16[416,512]{1,0:T(8,128)(2,1)S(1)} %get-tuple-element.256.refs_7_.refs_9_), channel_id=1, source_target_pairs={{0,1},{1,0},{2,3},{3,2},{4,5},{5,4},{6,7},{7,6},{8,9},{9,8},{10,11... | collective-permute-start | bytes 1277960 | tf_op jit(solution)/shard_map/ppermute | solution.py:44
  11.3 20.6 %collective-permute-start.3 = (bf16[416,512]{1,0:T(8,128)(2,1)S(1)}, bf16[416,512]{1,0:T(8,128)(2,1)S(1)}, u32[]{:S(2)}, u32[]{:S(2)}) collective-permute-start(bf16[416,512]{1,0:T(8,128)(2,1)S(1)} %get-tuple-element.257.refs_8_.refs_10_), channel_id=1, source_target_pairs={{0,2},{1,3},{2,0},{3,1},{4,6},{5,7},{6,4},{7,5},{8,10},{9,11},{10,... | collective-permute-start | bytes 1277960 | tf_op jit(solution)/shard_map/ppermute | solution.py:44
  16.5 23.1 %collective-permute-start.4 = (bf16[416,512]{1,0:T(8,128)(2,1)S(1)}, bf16[416,512]{1,0:T(8,128)(2,1)S(1)}, u32[]{:S(2)}, u32[]{:S(2)}) collective-permute-start(bf16[416,512]{1,0:T(8,128)(2,1)S(1)} %collective-permute-done.2.refs_11_.refs_13_), channel_id=1, source_target_pairs={{0,1},{1,0},{2,3},{3,2},{4,5},{5,4},{6,7},{7,6},{8,9},{9,8},{10,11... | collective-permute-start | bytes 1277960 | tf_op jit(solution)/shard_map/ppermute | solution.py:44
  18.6 21.0 %collective-permute-start.5 = (bf16[416,512]{1,0:T(8,128)(2,1)S(1)}, bf16[416,512]{1,0:T(8,128)(2,1)S(1)}, u32[]{:S(2)}, u32[]{:S(2)}) collective-permute-start(bf16[416,512]{1,0:T(8,128)(2,1)S(1)} %collective-permute-done.1.refs_10_.refs_12_), channel_id=1, source_target_pairs={{0,2},{1,3},{2,0},{3,1},{4,6},{5,7},{6,4},{7,5},{8,10},{9,11},{10,... | collective-permute-start | bytes 1277960 | tf_op jit(solution)/shard_map/ppermute | solution.py:44
  24.3 18.2 %collective-permute-start.8 = (bf16[192,1024]{1,0:T(8,128)(2,1)}, bf16[192,1024]{1,0:T(8,128)(2,1)}, u32[]{:S(2)}, u32[]{:S(2)}) collective-permute-start(bf16[192,1024]{1,0:T(8,128)(2,1)} %pad_maximum_fusion), channel_id=1, source_target_pairs={{0,2},{1,3},{2,0},{3,1},{4,6},{5,7},{6,4},{7,5},{8,10},{9,11},{10,... | collective-permute-start | bytes 1179656 | tf_op jit(solution)/shard_map/ppermute | solution.py:44
  29.8 12.6 %copy-start.4 = (bf16[96,1024]{1,0:T(8,128)(2,1)S(1)}, bf16[96,1024]{1,0:T(8,128)(2,1)}, u32[]{:S(2)}) copy-start(bf16[96,1024]{1,0:T(8,128)(2,1)} %copy-done.3) | copy-start | bytes 589828
  45.3 14.3 %collective-permute-start.10 = (bf16[3136,1024]{1,0:T(8,128)(2,1)S(1)}, bf16[3136,1024]{1,0:T(8,128)(2,1)S(1)}, u32[]{:S(2)}, u32[]{:S(2)}) collective-permute-start(bf16[3136,1024]{1,0:T(8,128)(2,1)S(1)} %get-tuple-element.316), channel_id=1, source_target_pairs={{8,12},{9,13},{10,14},{11,15},{16,20},{17,21},{18,22},{19,23}} | collective-permute-start | bytes 19267592 | tf_op jit(solution)/shard_map/ppermute | solution.py:44
  46.4 0.7 collective-permute-start.6
  47.7 9.7 %collective-permute-start.9 = (bf16[64,4096]{1,0:T(8,128)(2,1)S(1)}, bf16[64,4096]{1,0:T(8,128)(2,1)S(1)}, u32[]{:S(2)}, u32[]{:S(2)}) collective-permute-start(bf16[64,4096]{1,0:T(8,128)(2,1)S(1)} %get-tuple-element.283), channel_id=1, source_target_pairs={{24,20},{25,21},{26,22},{27,23}} | collective-permute-start | bytes 1572872 | tf_op jit(solution)/shard_map/ppermute | solution.py:44
  49.0 21.8 %collective-permute-start.12 = (bf16[64,4096]{1,0:T(8,128)(2,1)S(1)}, bf16[64,4096]{1,0:T(8,128)(2,1)S(1)}, u32[]{:S(2)}, u32[]{:S(2)}) collective-permute-start(bf16[64,4096]{1,0:T(8,128)(2,1)S(1)} %get-tuple-element.318), channel_id=1, source_target_pairs={{24,20},{25,21},{26,22},{27,23}} | collective-permute-start | bytes 1572872 | tf_op jit(solution)/shard_map/ppermute | solution.py:44
  50.3 11.2 %collective-permute-start.13 = (bf16[128,1280]{1,0:T(8,128)(2,1)S(1)}, bf16[128,1280]{1,0:T(8,128)(2,1)S(1)}, u32[]{:S(2)}, u32[]{:S(2)}) collective-permute-start(bf16[128,1280]{1,0:T(8,128)(2,1)S(1)} %get-tuple-element.323), channel_id=1, source_target_pairs={{0,1},{1,0},{2,3},{3,2},{4,5},{5,4},{6,7},{7,6},{8,9},{9,8},{10,11... | collective-permute-start | bytes 983048 | tf_op jit(solution)/shard_map/ppermute | solution.py:44
  53.9 16.8 %collective-permute-start.14 = (bf16[128,1280]{1,0:T(8,128)(2,1)S(1)}, bf16[128,1280]{1,0:T(8,128)(2,1)S(1)}, u32[]{:S(2)}, u32[]{:S(2)}) collective-permute-start(bf16[128,1280]{1,0:T(8,128)(2,1)S(1)} %get-tuple-element.324), channel_id=1, source_target_pairs={{0,2},{1,3},{2,0},{3,1},{4,6},{5,7},{6,4},{7,5},{8,10},{9,11},{10,... | collective-permute-start | bytes 983048 | tf_op jit(solution)/shard_map/ppermute | solution.py:44
  57.4 13.4 %collective-permute-start.15 = (bf16[128,1280]{1,0:T(8,128)(2,1)S(1)}, bf16[128,1280]{1,0:T(8,128)(2,1)S(1)}, u32[]{:S(2)}, u32[]{:S(2)}) collective-permute-start(bf16[128,1280]{1,0:T(8,128)(2,1)S(1)} %get-tuple-element.325), channel_id=1, source_target_pairs={{0,3},{1,2},{2,1},{3,0},{4,7},{5,6},{6,5},{7,4},{8,11},{9,10},{10,... | collective-permute-start | bytes 983048 | tf_op jit(solution)/shard_map/ppermute | solution.py:44
  60.2 13.5 %collective-permute-start.11 = (bf16[64,4096]{1,0:T(8,128)(2,1)S(1)}, bf16[64,4096]{1,0:T(8,128)(2,1)S(1)}, u32[]{:S(2)}, u32[]{:S(2)}) collective-permute-start(bf16[64,4096]{1,0:T(8,128)(2,1)S(1)} %get-tuple-element.317), channel_id=1, source_target_pairs={{20,12},{21,13},{22,14},{23,15}} | collective-permute-start | bytes 1572872 | tf_op jit(solution)/shard_map/ppermute | solution.py:44
  71.5 3.4 %collective-permute-start.19 = (bf16[64,4096]{1,0:T(8,128)(2,1)S(1)}, bf16[64,4096]{1,0:T(8,128)(2,1)S(1)}, u32[]{:S(2)}, u32[]{:S(2)}) collective-permute-start(bf16[64,4096]{1,0:T(8,128)(2,1)S(1)} %get-tuple-element.359), channel_id=1, source_target_pairs={{20,12},{21,13},{22,14},{23,15}} | collective-permute-start | bytes 1572872 | tf_op jit(solution)/shard_map/ppermute | solution.py:44
  72.3 4.7 %collective-permute-start.18 = (bf16[64,4096]{1,0:T(8,128)(2,1)S(1)}, bf16[64,4096]{1,0:T(8,128)(2,1)S(1)}, u32[]{:S(2)}, u32[]{:S(2)}) collective-permute-start(bf16[64,4096]{1,0:T(8,128)(2,1)S(1)} %get-tuple-element.358), channel_id=1, source_target_pairs={{20,16},{21,17},{22,18},{23,19}} | collective-permute-start | bytes 1572872 | tf_op jit(solution)/shard_map/ppermute | solution.py:44
  73.0 4.7 %collective-permute-start.17 = (bf16[64,4096]{1,0:T(8,128)(2,1)S(1)}, bf16[64,4096]{1,0:T(8,128)(2,1)S(1)}, u32[]{:S(2)}, u32[]{:S(2)}) collective-permute-start(bf16[64,4096]{1,0:T(8,128)(2,1)S(1)} %get-tuple-element.357), channel_id=1, source_target_pairs={{20,16},{21,17},{22,18},{23,19}} | collective-permute-start | bytes 1572872 | tf_op jit(solution)/shard_map/ppermute | solution.py:44
  74.3 7.6 %collective-permute-start.16 = (bf16[64,4096]{1,0:T(8,128)(2,1)S(1)}, bf16[64,4096]{1,0:T(8,128)(2,1)S(1)}, u32[]{:S(2)}, u32[]{:S(2)}) collective-permute-start(bf16[64,4096]{1,0:T(8,128)(2,1)S(1)} %get-tuple-element.356), channel_id=1, source_target_pairs={{12,4},{13,5},{14,6},{15,7}} | collective-permute-start | bytes 1572872 | tf_op jit(solution)/shard_map/ppermute | solution.py:44
  75.6 8.2 %collective-permute-start.24 = (bf16[64,4096]{1,0:T(8,128)(2,1)S(1)}, bf16[64,4096]{1,0:T(8,128)(2,1)S(1)}, u32[]{:S(2)}, u32[]{:S(2)}) collective-permute-start(bf16[64,4096]{1,0:T(8,128)(2,1)S(1)} %get-tuple-element.427), channel_id=1, source_target_pairs={{12,4},{13,5},{14,6},{15,7}} | collective-permute-start | bytes 1572872 | tf_op jit(solution)/shard_map/ppermute | solution.py:44
  76.3 3.3 %collective-permute-start.20 = (bf16[128,1280]{1,0:T(8,128)(2,1)S(1)}, bf16[128,1280]{1,0:T(8,128)(2,1)S(1)}, u32[]{:S(2)}, u32[]{:S(2)}) collective-permute-start(bf16[128,1280]{1,0:T(8,128)(2,1)S(1)} %get-tuple-element.323), channel_id=1, source_target_pairs={{16,17},{17,16},{18,19},{19,18},{20,21},{21,20},{22,23},{23,22},{2... | collective-permute-start | bytes 983048 | tf_op jit(solution)/shard_map/ppermute | solution.py:44
  77.0 3.3 %collective-permute-start.21 = (bf16[128,1280]{1,0:T(8,128)(2,1)S(1)}, bf16[128,1280]{1,0:T(8,128)(2,1)S(1)}, u32[]{:S(2)}, u32[]{:S(2)}) collective-permute-start(bf16[128,1280]{1,0:T(8,128)(2,1)S(1)} %get-tuple-element.324), channel_id=1, source_target_pairs={{16,18},{17,19},{18,16},{19,17},{20,22},{21,23},{22,20},{23,21},{2... | collective-permute-start | bytes 983048 | tf_op jit(solution)/shard_map/ppermute | solution.py:44
  77.7 3.3 %collective-permute-start.22 = (bf16[128,1280]{1,0:T(8,128)(2,1)S(1)}, bf16[128,1280]{1,0:T(8,128)(2,1)S(1)}, u32[]{:S(2)}, u32[]{:S(2)}) collective-permute-start(bf16[128,1280]{1,0:T(8,128)(2,1)S(1)} %get-tuple-element.325), channel_id=1, source_target_pairs={{16,19},{17,18},{18,17},{19,16},{20,23},{21,22},{22,21},{23,20},{2... | collective-permute-start | bytes 983048 | tf_op jit(solution)/shard_map/ppermute | solution.py:44
  79.5 6.4 %collective-permute-start.27 = (bf16[64,4096]{1,0:T(8,128)(2,1)S(1)}, bf16[64,4096]{1,0:T(8,128)(2,1)S(1)}, u32[]{:S(2)}, u32[]{:S(2)}) collective-permute-start(bf16[64,4096]{1,0:T(8,128)(2,1)S(1)} %get-tuple-element.445), channel_id=1, source_target_pairs={{12,8},{13,9},{14,10},{15,11}} | collective-permute-start | bytes 1572872 | tf_op jit(solution)/shard_map/ppermute | solution.py:44
  80.2 6.3 %collective-permute-start.26 = (bf16[64,4096]{1,0:T(8,128)(2,1)S(1)}, bf16[64,4096]{1,0:T(8,128)(2,1)S(1)}, u32[]{:S(2)}, u32[]{:S(2)}) collective-permute-start(bf16[64,4096]{1,0:T(8,128)(2,1)S(1)} %get-tuple-element.444), channel_id=1, source_target_pairs={{12,8},{13,9},{14,10},{15,11}} | collective-permute-start | bytes 1572872 | tf_op jit(solution)/shard_map/ppermute | solution.py:44
  82.5 6.5 %collective-permute-start.23 = (bf16[64,4096]{1,0:T(8,128)(2,1)S(1)}, bf16[64,4096]{1,0:T(8,128)(2,1)S(1)}, u32[]{:S(2)}, u32[]{:S(2)}) collective-permute-start(bf16[64,4096]{1,0:T(8,128)(2,1)S(1)} %get-tuple-element.426), channel_id=1, source_target_pairs={{4,0},{5,1},{6,2},{7,3}} | collective-permute-start | bytes 1572872 | tf_op jit(solution)/shard_map/ppermute | solution.py:44
  84.6 10.2 %collective-permute-start.25 = (bf16[64,4096]{1,0:T(8,128)(2,1)S(1)}, bf16[64,4096]{1,0:T(8,128)(2,1)S(1)}, u32[]{:S(2)}, u32[]{:S(2)}) collective-permute-start(bf16[64,4096]{1,0:T(8,128)(2,1)S(1)} %get-tuple-element.443), channel_id=1, source_target_pairs={{4,0},{5,1},{6,2},{7,3}} | collective-permute-start | bytes 1572872 | tf_op jit(solution)/shard_map/ppermute | solution.py:44
  96.9 10.8 %collective-permute-start.28 = (bf16[128,1280]{1,0:T(8,128)(2,1)S(1)}, bf16[128,1280]{1,0:T(8,128)(2,1)S(1)}, u32[]{:S(2)}, u32[]{:S(2)}) collective-permute-start(bf16[128,1280]{1,0:T(8,128)(2,1)S(1)} %get-tuple-element.494), channel_id=1, source_target_pairs={{0,1},{1,0},{2,3},{3,2},{4,5},{5,4},{6,7},{7,6},{8,9},{9,8},{10,11... | collective-permute-start | bytes 983048 | tf_op jit(solution)/shard_map/ppermute | solution.py:44
  99.1 15.0 %collective-permute-start.29 = (bf16[128,1280]{1,0:T(8,128)(2,1)S(1)}, bf16[128,1280]{1,0:T(8,128)(2,1)S(1)}, u32[]{:S(2)}, u32[]{:S(2)}) collective-permute-start(bf16[128,1280]{1,0:T(8,128)(2,1)S(1)} %get-tuple-element.495), channel_id=1, source_target_pairs={{0,2},{1,3},{2,0},{3,1},{4,6},{5,7},{6,4},{7,5},{8,10},{9,11},{10,... | collective-permute-start | bytes 983048 | tf_op jit(solution)/shard_map/ppermute | solution.py:44
  100.0 14.1 %collective-permute-start.30 = (bf16[128,1280]{1,0:T(8,128)(2,1)S(1)}, bf16[128,1280]{1,0:T(8,128)(2,1)S(1)}, u32[]{:S(2)}, u32[]{:S(2)}) collective-permute-start(bf16[128,1280]{1,0:T(8,128)(2,1)S(1)} %get-tuple-element.496), channel_id=1, source_target_pairs={{0,3},{1,2},{2,1},{3,0},{4,7},{5,6},{6,5},{7,4},{8,11},{9,10},{10,... | collective-permute-start | bytes 983048 | tf_op jit(solution)/shard_map/ppermute | solution.py:44
  (6 other events, 16.9 us)

commit v8 on v7

--- a/solution.py
+++ b/solution.py
@@ -453,7 +453,7 @@
 
 
 def weight_kernel(size, left, *refs):
-    late = refs[:size]
+    late = refs[:1] + refs[size - 1 : 0 : -1]
     down_grads, up_grads, right = refs[size:]
     tokens = late[0].shape[0]
     shard = down_grads.shape[0]
@@ -721,7 +721,7 @@
         out_specs=(VMEM,) * 2,
         scratch_shapes=[pltpu.VMEM((size * tokens, shard + latent_width), bf16)],
         compiler_params=PARAMS,
-    )(pin(left), *late)
+    )(pin(left), late[0], *late[:0:-1])
     return (state[6][None], down_grads[None], up_grads[None])
 
 

time: 116 us -> 116 us (level)
  transfers between devices with their start and end apart: 31 -> 31, of which waited for: 12 -> 13; matrix products, arithmetic and copies ran while one was open for 2% -> 2% of each run, Pallas kernels for 9% -> 9%
where the time goes in v8:
time: 116 us; the launch traced here: 115 us
  waiting for transfers between devices  48.1 us (41%)
  starting transfers between devices  40.7 us (35%)
  Pallas kernels  18.8 us (16%)
  local copies, waits for them, and re-layouts  4.68 us (4%)
  other arithmetic  1.54 us (1%)
    ppermute x31, waiting for transfers between devices, move(): return lax.ppermute(block, ('section', 'dp'), pairs)  48.1 us
    ppermute x31, starting transfers between devices, move(): return lax.ppermute(block, ('section', 'dp'), pairs)  40.7 us
    pallas_call x9, Pallas kernels, run_stage(): pl.pallas_call(functools.partial(stage_kernel, stage, bounds, size, len(s...  6.95 us
    unnamed x15, local copies, waits for them, and re-layouts  4.44 us
    pallas_call x1, Pallas kernels, per_device(): pl.pallas_call(functools.partial(keep_kernel, size, len(shards), more), o...  2.83 us
    pallas_call x4, Pallas kernels, run_pair(): pl.pallas_call(functools.partial(pair_kernel, stage, bound, size, len(sta...  2.49 us
  transfers between devices with their start and end apart: 31, of which 13 were waited for; matrix products, arithmetic and copies ran while one was open for 2% of the time, Pallas kernels for 9%

profile of v8, /device:TPU:0, one launch (start us, length us, event | category | flops | bytes accessed | tf_op | source)
XLA Modules:
  0.0 114.9 jit_solution(11531868297360150386)
XLA Ops:
  0.7 2.1 %shard_map.95 = (bf16[416,512]{1,0:T(8,128)(2,1)S(1)}, bf16[416,512]{1,0:T(8,128)(2,1)S(1)}, bf16[96,1024]{1,0:T(8,128)(2,1)S(1)}) custom-call(s32[5]{0:T(128)S(1)} %stack.35.flags.refs_0_, bf16[1,1024,256]{2,1,0:T(8,128)(2,1)} %down.1, bf16[1,256,1024]{2,1,0:T(8,128)(2,1)} %up.1, bf16[1024,128]{1,0:T(8,128)(2,1)} %readout.1), custom_call_target="tpu_custom_call" | custom-call | tf_op jit(solution)/shard_map/pallas_call | solution.py:498
  2.8 3.0 %collective-permute-start.2 = (bf16[416,512]{1,0:T(8,128)(2,1)S(1)}, bf16[416,512]{1,0:T(8,128)(2,1)S(1)}, u32[]{:S(2)}, u32[]{:S(2)}) collective-permute-start(bf16[416,512]{1,0:T(8,128)(2,1)S(1)} %get-tuple-element.256.refs_7_.refs_9_), channel_id=1, source_target_pairs={{0,2},{1,3},{2,0},{3,1},{4,6},{5,7},{6,4},{7,5},{8,10},{9,11},{10,... | collective-permute-start | bytes 1277960 | tf_op jit(solution)/shard_map/ppermute | solution.py:44
  5.8 1.5 %collective-permute-start.1 = (bf16[416,512]{1,0:T(8,128)(2,1)S(1)}, bf16[416,512]{1,0:T(8,128)(2,1)S(1)}, u32[]{:S(2)}, u32[]{:S(2)}) collective-permute-start(bf16[416,512]{1,0:T(8,128)(2,1)S(1)} %get-tuple-element.257.refs_8_.refs_10_), channel_id=1, source_target_pairs={{0,1},{1,0},{2,3},{3,2},{4,5},{5,4},{6,7},{7,6},{8,9},{9,8},{10,11... | collective-permute-start | bytes 1277960 | tf_op jit(solution)/shard_map/ppermute | solution.py:44
  7.3 2.4 %collective-permute-start.7 = (bf16[96,1024]{1,0:T(8,128)(2,1)S(1)}, bf16[96,1024]{1,0:T(8,128)(2,1)S(1)}, u32[]{:S(2)}, u32[]{:S(2)}) collective-permute-start(bf16[96,1024]{1,0:T(8,128)(2,1)S(1)} %get-tuple-element.267.refs_17_), channel_id=1, source_target_pairs={{0,1},{1,0},{2,3},{3,2},{4,5},{5,4},{6,7},{7,6},{8,9},{9,8},{10,11... | collective-permute-start | bytes 589832 | tf_op jit(solution)/shard_map/ppermute | solution.py:44
  9.8 1.6 %collective-permute-start = (bf16[416,512]{1,0:T(8,128)(2,1)S(1)}, bf16[416,512]{1,0:T(8,128)(2,1)S(1)}, u32[]{:S(2)}, u32[]{:S(2)}) collective-permute-start(bf16[416,512]{1,0:T(8,128)(2,1)S(1)} %get-tuple-element.256.refs_7_.refs_9_), channel_id=1, source_target_pairs={{0,1},{1,0},{2,3},{3,2},{4,5},{5,4},{6,7},{7,6},{8,9},{9,8},{10,11... | collective-permute-start | bytes 1277960 | tf_op jit(solution)/shard_map/ppermute | solution.py:44
  11.8 4.7 %collective-permute-done.2.refs_11_.refs_13_ = bf16[416,512]{1,0:T(8,128)(2,1)S(1)} collective-permute-done((bf16[416,512]{1,0:T(8,128)(2,1)S(1)}, bf16[416,512]{1,0:T(8,128)(2,1)S(1)}, u32[]{:S(2)}, u32[]{:S(2)}) %collective-permute-start.2) | collective-permute-done | bytes 426016 | tf_op jit(solution)/shard_map/ppermute | solution.py:44
  16.5 2.0 %collective-permute-start.4 = (bf16[416,512]{1,0:T(8,128)(2,1)S(1)}, bf16[416,512]{1,0:T(8,128)(2,1)S(1)}, u32[]{:S(2)}, u32[]{:S(2)}) collective-permute-start(bf16[416,512]{1,0:T(8,128)(2,1)S(1)} %collective-permute-done.2.refs_11_.refs_13_), channel_id=1, source_target_pairs={{0,1},{1,0},{2,3},{3,2},{4,5},{5,4},{6,7},{7,6},{8,9},{9,8},{10,11... | collective-permute-start | bytes 1277960 | tf_op jit(solution)/shard_map/ppermute | solution.py:44
  18.6 1.5 %collective-permute-start.5 = (bf16[416,512]{1,0:T(8,128)(2,1)S(1)}, bf16[416,512]{1,0:T(8,128)(2,1)S(1)}, u32[]{:S(2)}, u32[]{:S(2)}) collective-permute-start(bf16[416,512]{1,0:T(8,128)(2,1)S(1)} %collective-permute-done.1.refs_10_.refs_12_), channel_id=1, source_target_pairs={{0,2},{1,3},{2,0},{3,1},{4,6},{5,7},{6,4},{7,5},{8,10},{9,11},{10,... | collective-permute-start | bytes 1277960 | tf_op jit(solution)/shard_map/ppermute | solution.py:44
  20.0 2.8 %collective-permute-done.7.refs_18_ = bf16[96,1024]{1,0:T(8,128)(2,1)S(1)} collective-permute-done((bf16[96,1024]{1,0:T(8,128)(2,1)S(1)}, bf16[96,1024]{1,0:T(8,128)(2,1)S(1)}, u32[]{:S(2)}, u32[]{:S(2)}) %collective-permute-start.7) | collective-permute-done | bytes 196640 | tf_op jit(solution)/shard_map/ppermute | solution.py:44
  24.3 1.9 %collective-permute-start.8 = (bf16[192,1024]{1,0:T(8,128)(2,1)}, bf16[192,1024]{1,0:T(8,128)(2,1)}, u32[]{:S(2)}, u32[]{:S(2)}) collective-permute-start(bf16[192,1024]{1,0:T(8,128)(2,1)} %pad_maximum_fusion), channel_id=1, source_target_pairs={{0,2},{1,3},{2,0},{3,1},{4,6},{5,7},{6,4},{7,5},{8,10},{9,11},{10,... | collective-permute-start | bytes 1179656 | tf_op jit(solution)/shard_map/ppermute | solution.py:44
  27.0 1.2 %copy-done = bf16[1,128,4096]{2,1,0:T(8,128)(2,1)S(1)} copy-done((bf16[1,128,4096]{2,1,0:T(8,128)(2,1)S(1)}, bf16[1,128,4096]{2,1,0:T(8,128)(2,1)}, u32[]{:S(2)}) %copy-start) | copy-done | bytes 1048600
  30.5 1.4 %collective-permute-done.refs_9_.refs_11_ = bf16[416,512]{1,0:T(8,128)(2,1)S(1)} collective-permute-done((bf16[416,512]{1,0:T(8,128)(2,1)S(1)}, bf16[416,512]{1,0:T(8,128)(2,1)S(1)}, u32[]{:S(2)}, u32[]{:S(2)}) %collective-permute-start) | collective-permute-done | bytes 426016 | tf_op jit(solution)/shard_map/ppermute | solution.py:44
  31.9 7.7 %collective-permute-done.4.refs_13_.refs_15_ = bf16[416,512]{1,0:T(8,128)(2,1)S(1)} collective-permute-done((bf16[416,512]{1,0:T(8,128)(2,1)S(1)}, bf16[416,512]{1,0:T(8,128)(2,1)S(1)}, u32[]{:S(2)}, u32[]{:S(2)}) %collective-permute-start.4) | collective-permute-done | bytes 426016 | tf_op jit(solution)/shard_map/ppermute | solution.py:44
  40.2 2.2 %collective-permute-done.8.refs_19_ = bf16[192,1024]{1,0:T(8,128)(2,1)} collective-permute-done((bf16[192,1024]{1,0:T(8,128)(2,1)}, bf16[192,1024]{1,0:T(8,128)(2,1)}, u32[]{:S(2)}, u32[]{:S(2)}) %collective-permute-start.8) | collective-permute-done | bytes 393248 | tf_op jit(solution)/shard_map/ppermute | solution.py:44
  42.4 2.8 %shard_map.97 = (bf16[1,4096]{1,0:T(2,128)(2,1)S(1)}, f32[128,128]{1,0:T(8,128)S(1)}, f32[128,256]{1,0:T(8,128)S(1)}, bf16[128,4096]{1,0:T(8,128)(2,1)S(1)}, bf1...) custom-call(s32[5]{0:T(128)S(1)} %stack.35.flags.refs_0_, ...), custom_call_target="tpu_custom_call", output_to_operand_aliasing={{0}: (1, {}), {1}: (2, {}), {2}: (3, {}), {3}: (4, {}), {4}... | custom-call | tf_op jit(solution)/shard_map/pallas_call | solution.py:625
  45.3 1.1 collective-permute-start.10
  50.3 3.6 %collective-permute-start.13 = (bf16[128,1280]{1,0:T(8,128)(2,1)S(1)}, bf16[128,1280]{1,0:T(8,128)(2,1)S(1)}, u32[]{:S(2)}, u32[]{:S(2)}) collective-permute-start(bf16[128,1280]{1,0:T(8,128)(2,1)S(1)} %get-tuple-element.323), channel_id=1, source_target_pairs={{0,1},{1,0},{2,3},{3,2},{4,5},{5,4},{6,7},{7,6},{8,9},{9,8},{10,11... | collective-permute-start | bytes 983048 | tf_op jit(solution)/shard_map/ppermute | solution.py:44
  53.9 3.4 %collective-permute-start.14 = (bf16[128,1280]{1,0:T(8,128)(2,1)S(1)}, bf16[128,1280]{1,0:T(8,128)(2,1)S(1)}, u32[]{:S(2)}, u32[]{:S(2)}) collective-permute-start(bf16[128,1280]{1,0:T(8,128)(2,1)S(1)} %get-tuple-element.324), channel_id=1, source_target_pairs={{0,2},{1,3},{2,0},{3,1},{4,6},{5,7},{6,4},{7,5},{8,10},{9,11},{10,... | collective-permute-start | bytes 983048 | tf_op jit(solution)/shard_map/ppermute | solution.py:44
  57.4 2.2 %collective-permute-start.15 = (bf16[128,1280]{1,0:T(8,128)(2,1)S(1)}, bf16[128,1280]{1,0:T(8,128)(2,1)S(1)}, u32[]{:S(2)}, u32[]{:S(2)}) collective-permute-start(bf16[128,1280]{1,0:T(8,128)(2,1)S(1)} %get-tuple-element.325), channel_id=1, source_target_pairs={{0,3},{1,2},{2,1},{3,0},{4,7},{5,6},{6,5},{7,4},{8,11},{9,10},{10,... | collective-permute-start | bytes 983048 | tf_op jit(solution)/shard_map/ppermute | solution.py:44
  61.5 9.2 %collective-permute-done.14.refs_3_ = bf16[128,1280]{1,0:T(8,128)(2,1)S(1)} collective-permute-done((bf16[128,1280]{1,0:T(8,128)(2,1)S(1)}, bf16[128,1280]{1,0:T(8,128)(2,1)S(1)}, u32[]{:S(2)}, u32[]{:S(2)}) %collective-permute-start.14) | collective-permute-done | bytes 327712 | tf_op jit(solution)/shard_map/ppermute | solution.py:44
  80.9 0.9 shard_map.108
  82.5 1.3 %collective-permute-start.23 = (bf16[64,4096]{1,0:T(8,128)(2,1)S(1)}, bf16[64,4096]{1,0:T(8,128)(2,1)S(1)}, u32[]{:S(2)}, u32[]{:S(2)}) collective-permute-start(bf16[64,4096]{1,0:T(8,128)(2,1)S(1)} %get-tuple-element.426), channel_id=1, source_target_pairs={{4,0},{5,1},{6,2},{7,3}} | collective-permute-start | bytes 1572872 | tf_op jit(solution)/shard_map/ppermute | solution.py:44
  84.6 1.3 %collective-permute-start.25 = (bf16[64,4096]{1,0:T(8,128)(2,1)S(1)}, bf16[64,4096]{1,0:T(8,128)(2,1)S(1)}, u32[]{:S(2)}, u32[]{:S(2)}) collective-permute-start(bf16[64,4096]{1,0:T(8,128)(2,1)S(1)} %get-tuple-element.443), channel_id=1, source_target_pairs={{4,0},{5,1},{6,2},{7,3}} | collective-permute-start | bytes 1572872 | tf_op jit(solution)/shard_map/ppermute | solution.py:44
  87.1 1.8 %collective-permute-done.23.refs_1_ = bf16[64,4096]{1,0:T(8,128)(2,1)S(1)} collective-permute-done((bf16[64,4096]{1,0:T(8,128)(2,1)S(1)}, bf16[64,4096]{1,0:T(8,128)(2,1)S(1)}, u32[]{:S(2)}, u32[]{:S(2)}) %collective-permute-start.23) | collective-permute-done | bytes 524320 | tf_op jit(solution)/shard_map/ppermute | solution.py:44
  88.9 5.8 %collective-permute-done.25.refs_2_ = bf16[64,4096]{1,0:T(8,128)(2,1)S(1)} collective-permute-done((bf16[64,4096]{1,0:T(8,128)(2,1)S(1)}, bf16[64,4096]{1,0:T(8,128)(2,1)S(1)}, u32[]{:S(2)}, u32[]{:S(2)}) %collective-permute-start.25) | collective-permute-done | bytes 524320 | tf_op jit(solution)/shard_map/ppermute | solution.py:44
  94.8 2.1 %shard_map.113 = (bf16[1,4096]{1,0:T(2,128)(2,1)S(1)}, f32[128,128]{1,0:T(8,128)S(1)}, f32[128,256]{1,0:T(8,128)S(1)}, bf16[128,4096]{1,0:T(8,128)(2,1)S(1)}, bf...) custom-call(s32[5]{0:T(128)S(1)} %stack.35.flags.refs_0_, ...), custom_call_target="tpu_custom_call", output_to_operand_aliasing={{0}: (3, {}), {1}: (4, {}), {2}: (5, {}), {3}: (6, {}), {4}... | custom-call | tf_op jit(solution)/shard_map/pallas_call | solution.py:585
  96.9 2.5 %collective-permute-start.28 = (bf16[128,1280]{1,0:T(8,128)(2,1)S(1)}, bf16[128,1280]{1,0:T(8,128)(2,1)S(1)}, u32[]{:S(2)}, u32[]{:S(2)}) collective-permute-start(bf16[128,1280]{1,0:T(8,128)(2,1)S(1)} %get-tuple-element.494), channel_id=1, source_target_pairs={{0,3},{1,2},{2,1},{3,0},{4,7},{5,6},{6,5},{7,4},{8,11},{9,10},{10,... | collective-permute-start | bytes 983048 | tf_op jit(solution)/shard_map/ppermute | solution.py:44
  99.4 1.1 collective-permute-start.29
  100.6 1.0 copy.446
  101.5 7.0 %collective-permute-done.28.refs_1_ = bf16[128,1280]{1,0:T(8,128)(2,1)S(1)} collective-permute-done((bf16[128,1280]{1,0:T(8,128)(2,1)S(1)}, bf16[128,1280]{1,0:T(8,128)(2,1)S(1)}, u32[]{:S(2)}, u32[]{:S(2)}) %collective-permute-start.28) | collective-permute-done | bytes 327712 | tf_op jit(solution)/shard_map/ppermute | solution.py:44
  108.6 4.6 %collective-permute-done.29.refs_2_ = bf16[128,1280]{1,0:T(8,128)(2,1)S(1)} collective-permute-done((bf16[128,1280]{1,0:T(8,128)(2,1)S(1)}, bf16[128,1280]{1,0:T(8,128)(2,1)S(1)}, u32[]{:S(2)}, u32[]{:S(2)}) %collective-permute-start.29) | collective-permute-done | bytes 327712 | tf_op jit(solution)/shard_map/ppermute | solution.py:44
  113.3 1.7 %shard_map.114 = (bf16[1024,256]{1,0:T(8,128)(2,1)}, bf16[256,1024]{1,0:T(8,128)(2,1)}) custom-call(bf16[1280,512]{1,0:T(8,128)(2,1)S(1)} %get-tuple-element.492.left, bf16[128,1280]{1,0:T(8,128)(2,1)S(1)} %get-tuple-element.493.refs_0_, bf16[128,1280]{1,0:T(8,128)(2,1)S(1)} %collective-permute-done.28.refs_1_, ...), custom_call_target="tpu_custom_call" | custom-call | tf_op jit(solution)/shard_map/pallas_call | solution.py:714
  (71 shorter events, 24.3 us)
Async XLA Ops:
  2.8 13.7 %collective-permute-start.2 = (bf16[416,512]{1,0:T(8,128)(2,1)S(1)}, bf16[416,512]{1,0:T(8,128)(2,1)S(1)}, u32[]{:S(2)}, u32[]{:S(2)}) collective-permute-start(bf16[416,512]{1,0:T(8,128)(2,1)S(1)} %get-tuple-element.256.refs_7_.refs_9_), channel_id=1, source_target_pairs={{0,2},{1,3},{2,0},{3,1},{4,6},{5,7},{6,4},{7,5},{8,10},{9,11},{10,... | collective-permute-start | bytes 1277960 | tf_op jit(solution)/shard_map/ppermute | solution.py:44
  5.8 12.7 %collective-permute-start.1 = (bf16[416,512]{1,0:T(8,128)(2,1)S(1)}, bf16[416,512]{1,0:T(8,128)(2,1)S(1)}, u32[]{:S(2)}, u32[]{:S(2)}) collective-permute-start(bf16[416,512]{1,0:T(8,128)(2,1)S(1)} %get-tuple-element.257.refs_8_.refs_10_), channel_id=1, source_target_pairs={{0,1},{1,0},{2,3},{3,2},{4,5},{5,4},{6,7},{7,6},{8,9},{9,8},{10,11... | collective-permute-start | bytes 1277960 | tf_op jit(solution)/shard_map/ppermute | solution.py:44
  7.3 15.5 %collective-permute-start.7 = (bf16[96,1024]{1,0:T(8,128)(2,1)S(1)}, bf16[96,1024]{1,0:T(8,128)(2,1)S(1)}, u32[]{:S(2)}, u32[]{:S(2)}) collective-permute-start(bf16[96,1024]{1,0:T(8,128)(2,1)S(1)} %get-tuple-element.267.refs_17_), channel_id=1, source_target_pairs={{0,1},{1,0},{2,3},{3,2},{4,5},{5,4},{6,7},{7,6},{8,9},{9,8},{10,11... | collective-permute-start | bytes 589832 | tf_op jit(solution)/shard_map/ppermute | solution.py:44
  9.8 22.2 %collective-permute-start = (bf16[416,512]{1,0:T(8,128)(2,1)S(1)}, bf16[416,512]{1,0:T(8,128)(2,1)S(1)}, u32[]{:S(2)}, u32[]{:S(2)}) collective-permute-start(bf16[416,512]{1,0:T(8,128)(2,1)S(1)} %get-tuple-element.256.refs_7_.refs_9_), channel_id=1, source_target_pairs={{0,1},{1,0},{2,3},{3,2},{4,5},{5,4},{6,7},{7,6},{8,9},{9,8},{10,11... | collective-permute-start | bytes 1277960 | tf_op jit(solution)/shard_map/ppermute | solution.py:44
  11.3 20.6 %collective-permute-start.3 = (bf16[416,512]{1,0:T(8,128)(2,1)S(1)}, bf16[416,512]{1,0:T(8,128)(2,1)S(1)}, u32[]{:S(2)}, u32[]{:S(2)}) collective-permute-start(bf16[416,512]{1,0:T(8,128)(2,1)S(1)} %get-tuple-element.257.refs_8_.refs_10_), channel_id=1, source_target_pairs={{0,2},{1,3},{2,0},{3,1},{4,6},{5,7},{6,4},{7,5},{8,10},{9,11},{10,... | collective-permute-start | bytes 1277960 | tf_op jit(solution)/shard_map/ppermute | solution.py:44
  16.5 23.1 %collective-permute-start.4 = (bf16[416,512]{1,0:T(8,128)(2,1)S(1)}, bf16[416,512]{1,0:T(8,128)(2,1)S(1)}, u32[]{:S(2)}, u32[]{:S(2)}) collective-permute-start(bf16[416,512]{1,0:T(8,128)(2,1)S(1)} %collective-permute-done.2.refs_11_.refs_13_), channel_id=1, source_target_pairs={{0,1},{1,0},{2,3},{3,2},{4,5},{5,4},{6,7},{7,6},{8,9},{9,8},{10,11... | collective-permute-start | bytes 1277960 | tf_op jit(solution)/shard_map/ppermute | solution.py:44
  18.6 21.0 %collective-permute-start.5 = (bf16[416,512]{1,0:T(8,128)(2,1)S(1)}, bf16[416,512]{1,0:T(8,128)(2,1)S(1)}, u32[]{:S(2)}, u32[]{:S(2)}) collective-permute-start(bf16[416,512]{1,0:T(8,128)(2,1)S(1)} %collective-permute-done.1.refs_10_.refs_12_), channel_id=1, source_target_pairs={{0,2},{1,3},{2,0},{3,1},{4,6},{5,7},{6,4},{7,5},{8,10},{9,11},{10,... | collective-permute-start | bytes 1277960 | tf_op jit(solution)/shard_map/ppermute | solution.py:44
  24.3 18.2 %collective-permute-start.8 = (bf16[192,1024]{1,0:T(8,128)(2,1)}, bf16[192,1024]{1,0:T(8,128)(2,1)}, u32[]{:S(2)}, u32[]{:S(2)}) collective-permute-start(bf16[192,1024]{1,0:T(8,128)(2,1)} %pad_maximum_fusion), channel_id=1, source_target_pairs={{0,2},{1,3},{2,0},{3,1},{4,6},{5,7},{6,4},{7,5},{8,10},{9,11},{10,... | collective-permute-start | bytes 1179656 | tf_op jit(solution)/shard_map/ppermute | solution.py:44
  29.8 12.6 %copy-start.4 = (bf16[96,1024]{1,0:T(8,128)(2,1)S(1)}, bf16[96,1024]{1,0:T(8,128)(2,1)}, u32[]{:S(2)}) copy-start(bf16[96,1024]{1,0:T(8,128)(2,1)} %copy-done.3) | copy-start | bytes 589828
  45.3 14.3 %collective-permute-start.10 = (bf16[3136,1024]{1,0:T(8,128)(2,1)S(1)}, bf16[3136,1024]{1,0:T(8,128)(2,1)S(1)}, u32[]{:S(2)}, u32[]{:S(2)}) collective-permute-start(bf16[3136,1024]{1,0:T(8,128)(2,1)S(1)} %get-tuple-element.316), channel_id=1, source_target_pairs={{8,12},{9,13},{10,14},{11,15},{16,20},{17,21},{18,22},{19,23}} | collective-permute-start | bytes 19267592 | tf_op jit(solution)/shard_map/ppermute | solution.py:44
  46.4 0.7 collective-permute-start.6
  47.7 9.7 %collective-permute-start.9 = (bf16[64,4096]{1,0:T(8,128)(2,1)S(1)}, bf16[64,4096]{1,0:T(8,128)(2,1)S(1)}, u32[]{:S(2)}, u32[]{:S(2)}) collective-permute-start(bf16[64,4096]{1,0:T(8,128)(2,1)S(1)} %get-tuple-element.283), channel_id=1, source_target_pairs={{24,20},{25,21},{26,22},{27,23}} | collective-permute-start | bytes 1572872 | tf_op jit(solution)/shard_map/ppermute | solution.py:44
  49.0 21.8 %collective-permute-start.12 = (bf16[64,4096]{1,0:T(8,128)(2,1)S(1)}, bf16[64,4096]{1,0:T(8,128)(2,1)S(1)}, u32[]{:S(2)}, u32[]{:S(2)}) collective-permute-start(bf16[64,4096]{1,0:T(8,128)(2,1)S(1)} %get-tuple-element.318), channel_id=1, source_target_pairs={{24,20},{25,21},{26,22},{27,23}} | collective-permute-start | bytes 1572872 | tf_op jit(solution)/shard_map/ppermute | solution.py:44
  50.3 11.2 %collective-permute-start.13 = (bf16[128,1280]{1,0:T(8,128)(2,1)S(1)}, bf16[128,1280]{1,0:T(8,128)(2,1)S(1)}, u32[]{:S(2)}, u32[]{:S(2)}) collective-permute-start(bf16[128,1280]{1,0:T(8,128)(2,1)S(1)} %get-tuple-element.323), channel_id=1, source_target_pairs={{0,1},{1,0},{2,3},{3,2},{4,5},{5,4},{6,7},{7,6},{8,9},{9,8},{10,11... | collective-permute-start | bytes 983048 | tf_op jit(solution)/shard_map/ppermute | solution.py:44
  53.9 16.8 %collective-permute-start.14 = (bf16[128,1280]{1,0:T(8,128)(2,1)S(1)}, bf16[128,1280]{1,0:T(8,128)(2,1)S(1)}, u32[]{:S(2)}, u32[]{:S(2)}) collective-permute-start(bf16[128,1280]{1,0:T(8,128)(2,1)S(1)} %get-tuple-element.324), channel_id=1, source_target_pairs={{0,2},{1,3},{2,0},{3,1},{4,6},{5,7},{6,4},{7,5},{8,10},{9,11},{10,... | collective-permute-start | bytes 983048 | tf_op jit(solution)/shard_map/ppermute | solution.py:44
  57.4 13.4 %collective-permute-start.15 = (bf16[128,1280]{1,0:T(8,128)(2,1)S(1)}, bf16[128,1280]{1,0:T(8,128)(2,1)S(1)}, u32[]{:S(2)}, u32[]{:S(2)}) collective-permute-start(bf16[128,1280]{1,0:T(8,128)(2,1)S(1)} %get-tuple-element.325), channel_id=1, source_target_pairs={{0,3},{1,2},{2,1},{3,0},{4,7},{5,6},{6,5},{7,4},{8,11},{9,10},{10,... | collective-permute-start | bytes 983048 | tf_op jit(solution)/shard_map/ppermute | solution.py:44
  60.2 13.5 %collective-permute-start.11 = (bf16[64,4096]{1,0:T(8,128)(2,1)S(1)}, bf16[64,4096]{1,0:T(8,128)(2,1)S(1)}, u32[]{:S(2)}, u32[]{:S(2)}) collective-permute-start(bf16[64,4096]{1,0:T(8,128)(2,1)S(1)} %get-tuple-element.317), channel_id=1, source_target_pairs={{20,12},{21,13},{22,14},{23,15}} | collective-permute-start | bytes 1572872 | tf_op jit(solution)/shard_map/ppermute | solution.py:44
  71.5 3.4 %collective-permute-start.19 = (bf16[64,4096]{1,0:T(8,128)(2,1)S(1)}, bf16[64,4096]{1,0:T(8,128)(2,1)S(1)}, u32[]{:S(2)}, u32[]{:S(2)}) collective-permute-start(bf16[64,4096]{1,0:T(8,128)(2,1)S(1)} %get-tuple-element.359), channel_id=1, source_target_pairs={{20,12},{21,13},{22,14},{23,15}} | collective-permute-start | bytes 1572872 | tf_op jit(solution)/shard_map/ppermute | solution.py:44
  72.3 4.7 %collective-permute-start.18 = (bf16[64,4096]{1,0:T(8,128)(2,1)S(1)}, bf16[64,4096]{1,0:T(8,128)(2,1)S(1)}, u32[]{:S(2)}, u32[]{:S(2)}) collective-permute-start(bf16[64,4096]{1,0:T(8,128)(2,1)S(1)} %get-tuple-element.358), channel_id=1, source_target_pairs={{20,16},{21,17},{22,18},{23,19}} | collective-permute-start | bytes 1572872 | tf_op jit(solution)/shard_map/ppermute | solution.py:44
  73.0 4.7 %collective-permute-start.17 = (bf16[64,4096]{1,0:T(8,128)(2,1)S(1)}, bf16[64,4096]{1,0:T(8,128)(2,1)S(1)}, u32[]{:S(2)}, u32[]{:S(2)}) collective-permute-start(bf16[64,4096]{1,0:T(8,128)(2,1)S(1)} %get-tuple-element.357), channel_id=1, source_target_pairs={{20,16},{21,17},{22,18},{23,19}} | collective-permute-start | bytes 1572872 | tf_op jit(solution)/shard_map/ppermute | solution.py:44
  74.3 7.6 %collective-permute-start.16 = (bf16[64,4096]{1,0:T(8,128)(2,1)S(1)}, bf16[64,4096]{1,0:T(8,128)(2,1)S(1)}, u32[]{:S(2)}, u32[]{:S(2)}) collective-permute-start(bf16[64,4096]{1,0:T(8,128)(2,1)S(1)} %get-tuple-element.356), channel_id=1, source_target_pairs={{12,4},{13,5},{14,6},{15,7}} | collective-permute-start | bytes 1572872 | tf_op jit(solution)/shard_map/ppermute | solution.py:44
  75.6 8.2 %collective-permute-start.24 = (bf16[64,4096]{1,0:T(8,128)(2,1)S(1)}, bf16[64,4096]{1,0:T(8,128)(2,1)S(1)}, u32[]{:S(2)}, u32[]{:S(2)}) collective-permute-start(bf16[64,4096]{1,0:T(8,128)(2,1)S(1)} %get-tuple-element.427), channel_id=1, source_target_pairs={{12,4},{13,5},{14,6},{15,7}} | collective-permute-start | bytes 1572872 | tf_op jit(solution)/shard_map/ppermute | solution.py:44
  76.3 3.3 %collective-permute-start.20 = (bf16[128,1280]{1,0:T(8,128)(2,1)S(1)}, bf16[128,1280]{1,0:T(8,128)(2,1)S(1)}, u32[]{:S(2)}, u32[]{:S(2)}) collective-permute-start(bf16[128,1280]{1,0:T(8,128)(2,1)S(1)} %get-tuple-element.323), channel_id=1, source_target_pairs={{16,17},{17,16},{18,19},{19,18},{20,21},{21,20},{22,23},{23,22},{2... | collective-permute-start | bytes 983048 | tf_op jit(solution)/shard_map/ppermute | solution.py:44
  77.0 3.3 %collective-permute-start.21 = (bf16[128,1280]{1,0:T(8,128)(2,1)S(1)}, bf16[128,1280]{1,0:T(8,128)(2,1)S(1)}, u32[]{:S(2)}, u32[]{:S(2)}) collective-permute-start(bf16[128,1280]{1,0:T(8,128)(2,1)S(1)} %get-tuple-element.324), channel_id=1, source_target_pairs={{16,18},{17,19},{18,16},{19,17},{20,22},{21,23},{22,20},{23,21},{2... | collective-permute-start | bytes 983048 | tf_op jit(solution)/shard_map/ppermute | solution.py:44
  77.7 3.3 %collective-permute-start.22 = (bf16[128,1280]{1,0:T(8,128)(2,1)S(1)}, bf16[128,1280]{1,0:T(8,128)(2,1)S(1)}, u32[]{:S(2)}, u32[]{:S(2)}) collective-permute-start(bf16[128,1280]{1,0:T(8,128)(2,1)S(1)} %get-tuple-element.325), channel_id=1, source_target_pairs={{16,19},{17,18},{18,17},{19,16},{20,23},{21,22},{22,21},{23,20},{2... | collective-permute-start | bytes 983048 | tf_op jit(solution)/shard_map/ppermute | solution.py:44
  79.5 6.4 %collective-permute-start.27 = (bf16[64,4096]{1,0:T(8,128)(2,1)S(1)}, bf16[64,4096]{1,0:T(8,128)(2,1)S(1)}, u32[]{:S(2)}, u32[]{:S(2)}) collective-permute-start(bf16[64,4096]{1,0:T(8,128)(2,1)S(1)} %get-tuple-element.445), channel_id=1, source_target_pairs={{12,8},{13,9},{14,10},{15,11}} | collective-permute-start | bytes 1572872 | tf_op jit(solution)/shard_map/ppermute | solution.py:44
  80.2 6.3 %collective-permute-start.26 = (bf16[64,4096]{1,0:T(8,128)(2,1)S(1)}, bf16[64,4096]{1,0:T(8,128)(2,1)S(1)}, u32[]{:S(2)}, u32[]{:S(2)}) collective-permute-start(bf16[64,4096]{1,0:T(8,128)(2,1)S(1)} %get-tuple-element.444), channel_id=1, source_target_pairs={{12,8},{13,9},{14,10},{15,11}} | collective-permute-start | bytes 1572872 | tf_op jit(solution)/shard_map/ppermute | solution.py:44
  82.5 6.5 %collective-permute-start.23 = (bf16[64,4096]{1,0:T(8,128)(2,1)S(1)}, bf16[64,4096]{1,0:T(8,128)(2,1)S(1)}, u32[]{:S(2)}, u32[]{:S(2)}) collective-permute-start(bf16[64,4096]{1,0:T(8,128)(2,1)S(1)} %get-tuple-element.426), channel_id=1, source_target_pairs={{4,0},{5,1},{6,2},{7,3}} | collective-permute-start | bytes 1572872 | tf_op jit(solution)/shard_map/ppermute | solution.py:44
  84.6 10.2 %collective-permute-start.25 = (bf16[64,4096]{1,0:T(8,128)(2,1)S(1)}, bf16[64,4096]{1,0:T(8,128)(2,1)S(1)}, u32[]{:S(2)}, u32[]{:S(2)}) collective-permute-start(bf16[64,4096]{1,0:T(8,128)(2,1)S(1)} %get-tuple-element.443), channel_id=1, source_target_pairs={{4,0},{5,1},{6,2},{7,3}} | collective-permute-start | bytes 1572872 | tf_op jit(solution)/shard_map/ppermute | solution.py:44
  96.9 11.7 %collective-permute-start.28 = (bf16[128,1280]{1,0:T(8,128)(2,1)S(1)}, bf16[128,1280]{1,0:T(8,128)(2,1)S(1)}, u32[]{:S(2)}, u32[]{:S(2)}) collective-permute-start(bf16[128,1280]{1,0:T(8,128)(2,1)S(1)} %get-tuple-element.494), channel_id=1, source_target_pairs={{0,3},{1,2},{2,1},{3,0},{4,7},{5,6},{6,5},{7,4},{8,11},{9,10},{10,... | collective-permute-start | bytes 983048 | tf_op jit(solution)/shard_map/ppermute | solution.py:44
  99.4 13.7 %collective-permute-start.29 = (bf16[128,1280]{1,0:T(8,128)(2,1)S(1)}, bf16[128,1280]{1,0:T(8,128)(2,1)S(1)}, u32[]{:S(2)}, u32[]{:S(2)}) collective-permute-start(bf16[128,1280]{1,0:T(8,128)(2,1)S(1)} %get-tuple-element.495), channel_id=1, source_target_pairs={{0,2},{1,3},{2,0},{3,1},{4,6},{5,7},{6,4},{7,5},{8,10},{9,11},{10,... | collective-permute-start | bytes 983048 | tf_op jit(solution)/shard_map/ppermute | solution.py:44
  100.5 12.7 %collective-permute-start.30 = (bf16[128,1280]{1,0:T(8,128)(2,1)S(1)}, bf16[128,1280]{1,0:T(8,128)(2,1)S(1)}, u32[]{:S(2)}, u32[]{:S(2)}) collective-permute-start(bf16[128,1280]{1,0:T(8,128)(2,1)S(1)} %get-tuple-element.496), channel_id=1, source_target_pairs={{0,1},{1,0},{2,3},{3,2},{4,5},{5,4},{6,7},{7,6},{8,9},{9,8},{10,11... | collective-permute-start | bytes 983048 | tf_op jit(solution)/shard_map/ppermute | solution.py:44
  (6 other events, 16.9 us)

commit v9 on v8

--- a/solution.py
+++ b/solution.py
@@ -680,7 +680,8 @@
             sent.append(hop(outs[1], stage, 2))
             side.append(hop(outs[0], stage))
             if stage == pairs[-1] and len(sent) == 1:
-                state, early = hold(state, early)
+                state, held = hold(state, early[:-1])
+                early = [*held, early[-1]]
         received = sent
         for asides, bound, block in waiting:
             base, _ = run_stage(asides, [bound], [block], state[:-1], False)

time: 116 us -> 115 us (level)
  waiting for transfers between devices: 48.1 us -> 46.6 us
    ppermute x31, waiting for transfers between devices: 48.1 us -> 46.6 us  [move(): return lax.ppermute(block, ('section', 'dp'), pairs)]
  transfers between devices with their start and end apart: 31 -> 31, of which waited for: 13 -> 14; matrix products, arithmetic and copies ran while one was open for 2% -> 2% of each run, Pallas kernels for 9% -> 9%
where the time goes in v9:
time: 115 us
  waiting for transfers between devices  46.6 us (41%)
  starting transfers between devices  41.8 us (36%)
  Pallas kernels  18.8 us (16%)
  local copies, waits for them, and re-layouts  4.68 us (4%)
  other arithmetic  1.54 us (1%)
    ppermute x31, waiting for transfers between devices, move(): return lax.ppermute(block, ('section', 'dp'), pairs)  46.6 us
    ppermute x31, starting transfers between devices, move(): return lax.ppermute(block, ('section', 'dp'), pairs)  41.8 us
    pallas_call x9, Pallas kernels, run_stage(): pl.pallas_call(functools.partial(stage_kernel, stage, bounds, size, len(s...  6.95 us
    unnamed x15, local copies, waits for them, and re-layouts  4.44 us
    pallas_call x1, Pallas kernels, per_device(): pl.pallas_call(functools.partial(keep_kernel, size, len(shards), more), o...  2.83 us
    pallas_call x4, Pallas kernels, run_pair(): pl.pallas_call(functools.partial(pair_kernel, stage, bound, size, len(sta...  2.47 us
  transfers between devices with their start and end apart: 31, of which 14 were waited for; matrix products, arithmetic and copies ran while one was open for 2% of the time, Pallas kernels for 9%

profile of v9, /device:TPU:0, one launch (start us, length us, event | category | flops | bytes accessed | tf_op | source)
XLA Modules:
  0.0 114.5 jit_solution(17049284114845196783)
XLA Ops:
  0.7 2.1 %shard_map.95 = (bf16[416,512]{1,0:T(8,128)(2,1)S(1)}, bf16[416,512]{1,0:T(8,128)(2,1)S(1)}, bf16[96,1024]{1,0:T(8,128)(2,1)S(1)}) custom-call(s32[5]{0:T(128)S(1)} %stack.35.flags.refs_0_, bf16[1,1024,256]{2,1,0:T(8,128)(2,1)} %down.1, bf16[1,256,1024]{2,1,0:T(8,128)(2,1)} %up.1, bf16[1024,128]{1,0:T(8,128)(2,1)} %readout.1), custom_call_target="tpu_custom_call" | custom-call | tf_op jit(solution)/shard_map/pallas_call | solution.py:498
  2.8 3.0 %collective-permute-start.2 = (bf16[416,512]{1,0:T(8,128)(2,1)S(1)}, bf16[416,512]{1,0:T(8,128)(2,1)S(1)}, u32[]{:S(2)}, u32[]{:S(2)}) collective-permute-start(bf16[416,512]{1,0:T(8,128)(2,1)S(1)} %get-tuple-element.255.refs_7_.refs_9_), channel_id=1, source_target_pairs={{0,2},{1,3},{2,0},{3,1},{4,6},{5,7},{6,4},{7,5},{8,10},{9,11},{10,... | collective-permute-start | bytes 1277960 | tf_op jit(solution)/shard_map/ppermute | solution.py:44
  5.8 1.5 %collective-permute-start.1 = (bf16[416,512]{1,0:T(8,128)(2,1)S(1)}, bf16[416,512]{1,0:T(8,128)(2,1)S(1)}, u32[]{:S(2)}, u32[]{:S(2)}) collective-permute-start(bf16[416,512]{1,0:T(8,128)(2,1)S(1)} %get-tuple-element.256.refs_8_.refs_10_), channel_id=1, source_target_pairs={{0,1},{1,0},{2,3},{3,2},{4,5},{5,4},{6,7},{7,6},{8,9},{9,8},{10,11... | collective-permute-start | bytes 1277960 | tf_op jit(solution)/shard_map/ppermute | solution.py:44
  7.3 2.4 %collective-permute-start.7 = (bf16[96,1024]{1,0:T(8,128)(2,1)S(1)}, bf16[96,1024]{1,0:T(8,128)(2,1)S(1)}, u32[]{:S(2)}, u32[]{:S(2)}) collective-permute-start(bf16[96,1024]{1,0:T(8,128)(2,1)S(1)} %get-tuple-element.266.refs_17_), channel_id=1, source_target_pairs={{0,1},{1,0},{2,3},{3,2},{4,5},{5,4},{6,7},{7,6},{8,9},{9,8},{10,11... | collective-permute-start | bytes 589832 | tf_op jit(solution)/shard_map/ppermute | solution.py:44
  9.8 1.6 %collective-permute-start = (bf16[416,512]{1,0:T(8,128)(2,1)S(1)}, bf16[416,512]{1,0:T(8,128)(2,1)S(1)}, u32[]{:S(2)}, u32[]{:S(2)}) collective-permute-start(bf16[416,512]{1,0:T(8,128)(2,1)S(1)} %get-tuple-element.255.refs_7_.refs_9_), channel_id=1, source_target_pairs={{0,1},{1,0},{2,3},{3,2},{4,5},{5,4},{6,7},{7,6},{8,9},{9,8},{10,11... | collective-permute-start | bytes 1277960 | tf_op jit(solution)/shard_map/ppermute | solution.py:44
  11.8 4.7 %collective-permute-done.2.refs_11_.refs_13_ = bf16[416,512]{1,0:T(8,128)(2,1)S(1)} collective-permute-done((bf16[416,512]{1,0:T(8,128)(2,1)S(1)}, bf16[416,512]{1,0:T(8,128)(2,1)S(1)}, u32[]{:S(2)}, u32[]{:S(2)}) %collective-permute-start.2) | collective-permute-done | bytes 426016 | tf_op jit(solution)/shard_map/ppermute | solution.py:44
  16.5 2.0 %collective-permute-start.4 = (bf16[416,512]{1,0:T(8,128)(2,1)S(1)}, bf16[416,512]{1,0:T(8,128)(2,1)S(1)}, u32[]{:S(2)}, u32[]{:S(2)}) collective-permute-start(bf16[416,512]{1,0:T(8,128)(2,1)S(1)} %collective-permute-done.2.refs_11_.refs_13_), channel_id=1, source_target_pairs={{0,1},{1,0},{2,3},{3,2},{4,5},{5,4},{6,7},{7,6},{8,9},{9,8},{10,11... | collective-permute-start | bytes 1277960 | tf_op jit(solution)/shard_map/ppermute | solution.py:44
  18.6 1.5 %collective-permute-start.5 = (bf16[416,512]{1,0:T(8,128)(2,1)S(1)}, bf16[416,512]{1,0:T(8,128)(2,1)S(1)}, u32[]{:S(2)}, u32[]{:S(2)}) collective-permute-start(bf16[416,512]{1,0:T(8,128)(2,1)S(1)} %collective-permute-done.1.refs_10_.refs_12_), channel_id=1, source_target_pairs={{0,2},{1,3},{2,0},{3,1},{4,6},{5,7},{6,4},{7,5},{8,10},{9,11},{10,... | collective-permute-start | bytes 1277960 | tf_op jit(solution)/shard_map/ppermute | solution.py:44
  20.0 2.8 %collective-permute-done.7.refs_18_ = bf16[96,1024]{1,0:T(8,128)(2,1)S(1)} collective-permute-done((bf16[96,1024]{1,0:T(8,128)(2,1)S(1)}, bf16[96,1024]{1,0:T(8,128)(2,1)S(1)}, u32[]{:S(2)}, u32[]{:S(2)}) %collective-permute-start.7) | collective-permute-done | bytes 196640 | tf_op jit(solution)/shard_map/ppermute | solution.py:44
  24.3 1.9 %collective-permute-start.8 = (bf16[192,1024]{1,0:T(8,128)(2,1)}, bf16[192,1024]{1,0:T(8,128)(2,1)}, u32[]{:S(2)}, u32[]{:S(2)}) collective-permute-start(bf16[192,1024]{1,0:T(8,128)(2,1)} %pad_maximum_fusion), channel_id=1, source_target_pairs={{0,2},{1,3},{2,0},{3,1},{4,6},{5,7},{6,4},{7,5},{8,10},{9,11},{10,... | collective-permute-start | bytes 1179656 | tf_op jit(solution)/shard_map/ppermute | solution.py:44
  27.0 1.2 %copy-done = bf16[1,128,4096]{2,1,0:T(8,128)(2,1)S(1)} copy-done((bf16[1,128,4096]{2,1,0:T(8,128)(2,1)S(1)}, bf16[1,128,4096]{2,1,0:T(8,128)(2,1)}, u32[]{:S(2)}) %copy-start) | copy-done | bytes 1048600
  30.5 1.4 %collective-permute-done.refs_9_.refs_11_ = bf16[416,512]{1,0:T(8,128)(2,1)S(1)} collective-permute-done((bf16[416,512]{1,0:T(8,128)(2,1)S(1)}, bf16[416,512]{1,0:T(8,128)(2,1)S(1)}, u32[]{:S(2)}, u32[]{:S(2)}) %collective-permute-start) | collective-permute-done | bytes 426016 | tf_op jit(solution)/shard_map/ppermute | solution.py:44
  31.9 7.7 %collective-permute-done.4.refs_13_.refs_15_ = bf16[416,512]{1,0:T(8,128)(2,1)S(1)} collective-permute-done((bf16[416,512]{1,0:T(8,128)(2,1)S(1)}, bf16[416,512]{1,0:T(8,128)(2,1)S(1)}, u32[]{:S(2)}, u32[]{:S(2)}) %collective-permute-start.4) | collective-permute-done | bytes 426016 | tf_op jit(solution)/shard_map/ppermute | solution.py:44
  40.2 2.2 %collective-permute-done.8.refs_19_ = bf16[192,1024]{1,0:T(8,128)(2,1)} collective-permute-done((bf16[192,1024]{1,0:T(8,128)(2,1)}, bf16[192,1024]{1,0:T(8,128)(2,1)}, u32[]{:S(2)}, u32[]{:S(2)}) %collective-permute-start.8) | collective-permute-done | bytes 393248 | tf_op jit(solution)/shard_map/ppermute | solution.py:44
  42.4 2.8 %shard_map.97 = (bf16[1,4096]{1,0:T(2,128)(2,1)S(1)}, f32[128,128]{1,0:T(8,128)S(1)}, f32[128,256]{1,0:T(8,128)S(1)}, bf16[128,4096]{1,0:T(8,128)(2,1)S(1)}, bf1...) custom-call(s32[5]{0:T(128)S(1)} %stack.35.flags.refs_0_, ...), custom_call_target="tpu_custom_call", output_to_operand_aliasing={{0}: (1, {}), {1}: (2, {}), {2}: (3, {}), {3}: (4, {}), {4}... | custom-call | tf_op jit(solution)/shard_map/pallas_call | solution.py:625
  45.3 1.1 collective-permute-start.10
  50.3 3.6 %collective-permute-start.13 = (bf16[128,1280]{1,0:T(8,128)(2,1)S(1)}, bf16[128,1280]{1,0:T(8,128)(2,1)S(1)}, u32[]{:S(2)}, u32[]{:S(2)}) collective-permute-start(bf16[128,1280]{1,0:T(8,128)(2,1)S(1)} %get-tuple-element.322), channel_id=1, source_target_pairs={{0,1},{1,0},{2,3},{3,2},{4,5},{5,4},{6,7},{7,6},{8,9},{9,8},{10,11... | collective-permute-start | bytes 983048 | tf_op jit(solution)/shard_map/ppermute | solution.py:44
  53.9 3.4 %collective-permute-start.14 = (bf16[128,1280]{1,0:T(8,128)(2,1)S(1)}, bf16[128,1280]{1,0:T(8,128)(2,1)S(1)}, u32[]{:S(2)}, u32[]{:S(2)}) collective-permute-start(bf16[128,1280]{1,0:T(8,128)(2,1)S(1)} %get-tuple-element.323), channel_id=1, source_target_pairs={{0,2},{1,3},{2,0},{3,1},{4,6},{5,7},{6,4},{7,5},{8,10},{9,11},{10,... | collective-permute-start | bytes 983048 | tf_op jit(solution)/shard_map/ppermute | solution.py:44
  58.7 2.0 %collective-permute-done.13.refs_2_ = bf16[128,1280]{1,0:T(8,128)(2,1)S(1)} collective-permute-done((bf16[128,1280]{1,0:T(8,128)(2,1)S(1)}, bf16[128,1280]{1,0:T(8,128)(2,1)S(1)}, u32[]{:S(2)}, u32[]{:S(2)}) %collective-permute-start.13) | collective-permute-done | bytes 327712 | tf_op jit(solution)/shard_map/ppermute | solution.py:44
  60.7 3.0 %collective-permute-done.14.refs_3_ = bf16[128,1280]{1,0:T(8,128)(2,1)S(1)} collective-permute-done((bf16[128,1280]{1,0:T(8,128)(2,1)S(1)}, bf16[128,1280]{1,0:T(8,128)(2,1)S(1)}, u32[]{:S(2)}, u32[]{:S(2)}) %collective-permute-start.14) | collective-permute-done | bytes 327712 | tf_op jit(solution)/shard_map/ppermute | solution.py:44
  66.6 3.4 %collective-permute-start.19 = (bf16[128,1280]{1,0:T(8,128)(2,1)S(1)}, bf16[128,1280]{1,0:T(8,128)(2,1)S(1)}, u32[]{:S(2)}, u32[]{:S(2)}) collective-permute-start(bf16[128,1280]{1,0:T(8,128)(2,1)S(1)} %get-tuple-element.410), channel_id=1, source_target_pairs={{0,3},{1,2},{2,1},{3,0},{4,7},{5,6},{6,5},{7,4},{8,11},{9,10},{10,... | collective-permute-start | bytes 983048 | tf_op jit(solution)/shard_map/ppermute | solution.py:44
  72.6 3.9 %collective-permute-done.19.refs_5_ = bf16[128,1280]{1,0:T(8,128)(2,1)S(1)} collective-permute-done((bf16[128,1280]{1,0:T(8,128)(2,1)S(1)}, bf16[128,1280]{1,0:T(8,128)(2,1)S(1)}, u32[]{:S(2)}, u32[]{:S(2)}) %collective-permute-start.19) | collective-permute-done | bytes 327712 | tf_op jit(solution)/shard_map/ppermute | solution.py:44
  81.2 0.9 shard_map.108
  82.7 1.3 %collective-permute-start.23 = (bf16[64,4096]{1,0:T(8,128)(2,1)S(1)}, bf16[64,4096]{1,0:T(8,128)(2,1)S(1)}, u32[]{:S(2)}, u32[]{:S(2)}) collective-permute-start(bf16[64,4096]{1,0:T(8,128)(2,1)S(1)} %get-tuple-element.424), channel_id=1, source_target_pairs={{4,0},{5,1},{6,2},{7,3}} | collective-permute-start | bytes 1572872 | tf_op jit(solution)/shard_map/ppermute | solution.py:44
  84.8 1.3 %collective-permute-start.25 = (bf16[64,4096]{1,0:T(8,128)(2,1)S(1)}, bf16[64,4096]{1,0:T(8,128)(2,1)S(1)}, u32[]{:S(2)}, u32[]{:S(2)}) collective-permute-start(bf16[64,4096]{1,0:T(8,128)(2,1)S(1)} %get-tuple-element.441), channel_id=1, source_target_pairs={{4,0},{5,1},{6,2},{7,3}} | collective-permute-start | bytes 1572872 | tf_op jit(solution)/shard_map/ppermute | solution.py:44
  88.2 6.1 %collective-permute-done.25.refs_2_ = bf16[64,4096]{1,0:T(8,128)(2,1)S(1)} collective-permute-done((bf16[64,4096]{1,0:T(8,128)(2,1)S(1)}, bf16[64,4096]{1,0:T(8,128)(2,1)S(1)}, u32[]{:S(2)}, u32[]{:S(2)}) %collective-permute-start.25) | collective-permute-done | bytes 524320 | tf_op jit(solution)/shard_map/ppermute | solution.py:44
  94.3 2.1 %shard_map.113 = (bf16[1,4096]{1,0:T(2,128)(2,1)S(1)}, f32[128,128]{1,0:T(8,128)S(1)}, f32[128,256]{1,0:T(8,128)S(1)}, bf16[128,4096]{1,0:T(8,128)(2,1)S(1)}, bf...) custom-call(s32[5]{0:T(128)S(1)} %stack.35.flags.refs_0_, ...), custom_call_target="tpu_custom_call", output_to_operand_aliasing={{0}: (3, {}), {1}: (4, {}), {2}: (5, {}), {3}: (6, {}), {4}... | custom-call | tf_op jit(solution)/shard_map/pallas_call | solution.py:585
  96.5 2.4 %collective-permute-start.28 = (bf16[128,1280]{1,0:T(8,128)(2,1)S(1)}, bf16[128,1280]{1,0:T(8,128)(2,1)S(1)}, u32[]{:S(2)}, u32[]{:S(2)}) collective-permute-start(bf16[128,1280]{1,0:T(8,128)(2,1)S(1)} %get-tuple-element.492), channel_id=1, source_target_pairs={{0,3},{1,2},{2,1},{3,0},{4,7},{5,6},{6,5},{7,4},{8,11},{9,10},{10,... | collective-permute-start | bytes 983048 | tf_op jit(solution)/shard_map/ppermute | solution.py:44
  100.0 1.0 copy.444
  101.0 7.1 %collective-permute-done.28.refs_1_ = bf16[128,1280]{1,0:T(8,128)(2,1)S(1)} collective-permute-done((bf16[128,1280]{1,0:T(8,128)(2,1)S(1)}, bf16[128,1280]{1,0:T(8,128)(2,1)S(1)}, u32[]{:S(2)}, u32[]{:S(2)}) %collective-permute-start.28) | collective-permute-done | bytes 327712 | tf_op jit(solution)/shard_map/ppermute | solution.py:44
  108.1 4.6 %collective-permute-done.29.refs_2_ = bf16[128,1280]{1,0:T(8,128)(2,1)S(1)} collective-permute-done((bf16[128,1280]{1,0:T(8,128)(2,1)S(1)}, bf16[128,1280]{1,0:T(8,128)(2,1)S(1)}, u32[]{:S(2)}, u32[]{:S(2)}) %collective-permute-start.29) | collective-permute-done | bytes 327712 | tf_op jit(solution)/shard_map/ppermute | solution.py:44
  112.8 1.7 %shard_map.114 = (bf16[1024,256]{1,0:T(8,128)(2,1)}, bf16[256,1024]{1,0:T(8,128)(2,1)}) custom-call(bf16[1280,512]{1,0:T(8,128)(2,1)S(1)} %get-tuple-element.490.left, bf16[128,1280]{1,0:T(8,128)(2,1)S(1)} %get-tuple-element.491.refs_0_, bf16[128,1280]{1,0:T(8,128)(2,1)S(1)} %collective-permute-done.28.refs_1_, ...), custom_call_target="tpu_custom_call" | custom-call | tf_op jit(solution)/shard_map/pallas_call | solution.py:715
  (71 shorter events, 25.7 us)
Async XLA Ops:
  2.8 13.7 %collective-permute-start.2 = (bf16[416,512]{1,0:T(8,128)(2,1)S(1)}, bf16[416,512]{1,0:T(8,128)(2,1)S(1)}, u32[]{:S(2)}, u32[]{:S(2)}) collective-permute-start(bf16[416,512]{1,0:T(8,128)(2,1)S(1)} %get-tuple-element.255.refs_7_.refs_9_), channel_id=1, source_target_pairs={{0,2},{1,3},{2,0},{3,1},{4,6},{5,7},{6,4},{7,5},{8,10},{9,11},{10,... | collective-permute-start | bytes 1277960 | tf_op jit(solution)/shard_map/ppermute | solution.py:44
  5.8 12.7 %collective-permute-start.1 = (bf16[416,512]{1,0:T(8,128)(2,1)S(1)}, bf16[416,512]{1,0:T(8,128)(2,1)S(1)}, u32[]{:S(2)}, u32[]{:S(2)}) collective-permute-start(bf16[416,512]{1,0:T(8,128)(2,1)S(1)} %get-tuple-element.256.refs_8_.refs_10_), channel_id=1, source_target_pairs={{0,1},{1,0},{2,3},{3,2},{4,5},{5,4},{6,7},{7,6},{8,9},{9,8},{10,11... | collective-permute-start | bytes 1277960 | tf_op jit(solution)/shard_map/ppermute | solution.py:44
  7.3 15.5 %collective-permute-start.7 = (bf16[96,1024]{1,0:T(8,128)(2,1)S(1)}, bf16[96,1024]{1,0:T(8,128)(2,1)S(1)}, u32[]{:S(2)}, u32[]{:S(2)}) collective-permute-start(bf16[96,1024]{1,0:T(8,128)(2,1)S(1)} %get-tuple-element.266.refs_17_), channel_id=1, source_target_pairs={{0,1},{1,0},{2,3},{3,2},{4,5},{5,4},{6,7},{7,6},{8,9},{9,8},{10,11... | collective-permute-start | bytes 589832 | tf_op jit(solution)/shard_map/ppermute | solution.py:44
  9.8 22.2 %collective-permute-start = (bf16[416,512]{1,0:T(8,128)(2,1)S(1)}, bf16[416,512]{1,0:T(8,128)(2,1)S(1)}, u32[]{:S(2)}, u32[]{:S(2)}) collective-permute-start(bf16[416,512]{1,0:T(8,128)(2,1)S(1)} %get-tuple-element.255.refs_7_.refs_9_), channel_id=1, source_target_pairs={{0,1},{1,0},{2,3},{3,2},{4,5},{5,4},{6,7},{7,6},{8,9},{9,8},{10,11... | collective-permute-start | bytes 1277960 | tf_op jit(solution)/shard_map/ppermute | solution.py:44
  11.3 20.6 %collective-permute-start.3 = (bf16[416,512]{1,0:T(8,128)(2,1)S(1)}, bf16[416,512]{1,0:T(8,128)(2,1)S(1)}, u32[]{:S(2)}, u32[]{:S(2)}) collective-permute-start(bf16[416,512]{1,0:T(8,128)(2,1)S(1)} %get-tuple-element.256.refs_8_.refs_10_), channel_id=1, source_target_pairs={{0,2},{1,3},{2,0},{3,1},{4,6},{5,7},{6,4},{7,5},{8,10},{9,11},{10,... | collective-permute-start | bytes 1277960 | tf_op jit(solution)/shard_map/ppermute | solution.py:44
  16.5 23.1 %collective-permute-start.4 = (bf16[416,512]{1,0:T(8,128)(2,1)S(1)}, bf16[416,512]{1,0:T(8,128)(2,1)S(1)}, u32[]{:S(2)}, u32[]{:S(2)}) collective-permute-start(bf16[416,512]{1,0:T(8,128)(2,1)S(1)} %collective-permute-done.2.refs_11_.refs_13_), channel_id=1, source_target_pairs={{0,1},{1,0},{2,3},{3,2},{4,5},{5,4},{6,7},{7,6},{8,9},{9,8},{10,11... | collective-permute-start | bytes 1277960 | tf_op jit(solution)/shard_map/ppermute | solution.py:44
  18.6 21.0 %collective-permute-start.5 = (bf16[416,512]{1,0:T(8,128)(2,1)S(1)}, bf16[416,512]{1,0:T(8,128)(2,1)S(1)}, u32[]{:S(2)}, u32[]{:S(2)}) collective-permute-start(bf16[416,512]{1,0:T(8,128)(2,1)S(1)} %collective-permute-done.1.refs_10_.refs_12_), channel_id=1, source_target_pairs={{0,2},{1,3},{2,0},{3,1},{4,6},{5,7},{6,4},{7,5},{8,10},{9,11},{10,... | collective-permute-start | bytes 1277960 | tf_op jit(solution)/shard_map/ppermute | solution.py:44
  24.3 18.2 %collective-permute-start.8 = (bf16[192,1024]{1,0:T(8,128)(2,1)}, bf16[192,1024]{1,0:T(8,128)(2,1)}, u32[]{:S(2)}, u32[]{:S(2)}) collective-permute-start(bf16[192,1024]{1,0:T(8,128)(2,1)} %pad_maximum_fusion), channel_id=1, source_target_pairs={{0,2},{1,3},{2,0},{3,1},{4,6},{5,7},{6,4},{7,5},{8,10},{9,11},{10,... | collective-permute-start | bytes 1179656 | tf_op jit(solution)/shard_map/ppermute | solution.py:44
  29.8 12.6 %copy-start.4 = (bf16[96,1024]{1,0:T(8,128)(2,1)S(1)}, bf16[96,1024]{1,0:T(8,128)(2,1)}, u32[]{:S(2)}) copy-start(bf16[96,1024]{1,0:T(8,128)(2,1)} %copy-done.3) | copy-start | bytes 589828
  45.3 12.1 %collective-permute-start.10 = (bf16[3136,1024]{1,0:T(8,128)(2,1)S(1)}, bf16[3136,1024]{1,0:T(8,128)(2,1)S(1)}, u32[]{:S(2)}, u32[]{:S(2)}) collective-permute-start(bf16[3136,1024]{1,0:T(8,128)(2,1)S(1)} %get-tuple-element.315), channel_id=1, source_target_pairs={{8,12},{9,13},{10,14},{11,15},{16,20},{17,21},{18,22},{19,23}} | collective-permute-start | bytes 19267592 | tf_op jit(solution)/shard_map/ppermute | solution.py:44
  46.4 0.7 collective-permute-start.6
  47.7 9.7 %collective-permute-start.9 = (bf16[64,4096]{1,0:T(8,128)(2,1)S(1)}, bf16[64,4096]{1,0:T(8,128)(2,1)S(1)}, u32[]{:S(2)}, u32[]{:S(2)}) collective-permute-start(bf16[64,4096]{1,0:T(8,128)(2,1)S(1)} %get-tuple-element.282), channel_id=1, source_target_pairs={{24,20},{25,21},{26,22},{27,23}} | collective-permute-start | bytes 1572872 | tf_op jit(solution)/shard_map/ppermute | solution.py:44
  49.0 14.8 %collective-permute-start.12 = (bf16[64,4096]{1,0:T(8,128)(2,1)S(1)}, bf16[64,4096]{1,0:T(8,128)(2,1)S(1)}, u32[]{:S(2)}, u32[]{:S(2)}) collective-permute-start(bf16[64,4096]{1,0:T(8,128)(2,1)S(1)} %get-tuple-element.317), channel_id=1, source_target_pairs={{24,20},{25,21},{26,22},{27,23}} | collective-permute-start | bytes 1572872 | tf_op jit(solution)/shard_map/ppermute | solution.py:44
  50.3 10.4 %collective-permute-start.13 = (bf16[128,1280]{1,0:T(8,128)(2,1)S(1)}, bf16[128,1280]{1,0:T(8,128)(2,1)S(1)}, u32[]{:S(2)}, u32[]{:S(2)}) collective-permute-start(bf16[128,1280]{1,0:T(8,128)(2,1)S(1)} %get-tuple-element.322), channel_id=1, source_target_pairs={{0,1},{1,0},{2,3},{3,2},{4,5},{5,4},{6,7},{7,6},{8,9},{9,8},{10,11... | collective-permute-start | bytes 983048 | tf_op jit(solution)/shard_map/ppermute | solution.py:44
  53.9 9.8 %collective-permute-start.14 = (bf16[128,1280]{1,0:T(8,128)(2,1)S(1)}, bf16[128,1280]{1,0:T(8,128)(2,1)S(1)}, u32[]{:S(2)}, u32[]{:S(2)}) collective-permute-start(bf16[128,1280]{1,0:T(8,128)(2,1)S(1)} %get-tuple-element.323), channel_id=1, source_target_pairs={{0,2},{1,3},{2,0},{3,1},{4,6},{5,7},{6,4},{7,5},{8,10},{9,11},{10,... | collective-permute-start | bytes 983048 | tf_op jit(solution)/shard_map/ppermute | solution.py:44
  58.0 12.0 %collective-permute-start.11 = (bf16[64,4096]{1,0:T(8,128)(2,1)S(1)}, bf16[64,4096]{1,0:T(8,128)(2,1)S(1)}, u32[]{:S(2)}, u32[]{:S(2)}) collective-permute-start(bf16[64,4096]{1,0:T(8,128)(2,1)S(1)} %get-tuple-element.316), channel_id=1, source_target_pairs={{20,12},{21,13},{22,14},{23,15}} | collective-permute-start | bytes 1572872 | tf_op jit(solution)/shard_map/ppermute | solution.py:44
  64.5 6.8 %collective-permute-start.18 = (bf16[64,4096]{1,0:T(8,128)(2,1)S(1)}, bf16[64,4096]{1,0:T(8,128)(2,1)S(1)}, u32[]{:S(2)}, u32[]{:S(2)}) collective-permute-start(bf16[64,4096]{1,0:T(8,128)(2,1)S(1)} %get-tuple-element.357), channel_id=1, source_target_pairs={{20,12},{21,13},{22,14},{23,15}} | collective-permute-start | bytes 1572872 | tf_op jit(solution)/shard_map/ppermute | solution.py:44
  65.2 12.0 %collective-permute-start.16 = (bf16[64,4096]{1,0:T(8,128)(2,1)S(1)}, bf16[64,4096]{1,0:T(8,128)(2,1)S(1)}, u32[]{:S(2)}, u32[]{:S(2)}) collective-permute-start(bf16[64,4096]{1,0:T(8,128)(2,1)S(1)} %get-tuple-element.355), channel_id=1, source_target_pairs={{20,16},{21,17},{22,18},{23,19}} | collective-permute-start | bytes 1572872 | tf_op jit(solution)/shard_map/ppermute | solution.py:44
  65.9 12.0 %collective-permute-start.17 = (bf16[64,4096]{1,0:T(8,128)(2,1)S(1)}, bf16[64,4096]{1,0:T(8,128)(2,1)S(1)}, u32[]{:S(2)}, u32[]{:S(2)}) collective-permute-start(bf16[64,4096]{1,0:T(8,128)(2,1)S(1)} %get-tuple-element.356), channel_id=1, source_target_pairs={{20,16},{21,17},{22,18},{23,19}} | collective-permute-start | bytes 1572872 | tf_op jit(solution)/shard_map/ppermute | solution.py:44
  66.6 9.9 %collective-permute-start.19 = (bf16[128,1280]{1,0:T(8,128)(2,1)S(1)}, bf16[128,1280]{1,0:T(8,128)(2,1)S(1)}, u32[]{:S(2)}, u32[]{:S(2)}) collective-permute-start(bf16[128,1280]{1,0:T(8,128)(2,1)S(1)} %get-tuple-element.410), channel_id=1, source_target_pairs={{0,3},{1,2},{2,1},{3,0},{4,7},{5,6},{6,5},{7,4},{8,11},{9,10},{10,... | collective-permute-start | bytes 983048 | tf_op jit(solution)/shard_map/ppermute | solution.py:44
  70.6 11.5 %collective-permute-start.15 = (bf16[64,4096]{1,0:T(8,128)(2,1)S(1)}, bf16[64,4096]{1,0:T(8,128)(2,1)S(1)}, u32[]{:S(2)}, u32[]{:S(2)}) collective-permute-start(bf16[64,4096]{1,0:T(8,128)(2,1)S(1)} %get-tuple-element.354), channel_id=1, source_target_pairs={{12,4},{13,5},{14,6},{15,7}} | collective-permute-start | bytes 1572872 | tf_op jit(solution)/shard_map/ppermute | solution.py:44
  71.9 12.1 %collective-permute-start.24 = (bf16[64,4096]{1,0:T(8,128)(2,1)S(1)}, bf16[64,4096]{1,0:T(8,128)(2,1)S(1)}, u32[]{:S(2)}, u32[]{:S(2)}) collective-permute-start(bf16[64,4096]{1,0:T(8,128)(2,1)S(1)} %get-tuple-element.425), channel_id=1, source_target_pairs={{12,4},{13,5},{14,6},{15,7}} | collective-permute-start | bytes 1572872 | tf_op jit(solution)/shard_map/ppermute | solution.py:44
  76.5 3.2 %collective-permute-start.20 = (bf16[128,1280]{1,0:T(8,128)(2,1)S(1)}, bf16[128,1280]{1,0:T(8,128)(2,1)S(1)}, u32[]{:S(2)}, u32[]{:S(2)}) collective-permute-start(bf16[128,1280]{1,0:T(8,128)(2,1)S(1)} %get-tuple-element.322), channel_id=1, source_target_pairs={{16,17},{17,16},{18,19},{19,18},{20,21},{21,20},{22,23},{23,22},{2... | collective-permute-start | bytes 983048 | tf_op jit(solution)/shard_map/ppermute | solution.py:44
  77.2 3.3 %collective-permute-start.21 = (bf16[128,1280]{1,0:T(8,128)(2,1)S(1)}, bf16[128,1280]{1,0:T(8,128)(2,1)S(1)}, u32[]{:S(2)}, u32[]{:S(2)}) collective-permute-start(bf16[128,1280]{1,0:T(8,128)(2,1)S(1)} %get-tuple-element.323), channel_id=1, source_target_pairs={{16,18},{17,19},{18,16},{19,17},{20,22},{21,23},{22,20},{23,21},{2... | collective-permute-start | bytes 983048 | tf_op jit(solution)/shard_map/ppermute | solution.py:44
  77.9 3.3 %collective-permute-start.22 = (bf16[128,1280]{1,0:T(8,128)(2,1)S(1)}, bf16[128,1280]{1,0:T(8,128)(2,1)S(1)}, u32[]{:S(2)}, u32[]{:S(2)}) collective-permute-start(bf16[128,1280]{1,0:T(8,128)(2,1)S(1)} %get-tuple-element.410), channel_id=1, source_target_pairs={{16,19},{17,18},{18,17},{19,16},{20,23},{21,22},{22,21},{23,20},{2... | collective-permute-start | bytes 983048 | tf_op jit(solution)/shard_map/ppermute | solution.py:44
  79.7 7.0 %collective-permute-start.26 = (bf16[64,4096]{1,0:T(8,128)(2,1)S(1)}, bf16[64,4096]{1,0:T(8,128)(2,1)S(1)}, u32[]{:S(2)}, u32[]{:S(2)}) collective-permute-start(bf16[64,4096]{1,0:T(8,128)(2,1)S(1)} %get-tuple-element.442), channel_id=1, source_target_pairs={{12,8},{13,9},{14,10},{15,11}} | collective-permute-start | bytes 1572872 | tf_op jit(solution)/shard_map/ppermute | solution.py:44
  80.4 5.7 %collective-permute-start.27 = (bf16[64,4096]{1,0:T(8,128)(2,1)S(1)}, bf16[64,4096]{1,0:T(8,128)(2,1)S(1)}, u32[]{:S(2)}, u32[]{:S(2)}) collective-permute-start(bf16[64,4096]{1,0:T(8,128)(2,1)S(1)} %get-tuple-element.443), channel_id=1, source_target_pairs={{12,8},{13,9},{14,10},{15,11}} | collective-permute-start | bytes 1572872 | tf_op jit(solution)/shard_map/ppermute | solution.py:44
  82.7 5.5 %collective-permute-start.23 = (bf16[64,4096]{1,0:T(8,128)(2,1)S(1)}, bf16[64,4096]{1,0:T(8,128)(2,1)S(1)}, u32[]{:S(2)}, u32[]{:S(2)}) collective-permute-start(bf16[64,4096]{1,0:T(8,128)(2,1)S(1)} %get-tuple-element.424), channel_id=1, source_target_pairs={{4,0},{5,1},{6,2},{7,3}} | collective-permute-start | bytes 1572872 | tf_op jit(solution)/shard_map/ppermute | solution.py:44
  84.8 9.5 %collective-permute-start.25 = (bf16[64,4096]{1,0:T(8,128)(2,1)S(1)}, bf16[64,4096]{1,0:T(8,128)(2,1)S(1)}, u32[]{:S(2)}, u32[]{:S(2)}) collective-permute-start(bf16[64,4096]{1,0:T(8,128)(2,1)S(1)} %get-tuple-element.441), channel_id=1, source_target_pairs={{4,0},{5,1},{6,2},{7,3}} | collective-permute-start | bytes 1572872 | tf_op jit(solution)/shard_map/ppermute | solution.py:44
  96.5 11.7 %collective-permute-start.28 = (bf16[128,1280]{1,0:T(8,128)(2,1)S(1)}, bf16[128,1280]{1,0:T(8,128)(2,1)S(1)}, u32[]{:S(2)}, u32[]{:S(2)}) collective-permute-start(bf16[128,1280]{1,0:T(8,128)(2,1)S(1)} %get-tuple-element.492), channel_id=1, source_target_pairs={{0,3},{1,2},{2,1},{3,0},{4,7},{5,6},{6,5},{7,4},{8,11},{9,10},{10,... | collective-permute-start | bytes 983048 | tf_op jit(solution)/shard_map/ppermute | solution.py:44
  98.9 13.8 %collective-permute-start.29 = (bf16[128,1280]{1,0:T(8,128)(2,1)S(1)}, bf16[128,1280]{1,0:T(8,128)(2,1)S(1)}, u32[]{:S(2)}, u32[]{:S(2)}) collective-permute-start(bf16[128,1280]{1,0:T(8,128)(2,1)S(1)} %get-tuple-element.493), channel_id=1, source_target_pairs={{0,2},{1,3},{2,0},{3,1},{4,6},{5,7},{6,4},{7,5},{8,10},{9,11},{10,... | collective-permute-start | bytes 983048 | tf_op jit(solution)/shard_map/ppermute | solution.py:44
  99.4 13.4 %collective-permute-start.30 = (bf16[128,1280]{1,0:T(8,128)(2,1)S(1)}, bf16[128,1280]{1,0:T(8,128)(2,1)S(1)}, u32[]{:S(2)}, u32[]{:S(2)}) collective-permute-start(bf16[128,1280]{1,0:T(8,128)(2,1)S(1)} %get-tuple-element.494), channel_id=1, source_target_pairs={{0,1},{1,0},{2,3},{3,2},{4,5},{5,4},{6,7},{7,6},{8,9},{9,8},{10,11... | collective-permute-start | bytes 983048 | tf_op jit(solution)/shard_map/ppermute | solution.py:44
  (6 other events, 16.9 us)
